TPU v7x, 32 devices: a whole 2x2x4 slice. The times are simulated.
32 devices in a mesh: lon: 8 (over z, y), lat: 2 (over x), section: 2 (over core).
Axes of the slice: x: 2, y: 2, z: 4, core: 2. Of those that a mesh axis runs over, the one named last changes fastest.
Arguments:
- upper_fields: bfloat16 [5, 6, 48, 384], P(None, None, 'lat', 'lon'), may hold values from -6 to 6
- surface_fields: bfloat16 [4, 48, 384], P(None, 'lat', 'lon'), may hold values from -6 to 6
- upper_embed: bfloat16 [160, 192], replicated, may hold values from -0.5 to 0.5
- surface_embed: bfloat16 [64, 192], replicated, may hold values from -0.75 to 0.75
- norm_gains: float32 [2, 2, 192], replicated, may hold values from 0.1 to 1.9
- qkv_weight: bfloat16 [2, 192, 576], replicated, may hold values from -0.4375 to 0.4375
- proj_weight: bfloat16 [2, 192, 192], replicated, may hold values from -0.4375 to 0.4375
- up_weight: bfloat16 [2, 192, 768], replicated, may hold values from -0.4375 to 0.4375
- down_weight: bfloat16 [2, 768, 192], replicated, may hold values from -0.21875 to 0.21875
- earth_bias: float32 [2, 2, 2, 6, 3312], P(None, 'lat', 'section'), may hold values from -4 to 402
- out_grad: bfloat16 [4, 12, 96, 192], P('section', 'lat', 'lon'), may hold values from -6 to 6
Outputs:
- latent_grad: bfloat16 [4, 12, 96, 192], P('section', 'lat', 'lon')
- upper_embed_grad: float32 [160, 192], replicated
- surface_embed_grad: float32 [64, 192], replicated
All inputs are finite; a program needn't handle non-finite values.
Results may differ from a plain program's by a relative error of at most 0.024.
Values may be sent and summed in bfloat16 or wider, within the bound.
No kernel may reach another device: no remote copies, remote signals or barrier semaphores. Data moves between devices by JAX's collectives and lax.ppermute only.
A program may use at most 64 MiB of HBM per device.

v0:
```python
import jax
import jax.numpy as jnp
import numpy as np
from jax import lax
from jax.sharding import PartitionSpec as P

neg_fill = -1e30
norm_eps = 1e-05


def shifted(block, axis, distance):
    devices = range(lax.axis_size(axis))
    route = [((i - distance) % len(devices), i) for i in devices]
    return lax.ppermute(block, axis, route)


def layer_norm(values, gain):
    average = jnp.mean(values, -1, keepdims=True)
    centred = values - average
    variance = jnp.mean(centred * centred, -1, keepdims=True)
    return centred * lax.rsqrt(variance + norm_eps) * gain


def exact_gelu(values):
    return jax.nn.gelu(values, approximate=False)


def pinned_round(values):
    return lax.optimization_barrier(values.astype(jnp.bfloat16)).astype(jnp.float32)


def make_patches(upper_fields, surface_fields):
    up_vars, raw_levels, raw_rows, raw_cols = upper_fields.shape
    upper_patch = upper_fields.reshape(
        up_vars, raw_levels // 2, 2, raw_rows // 4, 4, raw_cols // 4, 4
    )
    upper_patch = upper_patch.transpose(1, 3, 5, 0, 2, 4, 6).reshape(
        raw_levels // 2, raw_rows // 4, raw_cols // 4, up_vars * 32
    )
    sf_vars = surface_fields.shape[0]
    surface_patch = surface_fields.reshape(sf_vars, raw_rows // 4, 4, raw_cols // 4, 4)
    surface_patch = surface_patch.transpose(1, 3, 0, 2, 4).reshape(
        raw_rows // 4, raw_cols // 4, sf_vars * 16
    )
    return (upper_patch, surface_patch)


def to_windows(volume):
    levels, rows, cols, channels = volume.shape
    split = volume.reshape(levels // 2, 2, rows // 6, 6, cols // 12, 12, channels)
    return split.transpose(0, 2, 4, 1, 3, 5, 6).reshape(
        levels // 2, rows // 6, cols // 12, 144, channels
    )


def from_windows(windows):
    zone_z, zone_lat, zone_lon, cells, channels = windows.shape
    split = windows.reshape(zone_z, zone_lat, zone_lon, 2, 6, 12, channels)
    return split.transpose(0, 3, 1, 4, 2, 5, 6).reshape(
        zone_z * 2, zone_lat * 6, zone_lon * 12, channels
    )


def bias_index():
    token = np.arange(144)
    level_part = token // 72
    row_part = token // 12 % 6
    col_part = token % 12
    pair = (
        (level_part[:, None] * 2 + level_part[None, :]) * 36
        + row_part[:, None] * 6
        + row_part[None, :]
    )
    return pair * 23 + col_part[:, None] - col_part[None, :] + 11


def window_bias(table):
    return table[..., bias_index()]


def region_valid(level_base, row_base, levels_total, rows_total, zone_z, zone_lat):
    level = level_base + jnp.arange(zone_z * 2, dtype=jnp.int32)
    row = row_base + jnp.arange(zone_lat * 6, dtype=jnp.int32)
    zone_level = (level >= levels_total - 2).astype(jnp.int32) + (level >= levels_total - 1).astype(
        jnp.int32
    )
    zone_row = (row >= rows_total - 6).astype(jnp.int32) + (row >= rows_total - 3).astype(jnp.int32)
    labels = zone_level.reshape(zone_z, 1, 2, 1, 1) * 3 + zone_row.reshape(1, zone_lat, 1, 6, 1)
    labels = (labels + jnp.zeros((1, 1, 1, 1, 12), jnp.int32)).reshape(zone_z, zone_lat, 144)
    return labels[:, :, :, None] == labels[:, :, None, :]


def attention_forward(qkv_win, bias, allowed):
    zone_z, zone_lat, zone_lon, cells, channels = qkv_win.shape
    head_count = bias.shape[2]
    head_size = channels // (3 * head_count)
    parts = qkv_win.reshape(zone_z, zone_lat, zone_lon, cells, 3, head_count, head_size)
    query = parts[:, :, :, :, 0]
    keys_all = parts[:, :, :, :, 1]
    values_all = parts[:, :, :, :, 2]
    score = jnp.einsum("zlwqhd,zlwkhd->zlwhqk", query, keys_all, preferred_element_type=jnp.float32)
    score = score * head_size ** (-0.5) + bias[:, :, None]
    score = jnp.where(allowed[:, :, None, None], score, neg_fill)
    highest = jnp.max(score, -1, keepdims=True)
    expo = jnp.exp(score - highest)
    prob = expo / jnp.sum(expo, -1, keepdims=True)
    weights = prob.astype(jnp.bfloat16)
    mixed = jnp.einsum(
        "zlwhqk,zlwkhd->zlwqhd", weights, values_all, preferred_element_type=jnp.float32
    )
    mixed = mixed.astype(jnp.bfloat16).reshape(zone_z, zone_lat, zone_lon, cells, channels // 3)
    return (mixed, (query, keys_all, values_all, prob, weights))


def attention_backward(dmixed_win, saved):
    query, keys_all, values_all, prob, weights = saved
    head_size = query.shape[-1]
    dmixed = dmixed_win.reshape(query.shape)
    dweights = jnp.einsum(
        "zlwqhd,zlwkhd->zlwhqk", dmixed, values_all, preferred_element_type=jnp.float32
    )
    dweights = pinned_round(dweights)
    dvalues = jnp.einsum(
        "zlwhqk,zlwqhd->zlwkhd", weights, dmixed, preferred_element_type=jnp.float32
    )
    inner = jnp.sum(dweights * prob, -1, keepdims=True)
    dscore = prob * (dweights - inner) * head_size ** (-0.5)
    dquery = jnp.einsum(
        "zlwhqk,zlwkhd->zlwqhd",
        dscore,
        keys_all.astype(jnp.float32),
        precision=lax.Precision.HIGHEST,
    )
    dkeys = jnp.einsum(
        "zlwhqk,zlwqhd->zlwkhd", dscore, query.astype(jnp.float32), precision=lax.Precision.HIGHEST
    )
    stacked = jnp.stack((dquery, dkeys, dvalues), 4).astype(jnp.bfloat16)
    shape = stacked.shape
    return stacked.reshape(shape[0], shape[1], shape[2], shape[3], shape[4] * shape[5] * shape[6])


def block_forward(volume, params, bias, allowed, final):
    gains, w_qkv, w_proj, w_up, w_down = params
    levels, rows, cols, width = volume.shape
    inputs = volume.reshape(-1, width).astype(jnp.float32)
    hidden = layer_norm(inputs, gains[0]).astype(jnp.bfloat16)
    qkv_rows = jnp.dot(hidden, w_qkv, preferred_element_type=jnp.float32).astype(jnp.bfloat16)
    qkv_win = to_windows(qkv_rows.reshape(levels, rows, cols, 3 * width))
    mixed_win, attend_saved = attention_forward(qkv_win, bias, allowed)
    mixed = from_windows(mixed_win).reshape(-1, width)
    resid = inputs + jnp.dot(mixed, w_proj, preferred_element_type=jnp.float32)
    normed = layer_norm(resid, gains[1]).astype(jnp.bfloat16)
    upward = jnp.dot(normed, w_up, preferred_element_type=jnp.float32)
    active = exact_gelu(upward).astype(jnp.bfloat16)
    saved = (volume.shape, inputs, attend_saved, resid, upward)
    if final:
        return (None, saved)
    output = resid + jnp.dot(active, w_down, preferred_element_type=jnp.float32)
    return (output.astype(jnp.bfloat16).reshape(volume.shape), saved)


def block_backward(dvolume, saved, params):
    gains, w_qkv, w_proj, w_up, w_down = params
    shape, inputs, attend_saved, resid, upward = saved
    levels, rows, cols, width = shape
    dflat = dvolume.reshape(-1, width)
    dactive = pinned_round(jnp.dot(dflat, w_down.T, preferred_element_type=jnp.float32))
    dupward = jax.vjp(exact_gelu, upward)[1](dactive)[0]
    dnormed = jnp.dot(dupward, w_up.astype(jnp.float32).T, precision=lax.Precision.HIGHEST)
    dnormed = pinned_round(dnormed)
    dresid = dflat.astype(jnp.float32) + jax.vjp(layer_norm, resid, gains[1])[1](dnormed)[0]
    dmixed = jnp.dot(dresid, w_proj.astype(jnp.float32).T, precision=lax.Precision.HIGHEST).astype(
        jnp.bfloat16
    )
    dqkv_win = attention_backward(
        to_windows(dmixed.reshape(levels, rows, cols, width)), attend_saved
    )
    dqkv = from_windows(dqkv_win).reshape(-1, 3 * width)
    dhidden = pinned_round(jnp.dot(dqkv, w_qkv.T, preferred_element_type=jnp.float32))
    dinputs = dresid + jax.vjp(layer_norm, inputs, gains[0])[1](dhidden)[0]
    return dinputs.astype(jnp.bfloat16).reshape(shape)


def move_edge(volume, axis_dim, edge_depth, direction, sender):
    length = volume.shape[axis_dim]
    if direction > 0:
        border = lax.slice_in_dim(volume, 0, edge_depth, axis=axis_dim)
        remain = lax.slice_in_dim(volume, edge_depth, length, axis=axis_dim)
        return jnp.concatenate((remain, sender(border)), axis_dim)
    border = lax.slice_in_dim(volume, length - edge_depth, length, axis=axis_dim)
    remain = lax.slice_in_dim(volume, 0, length - edge_depth, axis=axis_dim)
    return jnp.concatenate((sender(border), remain), axis_dim)


def roll_rows_levels(volume, direction):
    volume = move_edge(volume, 1, 3, direction, lambda border: shifted(border, "lat", -direction))
    return move_edge(volume, 0, 1, direction, lambda border: shifted(border, "section", -direction))


def roll_columns(volume, direction):
    return move_edge(volume, 2, 6, direction, lambda border: shifted(border, "lon", -direction))


def to_shifted(volume):
    volume = roll_rows_levels(volume, 1)
    return roll_columns(volume, 1)


def on_device(
    upper_fields,
    surface_fields,
    upper_embed,
    surface_embed,
    norm_gains,
    qkv_weight,
    proj_weight,
    up_weight,
    down_weight,
    earth_bias,
    out_grad,
):
    section_index = lax.axis_index("section")
    band_index = lax.axis_index("lat")
    level_count, row_count, column_count, width = out_grad.shape
    levels_total = level_count * lax.axis_size("section")
    rows_total = row_count * lax.axis_size("lat")
    upper_patch, surface_patch = make_patches(upper_fields, surface_fields)
    upper_latent = jnp.einsum(
        "zyxp,pc->zyxc", upper_patch, upper_embed, preferred_element_type=jnp.float32
    )
    surface_latent = jnp.einsum(
        "yxp,pc->yxc", surface_patch, surface_embed, preferred_element_type=jnp.float32
    )
    latent_all = jnp.concatenate((surface_latent[None], upper_latent), 0).astype(jnp.bfloat16)
    latent = lax.dynamic_slice_in_dim(latent_all, section_index * level_count, level_count, 0)
    zone_z = level_count // 2
    zone_lat = row_count // 6
    params_first = (norm_gains[0], qkv_weight[0], proj_weight[0], up_weight[0], down_weight[0])
    params_second = (norm_gains[1], qkv_weight[1], proj_weight[1], up_weight[1], down_weight[1])
    bias_first = window_bias(earth_bias[0].transpose(1, 0, 2, 3))
    bias_second = window_bias(earth_bias[1].transpose(1, 0, 2, 3))
    allow_all = jnp.ones((zone_z, zone_lat, 144, 144), jnp.bool_)
    allow_shifted = region_valid(
        section_index * level_count,
        band_index * row_count,
        levels_total,
        rows_total,
        zone_z,
        zone_lat,
    )
    first_out, first_saved = block_forward(latent, params_first, bias_first, allow_all, False)
    unused_out, second_saved = block_forward(
        to_shifted(first_out), params_second, bias_second, allow_shifted, True
    )
    dshifted = block_backward(to_shifted(out_grad), second_saved, params_second)
    dshifted = roll_columns(dshifted, -1)
    dmiddle = roll_rows_levels(dshifted, -1)
    latent_grad = block_backward(dmiddle, first_saved, params_first)
    spread_grad = jnp.zeros((levels_total, row_count, column_count, width), jnp.bfloat16)
    spread_grad = lax.dynamic_update_slice_in_dim(
        spread_grad, latent_grad, section_index * level_count, 0
    )
    upper_terms = jnp.einsum(
        "zyxp,zyxc->pc", upper_patch, spread_grad[1:], preferred_element_type=jnp.float32
    )
    surface_terms = jnp.einsum(
        "yxp,yxc->pc", surface_patch, spread_grad[0], preferred_element_type=jnp.float32
    )
    upper_total, surface_total = lax.psum((upper_terms, surface_terms), ("lon", "lat", "section"))
    scale = float(levels_total * rows_total * column_count * lax.axis_size("lon")) ** (-0.5)
    return (latent_grad, upper_total * scale, surface_total * scale)


def solution(mesh):
    placed = (
        P(None, None, "lat", "lon"),
        P(None, "lat", "lon"),
        P(),
        P(),
        P(),
        P(),
        P(),
        P(),
        P(),
        P(None, "lat", "section", None, None),
        P("section", "lat", "lon", None),
    )
    return jax.shard_map(
        on_device,
        mesh=mesh,
        in_specs=placed,
        out_specs=(P("section", "lat", "lon", None), P(), P()),
        check_vma=False,
    )
```

profile of v0, /device:TPU:0, one launch (start us, length us, event | category | flops | bytes accessed | tf_op | source)
XLA Modules:
  0.0 377.4 jit_solution(17686953681352184549)
XLA Ops:
  7.2 3.6 reshape.639
  10.9 5.5 %copy.49 = bf16[3,6,12,5,2,4,4]{2,6,5,4,3,1,0:T(4,128)(2,1)} copy(bf16[3,6,12,5,2,4,4]{6,2,5,1,4,0,3:T(8,128)(2,1)S(1)} %bitcast.209) | data formatting | bytes 138240 | tf_op jit(solution)/shard_map/transpose | solution.py:37
  18.1 1.5 convolution_convert_fusion.6
  21.6 1.4 fusion.265
  25.9 38.7 %gather_fusion = f32[20736,6]{1,0:T(8,128)} fusion(f32[6,3312]{0,1:T(8,128)S(1)} %bitcast.205, s32[21504]{0:T(1024)S(1)} %pad_clamp_fusion), kind=kCustom, calls=%fused_computation | custom fusion | bytes 1078272 | tf_op jit(solution)/shard_map/gather | solution.py:78
  64.6 11.7 %copy.54 = f32[144,144,6]{0,1,2:T(8,128)S(1)} copy(f32[144,144,6]{2,1,0:T(8,128)} %bitcast.208) | data formatting | bytes 995328 | tf_op jit(solution)/shard_map/gather | solution.py:78
  78.7 2.1 fusion.48
  81.7 2.9 collective-permute-start.3
  86.9 38.7 %gather_fusion.1 = f32[20736,6]{1,0:T(8,128)} fusion(f32[6,3312]{0,1:T(8,128)S(1)} %bitcast.206, s32[21504]{0:T(1024)S(1)} %pad_clamp_fusion), kind=kCustom, calls=%fused_computation.1 | custom fusion | bytes 1078272 | tf_op jit(solution)/shard_map/gather | solution.py:78
  125.6 11.7 %copy.59 = f32[144,144,6]{0,1,2:T(8,128)S(1)} copy(f32[144,144,6]{2,1,0:T(8,128)} %bitcast.207) | data formatting | bytes 995328 | tf_op jit(solution)/shard_map/gather | solution.py:78
  139.7 5.1 %collective-permute-start.5 = (bf16[2,6,6,192]{3,2,1,0:T(8,128)(2,1)S(1)}, bf16[2,6,6,192]{3,2,1,0:T(8,128)(2,1)S(1)}, u32[]{:S(2)}, u32[]{:S(2)}) collective-permute-start(bf16[2,6,6,192]{3,2,1,0:T(8,128)(2,1)S(1)} %get-tuple-element.24), channel_id=1, source_target_pairs={{4,0},{8,4},{12,8},{16,12},{20,16},{24,20},{28,24},{0,28},{5,1},{9... | collective-permute-start | bytes 82952 | tf_op jit(solution)/shard_map/ppermute | solution.py:14
  153.1 1.2 convolution_convert_fusion.3
  154.3 1.2 fusion.123
  155.5 2.4 convolution_convert_fusion.18
  158.9 1.2 fusion.9
  160.1 1.4 fusion.19
  161.5 2.4 fusion.12
  163.9 2.6 fusion.13
  168.6 1.3 convolution_convert_fusion.17
  174.0 6.0 %collective-permute-done.6 = bf16[2,6,6,192]{3,2,1,0:T(8,128)(2,1)S(1)} collective-permute-done((bf16[2,6,6,192]{3,2,1,0:T(8,128)(2,1)S(1)}, bf16[2,6,6,192]{3,2,1,0:T(8,128)(2,1)S(1)}, u32[]{:S(2)}, u32[]{:S(2)}) %collective-permute-start.6) | collective-permute-done | bytes 27680 | tf_op jit(solution)/shard_map/ppermute | solution.py:14
  180.0 1.6 collective-permute-start.7
  181.6 2.6 collective-permute-done.7
  187.0 1.2 convolution_convert_fusion.2
  188.2 1.8 convolution_convert_fusion.16
  192.6 1.3 convolution_convert_fusion.19
  194.6 1.3 fusion.10
  196.7 2.1 fusion.14
  198.8 2.2 fusion.15
  201.0 1.2 fusion.17
  208.4 37.6 %psum.15 = f32[64,192]{1,0:T(8,128)S(1)} all-reduce(f32[64,192]{1,0:T(8,128)S(1)} %convolution_bitcast_fusion.1), channel_id=1, replica_groups=mesh['lon'=8,'lat'=2,'section'=2] {'lon','lat','section'}, use_global_device_ids=true, to_apply=%region_23.24 | all-reduce | flops 12288 | bytes 98304 | tf_op jit(solution)/shard_map/psum | solution.py:269
  247.4 121.6 %all-reduce.2.cloned.1.call-done = f32[160,192]{1,0:T(8,128)} async-done(((f32[160,192]{1,0:T(8,128)}), f32[160,192]{1,0:T(8,128)}) %all-reduce.2.cloned.1.call-update) | async-done | bytes 122896 | tf_op jit(solution)/shard_map/psum | solution.py:269
  369.0 1.6 broadcast_multiply_fusion
  (186 shorter events, 44.0 us)
Async XLA Ops:
  7.2 11.0 %copy-start = (bf16[160,192]{1,0:T(8,128)(2,1)S(1)}, bf16[160,192]{1,0:T(8,128)(2,1)}, u32[]{:S(2)}) copy-start(bf16[160,192]{1,0:T(8,128)(2,1)} %param.17) | copy-start | bytes 184324
  7.2 17.2 %copy-start.17 = (f32[2,1,1,6,3312]{4,2,3,1,0:T(1,128)S(1)}, f32[2,1,1,6,3312]{4,2,3,1,0:T(1,128)}, u32[]{:S(2)}) copy-start(f32[2,1,1,6,3312]{4,2,3,1,0:T(1,128)} %param.24) | copy-start | bytes 476932
  7.2 361.8 %all-reduce.2.cloned.1.call-start = ((), (), s32[]{:S(2)}) async-start(), calls=%async_computation | async-start | bytes 327680 | tf_op jit(solution)/shard_map/psum | solution.py:269
  22.9 41.7 %copy-start.27 = (f32[1,1,192]{2,1,0:T(1,128)}, f32[1,1,192]{2,1,0:T(1,128)S(1)}, u32[]{:S(2)}) copy-start(f32[1,1,192]{2,1,0:T(1,128)S(1)} %get-tuple-element.39) | copy-start | bytes 2308
  22.9 55.7 %copy-start.32 = (f32[1,1,192]{2,1,0:T(1,128)}, f32[1,1,192]{2,1,0:T(1,128)S(1)}, u32[]{:S(2)}) copy-start(f32[1,1,192]{2,1,0:T(1,128)S(1)} %get-tuple-element.38) | copy-start | bytes 2308
  24.4 53.3 %copy-start.9 = (bf16[144,576]{0,1:T(8,128)(2,1)}, bf16[144,576]{0,1:T(8,128)(2,1)S(1)}, u32[]{:S(2)}) copy-start(bf16[144,576]{0,1:T(8,128)(2,1)S(1)} %copy.51) | copy-start | bytes 497668
  64.6 13.5 %copy-start.12 = (bf16[2,192,192]{2,1,0:T(8,128)(2,1)S(1)}, bf16[2,192,192]{2,1,0:T(8,128)(2,1)}, u32[]{:S(2)}) copy-start(bf16[2,192,192]{2,1,0:T(8,128)(2,1)} %param.21) | copy-start | bytes 442372
  77.7 9.1 %copy-start.24 = (f32[6,144]{1,0:T(8,128)}, f32[6,144]{1,0:T(8,128)S(1)}, u32[]{:S(2)}) copy-start(f32[6,144]{1,0:T(8,128)S(1)} %get-tuple-element.45) | copy-start | bytes 10372
  81.7 55.5 %collective-permute-start.3 = (bf16[2,3,12,192]{3,2,1,0:T(8,128)(2,1)}, bf16[2,3,12,192]{3,2,1,0:T(8,128)(2,1)}, u32[]{:S(2)}, u32[]{:S(2)}) collective-permute-start(bf16[2,3,12,192]{3,2,1,0:T(8,128)(2,1)} %get-tuple-element.28), channel_id=1, source_target_pairs={{2,0},{0,2},{3,1},{1,3},{6,4},{4,6},{7,5},{5,7},{10,8},{8,10},{11,... | collective-permute-start | bytes 82952 | tf_op jit(solution)/shard_map/ppermute | solution.py:14
  85.3 52.8 %collective-permute-start = (bf16[2,3,12,192]{3,0,2,1:T(2,128)(2,1)}, bf16[2,3,12,192]{3,0,2,1:T(2,128)(2,1)}, u32[]{:S(2)}, u32[]{:S(2)}) collective-permute-start(bf16[2,3,12,192]{3,0,2,1:T(2,128)(2,1)} %get-tuple-element.32), channel_id=1, source_target_pairs={{2,0},{0,2},{3,1},{1,3},{6,4},{4,6},{7,5},{5,7},{10,8},{8,10},{11,... | collective-permute-start | bytes 82952 | tf_op jit(solution)/shard_map/ppermute | solution.py:14
  86.9 61.5 %copy-start.3 = (bf16[2,192,576]{2,1,0:T(8,128)(2,1)S(1)}, bf16[2,192,576]{2,1,0:T(8,128)(2,1)}, u32[]{:S(2)}) copy-start(bf16[2,192,576]{2,1,0:T(8,128)(2,1)} %param.20) | copy-start | bytes 1327108
  125.6 11.7 %copy-start.16 = (bf16[2,3,12,192]{3,2,1,0:T(8,128)(2,1)S(1)}, bf16[2,3,12,192]{3,2,1,0:T(8,128)(2,1)}, u32[]{:S(2)}) copy-start(bf16[2,3,12,192]{3,2,1,0:T(8,128)(2,1)} %get-tuple-element.27) | copy-start | bytes 82948
  125.6 12.6 %copy-start.18 = (bf16[2,3,12,192]{3,0,2,1:T(2,128)(2,1)S(1)}, bf16[2,3,12,192]{3,0,2,1:T(2,128)(2,1)}, u32[]{:S(2)}) copy-start(bf16[2,3,12,192]{3,0,2,1:T(2,128)(2,1)} %get-tuple-element.31) | copy-start | bytes 82948
  125.6 23.2 %copy-start.19 = (pred[144,144]{0,1:T(8,128)(4,1)S(1)}, pred[144,144]{0,1:T(8,128)(4,1)}, u32[]{:S(2)}) copy-start(pred[144,144]{0,1:T(8,128)(4,1)} %broadcast_compare_fusion) | copy-start | bytes 62212
  138.0 1.7 collective-permute-start.4
  139.1 5.7 %collective-permute-start.1 = (bf16[1,6,12,192]{3,0,2,1:T(2,128)(2,1)S(1)}, bf16[1,6,12,192]{3,0,2,1:T(2,128)(2,1)S(1)}, u32[]{:S(2)}, u32[]{:S(2)}) collective-permute-start(bf16[1,6,12,192]{3,0,2,1:T(2,128)(2,1)S(1)} %get-tuple-element.30), channel_id=1, source_target_pairs={{1,0},{0,1},{3,2},{2,3},{5,4},{4,5},{7,6},{6,7},{9,8},{8,9},{11,10... | collective-permute-start | bytes 82952 | tf_op jit(solution)/shard_map/ppermute | solution.py:14
  139.7 6.9 %collective-permute-start.5 = (bf16[2,6,6,192]{3,2,1,0:T(8,128)(2,1)S(1)}, bf16[2,6,6,192]{3,2,1,0:T(8,128)(2,1)S(1)}, u32[]{:S(2)}, u32[]{:S(2)}) collective-permute-start(bf16[2,6,6,192]{3,2,1,0:T(8,128)(2,1)S(1)} %get-tuple-element.24), channel_id=1, source_target_pairs={{4,0},{8,4},{12,8},{16,12},{20,16},{24,20},{28,24},{0,28},{5,1},{9... | collective-permute-start | bytes 82952 | tf_op jit(solution)/shard_map/ppermute | solution.py:14
  145.7 6.4 %collective-permute-start.2 = (bf16[2,6,6,192]{3,0,2,1:T(2,128)(2,1)}, bf16[2,6,6,192]{3,0,2,1:T(2,128)(2,1)}, u32[]{:S(2)}, u32[]{:S(2)}) collective-permute-start(bf16[2,6,6,192]{3,0,2,1:T(2,128)(2,1)} %get-tuple-element.18), channel_id=1, source_target_pairs={{4,0},{8,4},{12,8},{16,12},{20,16},{24,20},{28,24},{0,28},{5,1},{9... | collective-permute-start | bytes 82952 | tf_op jit(solution)/shard_map/ppermute | solution.py:14
  149.1 9.3 %copy-start.13 = (bf16[2,192,192]{2,1,0:T(8,128)(2,1)S(1)}, bf16[2,192,192]{2,1,0:T(8,128)(2,1)}, u32[]{:S(2)}) copy-start(bf16[2,192,192]{2,1,0:T(8,128)(2,1)} %param.21) | copy-start | bytes 442372
  153.0 13.4 %copy-start.6 = (bf16[144,192]{1,0:T(8,128)(2,1)}, bf16[144,192]{1,0:T(8,128)(2,1)S(1)}, u32[]{:S(2)}) copy-start(bf16[144,192]{1,0:T(8,128)(2,1)S(1)} %reshape.636) | copy-start | bytes 165892
  155.5 12.0 %copy-start.21 = (f32[2,6,12]{2,1,0:T(8,128)S(1)}, f32[2,6,12]{2,1,0:T(8,128)}, u32[]{:S(2)}) copy-start(f32[2,6,12]{2,1,0:T(8,128)} %copy-done.20) | copy-start | bytes 1732
  157.9 12.0 %copy-start.26 = (f32[2,6,12]{2,1,0:T(8,128)S(1)}, f32[2,6,12]{2,1,0:T(8,128)}, u32[]{:S(2)}) copy-start(f32[2,6,12]{2,1,0:T(8,128)} %get-tuple-element.35) | copy-start | bytes 1732
  158.0 27.0 %copy-start.25 = (f32[2,6,12]{2,1,0:T(8,128)S(1)}, f32[2,6,12]{2,1,0:T(8,128)}, u32[]{:S(2)}) copy-start(f32[2,6,12]{2,1,0:T(8,128)} %get-tuple-element.33) | copy-start | bytes 1732
  158.4 9.1 %copy-start.31 = (f32[144]{0:T(256)}, f32[144]{0:T(256)S(1)}, u32[]{:S(2)}) copy-start(f32[144]{0:T(256)S(1)} %negate_multiply_fusion.7) | copy-start | bytes 1732
  160.1 35.7 %copy-start.1 = (f32[6,144,144]{1,2,0:T(8,128)S(1)}, f32[6,144,144]{1,2,0:T(8,128)}, u32[]{:S(2)}) copy-start(f32[6,144,144]{1,2,0:T(8,128)} %get-tuple-element.46) | copy-start | bytes 1492996
  168.6 34.7 %copy-start.4 = (bf16[2,192,576]{2,1,0:T(8,128)(2,1)S(1)}, bf16[2,192,576]{2,1,0:T(8,128)(2,1)}, u32[]{:S(2)}) copy-start(bf16[2,192,576]{2,1,0:T(8,128)(2,1)} %param.20) | copy-start | bytes 1327108
  172.8 7.2 %collective-permute-start.6 = (bf16[2,6,6,192]{3,2,1,0:T(8,128)(2,1)S(1)}, bf16[2,6,6,192]{3,2,1,0:T(8,128)(2,1)S(1)}, u32[]{:S(2)}, u32[]{:S(2)}) collective-permute-start(bf16[2,6,6,192]{3,2,1,0:T(8,128)(2,1)S(1)} %get-tuple-element.21), channel_id=1, source_target_pairs={{28,0},{0,4},{4,8},{8,12},{12,16},{16,20},{20,24},{24,28},{29,1},{... | collective-permute-start | bytes 82952 | tf_op jit(solution)/shard_map/ppermute | solution.py:14
  180.0 27.4 %copy-start.2 = (bf16[3,6,12,5,2,4,4]{2,6,5,4,3,1,0:T(4,128)(2,1)S(1)}, bf16[3,6,12,5,2,4,4]{2,6,5,4,3,1,0:T(4,128)(2,1)}, u32[]{:S(2)}) copy-start(bf16[3,6,12,5,2,4,4]{2,6,5,4,3,1,0:T(4,128)(2,1)} %copy.49) | copy-start | bytes 207364
  180.0 4.2 %collective-permute-start.7 = (bf16[2,3,12,192]{3,2,1,0:T(8,128)(2,1)S(1)}, bf16[2,3,12,192]{3,2,1,0:T(8,128)(2,1)S(1)}, u32[]{:S(2)}, u32[]{:S(2)}) collective-permute-start(bf16[2,3,12,192]{3,2,1,0:T(8,128)(2,1)S(1)} %fusion.203), channel_id=1, source_target_pairs={{2,0},{0,2},{3,1},{1,3},{6,4},{4,6},{7,5},{5,7},{10,8},{8,10},{11,... | collective-permute-start | bytes 82952 | tf_op jit(solution)/shard_map/ppermute | solution.py:14
  184.2 1.3 collective-permute-start.8
  184.9 18.6 %copy-start.28 = (f32[144]{0:T(256)S(1)}, f32[144]{0:T(256)}, u32[]{:S(2)}) copy-start(f32[144]{0:T(256)} %div.130) | copy-start | bytes 1732
  192.5 12.8 %copy-start.8 = (bf16[144,192]{1,0:T(8,128)(2,1)S(1)}, bf16[144,192]{1,0:T(8,128)(2,1)}, u32[]{:S(2)}) copy-start(bf16[144,192]{1,0:T(8,128)(2,1)} %copy-done.7) | copy-start | bytes 165892
  (13 other events, 58.5 us)
Sparse Core Ops, SparseCore 0:
  246.2 122.7 all-reduce.1
where the time goes:
time: 380 us; the launch traced here: 377 us
  waiting for transfers between devices  131 us (34%)
  local copies, waits for them, and re-layouts  119 us (31%)
  blocking collectives  37.6 us (10%)
  matrix products  36 us (9%)
  other arithmetic  26.3 us (7%)
  between operations  15 us (4%)
  starting transfers between devices  12.3 us (3%)
    psum x1, waiting for transfers between devices, on_device(): lax.psum((upper_terms, surface_terms), ('lon', 'lat', 'section'))  122 us
    gather x4, local copies, waits for them, and re-layouts, window_bias(): return table[..., bias_index()]  101 us
    psum x1, blocking collectives, on_device(): lax.psum((upper_terms, surface_terms), ('lon', 'lat', 'section'))  37.6 us
    ppermute x9, starting transfers between devices, shifted(): return lax.ppermute(block, axis, route)  12.3 us
    ppermute x9, waiting for transfers between devices, shifted(): return lax.ppermute(block, axis, route)  9.27 us
  transfers between devices with their start and end apart: 10, of which 5 were waited for; matrix products, arithmetic and copies ran while one was open for 17% of the time, Pallas kernels for 0%

commit v1 on v0

v1 whole, which is shorter than its diff:
```python
import jax
import jax.numpy as jnp
import ml_dtypes
import numpy as np
from jax import lax
from jax.experimental import pallas as pl
from jax.experimental.pallas import tpu as pltpu
from jax.sharding import PartitionSpec as P

neg_fill = -1e30
norm_eps = 1e-05
HEADS = 6
HEAD = 32
CELLS = 144
WIDTH = 192
FULL = jnp.float32
HALF = jnp.bfloat16


def inner_row(z, a, o):
    return o * 12 + z * 6 + a


def octant_of(z, a, o):
    return (z * 4 + (a // 3) * 2 + o // 6, (a % 3) * 6 + o % 6)


def as_half(array):
    return array.astype(ml_dtypes.bfloat16)


def patch_select():
    sel = np.zeros((512, 512), np.float32)
    for c in range(4):
        for b in range(4):
            base = c * 128 + b * 32
            for z in range(2):
                for a in range(2):
                    for v in range(5):
                        sel[base + (z * 2 + a) * 5 + v, z * 256 + v * 32 + a * 16 + b * 4 + c] = 1
            for v in range(4):
                sel[base + 20 + v, 160 + v * 16 + b * 4 + c] = 1
    return as_half(sel)


def cells():
    return [(z, a, o) for z in range(2) for a in range(6) for o in range(12)]


def natural_to_inner():
    move = np.zeros((CELLS, CELLS), np.float32)
    for z, a, o in cells():
        move[inner_row(z, a, o), (z * 6 + a) * 12 + o] = 1
    return as_half(move)


def inner_to_padded():
    move = np.zeros((192, CELLS), np.float32)
    for z, a, o in cells():
        move[(z * 6 + a) * 16 + o, inner_row(z, a, o)] = 1
    return as_half(move)


def octants_out(pitch, first, padded_source):
    move = np.zeros((8 * pitch, 192 if padded_source else CELLS), np.float32)
    for z, a, o in cells():
        part, place = octant_of(z, a, o)
        source = (z * 6 + a) * 16 + o if padded_source else inner_row(z, a, o)
        move[part * pitch + first + place, source] = 1
    return as_half(move)


def octants_in(pitch, first):
    move = np.zeros((CELLS, 8 * pitch), np.float32)
    for z, a, o in cells():
        part, place = octant_of(z, a, o)
        move[inner_row(z, a, o), part * pitch + first + place] = 1
    return as_half(move)


def bias_columns():
    move = np.zeros((2, 256, 384), np.float32)
    for z in range(2):
        for a in range(6):
            for k in range(23):
                move[z, a * 23 + k, (22 - k) * 12 + z * 6 + a] = 1
    return as_half(move)


def dot(a, b):
    return jnp.dot(a, b, preferred_element_type=FULL)


def dot_nt(a, b):
    return lax.dot_general(a, b, (((1,), (1,)), ((), ())), preferred_element_type=FULL)


def dot_tn(a, b):
    return lax.dot_general(a, b, (((0,), (0,)), ((), ())), preferred_element_type=FULL)


def normalise(v):
    mean = jnp.mean(v, -1, keepdims=True)
    centred = v - mean
    spread = lax.rsqrt(jnp.mean(centred * centred, -1, keepdims=True) + norm_eps)
    return centred * spread, spread


def normalise_back(dy, unit, spread, gain):
    dunit = dy * gain
    inner = jnp.mean(dunit * unit, -1, keepdims=True)
    return spread * (dunit - jnp.mean(dunit, -1, keepdims=True) - unit * inner)


def head_lanes(h):
    lane = lax.broadcasted_iota(jnp.int32, (1, WIDTH), 1)
    return (lane >= h * HEAD) & (lane < (h + 1) * HEAD)


def head_mask(h):
    return jnp.where(head_lanes(h), 1.0, 0.0).astype(HALF)


def build_bias(tbl, block, cols, xs, bias, edges):
    for z in range(2):
        for a in range(6):
            for zu in range(2):
                start = ((z * 2 + zu) * 6 + a) * 138
                piece = tbl[block, :, start : start + 138]
                piece = jnp.concatenate((piece, jnp.zeros((HEADS, 118), FULL)), 1)
                for p in range(2):
                    for half in range(2):
                        xs[zu * 2 + half, pl.ds(p * 12 + z * 6 + a, HEADS, stride=24), :] = piece[
                            :, half * 128 : half * 128 + 128
                        ]
    total = None
    for zu in range(2):
        x = jnp.concatenate((xs[zu * 2], xs[zu * 2 + 1]), 1)
        high = x.astype(HALF)
        left = x - high.astype(FULL)
        mid = left.astype(HALF)
        low = (left - mid.astype(FULL)).astype(HALF)
        term = dot(jnp.concatenate((high, mid, low), 0), cols[zu])
        total = term if total is None else total + term
    table = total[:CELLS] + total[CELLS : 2 * CELLS] + total[2 * CELLS :]
    row = lax.broadcasted_iota(jnp.int32, (CELLS, 1), 0).astype(FULL)
    lane = lax.broadcasted_iota(jnp.int32, (1, CELLS), 1).astype(FULL)

    def part(v, size):
        return jnp.floor((v + 0.5) * (1.0 / size))

    even = part(row, 12) - 2.0 * part(part(row, 12), 2) == 0.0
    table = jnp.where(even, pltpu.roll(table, 384 - 12, 1), table)
    if edges is not None:
        last_section, last_band = edges
        row12, lane12 = row - 12.0 * part(row, 12), lane - 12.0 * part(lane, 12)
        row_z, lane_z = part(row12, 6), part(lane12, 6)
        row_a, lane_a = part(row12 - 6.0 * row_z, 3), part(lane12 - 6.0 * lane_z, 3)
        apart = jnp.abs(row_z - lane_z) * last_section + jnp.abs(row_a - lane_a) * last_band
        blocked = apart > 0.5
    for j in range(6):
        shift = (10 - 2 * j) * 12
        moved = pltpu.roll(table, 384 - shift, 1) if shift else table
        moved = moved[:, :CELLS]
        if edges is not None:
            moved = jnp.where(blocked, neg_fill, moved)
        for h in range(HEADS):
            bias[h * CELLS + j * 24 : h * CELLS + j * 24 + 24, :] = moved[h * 24 : h * 24 + 24, :]


def attend(q, k, v, bias, prob):
    mixed = jnp.zeros((CELLS, WIDTH), FULL)
    for h in range(HEADS):
        rows = slice(h * CELLS, (h + 1) * CELLS)
        score = dot_nt(q * head_mask(h), k) * HEAD ** (-0.5) + bias[rows, :]
        expo = jnp.exp(score - jnp.max(score, -1, keepdims=True))
        weights = (expo * (1.0 / jnp.sum(expo, -1, keepdims=True))).astype(HALF)
        prob[rows, :] = weights
        mixed = jnp.where(head_lanes(h), dot(weights, v), mixed)
    return mixed.astype(HALF)


def attend_back(dmixed, q, k, v, prob):
    dq = jnp.zeros((CELLS, WIDTH), FULL)
    dk = jnp.zeros((CELLS, WIDTH), FULL)
    dv = jnp.zeros((CELLS, WIDTH), FULL)
    for h in range(HEADS):
        rows = slice(h * CELLS, (h + 1) * CELLS)
        weights = prob[rows, :]
        dhead = dmixed * head_mask(h)
        full = weights.astype(FULL)
        dweights = dot_nt(dhead, v)
        inner = jnp.sum(dweights * full, -1, keepdims=True)
        dscore = (full * (dweights - inner) * HEAD ** (-0.5)).astype(HALF)
        dv = dv + dot_tn(weights, dhead)
        dq = jnp.where(head_lanes(h), dot(dscore, k), dq)
        dk = dk + dot_tn(dscore, q * head_mask(h))
    return dq.astype(HALF), dk.astype(HALF), dv.astype(HALF)


def gelu_parts(u):
    below = 0.5 * (1.0 + lax.erf(u * (0.5**0.5)))
    slope = below + u * (jnp.exp(-0.5 * u * u) * (2.0 * np.pi) ** (-0.5))
    return below, slope


def forward_half(x, block, gains, wqkv, wproj, bias, prob):
    unit, spread = normalise(x)
    hidden = (unit * gains[block, 0:1, :]).astype(HALF)
    qkv = dot(hidden, wqkv[block]).astype(HALF)
    q, k, v = (qkv[:, n * WIDTH : (n + 1) * WIDTH] for n in range(3))
    mixed = attend(q, k, v, bias, prob)
    return (q, k, v), x + dot(mixed, wproj[block])


def backward(dflat, block, x, qkv, prob, resid, slope, gains, wqkv, wproj, wup, wdown):
    q, k, v = qkv
    dactive = dot_nt(dflat, wdown[block])
    dupward = (dactive * slope).astype(HALF)
    dnormed = dot_nt(dupward, wup[block])
    unit, spread = normalise(resid)
    dresid = dflat.astype(FULL) + normalise_back(dnormed, unit, spread, gains[block, 1:2, :])
    dmixed = dot_nt(dresid.astype(HALF), wproj[block]).astype(HALF)
    dq, dk, dv = attend_back(dmixed, q, k, v, prob)
    weight = wqkv[block]
    dhidden = dot_nt(dq, weight[:, :WIDTH])
    dhidden = dhidden + dot_nt(dk, weight[:, WIDTH : 2 * WIDTH])
    dhidden = dhidden + dot_nt(dv, weight[:, 2 * WIDTH :])
    unit, spread = normalise(x)
    return dresid + normalise_back(dhidden, unit, spread, gains[block, 0:1, :])


def gather_patches(upper, surface, section, sections, select, ff, ft):
    base = 4 * section - 2
    for z in range(2):
        for a in range(2):
            level = jnp.maximum(base + 2 * z + a, 0)
            for v in range(5):
                field = upper[v, level].astype(FULL)
                if z == 0:
                    field = jnp.where(section == 0, 0.0, field)
                slot = (z * 2 + a) * 5 + v
                ff[slot * 24 : slot * 24 + 24, 0:48] = field
    for v in range(4):
        field = jnp.where(section == 0, surface[v].astype(FULL), 0.0)
        ff[(20 + v) * 24 : (21 + v) * 24, 0:48] = field
    pad = jnp.zeros((8, 128), FULL)
    for i in range(6):
        pieces = []
        for b in range(4):
            pieces += [ff[pl.ds(4 * i + b, 24, stride=24), :], pad]
        ft[i * 48 : i * 48 + 48, :] = jnp.concatenate(pieces, 0).T[:48]
    raw = [ft[pl.ds(c, 72, stride=4), :].astype(HALF) for c in range(4)]
    both = dot(jnp.concatenate(raw, 1), select[...])
    return jnp.concatenate((both[:, :256], both[:, 256:]), 0).astype(HALF)


def first_kernel(
    flags, upper, surface, cot, uembed, sembed, gains, wqkv, wproj, wup, wdown, tbl,
    select, to_inner, out_first, out_cot, cols, *rest
):
    octants, rest = rest[:8], rest[8:]
    patch_o, x_o, qkv_o, prob, resid_o, slope_o, ff, ft, emb, cots, xs, bias = rest
    section = flags[0]
    emb[0:160, :] = uembed[...]
    emb[160:224, :] = sembed[...]
    emb[224:256, :] = jnp.zeros((32, WIDTH), HALF)
    cots[...] = jnp.zeros_like(cots)
    for z in range(2):
        for a in range(6):
            cots[(z * 6 + a) * 16 : (z * 6 + a) * 16 + 12, :] = cot[z, a]
    build_bias(tbl, 0, cols, xs, bias, None)
    patch = gather_patches(upper, surface, section, None, select, ff, ft)
    patch = dot(to_inner[...], patch).astype(HALF)
    patch_o[...] = patch
    latent = dot(patch, emb[...]).astype(HALF)
    x_o[...] = latent
    x = latent.astype(FULL)
    qkv, resid = forward_half(x, 0, gains, wqkv, wproj, bias, prob)
    for n in range(3):
        qkv_o[n] = qkv[n]
    resid_o[...] = resid
    unit, spread = normalise(resid)
    normed = (unit * gains[0, 1:2, :]).astype(HALF)
    upward = dot(normed, wup[0])
    below, slope = gelu_parts(upward)
    slope_o[...] = slope.astype(HALF)
    active = (upward * below).astype(HALF)
    result = (resid + dot(active, wdown[0])).astype(HALF)
    moved = (dot(out_first[...], result) + dot(out_cot[...], cots[...])).astype(HALF)
    for n in range(8):
        octants[n][...] = moved[n * 48 : n * 48 + 48]


def second_kernel(flags, *rest):
    parts, rest = rest[:8], rest[8:]
    gains, wqkv, wproj, wup, wdown, tbl, cols, into, out_of = rest[:9]
    octants, rest = rest[9:17], rest[17:]
    stack, xs, bias, prob = rest
    build_bias(tbl, 1, cols, xs, bias, (flags[1].astype(FULL), flags[2].astype(FULL)))
    for n in range(8):
        stack[n * 48 : n * 48 + 48, :] = parts[n][...]
    both = dot(into[...], stack[...])
    x, dflat = both[:CELLS], both[CELLS:].astype(HALF)
    qkv, resid = forward_half(x, 1, gains, wqkv, wproj, bias, prob)
    unit, spread = normalise(resid)
    normed = (unit * gains[1, 1:2, :]).astype(HALF)
    upward = dot(normed, wup[1])
    slope = gelu_parts(upward)[1]
    dx = backward(dflat, 1, x, qkv, prob, resid, slope, gains, wqkv, wproj, wup, wdown)
    moved = dot(out_of[...], dx.astype(HALF)).astype(HALF)
    for n in range(8):
        octants[n][...] = moved[n * 32 : n * 32 + 32]


def third_kernel(*rest):
    parts, rest = rest[:8], rest[8:]
    gains, wqkv, wproj, wup, wdown, patch, x_i, qkv_i, prob, resid, slope, into, out_of = rest[:13]
    grad_o, terms_o, stack = rest[13:]
    for n in range(8):
        stack[n * 32 : n * 32 + 32, :] = parts[n][...]
    dflat = dot(into[...], stack[...]).astype(HALF)
    qkv = tuple(qkv_i[n] for n in range(3))
    dx = backward(
        dflat, 0, x_i[...].astype(FULL), qkv, prob, resid[...], slope[...].astype(FULL),
        gains, wqkv, wproj, wup, wdown,
    )
    grad = dx.astype(HALF)
    moved = dot(out_of[...], grad).astype(HALF)
    for z in range(2):
        for a in range(6):
            grad_o[z, a] = moved[(z * 6 + a) * 16 : (z * 6 + a) * 16 + 12]
    terms_o[...] = dot_tn(patch[...], grad)[:224].astype(HALF)


def call(kernel, outs, scratch, *args):
    vmem = pl.BlockSpec(memory_space=pltpu.VMEM)
    smem = pl.BlockSpec(memory_space=pltpu.SMEM)
    return pl.pallas_call(
        kernel,
        out_shape=outs,
        in_specs=[smem if a.dtype == jnp.int32 else vmem for a in args],
        out_specs=jax.tree.map(lambda _: vmem, outs),
        scratch_shapes=scratch,
        compiler_params=pltpu.CompilerParams(vmem_limit_bytes=30 * 2**20),
    )(*args)


def shape(dims, dtype=HALF):
    return jax.ShapeDtypeStruct(dims, dtype)


def move_octant(block, step):
    names, step = ("lon", "lat", "section"), step[::-1]
    if not any(step):
        return block
    sizes = [lax.axis_size(name) for name in names]
    pairs = []
    for place in np.ndindex(*sizes):
        source = [(p + s) % n for p, s, n in zip(place, step, sizes)]
        pairs.append((int(np.ravel_multi_index(source, sizes)), int(np.ravel_multi_index(place, sizes))))
    return lax.ppermute(block, names, pairs)


def add_up(terms):
    for name in ("section", "lat", "lon"):
        size = lax.axis_size(name)
        if size & (size - 1):
            terms = lax.psum(terms.astype(FULL), name).astype(HALF)
            continue
        step = 1
        while step < size:
            other = lax.ppermute(terms, name, [(i, i ^ step) for i in range(size)])
            terms = (terms.astype(FULL) + other.astype(FULL)).astype(HALF)
            step *= 2
    return terms.astype(FULL)


def on_device(
    upper_fields,
    surface_fields,
    upper_embed,
    surface_embed,
    norm_gains,
    qkv_weight,
    proj_weight,
    up_weight,
    down_weight,
    earth_bias,
    out_grad,
):
    section, band = lax.axis_index("section"), lax.axis_index("lat")
    sections, bands = lax.axis_size("section"), lax.axis_size("lat")
    levels, rows, columns, width = out_grad.shape
    flags = jnp.stack((section, section == sections - 1, band == bands - 1)).astype(jnp.int32)
    table = earth_bias.reshape(2, HEADS, earth_bias.shape[-1])
    weights = (norm_gains, qkv_weight, proj_weight, up_weight, down_weight)
    cols = jnp.asarray(bias_columns())
    scratch_bias = [pltpu.VMEM((4, CELLS, 128), FULL), pltpu.VMEM((HEADS * CELLS, CELLS), FULL)]
    results = call(
        first_kernel,
        [shape((48, WIDTH))] * 8
        + [
            shape((CELLS, 256)),
            shape((CELLS, WIDTH)),
            shape((3, CELLS, WIDTH)),
            shape((HEADS * CELLS, CELLS)),
            shape((CELLS, WIDTH), FULL),
            shape((CELLS, 4 * WIDTH)),
        ],
        [
            pltpu.VMEM((576, 128), FULL),
            pltpu.VMEM((288, 128), FULL),
            pltpu.VMEM((256, WIDTH), HALF),
            pltpu.VMEM((192, WIDTH), HALF),
        ]
        + scratch_bias,
        flags, upper_fields, surface_fields, out_grad, upper_embed, surface_embed, *weights, table,
        jnp.asarray(patch_select()), jnp.asarray(natural_to_inner()),
        jnp.asarray(octants_out(48, 0, False)), jnp.asarray(octants_out(48, 18, True)), cols,
    )
    octants, (patch, x, qkv, prob, resid, slope) = results[:8], results[8:]
    steps = list(np.ndindex(2, 2, 2))
    shifted = [move_octant(octants[7 - n], steps[n]) for n in range(8)]
    into = np.concatenate((octants_in(48, 0), octants_in(48, 18)), 0)
    back = call(
        second_kernel,
        [shape((32, WIDTH))] * 8,
        [pltpu.VMEM((8 * 48, WIDTH), HALF)]
        + scratch_bias
        + [pltpu.VMEM((HEADS * CELLS, CELLS), HALF)],
        flags, *shifted, *weights, table, cols,
        jnp.asarray(into), jnp.asarray(octants_out(32, 0, False)),
    )
    returned = [move_octant(back[n], tuple(-s for s in steps[n])) for n in range(8)][::-1]
    latent_grad, terms = call(
        third_kernel,
        [shape((2, 6, 12, WIDTH)), shape((224, WIDTH))],
        [pltpu.VMEM((8 * 32, WIDTH), HALF)],
        *returned, *weights, patch, x, qkv, prob, resid, slope,
        jnp.asarray(octants_in(32, 0)), jnp.asarray(inner_to_padded()),
    )
    total = add_up(terms)
    scale = float(levels * sections * rows * bands * columns * lax.axis_size("lon")) ** (-0.5)
    return (latent_grad, total[:160] * scale, total[160:] * scale)


def solution(mesh):
    placed = (
        P(None, None, "lat", "lon"),
        P(None, "lat", "lon"),
        P(),
        P(),
        P(),
        P(),
        P(),
        P(),
        P(),
        P(None, "lat", "section", None, None),
        P("section", "lat", "lon", None),
    )
    return jax.shard_map(
        on_device,
        mesh=mesh,
        in_specs=placed,
        out_specs=(P("section", "lat", "lon", None), P(), P()),
        check_vma=False,
    )
```

time: 380 us -> 77.1 us (0.20)
  local copies, waits for them, and re-layouts: 119 us -> 9.92 us
  waiting for transfers between devices: 131 us -> 31 us
  blocking collectives: 37.6 us -> 0 us
  matrix products: 36 us -> 0 us
  other arithmetic: 26.3 us -> 1.54 us
  between operations: 15 us -> 0.86 us
  Pallas kernels: 0 us -> 12.2 us
  starting transfers between devices: 12.3 us -> 21.1 us
    psum x1 -> x0, waiting for transfers between devices: 122 us -> none  [on_device(): lax.psum((upper_terms, surface_terms), ('lon', 'lat', 'section'))]
    gather x4 -> x0, local copies, waits for them, and re-layouts: 101 us -> none  [window_bias(): return table[..., bias_index()]]
    psum x1 -> x0, blocking collectives: 37.6 us -> none  [on_device(): lax.psum((upper_terms, surface_terms), ('lon', 'lat', 'section'))]
    dot_general x31 -> x0, matrix products: 36 us -> none  [the longest x2 4.82 us: attention_backward(): jnp.einsum('zlwhqk,zlwqhd->zlwkhd', dscore, query.astype(jnp.float32), pr...]
    ppermute x9 -> x19, waiting for transfers between devices: 9.27 us -> 31 us  [the longest x5 20.7 us: add_up(): other = lax.ppermute(terms, name, [(i, i ^ step) for i in range(size)])]
    pallas_call x0 -> x3, Pallas kernels: none -> 12.2 us  [call(): pl.pallas_call(kernel, out_shape=outs, in_specs=[smem if a.dtype == jnp.i...]
    reduce_sum x16 -> x0, other arithmetic: 8.95 us -> none  [the longest x4 2.94 us: layer_norm(): centred = values - average]
    ppermute x9 -> x19, starting transfers between devices: 12.3 us -> 21.1 us  [the longest x14 19.6 us: move_octant(): return lax.ppermute(block, names, pairs)]
  transfers between devices with their start and end apart: 10 -> 19, of which waited for: 5 -> 9; matrix products, arithmetic and copies ran while one was open for 17% -> 1% of each run, Pallas kernels for 0% -> 0%
where the time goes in v1:
time: 77.1 us; the launch traced here: 76.6 us
  waiting for transfers between devices  31 us (40%)
  starting transfers between devices  21.1 us (27%)
  Pallas kernels  12.2 us (16%)
  local copies, waits for them, and re-layouts  9.92 us (13%)
  other arithmetic  1.54 us (2%)
  between operations  0.86 us (1%)
    ppermute x5, waiting for transfers between devices, add_up(): other = lax.ppermute(terms, name, [(i, i ^ step) for i in range(size)])  20.7 us
    ppermute x14, starting transfers between devices, move_octant(): return lax.ppermute(block, names, pairs)  19.6 us
    pallas_call x3, Pallas kernels, call(): pl.pallas_call(kernel, out_shape=outs, in_specs=[smem if a.dtype == jnp.i...  12.2 us
    ppermute x14, waiting for transfers between devices, move_octant(): return lax.ppermute(block, names, pairs)  10.4 us
    unnamed x38, local copies, waits for them, and re-layouts  9.89 us
  transfers between devices with their start and end apart: 19, of which 9 were waited for; matrix products, arithmetic and copies ran while one was open for 1% of the time, Pallas kernels for 0%

profile of v1, /device:TPU:0, one launch (start us, length us, event | category | flops | bytes accessed | tf_op | source)
XLA Modules:
  0.0 76.6 jit_solution(10146956349399466166)
XLA Ops:
  0.7 1.0 %copy.29.cot = bf16[2,6,12,192]{3,2,1,0:T(8,128)(2,1)S(1)} copy(bf16[2,6,12,192]{3,0,2,1:T(2,128)(2,1)} %param.30) | data formatting | bytes 110592 | tf_op args[10]
  1.6 1.0 %copy.37 = f32[2,1,1,6,3312]{4,0,3,2,1:T(2,128)S(1)} copy(f32[2,1,1,6,3312]{4,2,3,1,0:T(1,128)} %param.29) | data formatting | bytes 317952 | tf_op args[9]
  2.7 1.4 %copy.30.wdown.rest_12_ = bf16[2,768,192]{2,1,0:T(8,128)(2,1)S(1)} copy(bf16[2,768,192]{1,2,0:T(8,128)(2,1)} %param.28) | data formatting | bytes 1179648 | tf_op args[8]
  4.9 0.9 %copy-done.6 = bf16[384,192]{1,0:T(8,128)(2,1)S(1)} copy-done((bf16[384,192]{1,0:T(8,128)(2,1)S(1)}, bf16[384,192]{1,0:T(8,128)(2,1)}, u32[]{:S(2)}) %copy-start.6) | copy-done | bytes 147480
  5.8 0.9 %copy-done.7 = bf16[384,144]{1,0:T(8,128)(2,1)S(1)} copy-done((bf16[384,144]{1,0:T(8,128)(2,1)S(1)}, bf16[384,144]{1,0:T(8,128)(2,1)}, u32[]{:S(2)}) %copy-start.7) | copy-done | bytes 110616
  6.7 0.9 %copy-done.8 = bf16[5,6,24,48]{3,2,1,0:T(8,128)(2,1)S(1)} copy-done((bf16[5,6,24,48]{3,2,1,0:T(8,128)(2,1)S(1)}, bf16[5,6,24,48]{3,2,1,0:T(8,128)(2,1)}, u32[]{:S(2)}) %copy-start.8) | copy-done | bytes 69144
  7.6 0.9 %copy-done.11 = bf16[160,192]{1,0:T(8,128)(2,1)S(1)} copy-done((bf16[160,192]{1,0:T(8,128)(2,1)S(1)}, bf16[160,192]{1,0:T(8,128)(2,1)}, u32[]{:S(2)}) %copy-start.11) | copy-done | bytes 61464
  8.5 0.8 copy-done.15
  9.3 0.7 copy-done.16
  10.0 3.8 %shard_map.211 = (bf16[48,192]{1,0:T(8,128)(2,1)S(1)}, bf16[48,192]{1,0:T(8,128)(2,1)S(1)}, bf16[48,192]{1,0:T(8,128)(2,1)S(1)}, bf16[48,192]{1,0:T(8,128)(2,1)S...) custom-call(s32[3]{0:T(128)S(1)} %pad_add_fusion.flags, ...), custom_call_target="tpu_custom_call" | custom-call | tf_op jit(solution)/shard_map/pallas_call | solution.py:339
  13.8 6.1 %collective-permute-start = (bf16[48,192]{1,0:T(8,128)(2,1)S(1)}, bf16[48,192]{1,0:T(8,128)(2,1)S(1)}, u32[]{:S(2)}, u32[]{:S(2)}) collective-permute-start(bf16[48,192]{1,0:T(8,128)(2,1)S(1)} %get-tuple-element.28), channel_id=1, source_target_pairs={{4,0},{5,1},{6,2},{7,3},{8,4},{9,5},{10,6},{11,7},{12,8},{13,9},{1... | collective-permute-start | bytes 55304 | tf_op jit(solution)/shard_map/ppermute | solution.py:362
  19.9 1.5 %collective-permute-start.1 = (bf16[48,192]{1,0:T(8,128)(2,1)S(1)}, bf16[48,192]{1,0:T(8,128)(2,1)S(1)}, u32[]{:S(2)}, u32[]{:S(2)}) collective-permute-start(bf16[48,192]{1,0:T(8,128)(2,1)S(1)} %get-tuple-element.29), channel_id=1, source_target_pairs={{2,0},{3,1},{0,2},{1,3},{6,4},{7,5},{4,6},{5,7},{10,8},{11,9},{8,1... | collective-permute-start | bytes 55304 | tf_op jit(solution)/shard_map/ppermute | solution.py:362
  21.9 1.5 %collective-permute-start.4 = (bf16[48,192]{1,0:T(8,128)(2,1)S(1)}, bf16[48,192]{1,0:T(8,128)(2,1)S(1)}, u32[]{:S(2)}, u32[]{:S(2)}) collective-permute-start(bf16[48,192]{1,0:T(8,128)(2,1)S(1)} %get-tuple-element.32), channel_id=1, source_target_pairs={{5,0},{4,1},{7,2},{6,3},{9,4},{8,5},{11,6},{10,7},{13,8},{12,9},{1... | collective-permute-start | bytes 55304 | tf_op jit(solution)/shard_map/ppermute | solution.py:362
  23.4 1.1 %collective-permute-start.5 = (bf16[48,192]{1,0:T(8,128)(2,1)S(1)}, bf16[48,192]{1,0:T(8,128)(2,1)S(1)}, u32[]{:S(2)}, u32[]{:S(2)}) collective-permute-start(bf16[48,192]{1,0:T(8,128)(2,1)S(1)} %get-tuple-element.33), channel_id=1, source_target_pairs={{3,0},{2,1},{1,2},{0,3},{7,4},{6,5},{5,6},{4,7},{11,8},{10,9},{9,1... | collective-permute-start | bytes 55304 | tf_op jit(solution)/shard_map/ppermute | solution.py:362
  24.5 3.1 %collective-permute-start.6 = (bf16[48,192]{1,0:T(8,128)(2,1)S(1)}, bf16[48,192]{1,0:T(8,128)(2,1)S(1)}, u32[]{:S(2)}, u32[]{:S(2)}) collective-permute-start(bf16[48,192]{1,0:T(8,128)(2,1)S(1)} %get-tuple-element.34), channel_id=1, source_target_pairs={{7,0},{6,1},{5,2},{4,3},{11,4},{10,5},{9,6},{8,7},{15,8},{14,9},{1... | collective-permute-start | bytes 55304 | tf_op jit(solution)/shard_map/ppermute | solution.py:362
  27.6 1.5 %collective-permute-done.6.rest_7_ = bf16[48,192]{1,0:T(8,128)(2,1)S(1)} collective-permute-done((bf16[48,192]{1,0:T(8,128)(2,1)S(1)}, bf16[48,192]{1,0:T(8,128)(2,1)S(1)}, u32[]{:S(2)}, u32[]{:S(2)}) %collective-permute-start.6) | collective-permute-done | bytes 18464 | tf_op jit(solution)/shard_map/ppermute | solution.py:362
  29.1 6.0 %shard_map.212 = (bf16[32,192]{1,0:T(8,128)(2,1)S(1)}, bf16[32,192]{1,0:T(8,128)(2,1)S(1)}, bf16[32,192]{1,0:T(8,128)(2,1)S(1)}, bf16[32,192]{1,0:T(8,128)(2,1)S...) custom-call(s32[3]{0:T(128)S(1)} %pad_add_fusion.flags, ...), custom_call_target="tpu_custom_call" | custom-call | tf_op jit(solution)/shard_map/pallas_call | solution.py:339
  35.2 1.2 %collective-permute-start.7 = (bf16[32,192]{1,0:T(8,128)(2,1)S(1)}, bf16[32,192]{1,0:T(8,128)(2,1)S(1)}, u32[]{:S(2)}, u32[]{:S(2)}) collective-permute-start(bf16[32,192]{1,0:T(8,128)(2,1)S(1)} %get-tuple-element.35), channel_id=1, source_target_pairs={{31,0},{30,1},{29,2},{28,3},{3,4},{2,5},{1,6},{0,7},{7,8},{6,9},{5... | collective-permute-start | bytes 36872 | tf_op jit(solution)/shard_map/ppermute | solution.py:362
  36.3 1.1 %collective-permute-start.8 = (bf16[32,192]{1,0:T(8,128)(2,1)S(1)}, bf16[32,192]{1,0:T(8,128)(2,1)S(1)}, u32[]{:S(2)}, u32[]{:S(2)}) collective-permute-start(bf16[32,192]{1,0:T(8,128)(2,1)S(1)} %get-tuple-element.36), channel_id=1, source_target_pairs={{3,0},{2,1},{1,2},{0,3},{7,4},{6,5},{5,6},{4,7},{11,8},{10,9},{9,1... | collective-permute-start | bytes 36872 | tf_op jit(solution)/shard_map/ppermute | solution.py:362
  37.4 1.6 %collective-permute-start.9 = (bf16[32,192]{1,0:T(8,128)(2,1)S(1)}, bf16[32,192]{1,0:T(8,128)(2,1)S(1)}, u32[]{:S(2)}, u32[]{:S(2)}) collective-permute-start(bf16[32,192]{1,0:T(8,128)(2,1)S(1)} %get-tuple-element.37), channel_id=1, source_target_pairs={{29,0},{28,1},{31,2},{30,3},{1,4},{0,5},{3,6},{2,7},{5,8},{4,9},{7... | collective-permute-start | bytes 36872 | tf_op jit(solution)/shard_map/ppermute | solution.py:362
  39.6 2.4 %collective-permute-done.7.rest_0_ = bf16[32,192]{1,0:T(8,128)(2,1)S(1)} collective-permute-done((bf16[32,192]{1,0:T(8,128)(2,1)S(1)}, bf16[32,192]{1,0:T(8,128)(2,1)S(1)}, u32[]{:S(2)}, u32[]{:S(2)}) %collective-permute-start.7) | collective-permute-done | bytes 12320 | tf_op jit(solution)/shard_map/ppermute | solution.py:362
  42.0 1.5 %collective-permute-start.12 = (bf16[32,192]{1,0:T(8,128)(2,1)S(1)}, bf16[32,192]{1,0:T(8,128)(2,1)S(1)}, u32[]{:S(2)}, u32[]{:S(2)}) collective-permute-start(bf16[32,192]{1,0:T(8,128)(2,1)S(1)} %get-tuple-element.40), channel_id=1, source_target_pairs={{2,0},{3,1},{0,2},{1,3},{6,4},{7,5},{4,6},{5,7},{10,8},{11,9},{8,1... | collective-permute-start | bytes 36872 | tf_op jit(solution)/shard_map/ppermute | solution.py:362
  43.5 2.9 %collective-permute-done.11.rest_4_ = bf16[32,192]{1,0:T(8,128)(2,1)S(1)} collective-permute-done((bf16[32,192]{1,0:T(8,128)(2,1)S(1)}, bf16[32,192]{1,0:T(8,128)(2,1)S(1)}, u32[]{:S(2)}, u32[]{:S(2)}) %collective-permute-start.11) | collective-permute-done | bytes 12320 | tf_op jit(solution)/shard_map/ppermute | solution.py:362
  46.4 3.5 %collective-permute-done.13.rest_6_ = bf16[32,192]{1,0:T(8,128)(2,1)S(1)} collective-permute-done((bf16[32,192]{1,0:T(8,128)(2,1)S(1)}, bf16[32,192]{1,0:T(8,128)(2,1)S(1)}, u32[]{:S(2)}, u32[]{:S(2)}) %collective-permute-start.13) | collective-permute-done | bytes 12320 | tf_op jit(solution)/shard_map/ppermute | solution.py:362
  49.9 2.4 %shard_map.213 = (bf16[2,6,12,192]{3,2,1,0:T(8,128)(2,1)S(1)}, bf16[224,192]{1,0:T(8,128)(2,1)S(1)}) custom-call(bf16[32,192]{1,0:T(8,128)(2,1)S(1)} %collective-permute-done.7.rest_0_, bf16[32,192]{1,0:T(8,128)(2,1)S(1)} %collective-permute-done.8.rest_1_, bf16[32,192]{1,0:T(8,128)(2,1)S(1)} %collective-permute-done.9.rest_2_, ...), custom_call_target="tpu_custom_call" | custom-call | tf_op jit(solution)/shard_map/pallas_call | solution.py:339
  52.4 1.3 %collective-permute-done.14 = bf16[224,192]{1,0:T(8,128)(2,1)S(1)} collective-permute-done((bf16[224,192]{1,0:T(8,128)(2,1)S(1)}, bf16[224,192]{1,0:T(8,128)(2,1)S(1)}, u32[]{:S(2)}, u32[]{:S(2)}) %collective-permute-start.14) | collective-permute-done | bytes 86048 | tf_op jit(solution)/shard_map/ppermute | solution.py:373
  54.4 4.7 %collective-permute-done.15 = bf16[224,192]{1,0:T(8,128)(2,1)S(1)} collective-permute-done((bf16[224,192]{1,0:T(8,128)(2,1)S(1)}, bf16[224,192]{1,0:T(8,128)(2,1)S(1)}, u32[]{:S(2)}, u32[]{:S(2)}) %collective-permute-start.15) | collective-permute-done | bytes 86048 | tf_op jit(solution)/shard_map/ppermute | solution.py:373
  59.2 4.8 %collective-permute-done.16 = bf16[224,192]{1,0:T(8,128)(2,1)S(1)} collective-permute-done((bf16[224,192]{1,0:T(8,128)(2,1)S(1)}, bf16[224,192]{1,0:T(8,128)(2,1)S(1)}, u32[]{:S(2)}, u32[]{:S(2)}) %collective-permute-start.16) | collective-permute-done | bytes 86048 | tf_op jit(solution)/shard_map/ppermute | solution.py:373
  64.0 4.8 %collective-permute-done.17 = bf16[224,192]{1,0:T(8,128)(2,1)S(1)} collective-permute-done((bf16[224,192]{1,0:T(8,128)(2,1)S(1)}, bf16[224,192]{1,0:T(8,128)(2,1)S(1)}, u32[]{:S(2)}, u32[]{:S(2)}) %collective-permute-start.17) | collective-permute-done | bytes 86048 | tf_op jit(solution)/shard_map/ppermute | solution.py:373
  69.5 0.7 copy.35
  70.2 5.1 %collective-permute-done.18 = bf16[224,192]{1,0:T(8,128)(2,1)S(1)} collective-permute-done((bf16[224,192]{1,0:T(8,128)(2,1)S(1)}, bf16[224,192]{1,0:T(8,128)(2,1)S(1)}, u32[]{:S(2)}, u32[]{:S(2)}) %collective-permute-start.18) | collective-permute-done | bytes 86048 | tf_op jit(solution)/shard_map/ppermute | solution.py:373
  76.0 0.7 slice_multiply_fusion
  (56 shorter events, 3.9 us)
Async XLA Ops:
  0.6 3.6 %copy-start.13 = (bf16[144,144]{1,0:T(8,128)(2,1)S(1)}, bf16[144,144]{1,0:T(8,128)(2,1)}, u32[]{:S(2)}) copy-start(bf16[144,144]{1,0:T(8,128)(2,1)} %constant.31.clone.to_inner) | copy-start | bytes 124420
  0.6 3.6 %copy-start.4 = (bf16[512,512]{1,0:T(8,128)(2,1)S(1)}, bf16[512,512]{1,0:T(8,128)(2,1)}, u32[]{:S(2)}) copy-start(bf16[512,512]{1,0:T(8,128)(2,1)} %constant.30.clone.select) | copy-start | bytes 1572868
  2.6 1.6 %copy-start.3 = (bf16[2,256,384]{2,1,0:T(8,128)(2,1)S(1)}, bf16[2,256,384]{2,1,0:T(8,128)(2,1)}, u32[]{:S(2)}) copy-start(bf16[2,256,384]{2,1,0:T(8,128)(2,1)} %constant.29.clone.cols.rest_14_) | copy-start | bytes 1179652
  2.7 1.6 %copy-start = (bf16[2,192,768]{2,1,0:T(8,128)(2,1)S(1)}, bf16[2,192,768]{2,1,0:T(8,128)(2,1)}, u32[]{:S(2)}) copy-start(bf16[2,192,768]{2,1,0:T(8,128)(2,1)} %rest_11_.3) | copy-start | bytes 1769476
  2.7 1.6 %copy-start.1 = (bf16[2,192,576]{2,1,0:T(8,128)(2,1)S(1)}, bf16[2,192,576]{2,1,0:T(8,128)(2,1)}, u32[]{:S(2)}) copy-start(bf16[2,192,576]{2,1,0:T(8,128)(2,1)} %rest_9_.3) | copy-start | bytes 1327108
  2.7 1.6 %copy-start.2 = (bf16[2,192,192]{2,1,0:T(8,128)(2,1)S(1)}, bf16[2,192,192]{2,1,0:T(8,128)(2,1)}, u32[]{:S(2)}) copy-start(bf16[2,192,192]{2,1,0:T(8,128)(2,1)} %rest_10_.3) | copy-start | bytes 442372
  4.9 0.9 %copy-start.6 = (bf16[384,192]{1,0:T(8,128)(2,1)S(1)}, bf16[384,192]{1,0:T(8,128)(2,1)}, u32[]{:S(2)}) copy-start(bf16[384,192]{1,0:T(8,128)(2,1)} %constant.33.clone.out_cot) | copy-start | bytes 442372
  5.8 0.9 %copy-start.7 = (bf16[384,144]{1,0:T(8,128)(2,1)S(1)}, bf16[384,144]{1,0:T(8,128)(2,1)}, u32[]{:S(2)}) copy-start(bf16[384,144]{1,0:T(8,128)(2,1)} %constant.32.clone.out_first) | copy-start | bytes 331780
  6.7 0.9 %copy-start.8 = (bf16[5,6,24,48]{3,2,1,0:T(8,128)(2,1)S(1)}, bf16[5,6,24,48]{3,2,1,0:T(8,128)(2,1)}, u32[]{:S(2)}) copy-start(bf16[5,6,24,48]{3,2,1,0:T(8,128)(2,1)} %upper.1) | copy-start | bytes 207364
  10.0 19.1 %copy-start.5 = (bf16[288,384]{1,0:T(8,128)(2,1)S(1)}, bf16[288,384]{1,0:T(8,128)(2,1)}, u32[]{:S(2)}) copy-start(bf16[288,384]{1,0:T(8,128)(2,1)} %constant.34.clone.rest_15_) | copy-start | bytes 663556
  10.0 19.1 %copy-start.9 = (bf16[256,144]{1,0:T(8,128)(2,1)S(1)}, bf16[256,144]{1,0:T(8,128)(2,1)}, u32[]{:S(2)}) copy-start(bf16[256,144]{1,0:T(8,128)(2,1)} %constant.35.clone.rest_16_) | copy-start | bytes 221188
  13.8 9.6 %collective-permute-start = (bf16[48,192]{1,0:T(8,128)(2,1)S(1)}, bf16[48,192]{1,0:T(8,128)(2,1)S(1)}, u32[]{:S(2)}, u32[]{:S(2)}) collective-permute-start(bf16[48,192]{1,0:T(8,128)(2,1)S(1)} %get-tuple-element.28), channel_id=1, source_target_pairs={{4,0},{5,1},{6,2},{7,3},{8,4},{9,5},{10,6},{11,7},{12,8},{13,9},{1... | collective-permute-start | bytes 55304 | tf_op jit(solution)/shard_map/ppermute | solution.py:362
  19.9 4.6 %collective-permute-start.1 = (bf16[48,192]{1,0:T(8,128)(2,1)S(1)}, bf16[48,192]{1,0:T(8,128)(2,1)S(1)}, u32[]{:S(2)}, u32[]{:S(2)}) collective-permute-start(bf16[48,192]{1,0:T(8,128)(2,1)S(1)} %get-tuple-element.29), channel_id=1, source_target_pairs={{2,0},{3,1},{0,2},{1,3},{6,4},{7,5},{4,6},{5,7},{10,8},{11,9},{8,1... | collective-permute-start | bytes 55304 | tf_op jit(solution)/shard_map/ppermute | solution.py:362
  21.4 6.2 %collective-permute-start.2 = (bf16[48,192]{1,0:T(8,128)(2,1)S(1)}, bf16[48,192]{1,0:T(8,128)(2,1)S(1)}, u32[]{:S(2)}, u32[]{:S(2)}) collective-permute-start(bf16[48,192]{1,0:T(8,128)(2,1)S(1)} %get-tuple-element.30), channel_id=1, source_target_pairs={{6,0},{7,1},{4,2},{5,3},{10,4},{11,5},{8,6},{9,7},{14,8},{15,9},{1... | collective-permute-start | bytes 55304 | tf_op jit(solution)/shard_map/ppermute | solution.py:362
  21.9 5.7 %collective-permute-start.3 = (bf16[48,192]{1,0:T(8,128)(2,1)S(1)}, bf16[48,192]{1,0:T(8,128)(2,1)S(1)}, u32[]{:S(2)}, u32[]{:S(2)}) collective-permute-start(bf16[48,192]{1,0:T(8,128)(2,1)S(1)} %get-tuple-element.31), channel_id=1, source_target_pairs={{1,0},{0,1},{3,2},{2,3},{5,4},{4,5},{7,6},{6,7},{9,8},{8,9},{11,10... | collective-permute-start | bytes 55304 | tf_op jit(solution)/shard_map/ppermute | solution.py:362
  21.9 5.7 %collective-permute-start.4 = (bf16[48,192]{1,0:T(8,128)(2,1)S(1)}, bf16[48,192]{1,0:T(8,128)(2,1)S(1)}, u32[]{:S(2)}, u32[]{:S(2)}) collective-permute-start(bf16[48,192]{1,0:T(8,128)(2,1)S(1)} %get-tuple-element.32), channel_id=1, source_target_pairs={{5,0},{4,1},{7,2},{6,3},{9,4},{8,5},{11,6},{10,7},{13,8},{12,9},{1... | collective-permute-start | bytes 55304 | tf_op jit(solution)/shard_map/ppermute | solution.py:362
  23.4 4.2 %collective-permute-start.5 = (bf16[48,192]{1,0:T(8,128)(2,1)S(1)}, bf16[48,192]{1,0:T(8,128)(2,1)S(1)}, u32[]{:S(2)}, u32[]{:S(2)}) collective-permute-start(bf16[48,192]{1,0:T(8,128)(2,1)S(1)} %get-tuple-element.33), channel_id=1, source_target_pairs={{3,0},{2,1},{1,2},{0,3},{7,4},{6,5},{5,6},{4,7},{11,8},{10,9},{9,1... | collective-permute-start | bytes 55304 | tf_op jit(solution)/shard_map/ppermute | solution.py:362
  24.5 4.6 %collective-permute-start.6 = (bf16[48,192]{1,0:T(8,128)(2,1)S(1)}, bf16[48,192]{1,0:T(8,128)(2,1)S(1)}, u32[]{:S(2)}, u32[]{:S(2)}) collective-permute-start(bf16[48,192]{1,0:T(8,128)(2,1)S(1)} %get-tuple-element.34), channel_id=1, source_target_pairs={{7,0},{6,1},{5,2},{4,3},{11,4},{10,5},{9,6},{8,7},{15,8},{14,9},{1... | collective-permute-start | bytes 55304 | tf_op jit(solution)/shard_map/ppermute | solution.py:362
  29.1 20.8 %copy-start.10 = (bf16[192,144]{1,0:T(8,128)(2,1)S(1)}, bf16[192,144]{1,0:T(8,128)(2,1)}, u32[]{:S(2)}) copy-start(bf16[192,144]{1,0:T(8,128)(2,1)} %constant.37.clone.rest_20_) | copy-start | bytes 165892
  29.1 20.8 %copy-start.12 = (bf16[144,256]{1,0:T(8,128)(2,1)S(1)}, bf16[144,256]{1,0:T(8,128)(2,1)}, u32[]{:S(2)}) copy-start(bf16[144,256]{1,0:T(8,128)(2,1)} %constant.36.clone.rest_19_) | copy-start | bytes 221188
  35.2 6.8 %collective-permute-start.7 = (bf16[32,192]{1,0:T(8,128)(2,1)S(1)}, bf16[32,192]{1,0:T(8,128)(2,1)S(1)}, u32[]{:S(2)}, u32[]{:S(2)}) collective-permute-start(bf16[32,192]{1,0:T(8,128)(2,1)S(1)} %get-tuple-element.35), channel_id=1, source_target_pairs={{31,0},{30,1},{29,2},{28,3},{3,4},{2,5},{1,6},{0,7},{7,8},{6,9},{5... | collective-permute-start | bytes 36872 | tf_op jit(solution)/shard_map/ppermute | solution.py:362
  36.3 7.1 %collective-permute-start.8 = (bf16[32,192]{1,0:T(8,128)(2,1)S(1)}, bf16[32,192]{1,0:T(8,128)(2,1)S(1)}, u32[]{:S(2)}, u32[]{:S(2)}) collective-permute-start(bf16[32,192]{1,0:T(8,128)(2,1)S(1)} %get-tuple-element.36), channel_id=1, source_target_pairs={{3,0},{2,1},{1,2},{0,3},{7,4},{6,5},{5,6},{4,7},{11,8},{10,9},{9,1... | collective-permute-start | bytes 36872 | tf_op jit(solution)/shard_map/ppermute | solution.py:362
  37.4 6.0 %collective-permute-start.9 = (bf16[32,192]{1,0:T(8,128)(2,1)S(1)}, bf16[32,192]{1,0:T(8,128)(2,1)S(1)}, u32[]{:S(2)}, u32[]{:S(2)}) collective-permute-start(bf16[32,192]{1,0:T(8,128)(2,1)S(1)} %get-tuple-element.37), channel_id=1, source_target_pairs={{29,0},{28,1},{31,2},{30,3},{1,4},{0,5},{3,6},{2,7},{5,8},{4,9},{7... | collective-permute-start | bytes 36872 | tf_op jit(solution)/shard_map/ppermute | solution.py:362
  39.1 4.4 %collective-permute-start.10 = (bf16[32,192]{1,0:T(8,128)(2,1)S(1)}, bf16[32,192]{1,0:T(8,128)(2,1)S(1)}, u32[]{:S(2)}, u32[]{:S(2)}) collective-permute-start(bf16[32,192]{1,0:T(8,128)(2,1)S(1)} %get-tuple-element.38), channel_id=1, source_target_pairs={{1,0},{0,1},{3,2},{2,3},{5,4},{4,5},{7,6},{6,7},{9,8},{8,9},{11,10... | collective-permute-start | bytes 36872 | tf_op jit(solution)/shard_map/ppermute | solution.py:362
  39.1 7.3 %collective-permute-start.11 = (bf16[32,192]{1,0:T(8,128)(2,1)S(1)}, bf16[32,192]{1,0:T(8,128)(2,1)S(1)}, u32[]{:S(2)}, u32[]{:S(2)}) collective-permute-start(bf16[32,192]{1,0:T(8,128)(2,1)S(1)} %get-tuple-element.39), channel_id=1, source_target_pairs={{30,0},{31,1},{28,2},{29,3},{2,4},{3,5},{0,6},{1,7},{6,8},{7,9},{4... | collective-permute-start | bytes 36872 | tf_op jit(solution)/shard_map/ppermute | solution.py:362
  42.0 4.4 %collective-permute-start.12 = (bf16[32,192]{1,0:T(8,128)(2,1)S(1)}, bf16[32,192]{1,0:T(8,128)(2,1)S(1)}, u32[]{:S(2)}, u32[]{:S(2)}) collective-permute-start(bf16[32,192]{1,0:T(8,128)(2,1)S(1)} %get-tuple-element.40), channel_id=1, source_target_pairs={{2,0},{3,1},{0,2},{1,3},{6,4},{7,5},{4,6},{5,7},{10,8},{11,9},{8,1... | collective-permute-start | bytes 36872 | tf_op jit(solution)/shard_map/ppermute | solution.py:362
  43.5 6.4 %collective-permute-start.13 = (bf16[32,192]{1,0:T(8,128)(2,1)S(1)}, bf16[32,192]{1,0:T(8,128)(2,1)S(1)}, u32[]{:S(2)}, u32[]{:S(2)}) collective-permute-start(bf16[32,192]{1,0:T(8,128)(2,1)S(1)} %get-tuple-element.41), channel_id=1, source_target_pairs={{28,0},{29,1},{30,2},{31,3},{0,4},{1,5},{2,6},{3,7},{4,8},{5,9},{6... | collective-permute-start | bytes 36872 | tf_op jit(solution)/shard_map/ppermute | solution.py:362
  52.3 1.4 %collective-permute-start.14 = (bf16[224,192]{1,0:T(8,128)(2,1)S(1)}, bf16[224,192]{1,0:T(8,128)(2,1)S(1)}, u32[]{:S(2)}, u32[]{:S(2)}) collective-permute-start(bf16[224,192]{1,0:T(8,128)(2,1)S(1)} %get-tuple-element.50), channel_id=1, source_target_pairs={{0,1},{1,0},{2,3},{3,2},{4,5},{5,4},{6,7},{7,6},{8,9},{9,8},{10,11... | collective-permute-start | bytes 258056 | tf_op jit(solution)/shard_map/ppermute | solution.py:373
  53.8 5.3 %collective-permute-start.15 = (bf16[224,192]{1,0:T(8,128)(2,1)S(1)}, bf16[224,192]{1,0:T(8,128)(2,1)S(1)}, u32[]{:S(2)}, u32[]{:S(2)}) collective-permute-start(bf16[224,192]{1,0:T(8,128)(2,1)S(1)} %add_convert_fusion.4), channel_id=1, source_target_pairs={{0,2},{2,0},{1,3},{3,1},{4,6},{6,4},{5,7},{7,5},{8,10},{10,8},{9,1... | collective-permute-start | bytes 258056 | tf_op jit(solution)/shard_map/ppermute | solution.py:373
  59.1 4.9 %collective-permute-start.16 = (bf16[224,192]{1,0:T(8,128)(2,1)S(1)}, bf16[224,192]{1,0:T(8,128)(2,1)S(1)}, u32[]{:S(2)}, u32[]{:S(2)}) collective-permute-start(bf16[224,192]{1,0:T(8,128)(2,1)S(1)} %add_convert_fusion.3), channel_id=1, source_target_pairs={{0,4},{4,0},{8,12},{12,8},{16,20},{20,16},{24,28},{28,24},{1,5},{5... | collective-permute-start | bytes 258056 | tf_op jit(solution)/shard_map/ppermute | solution.py:373
  64.0 4.9 %collective-permute-start.17 = (bf16[224,192]{1,0:T(8,128)(2,1)S(1)}, bf16[224,192]{1,0:T(8,128)(2,1)S(1)}, u32[]{:S(2)}, u32[]{:S(2)}) collective-permute-start(bf16[224,192]{1,0:T(8,128)(2,1)S(1)} %add_convert_fusion.2), channel_id=1, source_target_pairs={{0,8},{4,12},{8,0},{12,4},{16,24},{20,28},{24,16},{28,20},{1,9},{5... | collective-permute-start | bytes 258056 | tf_op jit(solution)/shard_map/ppermute | solution.py:373
  68.9 6.4 %collective-permute-start.18 = (bf16[224,192]{1,0:T(8,128)(2,1)S(1)}, bf16[224,192]{1,0:T(8,128)(2,1)S(1)}, u32[]{:S(2)}, u32[]{:S(2)}) collective-permute-start(bf16[224,192]{1,0:T(8,128)(2,1)S(1)} %add_convert_fusion.1), channel_id=1, source_target_pairs={{0,16},{4,20},{8,24},{12,28},{16,0},{20,4},{24,8},{28,12},{1,17},{... | collective-permute-start | bytes 258056 | tf_op jit(solution)/shard_map/ppermute | solution.py:373
  (4 other events, 3.1 us)

commit v2 on v1

--- a/solution.py
+++ b/solution.py
@@ -61,20 +61,21 @@
     return as_half(move)
 
 
-def octants_out(pitch, first, padded_source):
-    move = np.zeros((8 * pitch, 192 if padded_source else CELLS), np.float32)
+def octants_out(pitch, first, flip, source):
+    move = np.zeros((8 * pitch, CELLS), np.float32)
     for z, a, o in cells():
         part, place = octant_of(z, a, o)
-        source = (z * 6 + a) * 16 + o if padded_source else inner_row(z, a, o)
-        move[part * pitch + first + place, source] = 1
+        move[(7 - part if flip else part) * pitch + first + place, source(z, a, o)] = 1
     return as_half(move)
 
 
-def octants_in(pitch, first):
+def octants_in(pitch, first, flip):
     move = np.zeros((CELLS, 8 * pitch), np.float32)
     for z, a, o in cells():
         part, place = octant_of(z, a, o)
-        move[inner_row(z, a, o), part * pitch + first + place] = 1
+        part = 7 - part if flip else part
+        block = (part % 4) * 2 + part // 4
+        move[inner_row(z, a, o), block * pitch + first + place] = 1
     return as_half(move)
 
 
@@ -121,12 +122,12 @@
     return jnp.where(head_lanes(h), 1.0, 0.0).astype(HALF)
 
 
-def build_bias(tbl, block, cols, xs, bias, edges):
+def build_bias(tbl, cols, xs, bias, edges):
     for z in range(2):
         for a in range(6):
             for zu in range(2):
                 start = ((z * 2 + zu) * 6 + a) * 138
-                piece = tbl[block, :, start : start + 138]
+                piece = tbl[0:HEADS, start : start + 138]
                 piece = jnp.concatenate((piece, jnp.zeros((HEADS, 118), FULL)), 1)
                 for p in range(2):
                     for half in range(2):
@@ -204,33 +205,32 @@
     return below, slope
 
 
-def forward_half(x, block, gains, wqkv, wproj, bias, prob):
+def forward_half(x, gains, wqkv, wproj, bias, prob):
     unit, spread = normalise(x)
-    hidden = (unit * gains[block, 0:1, :]).astype(HALF)
-    qkv = dot(hidden, wqkv[block]).astype(HALF)
+    hidden = (unit * gains[0:1, :]).astype(HALF)
+    qkv = dot(hidden, wqkv[...]).astype(HALF)
     q, k, v = (qkv[:, n * WIDTH : (n + 1) * WIDTH] for n in range(3))
     mixed = attend(q, k, v, bias, prob)
-    return (q, k, v), x + dot(mixed, wproj[block])
-
-
-def backward(dflat, block, x, qkv, prob, resid, slope, gains, wqkv, wproj, wup, wdown):
+    return (q, k, v), x + dot(mixed, wproj[...])
+
+
+def backward(dflat, x, qkv, prob, resid, slope, gains, wqkv, wproj, wup, wdown):
     q, k, v = qkv
-    dactive = dot_nt(dflat, wdown[block])
+    dactive = dot(dflat, wdown[...])
     dupward = (dactive * slope).astype(HALF)
-    dnormed = dot_nt(dupward, wup[block])
+    dnormed = dot_nt(dupward, wup[...])
     unit, spread = normalise(resid)
-    dresid = dflat.astype(FULL) + normalise_back(dnormed, unit, spread, gains[block, 1:2, :])
-    dmixed = dot_nt(dresid.astype(HALF), wproj[block]).astype(HALF)
+    dresid = dflat.astype(FULL) + normalise_back(dnormed, unit, spread, gains[1:2, :])
+    dmixed = dot_nt(dresid.astype(HALF), wproj[...]).astype(HALF)
     dq, dk, dv = attend_back(dmixed, q, k, v, prob)
-    weight = wqkv[block]
-    dhidden = dot_nt(dq, weight[:, :WIDTH])
-    dhidden = dhidden + dot_nt(dk, weight[:, WIDTH : 2 * WIDTH])
-    dhidden = dhidden + dot_nt(dv, weight[:, 2 * WIDTH :])
+    dhidden = dot_nt(dq, wqkv[:, :WIDTH])
+    dhidden = dhidden + dot_nt(dk, wqkv[:, WIDTH : 2 * WIDTH])
+    dhidden = dhidden + dot_nt(dv, wqkv[:, 2 * WIDTH :])
     unit, spread = normalise(x)
-    return dresid + normalise_back(dhidden, unit, spread, gains[block, 0:1, :])
-
-
-def gather_patches(upper, surface, section, sections, select, ff, ft):
+    return dresid + normalise_back(dhidden, unit, spread, gains[0:1, :])
+
+
+def gather_patches(upper, surface, section, select, ff, ft):
     base = 4 * section - 2
     for z in range(2):
         for a in range(2):
@@ -255,74 +255,113 @@
     return jnp.concatenate((both[:, :256], both[:, 256:]), 0).astype(HALF)
 
 
-def first_kernel(
-    flags, upper, surface, cot, uembed, sembed, gains, wqkv, wproj, wup, wdown, tbl,
-    select, to_inner, out_first, out_cot, cols, *rest
-):
-    octants, rest = rest[:8], rest[8:]
-    patch_o, x_o, qkv_o, prob, resid_o, slope_o, ff, ft, emb, cots, xs, bias = rest
-    section = flags[0]
-    emb[0:160, :] = uembed[...]
-    emb[160:224, :] = sembed[...]
+def flag(axis):
+    last = lax.axis_index(axis) == lax.axis_size(axis) - 1
+    return jnp.where(last, 1.0, 0.0)
+
+
+def table_rows(tbl, block, table):
+    for h in range(HEADS):
+        table[h : h + 1, 0 : tbl.shape[-1]] = tbl[block * HEADS + h]
+
+
+def first_kernel(*refs):
+    names = (
+        "tbl", "cols", "upper", "surface", "select", "to_inner", "uembed", "sembed", "gains",
+        "wqkv", "wproj", "wup", "wdown", "cot", "out_first", "out_cot",
+    )
+    count = len(names)
+    source, rest = refs[:count], refs[count:]
+    keep_o, send_o, patch_o, x_o, qkv_o, prob, resid_o, slope_o = rest[:8]
+    local, rest = rest[8 : 8 + count], rest[8 + count :]
+    ff, ft, emb, cots, table, xs, bias, sems = rest
+    copies = {}
+    for n, name in enumerate(names):
+        start = source[n].at[0] if name[0] == "w" else source[n]
+        if name == "uembed":
+            target = emb.at[pl.ds(0, 160)]
+        elif name == "sembed":
+            target = emb.at[pl.ds(160, 64)]
+        else:
+            target = local[n]
+        copies[name] = pltpu.make_async_copy(start, target, sems.at[n])
+        copies[name].start()
+    have = dict(zip(names, local))
+
+    def wait(*which):
+        for name in which:
+            copies[name].wait()
+
     emb[224:256, :] = jnp.zeros((32, WIDTH), HALF)
-    cots[...] = jnp.zeros_like(cots)
-    for z in range(2):
-        for a in range(6):
-            cots[(z * 6 + a) * 16 : (z * 6 + a) * 16 + 12, :] = cot[z, a]
-    build_bias(tbl, 0, cols, xs, bias, None)
-    patch = gather_patches(upper, surface, section, None, select, ff, ft)
-    patch = dot(to_inner[...], patch).astype(HALF)
+    wait("tbl", "cols")
+    table_rows(have["tbl"], 0, table)
+    build_bias(table, have["cols"], xs, bias, None)
+    wait("upper", "surface", "select", "to_inner", "uembed", "sembed", "gains", "wqkv")
+    section = lax.axis_index("section")
+    patch = gather_patches(have["upper"], have["surface"], section, have["select"], ff, ft)
+    patch = dot(have["to_inner"][...], patch).astype(HALF)
     patch_o[...] = patch
     latent = dot(patch, emb[...]).astype(HALF)
     x_o[...] = latent
     x = latent.astype(FULL)
-    qkv, resid = forward_half(x, 0, gains, wqkv, wproj, bias, prob)
+    gains = have["gains"].at[0]
+    wait("wproj", "wup", "wdown", "cot", "out_first", "out_cot")
+    cot = have["cot"]
+    for a in range(6):
+        for o in range(12):
+            cots[(a * 12 + o) * 2 : (a * 12 + o) * 2 + 2, :] = cot[a, o].astype(FULL)
+    qkv, resid = forward_half(x, gains, have["wqkv"], have["wproj"], bias, prob)
     for n in range(3):
         qkv_o[n] = qkv[n]
     resid_o[...] = resid
     unit, spread = normalise(resid)
-    normed = (unit * gains[0, 1:2, :]).astype(HALF)
-    upward = dot(normed, wup[0])
+    normed = (unit * gains[1:2, :]).astype(HALF)
+    upward = dot(normed, have["wup"][...])
     below, slope = gelu_parts(upward)
     slope_o[...] = slope.astype(HALF)
     active = (upward * below).astype(HALF)
-    result = (resid + dot(active, wdown[0])).astype(HALF)
-    moved = (dot(out_first[...], result) + dot(out_cot[...], cots[...])).astype(HALF)
-    for n in range(8):
-        octants[n][...] = moved[n * 48 : n * 48 + 48]
-
-
-def second_kernel(flags, *rest):
-    parts, rest = rest[:8], rest[8:]
-    gains, wqkv, wproj, wup, wdown, tbl, cols, into, out_of = rest[:9]
-    octants, rest = rest[9:17], rest[17:]
-    stack, xs, bias, prob = rest
-    build_bias(tbl, 1, cols, xs, bias, (flags[1].astype(FULL), flags[2].astype(FULL)))
-    for n in range(8):
-        stack[n * 48 : n * 48 + 48, :] = parts[n][...]
+    result = (resid + dot_nt(active, have["wdown"][...])).astype(HALF)
+    moved = dot(have["out_first"][...], result)
+    moved = (moved + dot(have["out_cot"][...], cots[...].astype(HALF))).astype(HALF)
+    keep_o[...] = moved[:192]
+    send_o[...] = moved[192:]
+
+
+def bias_kernel(tbl, cols, bias, table, xs):
+    table_rows(tbl, 1, table)
+    build_bias(table, cols, xs, bias, (flag("section"), flag("lat")))
+
+
+def second_kernel(*refs):
+    parts, rest = refs[:4], refs[4:]
+    gains, wqkv, wproj, wup, wdown, bias, into, out_of, keep_o, send_o, stack, prob = rest
+    for n in range(4):
+        stack[n * 96 : n * 96 + 96, :] = parts[n][...]
     both = dot(into[...], stack[...])
     x, dflat = both[:CELLS], both[CELLS:].astype(HALF)
-    qkv, resid = forward_half(x, 1, gains, wqkv, wproj, bias, prob)
+    gains, wqkv, wproj, wup, wdown = (w.at[1] for w in (gains, wqkv, wproj, wup, wdown))
+    qkv, resid = forward_half(x, gains, wqkv, wproj, bias, prob)
     unit, spread = normalise(resid)
-    normed = (unit * gains[1, 1:2, :]).astype(HALF)
-    upward = dot(normed, wup[1])
+    normed = (unit * gains[1:2, :]).astype(HALF)
+    upward = dot(normed, wup[...])
     slope = gelu_parts(upward)[1]
-    dx = backward(dflat, 1, x, qkv, prob, resid, slope, gains, wqkv, wproj, wup, wdown)
+    dx = backward(dflat, x, qkv, prob, resid, slope, gains, wqkv, wproj, wup, wdown)
     moved = dot(out_of[...], dx.astype(HALF)).astype(HALF)
-    for n in range(8):
-        octants[n][...] = moved[n * 32 : n * 32 + 32]
-
-
-def third_kernel(*rest):
-    parts, rest = rest[:8], rest[8:]
+    keep_o[...] = moved[:128]
+    send_o[...] = moved[128:]
+
+
+def third_kernel(*refs):
+    parts, rest = refs[:4], refs[4:]
     gains, wqkv, wproj, wup, wdown, patch, x_i, qkv_i, prob, resid, slope, into, out_of = rest[:13]
-    grad_o, terms_o, stack = rest[13:]
-    for n in range(8):
-        stack[n * 32 : n * 32 + 32, :] = parts[n][...]
+    grad_o, mine_o, other_o, stack, terms = rest[13:]
+    for n in range(4):
+        stack[n * 64 : n * 64 + 64, :] = parts[n][...]
     dflat = dot(into[...], stack[...]).astype(HALF)
     qkv = tuple(qkv_i[n] for n in range(3))
+    gains, wqkv, wproj, wup, wdown = (w.at[0] for w in (gains, wqkv, wproj, wup, wdown))
     dx = backward(
-        dflat, 0, x_i[...].astype(FULL), qkv, prob, resid[...], slope[...].astype(FULL),
+        dflat, x_i[...].astype(FULL), qkv, prob, resid[...], slope[...].astype(FULL),
         gains, wqkv, wproj, wup, wdown,
     )
     grad = dx.astype(HALF)
@@ -330,19 +369,25 @@
     for z in range(2):
         for a in range(6):
             grad_o[z, a] = moved[(z * 6 + a) * 16 : (z * 6 + a) * 16 + 12]
-    terms_o[...] = dot_tn(patch[...], grad)[:224].astype(HALF)
-
-
-def call(kernel, outs, scratch, *args):
-    vmem = pl.BlockSpec(memory_space=pltpu.VMEM)
-    smem = pl.BlockSpec(memory_space=pltpu.SMEM)
+    terms[...] = dot_tn(patch[...], grad)
+    place = lax.axis_index("section") % 2
+    mine_o[...] = terms[pl.ds(pl.multiple_of(place * 112, 16), 112), :].astype(HALF)
+    other_o[...] = terms[pl.ds(pl.multiple_of(112 - place * 112, 16), 112), :].astype(HALF)
+
+
+vmem = pl.BlockSpec(memory_space=pltpu.VMEM)
+where_it_lies = pl.BlockSpec(memory_space=pl.ANY)
+
+
+def call(kernel, outs, scratch, *args, spec=vmem, flops=1000000):
     return pl.pallas_call(
         kernel,
         out_shape=outs,
-        in_specs=[smem if a.dtype == jnp.int32 else vmem for a in args],
+        in_specs=[spec for a in args],
         out_specs=jax.tree.map(lambda _: vmem, outs),
         scratch_shapes=scratch,
         compiler_params=pltpu.CompilerParams(vmem_limit_bytes=30 * 2**20),
+        cost_estimate=pl.CostEstimate(flops=flops, bytes_accessed=1000000, transcendentals=0),
     )(*args)
 
 
@@ -350,30 +395,56 @@
     return jax.ShapeDtypeStruct(dims, dtype)
 
 
-def move_octant(block, step):
-    names, step = ("lon", "lat", "section"), step[::-1]
-    if not any(step):
+def fetch(block, steps):
+    names = ("lon", "lat", "section")
+    axes = [name for name in names if steps.get(name, 0)]
+    if not axes:
         return block
-    sizes = [lax.axis_size(name) for name in names]
+    sizes = [lax.axis_size(name) for name in axes]
     pairs = []
     for place in np.ndindex(*sizes):
-        source = [(p + s) % n for p, s, n in zip(place, step, sizes)]
-        pairs.append((int(np.ravel_multi_index(source, sizes)), int(np.ravel_multi_index(place, sizes))))
-    return lax.ppermute(block, names, pairs)
-
-
-def add_up(terms):
+        source = [(p + steps[name]) % n for p, name, n in zip(place, axes, sizes)]
+        pairs.append(
+            (int(np.ravel_multi_index(source, sizes)), int(np.ravel_multi_index(place, sizes)))
+        )
+    return lax.ppermute(block, tuple(axes), pairs)
+
+
+def exchange(keep, send, way):
+    pitch = keep.shape[0] // 4
+    got = fetch(send, {"section": way})
+    blocks = []
+    for n in range(4):
+        rows = slice(n * pitch, (n + 1) * pitch)
+        block = jnp.concatenate((keep[rows], got[rows]), 0)
+        blocks.append(fetch(block, {"lat": way * (n // 2), "lon": way * (n % 2)}))
+    return blocks
+
+
+def add_up(mine, other):
+    sections = lax.axis_size("section")
+    place = lax.axis_index("section") % 2
+    if sections % 2:
+        raise ValueError("odd sections")
+    swap = [(i, i ^ 1) for i in range(sections)]
+
+    def both(a, b):
+        return (a.astype(FULL) + b.astype(FULL)).astype(HALF)
+
+    total = both(mine, lax.ppermute(other, "section", swap))
     for name in ("section", "lat", "lon"):
         size = lax.axis_size(name)
         if size & (size - 1):
-            terms = lax.psum(terms.astype(FULL), name).astype(HALF)
-            continue
-        step = 1
+            raise ValueError("axis size")
+        step = 2 if name == "section" else 1
         while step < size:
-            other = lax.ppermute(terms, name, [(i, i ^ step) for i in range(size)])
-            terms = (terms.astype(FULL) + other.astype(FULL)).astype(HALF)
+            pairs = [(i, i ^ step) for i in range(size)]
+            total = both(total, lax.ppermute(total, name, pairs))
             step *= 2
-    return terms.astype(FULL)
+    far = lax.ppermute(total, "section", swap)
+    first = jnp.where(place == 0, total, far)
+    second = jnp.where(place == 0, far, total)
+    return jnp.concatenate((first, second), 0).astype(FULL)
 
 
 def on_device(
@@ -389,18 +460,33 @@
     earth_bias,
     out_grad,
 ):
-    section, band = lax.axis_index("section"), lax.axis_index("lat")
     sections, bands = lax.axis_size("section"), lax.axis_size("lat")
     levels, rows, columns, width = out_grad.shape
-    flags = jnp.stack((section, section == sections - 1, band == bands - 1)).astype(jnp.int32)
-    table = earth_bias.reshape(2, HEADS, earth_bias.shape[-1])
-    weights = (norm_gains, qkv_weight, proj_weight, up_weight, down_weight)
+    positions = earth_bias.shape[-1]
+    table = earth_bias.transpose(0, 1, 3, 2, 4).reshape(2 * HEADS, 1, positions)
+    weights = (norm_gains, qkv_weight, proj_weight, up_weight, down_weight.transpose(0, 2, 1))
     cols = jnp.asarray(bias_columns())
-    scratch_bias = [pltpu.VMEM((4, CELLS, 128), FULL), pltpu.VMEM((HEADS * CELLS, CELLS), FULL)]
-    results = call(
+
+    def from_cot(z, a, o):
+        return (a * 12 + o) * 2 + z
+
+    operands = (
+        table, cols, upper_fields, surface_fields, jnp.asarray(patch_select()),
+        jnp.asarray(natural_to_inner()), upper_embed, surface_embed, *weights,
+        out_grad.transpose(1, 2, 0, 3),
+        jnp.asarray(octants_out(48, 0, True, inner_row)),
+        jnp.asarray(octants_out(48, 18, True, from_cot)),
+    )
+    local = [
+        pltpu.VMEM(v.shape[1:] if 9 <= n < 13 else v.shape, v.dtype) for n, v in enumerate(operands)
+    ]
+    local[6] = local[7] = pltpu.VMEM((16, 128), HALF)
+    scratch_bias = [pltpu.VMEM((8, 3328), FULL), pltpu.VMEM((4, CELLS, 128), FULL)]
+    keep, send, patch, x, qkv, prob, resid, slope = call(
         first_kernel,
-        [shape((48, WIDTH))] * 8
-        + [
+        [
+            shape((192, WIDTH)),
+            shape((192, WIDTH)),
             shape((CELLS, 256)),
             shape((CELLS, WIDTH)),
             shape((3, CELLS, WIDTH)),
@@ -408,39 +494,38 @@
             shape((CELLS, WIDTH), FULL),
             shape((CELLS, 4 * WIDTH)),
         ],
-        [
+        local
+        + [
             pltpu.VMEM((576, 128), FULL),
             pltpu.VMEM((288, 128), FULL),
             pltpu.VMEM((256, WIDTH), HALF),
-            pltpu.VMEM((192, WIDTH), HALF),
+            pltpu.VMEM((CELLS, WIDTH), FULL),
         ]
-        + scratch_bias,
-        flags, upper_fields, surface_fields, out_grad, upper_embed, surface_embed, *weights, table,
-        jnp.asarray(patch_select()), jnp.asarray(natural_to_inner()),
-        jnp.asarray(octants_out(48, 0, False)), jnp.asarray(octants_out(48, 18, True)), cols,
-    )
-    octants, (patch, x, qkv, prob, resid, slope) = results[:8], results[8:]
-    steps = list(np.ndindex(2, 2, 2))
-    shifted = [move_octant(octants[7 - n], steps[n]) for n in range(8)]
-    into = np.concatenate((octants_in(48, 0), octants_in(48, 18)), 0)
-    back = call(
+        + scratch_bias
+        + [
+            pltpu.VMEM((HEADS * CELLS, CELLS), FULL),
+            pltpu.SemaphoreType.DMA((len(operands),)),
+        ],
+        *operands,
+        spec=where_it_lies,
+    )
+    bias = call(bias_kernel, shape((HEADS * CELLS, CELLS), FULL), scratch_bias, table, cols)
+    into = np.concatenate((octants_in(48, 0, False), octants_in(48, 18, False)), 0)
+    keep, send = call(
         second_kernel,
-        [shape((32, WIDTH))] * 8,
-        [pltpu.VMEM((8 * 48, WIDTH), HALF)]
-        + scratch_bias
-        + [pltpu.VMEM((HEADS * CELLS, CELLS), HALF)],
-        flags, *shifted, *weights, table, cols,
-        jnp.asarray(into), jnp.asarray(octants_out(32, 0, False)),
-    )
-    returned = [move_octant(back[n], tuple(-s for s in steps[n])) for n in range(8)][::-1]
-    latent_grad, terms = call(
+        [shape((128, WIDTH))] * 2,
+        [pltpu.VMEM((8 * 48, WIDTH), HALF), pltpu.VMEM((HEADS * CELLS, CELLS), HALF)],
+        *exchange(keep, send, 1), *weights, bias,
+        jnp.asarray(into), jnp.asarray(octants_out(32, 0, False, inner_row)),
+    )
+    latent_grad, mine, other = call(
         third_kernel,
-        [shape((2, 6, 12, WIDTH)), shape((224, WIDTH))],
-        [pltpu.VMEM((8 * 32, WIDTH), HALF)],
-        *returned, *weights, patch, x, qkv, prob, resid, slope,
-        jnp.asarray(octants_in(32, 0)), jnp.asarray(inner_to_padded()),
-    )
-    total = add_up(terms)
+        [shape((2, 6, 12, WIDTH)), shape((112, WIDTH)), shape((112, WIDTH))],
+        [pltpu.VMEM((8 * 32, WIDTH), HALF), pltpu.VMEM((256, WIDTH), FULL)],
+        *exchange(keep, send, -1), *weights, patch, x, qkv, prob, resid, slope,
+        jnp.asarray(octants_in(32, 0, True)), jnp.asarray(inner_to_padded()),
+    )
+    total = add_up(mine, other)
     scale = float(levels * sections * rows * bands * columns * lax.axis_size("lon")) ** (-0.5)
     return (latent_grad, total[:160] * scale, total[160:] * scale)
 

time: 77.1 us -> 73.7 us (0.956)
  starting transfers between devices: 21.1 us -> 12.6 us
  local copies, waits for them, and re-layouts: 9.92 us -> 15.4 us
  waiting for transfers between devices: 31 us -> 28.9 us
  Pallas kernels: 12.2 us -> 13.7 us
    ppermute x19 -> x14, starting transfers between devices: 21.1 us -> 12.6 us  [the longest x8 10.3 us: fetch(): return lax.ppermute(block, tuple(axes), pairs)]
    unnamed x38 -> x49, local copies, waits for them, and re-layouts: 9.89 us -> 15.4 us
    ppermute x19 -> x14, waiting for transfers between devices: 31 us -> 28.9 us  [the longest x4 15.8 us: add_up(): total = both(total, lax.ppermute(total, name, pairs))]
    pallas_call x3 -> x4, Pallas kernels: 12.2 us -> 13.7 us  [call(): pl.pallas_call(kernel, out_shape=outs, in_specs=[spec for a in args], out...]
  transfers between devices with their start and end apart: 19 -> 14, of which waited for: 9 -> 12; matrix products, arithmetic and copies ran while one was open for 1% -> 1% of each run, Pallas kernels for 0% -> 1%
where the time goes in v2:
time: 73.7 us; the launch traced here: 73 us
  waiting for transfers between devices  28.9 us (39%)
  local copies, waits for them, and re-layouts  15.4 us (21%)
  Pallas kernels  13.7 us (19%)
  starting transfers between devices  12.6 us (17%)
  other arithmetic  1.51 us (2%)
  between operations  0.91 us (1%)
    ppermute x4, waiting for transfers between devices, add_up(): total = both(total, lax.ppermute(total, name, pairs))  15.8 us
    unnamed x49, local copies, waits for them, and re-layouts  15.4 us
    pallas_call x4, Pallas kernels, call(): pl.pallas_call(kernel, out_shape=outs, in_specs=[spec for a in args], out...  13.7 us
    ppermute x8, waiting for transfers between devices, fetch(): return lax.ppermute(block, tuple(axes), pairs)  11.4 us
    ppermute x8, starting transfers between devices, fetch(): return lax.ppermute(block, tuple(axes), pairs)  10.3 us
    ppermute x4, starting transfers between devices, add_up(): total = both(total, lax.ppermute(total, name, pairs))  2.16 us
  transfers between devices with their start and end apart: 14, of which 12 were waited for; matrix products, arithmetic and copies ran while one was open for 1% of the time, Pallas kernels for 1%

profile of v2, /device:TPU:0, one launch (start us, length us, event | category | flops | bytes accessed | tf_op | source)
XLA Modules:
  0.0 73.0 jit_solution(13941368863220391421)
XLA Ops:
  1.3 1.1 %copy-done = bf16[2,192,768]{2,1,0:T(8,128)(2,1)S(1)} copy-done((bf16[2,192,768]{2,1,0:T(8,128)(2,1)S(1)}, bf16[2,192,768]{2,1,0:T(8,128)(2,1)}, u32[]{:S(2)}) %copy-start) | copy-done | bytes 589848
  2.4 1.1 %copy-done.2 = bf16[2,768,192]{1,2,0:T(8,128)(2,1)S(1)} copy-done((bf16[2,768,192]{1,2,0:T(8,128)(2,1)S(1)}, bf16[2,768,192]{1,2,0:T(8,128)(2,1)}, u32[]{:S(2)}) %copy-start.2) | copy-done | bytes 589848
  3.5 1.0 %copy-done.4 = bf16[2,192,576]{2,1,0:T(8,128)(2,1)S(1)} copy-done((bf16[2,192,576]{2,1,0:T(8,128)(2,1)S(1)}, bf16[2,192,576]{2,1,0:T(8,128)(2,1)}, u32[]{:S(2)}) %copy-start.4) | copy-done | bytes 442392
  4.5 0.9 %copy-done.6 = bf16[2,192,192]{2,1,0:T(8,128)(2,1)S(1)} copy-done((bf16[2,192,192]{2,1,0:T(8,128)(2,1)S(1)}, bf16[2,192,192]{2,1,0:T(8,128)(2,1)}, u32[]{:S(2)}) %copy-start.6) | copy-done | bytes 147480
  5.4 1.0 %copy-done.8 = bf16[2,256,384]{2,1,0:T(8,128)(2,1)S(1)} copy-done((bf16[2,256,384]{2,1,0:T(8,128)(2,1)S(1)}, bf16[2,256,384]{2,1,0:T(8,128)(2,1)}, u32[]{:S(2)}) %copy-start.8) | copy-done | bytes 393240
  6.4 0.9 %copy-done.9 = f32[2,1,1,6,3312]{4,2,3,1,0:T(1,128)S(1)} copy-done((f32[2,1,1,6,3312]{4,2,3,1,0:T(1,128)S(1)}, f32[2,1,1,6,3312]{4,2,3,1,0:T(1,128)}, u32[]{:S(2)}) %copy-start.9) | copy-done | bytes 159000
  7.3 1.0 %copy-done.10 = bf16[512,512]{1,0:T(8,128)(2,1)S(1)} copy-done((bf16[512,512]{1,0:T(8,128)(2,1)S(1)}, bf16[512,512]{1,0:T(8,128)(2,1)}, u32[]{:S(2)}) %copy-start.10) | copy-done | bytes 524312
  8.4 0.9 %copy-done.12 = bf16[384,144]{1,0:T(8,128)(2,1)S(1)} copy-done((bf16[384,144]{1,0:T(8,128)(2,1)S(1)}, bf16[384,144]{1,0:T(8,128)(2,1)}, u32[]{:S(2)}) %copy-start.12) | copy-done | bytes 110616
  9.3 0.9 %copy-done.13 = bf16[384,144]{1,0:T(8,128)(2,1)S(1)} copy-done((bf16[384,144]{1,0:T(8,128)(2,1)S(1)}, bf16[384,144]{1,0:T(8,128)(2,1)}, u32[]{:S(2)}) %copy-start.13) | copy-done | bytes 110616
  10.2 0.9 %copy-done.14 = bf16[5,6,24,48]{3,2,1,0:T(8,128)(2,1)S(1)} copy-done((bf16[5,6,24,48]{3,2,1,0:T(8,128)(2,1)S(1)}, bf16[5,6,24,48]{3,2,1,0:T(8,128)(2,1)}, u32[]{:S(2)}) %copy-start.14) | copy-done | bytes 69144
  11.1 0.9 %copy-done.17 = bf16[160,192]{1,0:T(8,128)(2,1)S(1)} copy-done((bf16[160,192]{1,0:T(8,128)(2,1)S(1)}, bf16[160,192]{1,0:T(8,128)(2,1)}, u32[]{:S(2)}) %copy-start.17) | copy-done | bytes 61464
  12.0 0.9 %copy-done.19 = bf16[2,6,12,192]{3,0,2,1:T(2,128)(2,1)S(1)} copy-done((bf16[2,6,12,192]{3,0,2,1:T(2,128)(2,1)S(1)}, bf16[2,6,12,192]{3,0,2,1:T(2,128)(2,1)}, u32[]{:S(2)}) %copy-start.19) | copy-done | bytes 55320
  12.9 0.9 %copy-done.20 = bf16[144,144]{1,0:T(8,128)(2,1)S(1)} copy-done((bf16[144,144]{1,0:T(8,128)(2,1)S(1)}, bf16[144,144]{1,0:T(8,128)(2,1)}, u32[]{:S(2)}) %copy-start.20) | copy-done | bytes 41496
  13.8 0.8 %copy-done.22 = bf16[64,192]{1,0:T(8,128)(2,1)S(1)} copy-done((bf16[64,192]{1,0:T(8,128)(2,1)S(1)}, bf16[64,192]{1,0:T(8,128)(2,1)}, u32[]{:S(2)}) %copy-start.22) | copy-done | bytes 24600
  14.6 0.7 %copy-done.23 = bf16[4,24,48]{2,1,0:T(8,128)(2,1)S(1)} copy-done((bf16[4,24,48]{2,1,0:T(8,128)(2,1)S(1)}, bf16[4,24,48]{2,1,0:T(8,128)(2,1)}, u32[]{:S(2)}) %copy-start.23) | copy-done | bytes 9240
  15.3 6.1 %shard_map.211 = (bf16[192,192]{1,0:T(8,128)(2,1)S(1)}, bf16[192,192]{1,0:T(8,128)(2,1)S(1)}, bf16[144,256]{1,0:T(8,128)(2,1)S(1)}, bf16[144,192]{1,0:T(8,128)(2...) custom-call(f32[12,1,3312]{2,1,0:T(1,128)S(1)} %bitcast.6, ...), custom_call_target="tpu_custom_call" | custom-call | flops 1000000 | bytes 1000000 | tf_op jit(solution)/shard_map/pallas_call | solution.py:383
  21.9 0.9 %shard_map.212.refs_9_ = f32[864,144]{1,0:T(8,128)S(1)} custom-call(f32[12,1,3312]{2,1,0:T(1,128)S(1)} %bitcast.7, bf16[2,256,384]{2,1,0:T(8,128)(2,1)S(1)} %copy-done.8), custom_call_target="tpu_custom_call" | custom-call | flops 1000000 | bytes 1000000 | tf_op jit(solution)/shard_map/pallas_call | solution.py:383
  22.9 6.9 %collective-permute-start.3 = (bf16[96,192]{1,0:T(8,128)(2,1)S(1)}, bf16[96,192]{1,0:T(8,128)(2,1)S(1)}, u32[]{:S(2)}, u32[]{:S(2)}) collective-permute-start(bf16[96,192]{1,0:T(8,128)(2,1)S(1)} %pad_maximum_fusion.3), channel_id=1, source_target_pairs={{6,0},{4,2},{10,4},{8,6},{14,8},{12,10},{18,12},{16,14},{22,16},{2... | collective-permute-start | bytes 110600 | tf_op jit(solution)/shard_map/ppermute | solution.py:410
  30.9 0.8 %collective-permute-done.3.refs_3_ = bf16[96,192]{1,0:T(8,128)(2,1)S(1)} collective-permute-done((bf16[96,192]{1,0:T(8,128)(2,1)S(1)}, bf16[96,192]{1,0:T(8,128)(2,1)S(1)}, u32[]{:S(2)}, u32[]{:S(2)}) %collective-permute-start.3) | collective-permute-done | bytes 36896 | tf_op jit(solution)/shard_map/ppermute | solution.py:410
  31.7 2.2 %collective-permute-done.2.refs_2_ = bf16[96,192]{1,0:T(8,128)(2,1)S(1)} collective-permute-done((bf16[96,192]{1,0:T(8,128)(2,1)S(1)}, bf16[96,192]{1,0:T(8,128)(2,1)S(1)}, u32[]{:S(2)}, u32[]{:S(2)}) %collective-permute-start.2) | collective-permute-done | bytes 36896 | tf_op jit(solution)/shard_map/ppermute | solution.py:410
  34.5 4.1 %shard_map.213 = (bf16[128,192]{1,0:T(8,128)(2,1)S(1)}, bf16[128,192]{1,0:T(8,128)(2,1)S(1)}) custom-call(bf16[96,192]{1,0:T(8,128)(2,1)S(1)} %pad_maximum_fusion.refs_0_, bf16[96,192]{1,0:T(8,128)(2,1)S(1)} %collective-permute-done.1.refs_1_, bf16[96,192]{1,0:T(8,128)(2,1)S(1)} %collective-permute-done.2.refs_2_, ...), custom_call_target="tpu_custom_call" | custom-call | flops 1000000 | bytes 1000000 | tf_op jit(solution)/shard_map/pallas_call | solution.py:383
  38.8 1.2 %collective-permute-done.4 = bf16[128,192]{1,0:T(8,128)(2,1)S(1)} collective-permute-done((bf16[128,192]{1,0:T(8,128)(2,1)S(1)}, bf16[128,192]{1,0:T(8,128)(2,1)S(1)}, u32[]{:S(2)}, u32[]{:S(2)}) %collective-permute-start.4) | collective-permute-done | bytes 49184 | tf_op jit(solution)/shard_map/ppermute | solution.py:410
  40.7 1.0 %collective-permute-start.6 = (bf16[64,192]{1,0:T(8,128)(2,1)S(1)}, bf16[64,192]{1,0:T(8,128)(2,1)S(1)}, u32[]{:S(2)}, u32[]{:S(2)}) collective-permute-start(bf16[64,192]{1,0:T(8,128)(2,1)S(1)} %pad_maximum_fusion.6), channel_id=1, source_target_pairs={{2,0},{0,2},{3,1},{1,3},{6,4},{4,6},{7,5},{5,7},{10,8},{8,10},{11,... | collective-permute-start | bytes 73736 | tf_op jit(solution)/shard_map/ppermute | solution.py:410
  41.8 5.8 %collective-permute-done.7.refs_3_ = bf16[64,192]{1,0:T(8,128)(2,1)S(1)} collective-permute-done((bf16[64,192]{1,0:T(8,128)(2,1)S(1)}, bf16[64,192]{1,0:T(8,128)(2,1)S(1)}, u32[]{:S(2)}, u32[]{:S(2)}) %collective-permute-start.7) | collective-permute-done | bytes 24608 | tf_op jit(solution)/shard_map/ppermute | solution.py:410
  47.6 0.7 %collective-permute-done.5.refs_1_ = bf16[64,192]{1,0:T(8,128)(2,1)S(1)} collective-permute-done((bf16[64,192]{1,0:T(8,128)(2,1)S(1)}, bf16[64,192]{1,0:T(8,128)(2,1)S(1)}, u32[]{:S(2)}, u32[]{:S(2)}) %collective-permute-start.5) | collective-permute-done | bytes 24608 | tf_op jit(solution)/shard_map/ppermute | solution.py:410
  48.4 2.6 %shard_map.214 = (bf16[2,6,12,192]{3,2,1,0:T(8,128)(2,1)S(1)}, bf16[112,192]{1,0:T(8,128)(2,1)S(1)}, bf16[112,192]{1,0:T(8,128)(2,1)S(1)}) custom-call(bf16[64,192]{1,0:T(8,128)(2,1)S(1)} %pad_maximum_fusion.4.refs_0_, bf16[64,192]{1,0:T(8,128)(2,1)S(1)} %collective-permute-done.5.refs_1_, bf16[64,192]{1,0:T(8,128)(2,1)S(1)} %collective-permute-done.6.refs_2_, ...), custom_call_target="tpu_custom_call" | custom-call | flops 1000000 | bytes 1000000 | tf_op jit(solution)/shard_map/pallas_call | solution.py:383
  51.0 1.2 %collective-permute-done.8 = bf16[112,192]{1,0:T(8,128)(2,1)S(1)} collective-permute-done((bf16[112,192]{1,0:T(8,128)(2,1)S(1)}, bf16[112,192]{1,0:T(8,128)(2,1)S(1)}, u32[]{:S(2)}, u32[]{:S(2)}) %collective-permute-start.8) | collective-permute-done | bytes 43040 | tf_op jit(solution)/shard_map/ppermute | solution.py:434
  52.3 1.5 %collective-permute-start.9 = (bf16[112,192]{1,0:T(8,128)(2,1)S(1)}, bf16[112,192]{1,0:T(8,128)(2,1)S(1)}, u32[]{:S(2)}, u32[]{:S(2)}) collective-permute-start(bf16[112,192]{1,0:T(8,128)(2,1)S(1)} %add_convert_fusion.4), channel_id=1, source_target_pairs={{0,2},{2,0},{1,3},{3,1},{4,6},{6,4},{5,7},{7,5},{8,10},{10,8},{9,1... | collective-permute-start | bytes 129032 | tf_op jit(solution)/shard_map/ppermute | solution.py:442
  53.8 2.7 %collective-permute-done.9 = bf16[112,192]{1,0:T(8,128)(2,1)S(1)} collective-permute-done((bf16[112,192]{1,0:T(8,128)(2,1)S(1)}, bf16[112,192]{1,0:T(8,128)(2,1)S(1)}, u32[]{:S(2)}, u32[]{:S(2)}) %collective-permute-start.9) | collective-permute-done | bytes 43040 | tf_op jit(solution)/shard_map/ppermute | solution.py:442
  56.6 4.2 %collective-permute-done.10 = bf16[112,192]{1,0:T(8,128)(2,1)S(1)} collective-permute-done((bf16[112,192]{1,0:T(8,128)(2,1)S(1)}, bf16[112,192]{1,0:T(8,128)(2,1)S(1)}, u32[]{:S(2)}, u32[]{:S(2)}) %collective-permute-start.10) | collective-permute-done | bytes 43040 | tf_op jit(solution)/shard_map/ppermute | solution.py:442
  60.9 4.2 %collective-permute-done.11 = bf16[112,192]{1,0:T(8,128)(2,1)S(1)} collective-permute-done((bf16[112,192]{1,0:T(8,128)(2,1)S(1)}, bf16[112,192]{1,0:T(8,128)(2,1)S(1)}, u32[]{:S(2)}, u32[]{:S(2)}) %collective-permute-start.11) | collective-permute-done | bytes 43040 | tf_op jit(solution)/shard_map/ppermute | solution.py:442
  65.6 4.7 %collective-permute-done.12 = bf16[112,192]{1,0:T(8,128)(2,1)S(1)} collective-permute-done((bf16[112,192]{1,0:T(8,128)(2,1)S(1)}, bf16[112,192]{1,0:T(8,128)(2,1)S(1)}, u32[]{:S(2)}, u32[]{:S(2)}) %collective-permute-start.12) | collective-permute-done | bytes 43040 | tf_op jit(solution)/shard_map/ppermute | solution.py:442
  (70 shorter events, 7.4 us)
Async XLA Ops:
  1.3 1.1 %copy-start = (bf16[2,192,768]{2,1,0:T(8,128)(2,1)S(1)}, bf16[2,192,768]{2,1,0:T(8,128)(2,1)}, u32[]{:S(2)}) copy-start(bf16[2,192,768]{2,1,0:T(8,128)(2,1)} %refs_7_.5) | copy-start | bytes 1769476
  2.4 1.1 %copy-start.2 = (bf16[2,768,192]{1,2,0:T(8,128)(2,1)S(1)}, bf16[2,768,192]{1,2,0:T(8,128)(2,1)}, u32[]{:S(2)}) copy-start(bf16[2,768,192]{1,2,0:T(8,128)(2,1)} %param.28) | copy-start | bytes 1769476
  3.5 1.0 %copy-start.4 = (bf16[2,192,576]{2,1,0:T(8,128)(2,1)S(1)}, bf16[2,192,576]{2,1,0:T(8,128)(2,1)}, u32[]{:S(2)}) copy-start(bf16[2,192,576]{2,1,0:T(8,128)(2,1)} %refs_5_.4) | copy-start | bytes 1327108
  4.5 0.9 %copy-start.6 = (bf16[2,192,192]{2,1,0:T(8,128)(2,1)S(1)}, bf16[2,192,192]{2,1,0:T(8,128)(2,1)}, u32[]{:S(2)}) copy-start(bf16[2,192,192]{2,1,0:T(8,128)(2,1)} %refs_6_.5) | copy-start | bytes 442372
  5.4 1.0 %copy-start.8 = (bf16[2,256,384]{2,1,0:T(8,128)(2,1)S(1)}, bf16[2,256,384]{2,1,0:T(8,128)(2,1)}, u32[]{:S(2)}) copy-start(bf16[2,256,384]{2,1,0:T(8,128)(2,1)} %constant.39.clone.refs_1_.cols) | copy-start | bytes 1179652
  6.4 0.9 %copy-start.9 = (f32[2,1,1,6,3312]{4,2,3,1,0:T(1,128)S(1)}, f32[2,1,1,6,3312]{4,2,3,1,0:T(1,128)}, u32[]{:S(2)}) copy-start(f32[2,1,1,6,3312]{4,2,3,1,0:T(1,128)} %param.29) | copy-start | bytes 476932
  7.3 1.0 %copy-start.10 = (bf16[512,512]{1,0:T(8,128)(2,1)S(1)}, bf16[512,512]{1,0:T(8,128)(2,1)}, u32[]{:S(2)}) copy-start(bf16[512,512]{1,0:T(8,128)(2,1)} %constant.40.clone.refs_4_) | copy-start | bytes 1572868
  8.4 0.9 %copy-start.12 = (bf16[384,144]{1,0:T(8,128)(2,1)S(1)}, bf16[384,144]{1,0:T(8,128)(2,1)}, u32[]{:S(2)}) copy-start(bf16[384,144]{1,0:T(8,128)(2,1)} %constant.42.clone.refs_14_) | copy-start | bytes 331780
  9.3 0.9 %copy-start.13 = (bf16[384,144]{1,0:T(8,128)(2,1)S(1)}, bf16[384,144]{1,0:T(8,128)(2,1)}, u32[]{:S(2)}) copy-start(bf16[384,144]{1,0:T(8,128)(2,1)} %constant.43.clone.refs_15_) | copy-start | bytes 331780
  10.2 0.9 %copy-start.14 = (bf16[5,6,24,48]{3,2,1,0:T(8,128)(2,1)S(1)}, bf16[5,6,24,48]{3,2,1,0:T(8,128)(2,1)}, u32[]{:S(2)}) copy-start(bf16[5,6,24,48]{3,2,1,0:T(8,128)(2,1)} %refs_2_.1) | copy-start | bytes 207364
  21.4 1.5 %collective-permute-start = (bf16[192,192]{1,0:T(8,128)(2,1)S(1)}, bf16[192,192]{1,0:T(8,128)(2,1)S(1)}, u32[]{:S(2)}, u32[]{:S(2)}) collective-permute-start(bf16[192,192]{1,0:T(8,128)(2,1)S(1)} %get-tuple-element.17), channel_id=1, source_target_pairs={{1,0},{0,1},{3,2},{2,3},{5,4},{4,5},{7,6},{6,7},{9,8},{8,9},{11,10... | collective-permute-start | bytes 221192 | tf_op jit(solution)/shard_map/ppermute | solution.py:410
  21.9 12.6 %copy-start.3 = (bf16[2,768,192]{1,2,0:T(8,128)(2,1)S(1)}, bf16[2,768,192]{1,2,0:T(8,128)(2,1)}, u32[]{:S(2)}) copy-start(bf16[2,768,192]{1,2,0:T(8,128)(2,1)} %param.28) | copy-start | bytes 1769476
  21.9 12.6 %copy-start.5 = (bf16[2,192,576]{2,1,0:T(8,128)(2,1)S(1)}, bf16[2,192,576]{2,1,0:T(8,128)(2,1)}, u32[]{:S(2)}) copy-start(bf16[2,192,576]{2,1,0:T(8,128)(2,1)} %refs_5_.4) | copy-start | bytes 1327108
  21.9 12.6 %copy-start.11 = (bf16[288,384]{1,0:T(8,128)(2,1)S(1)}, bf16[288,384]{1,0:T(8,128)(2,1)}, u32[]{:S(2)}) copy-start(bf16[288,384]{1,0:T(8,128)(2,1)} %constant.44.clone.refs_10_) | copy-start | bytes 663556
  21.9 12.6 %copy-start.15 = (bf16[256,144]{1,0:T(8,128)(2,1)S(1)}, bf16[256,144]{1,0:T(8,128)(2,1)}, u32[]{:S(2)}) copy-start(bf16[256,144]{1,0:T(8,128)(2,1)} %constant.45.clone.refs_11_) | copy-start | bytes 221188
  22.8 11.7 %copy-start.1 = (bf16[2,192,768]{2,1,0:T(8,128)(2,1)S(1)}, bf16[2,192,768]{2,1,0:T(8,128)(2,1)}, u32[]{:S(2)}) copy-start(bf16[2,192,768]{2,1,0:T(8,128)(2,1)} %refs_7_.5) | copy-start | bytes 1769476
  22.9 8.8 %collective-permute-start.3 = (bf16[96,192]{1,0:T(8,128)(2,1)S(1)}, bf16[96,192]{1,0:T(8,128)(2,1)S(1)}, u32[]{:S(2)}, u32[]{:S(2)}) collective-permute-start(bf16[96,192]{1,0:T(8,128)(2,1)S(1)} %pad_maximum_fusion.3), channel_id=1, source_target_pairs={{6,0},{4,2},{10,4},{8,6},{14,8},{12,10},{18,12},{16,14},{22,16},{2... | collective-permute-start | bytes 110600 | tf_op jit(solution)/shard_map/ppermute | solution.py:410
  29.8 4.2 %collective-permute-start.2 = (bf16[96,192]{1,0:T(8,128)(2,1)S(1)}, bf16[96,192]{1,0:T(8,128)(2,1)S(1)}, u32[]{:S(2)}, u32[]{:S(2)}) collective-permute-start(bf16[96,192]{1,0:T(8,128)(2,1)S(1)} %pad_maximum_fusion.2), channel_id=1, source_target_pairs={{2,0},{0,2},{3,1},{1,3},{6,4},{4,6},{7,5},{5,7},{10,8},{8,10},{11,... | collective-permute-start | bytes 110600 | tf_op jit(solution)/shard_map/ppermute | solution.py:410
  30.4 4.1 %collective-permute-start.1 = (bf16[96,192]{1,0:T(8,128)(2,1)S(1)}, bf16[96,192]{1,0:T(8,128)(2,1)S(1)}, u32[]{:S(2)}, u32[]{:S(2)}) collective-permute-start(bf16[96,192]{1,0:T(8,128)(2,1)S(1)} %pad_maximum_fusion.1), channel_id=1, source_target_pairs={{4,0},{8,4},{12,8},{16,12},{20,16},{24,20},{28,24},{0,28},{5,1},{9... | collective-permute-start | bytes 110600 | tf_op jit(solution)/shard_map/ppermute | solution.py:410
  38.7 1.3 %collective-permute-start.4 = (bf16[128,192]{1,0:T(8,128)(2,1)S(1)}, bf16[128,192]{1,0:T(8,128)(2,1)S(1)}, u32[]{:S(2)}, u32[]{:S(2)}) collective-permute-start(bf16[128,192]{1,0:T(8,128)(2,1)S(1)} %get-tuple-element.19), channel_id=1, source_target_pairs={{1,0},{0,1},{3,2},{2,3},{5,4},{4,5},{7,6},{6,7},{9,8},{8,9},{11,10... | collective-permute-start | bytes 147464 | tf_op jit(solution)/shard_map/ppermute | solution.py:410
  38.8 9.6 %copy-start.7 = (bf16[2,192,192]{2,1,0:T(8,128)(2,1)S(1)}, bf16[2,192,192]{2,1,0:T(8,128)(2,1)}, u32[]{:S(2)}) copy-start(bf16[2,192,192]{2,1,0:T(8,128)(2,1)} %refs_6_.5) | copy-start | bytes 442372
  40.0 7.6 %collective-permute-start.7 = (bf16[64,192]{1,0:T(8,128)(2,1)S(1)}, bf16[64,192]{1,0:T(8,128)(2,1)S(1)}, u32[]{:S(2)}, u32[]{:S(2)}) collective-permute-start(bf16[64,192]{1,0:T(8,128)(2,1)S(1)} %pad_maximum_fusion.7), channel_id=1, source_target_pairs={{30,0},{28,2},{2,4},{0,6},{6,8},{4,10},{10,12},{8,14},{14,16},{12,... | collective-permute-start | bytes 73736 | tf_op jit(solution)/shard_map/ppermute | solution.py:410
  40.7 7.7 %copy-start.16 = (bf16[192,144]{1,0:T(8,128)(2,1)S(1)}, bf16[192,144]{1,0:T(8,128)(2,1)}, u32[]{:S(2)}) copy-start(bf16[192,144]{1,0:T(8,128)(2,1)} %constant.47.clone.refs_16_) | copy-start | bytes 165892
  40.7 6.9 %collective-permute-start.6 = (bf16[64,192]{1,0:T(8,128)(2,1)S(1)}, bf16[64,192]{1,0:T(8,128)(2,1)S(1)}, u32[]{:S(2)}, u32[]{:S(2)}) collective-permute-start(bf16[64,192]{1,0:T(8,128)(2,1)S(1)} %pad_maximum_fusion.6), channel_id=1, source_target_pairs={{2,0},{0,2},{3,1},{1,3},{6,4},{4,6},{7,5},{5,7},{10,8},{8,10},{11,... | collective-permute-start | bytes 73736 | tf_op jit(solution)/shard_map/ppermute | solution.py:410
  41.7 6.7 %copy-start.18 = (bf16[144,256]{1,0:T(8,128)(2,1)S(1)}, bf16[144,256]{1,0:T(8,128)(2,1)}, u32[]{:S(2)}) copy-start(bf16[144,256]{1,0:T(8,128)(2,1)} %constant.46.clone.refs_15_) | copy-start | bytes 221188
  41.7 6.7 %collective-permute-start.5 = (bf16[64,192]{1,0:T(8,128)(2,1)S(1)}, bf16[64,192]{1,0:T(8,128)(2,1)S(1)}, u32[]{:S(2)}, u32[]{:S(2)}) collective-permute-start(bf16[64,192]{1,0:T(8,128)(2,1)S(1)} %pad_maximum_fusion.5), channel_id=1, source_target_pairs={{28,0},{0,4},{4,8},{8,12},{12,16},{16,20},{20,24},{24,28},{29,1},{... | collective-permute-start | bytes 73736 | tf_op jit(solution)/shard_map/ppermute | solution.py:410
  50.9 1.3 %collective-permute-start.8 = (bf16[112,192]{1,0:T(8,128)(2,1)S(1)}, bf16[112,192]{1,0:T(8,128)(2,1)S(1)}, u32[]{:S(2)}, u32[]{:S(2)}) collective-permute-start(bf16[112,192]{1,0:T(8,128)(2,1)S(1)} %get-tuple-element.28), channel_id=1, source_target_pairs={{0,1},{1,0},{2,3},{3,2},{4,5},{5,4},{6,7},{7,6},{8,9},{9,8},{10,11... | collective-permute-start | bytes 129032 | tf_op jit(solution)/shard_map/ppermute | solution.py:434
  52.3 4.2 %collective-permute-start.9 = (bf16[112,192]{1,0:T(8,128)(2,1)S(1)}, bf16[112,192]{1,0:T(8,128)(2,1)S(1)}, u32[]{:S(2)}, u32[]{:S(2)}) collective-permute-start(bf16[112,192]{1,0:T(8,128)(2,1)S(1)} %add_convert_fusion.4), channel_id=1, source_target_pairs={{0,2},{2,0},{1,3},{3,1},{4,6},{6,4},{5,7},{7,5},{8,10},{10,8},{9,1... | collective-permute-start | bytes 129032 | tf_op jit(solution)/shard_map/ppermute | solution.py:442
  56.5 4.2 %collective-permute-start.10 = (bf16[112,192]{1,0:T(8,128)(2,1)S(1)}, bf16[112,192]{1,0:T(8,128)(2,1)S(1)}, u32[]{:S(2)}, u32[]{:S(2)}) collective-permute-start(bf16[112,192]{1,0:T(8,128)(2,1)S(1)} %add_convert_fusion.3), channel_id=1, source_target_pairs={{0,4},{4,0},{8,12},{12,8},{16,20},{20,16},{24,28},{28,24},{1,5},{5... | collective-permute-start | bytes 129032 | tf_op jit(solution)/shard_map/ppermute | solution.py:442
  60.8 4.2 %collective-permute-start.11 = (bf16[112,192]{1,0:T(8,128)(2,1)S(1)}, bf16[112,192]{1,0:T(8,128)(2,1)S(1)}, u32[]{:S(2)}, u32[]{:S(2)}) collective-permute-start(bf16[112,192]{1,0:T(8,128)(2,1)S(1)} %add_convert_fusion.2), channel_id=1, source_target_pairs={{0,8},{4,12},{8,0},{12,4},{16,24},{20,28},{24,16},{28,20},{1,9},{5... | collective-permute-start | bytes 129032 | tf_op jit(solution)/shard_map/ppermute | solution.py:442
  65.1 5.2 %collective-permute-start.12 = (bf16[112,192]{1,0:T(8,128)(2,1)S(1)}, bf16[112,192]{1,0:T(8,128)(2,1)S(1)}, u32[]{:S(2)}, u32[]{:S(2)}) collective-permute-start(bf16[112,192]{1,0:T(8,128)(2,1)S(1)} %add_convert_fusion.1), channel_id=1, source_target_pairs={{0,16},{4,20},{8,24},{12,28},{16,0},{20,4},{24,8},{28,12},{1,17},{... | collective-permute-start | bytes 129032 | tf_op jit(solution)/shard_map/ppermute | solution.py:442
  70.3 1.3 %collective-permute-start.13 = (bf16[112,192]{1,0:T(8,128)(2,1)S(1)}, bf16[112,192]{1,0:T(8,128)(2,1)S(1)}, u32[]{:S(2)}, u32[]{:S(2)}) collective-permute-start(bf16[112,192]{1,0:T(8,128)(2,1)S(1)} %add_convert_fusion), channel_id=1, source_target_pairs={{0,1},{1,0},{2,3},{3,2},{4,5},{5,4},{6,7},{7,6},{8,9},{9,8},{10,11... | collective-permute-start | bytes 129032 | tf_op jit(solution)/shard_map/ppermute | solution.py:444
  (6 other events, 4.8 us)

commit v3 on v2

--- a/solution.py
+++ b/solution.py
@@ -1,3 +1,5 @@
+import functools
+
 import jax
 import jax.numpy as jnp
 import ml_dtypes
@@ -376,18 +378,18 @@
 
 
 vmem = pl.BlockSpec(memory_space=pltpu.VMEM)
-where_it_lies = pl.BlockSpec(memory_space=pl.ANY)
-
-
-def call(kernel, outs, scratch, *args, spec=vmem, flops=1000000):
+hbm = pl.BlockSpec(memory_space=pltpu.HBM)
+
+
+def call(kernel, outs, scratch, *args, spec=vmem, out=vmem, room=30):
     return pl.pallas_call(
         kernel,
         out_shape=outs,
         in_specs=[spec for a in args],
-        out_specs=jax.tree.map(lambda _: vmem, outs),
+        out_specs=jax.tree.map(lambda _: out, outs),
         scratch_shapes=scratch,
-        compiler_params=pltpu.CompilerParams(vmem_limit_bytes=30 * 2**20),
-        cost_estimate=pl.CostEstimate(flops=flops, bytes_accessed=1000000, transcendentals=0),
+        compiler_params=pltpu.CompilerParams(vmem_limit_bytes=room * 2**20),
+        cost_estimate=pl.CostEstimate(flops=1000000, bytes_accessed=1000000, transcendentals=0),
     )(*args)
 
 
@@ -421,30 +423,54 @@
     return blocks
 
 
+def swap(block, flips):
+    names = ("lon", "lat", "section")
+    axes = [name for name in names if flips.get(name, 0)]
+    sizes = [lax.axis_size(name) for name in axes]
+    pairs = []
+    for place in np.ndindex(*sizes):
+        source = [p ^ flips[name] for p, name in zip(place, axes)]
+        pairs.append(
+            (int(np.ravel_multi_index(source, sizes)), int(np.ravel_multi_index(place, sizes)))
+        )
+    return lax.ppermute(block, tuple(axes), pairs)
+
+
 def add_up(mine, other):
-    sections = lax.axis_size("section")
-    place = lax.axis_index("section") % 2
-    if sections % 2:
-        raise ValueError("odd sections")
-    swap = [(i, i ^ 1) for i in range(sections)]
-
-    def both(a, b):
-        return (a.astype(FULL) + b.astype(FULL)).astype(HALF)
-
-    total = both(mine, lax.ppermute(other, "section", swap))
+    total = (mine.astype(FULL) + swap(other, {"section": 1}).astype(FULL)).astype(HALF)
+    bits = []
     for name in ("section", "lat", "lon"):
         size = lax.axis_size(name)
-        if size & (size - 1):
+        if size & (size - 1) or size < 2:
             raise ValueError("axis size")
-        step = 2 if name == "section" else 1
-        while step < size:
-            pairs = [(i, i ^ step) for i in range(size)]
-            total = both(total, lax.ppermute(total, name, pairs))
-            step *= 2
-    far = lax.ppermute(total, "section", swap)
-    first = jnp.where(place == 0, total, far)
-    second = jnp.where(place == 0, far, total)
-    return jnp.concatenate((first, second), 0).astype(FULL)
+        bits += [(name, 1 << n) for n in range(name == "section", size.bit_length() - 1)]
+    for n in range(0, len(bits), 2):
+        pair = [{name: bit} for name, bit in bits[n : n + 2]]
+        if len(pair) == 1:
+            total = total.astype(FULL) + swap(total, pair[0]).astype(FULL)
+        else:
+            one, two = pair
+            three = dict(one)
+            for name, bit in two.items():
+                three[name] = three.get(name, 0) | bit
+            near, far, last = (swap(total, step).astype(FULL) for step in (one, two, three))
+            total = (total.astype(FULL) + near) + (far + last)
+        total = total.astype(HALF)
+    return total, swap(total, {"section": 1})
+
+
+def last_kernel(scale, mine, other, upper_o, surface_o, both, sems):
+    place = lax.axis_index("section") % 2
+    both[pl.ds(pl.multiple_of(place * 112, 16), 112), :] = mine[...].astype(FULL) * scale
+    both[pl.ds(pl.multiple_of(112 - place * 112, 16), 112), :] = other[...].astype(FULL) * scale
+    copies = [
+        pltpu.make_async_copy(both.at[pl.ds(0, 160)], upper_o, sems.at[0]),
+        pltpu.make_async_copy(both.at[pl.ds(160, 64)], surface_o, sems.at[1]),
+    ]
+    for copy in copies:
+        copy.start()
+    for copy in copies:
+        copy.wait()
 
 
 def on_device(
@@ -507,7 +533,8 @@
             pltpu.SemaphoreType.DMA((len(operands),)),
         ],
         *operands,
-        spec=where_it_lies,
+        spec=hbm,
+        room=60,
     )
     bias = call(bias_kernel, shape((HEADS * CELLS, CELLS), FULL), scratch_bias, table, cols)
     into = np.concatenate((octants_in(48, 0, False), octants_in(48, 18, False)), 0)
@@ -525,9 +552,15 @@
         *exchange(keep, send, -1), *weights, patch, x, qkv, prob, resid, slope,
         jnp.asarray(octants_in(32, 0, True)), jnp.asarray(inner_to_padded()),
     )
-    total = add_up(mine, other)
     scale = float(levels * sections * rows * bands * columns * lax.axis_size("lon")) ** (-0.5)
-    return (latent_grad, total[:160] * scale, total[160:] * scale)
+    upper_grad, surface_grad = call(
+        functools.partial(last_kernel, scale),
+        [shape((160, WIDTH), FULL), shape((64, WIDTH), FULL)],
+        [pltpu.VMEM((224, WIDTH), FULL), pltpu.SemaphoreType.DMA((2,))],
+        *add_up(mine, other),
+        out=hbm,
+    )
+    return (latent_grad, upper_grad, surface_grad)
 
 
 def solution(mesh):

time: 73.7 us -> 55.9 us (0.76)
  local copies, waits for them, and re-layouts: 15.4 us -> 1.63 us
  waiting for transfers between devices: 28.9 us -> 21.1 us
  starting transfers between devices: 12.6 us -> 17.9 us
  other arithmetic: 1.51 us -> 0.16 us
    unnamed x49 -> x35, local copies, waits for them, and re-layouts: 15.4 us -> 0.81 us
    ppermute x6 -> x8, waiting for transfers between devices: 17.5 us -> 8.64 us  [swap(): return lax.ppermute(block, tuple(axes), pairs)]
    ppermute x6 -> x8, starting transfers between devices: 2.3 us -> 8.14 us  [swap(): return lax.ppermute(block, tuple(axes), pairs)]
    mul x2 -> x0, other arithmetic: 1.32 us -> none  [on_device(): return (latent_grad, total[:160] * scale, total[160:] * scale)]
    ppermute x8, waiting for transfers between devices: 11.4 us -> 12.4 us  [fetch(): return lax.ppermute(block, tuple(axes), pairs)]
    slice x4, local copies, waits for them, and re-layouts: 0.03 us -> 0.82 us  [exchange(): block = jnp.concatenate((keep[rows], got[rows]), 0)]
    pallas_call x4 -> x5, Pallas kernels: 13.7 us -> 13.9 us  [call(): pl.pallas_call(kernel, out_shape=outs, in_specs=[spec for a in args], out...]
  transfers between devices with their start and end apart: 14 -> 16, of which waited for: 12 -> 12; matrix products, arithmetic and copies ran while one was open for 1% -> 3% of each run, Pallas kernels for 1% -> 2%
where the time goes in v3:
time: 55.9 us; the launch traced here: 55.7 us
  waiting for transfers between devices  21.1 us (38%)
  starting transfers between devices  17.9 us (32%)
  Pallas kernels  13.9 us (25%)
  local copies, waits for them, and re-layouts  1.63 us (3%)
  between operations  1.01 us (2%)
    pallas_call x5, Pallas kernels, call(): pl.pallas_call(kernel, out_shape=outs, in_specs=[spec for a in args], out...  13.9 us
    ppermute x8, waiting for transfers between devices, fetch(): return lax.ppermute(block, tuple(axes), pairs)  12.4 us
    ppermute x8, starting transfers between devices, fetch(): return lax.ppermute(block, tuple(axes), pairs)  9.79 us
    ppermute x8, waiting for transfers between devices, swap(): return lax.ppermute(block, tuple(axes), pairs)  8.64 us
    ppermute x8, starting transfers between devices, swap(): return lax.ppermute(block, tuple(axes), pairs)  8.14 us
  transfers between devices with their start and end apart: 16, of which 12 were waited for; matrix products, arithmetic and copies ran while one was open for 3% of the time, Pallas kernels for 2%

profile of v3, /device:TPU:0, one launch (start us, length us, event | category | flops | bytes accessed | tf_op | source)
XLA Modules:
  0.0 55.7 jit_solution(9723887812323748051)
XLA Ops:
  0.7 5.6 %shard_map.211 = (bf16[192,192]{1,0:T(8,128)(2,1)}, bf16[192,192]{1,0:T(8,128)(2,1)}, bf16[144,256]{1,0:T(8,128)(2,1)}, bf16[144,192]{1,0:T(8,128)(2,1)}, bf16[3...) custom-call(f32[12,1,3312]{2,1,0:T(1,128)} %bitcast.6, ...), custom_call_target="tpu_custom_call" | custom-call | flops 1000000 | bytes 1000000 | tf_op jit(solution)/shard_map/pallas_call | solution.py:385
  6.3 0.5 collective-permute-start
  6.8 0.8 %fusion = (bf16[48,192]{1,0:T(8,128)(2,1)S(1)}, bf16[48,192]{1,0:T(8,128)(2,1)S(1)}, bf16[48,192]{1,0:T(8,128)(2,1)S(1)}, bf16[48,192]{1,0:T(8,128)(2,1)S(1)}) fusion(bf16[192,192]{1,0:T(8,128)(2,1)} %get-tuple-element.18), kind=kLoop, calls=%fused_computation.11 | loop fusion | bytes 147456 | tf_op jit(solution)/shard_map/slice | solution.py:421
  7.7 0.9 %shard_map.212.refs_9_ = f32[864,144]{1,0:T(8,128)S(1)} custom-call(f32[12,1,3312]{2,1,0:T(1,128)S(1)} %bitcast.7, bf16[2,256,384]{2,1,0:T(8,128)(2,1)S(1)} %copy-done.4), custom_call_target="tpu_custom_call" | custom-call | flops 1000000 | bytes 1000000 | tf_op jit(solution)/shard_map/pallas_call | solution.py:385
  8.6 5.6 %collective-permute-start.1 = (bf16[96,192]{1,0:T(8,128)(2,1)S(1)}, bf16[96,192]{1,0:T(8,128)(2,1)S(1)}, u32[]{:S(2)}, u32[]{:S(2)}) collective-permute-start(bf16[96,192]{1,0:T(8,128)(2,1)S(1)} %pad_maximum_fusion.1), channel_id=1, source_target_pairs={{4,0},{8,4},{12,8},{16,12},{20,16},{24,20},{28,24},{0,28},{5,1},{9... | collective-permute-start | bytes 110600 | tf_op jit(solution)/shard_map/ppermute | solution.py:412
  14.3 1.6 %collective-permute-start.2 = (bf16[96,192]{1,0:T(8,128)(2,1)S(1)}, bf16[96,192]{1,0:T(8,128)(2,1)S(1)}, u32[]{:S(2)}, u32[]{:S(2)}) collective-permute-start(bf16[96,192]{1,0:T(8,128)(2,1)S(1)} %pad_maximum_fusion.2), channel_id=1, source_target_pairs={{2,0},{0,2},{3,1},{1,3},{6,4},{4,6},{7,5},{5,7},{10,8},{8,10},{11,... | collective-permute-start | bytes 110600 | tf_op jit(solution)/shard_map/ppermute | solution.py:412
  15.8 0.5 collective-permute-start.3
  16.4 2.3 %collective-permute-done.2.refs_2_ = bf16[96,192]{1,0:T(8,128)(2,1)S(1)} collective-permute-done((bf16[96,192]{1,0:T(8,128)(2,1)S(1)}, bf16[96,192]{1,0:T(8,128)(2,1)S(1)}, u32[]{:S(2)}, u32[]{:S(2)}) %collective-permute-start.2) | collective-permute-done | bytes 36896 | tf_op jit(solution)/shard_map/ppermute | solution.py:412
  18.7 2.2 %collective-permute-done.3.refs_3_ = bf16[96,192]{1,0:T(8,128)(2,1)S(1)} collective-permute-done((bf16[96,192]{1,0:T(8,128)(2,1)S(1)}, bf16[96,192]{1,0:T(8,128)(2,1)S(1)}, u32[]{:S(2)}, u32[]{:S(2)}) %collective-permute-start.3) | collective-permute-done | bytes 36896 | tf_op jit(solution)/shard_map/ppermute | solution.py:412
  21.0 4.1 %shard_map.213 = (bf16[128,192]{1,0:T(8,128)(2,1)S(1)}, bf16[128,192]{1,0:T(8,128)(2,1)S(1)}) custom-call(bf16[96,192]{1,0:T(8,128)(2,1)S(1)} %pad_maximum_fusion.refs_0_, bf16[96,192]{1,0:T(8,128)(2,1)S(1)} %collective-permute-done.1.refs_1_, bf16[96,192]{1,0:T(8,128)(2,1)S(1)} %collective-permute-done.2.refs_2_, ...), custom_call_target="tpu_custom_call" | custom-call | flops 1000000 | bytes 1000000 | tf_op jit(solution)/shard_map/pallas_call | solution.py:385
  25.1 0.1 collective-permute-start.4
  25.2 1.2 %collective-permute-done.4 = bf16[128,192]{1,0:T(8,128)(2,1)S(1)} collective-permute-done((bf16[128,192]{1,0:T(8,128)(2,1)S(1)}, bf16[128,192]{1,0:T(8,128)(2,1)S(1)}, u32[]{:S(2)}, u32[]{:S(2)}) %collective-permute-start.4) | collective-permute-done | bytes 49184 | tf_op jit(solution)/shard_map/ppermute | solution.py:412
  26.6 0.6 %collective-permute-start.6 = (bf16[64,192]{1,0:T(8,128)(2,1)S(1)}, bf16[64,192]{1,0:T(8,128)(2,1)S(1)}, u32[]{:S(2)}, u32[]{:S(2)}) collective-permute-start(bf16[64,192]{1,0:T(8,128)(2,1)S(1)} %pad_maximum_fusion.6), channel_id=1, source_target_pairs={{2,0},{0,2},{3,1},{1,3},{6,4},{4,6},{7,5},{5,7},{10,8},{8,10},{11,... | collective-permute-start | bytes 73736 | tf_op jit(solution)/shard_map/ppermute | solution.py:412
  27.2 0.8 %collective-permute-start.7 = (bf16[64,192]{1,0:T(8,128)(2,1)S(1)}, bf16[64,192]{1,0:T(8,128)(2,1)S(1)}, u32[]{:S(2)}, u32[]{:S(2)}) collective-permute-start(bf16[64,192]{1,0:T(8,128)(2,1)S(1)} %pad_maximum_fusion.7), channel_id=1, source_target_pairs={{30,0},{28,2},{2,4},{0,6},{6,8},{4,10},{10,12},{8,14},{14,16},{12,... | collective-permute-start | bytes 73736 | tf_op jit(solution)/shard_map/ppermute | solution.py:412
  28.0 5.1 %collective-permute-done.5.refs_1_ = bf16[64,192]{1,0:T(8,128)(2,1)S(1)} collective-permute-done((bf16[64,192]{1,0:T(8,128)(2,1)S(1)}, bf16[64,192]{1,0:T(8,128)(2,1)S(1)}, u32[]{:S(2)}, u32[]{:S(2)}) %collective-permute-start.5) | collective-permute-done | bytes 24608 | tf_op jit(solution)/shard_map/ppermute | solution.py:412
  33.1 1.6 %collective-permute-done.7.refs_3_ = bf16[64,192]{1,0:T(8,128)(2,1)S(1)} collective-permute-done((bf16[64,192]{1,0:T(8,128)(2,1)S(1)}, bf16[64,192]{1,0:T(8,128)(2,1)S(1)}, u32[]{:S(2)}, u32[]{:S(2)}) %collective-permute-start.7) | collective-permute-done | bytes 24608 | tf_op jit(solution)/shard_map/ppermute | solution.py:412
  34.8 2.6 %shard_map.214 = (bf16[2,6,12,192]{3,2,1,0:T(8,128)(2,1)S(1)}, bf16[112,192]{1,0:T(8,128)(2,1)S(1)}, bf16[112,192]{1,0:T(8,128)(2,1)S(1)}) custom-call(bf16[64,192]{1,0:T(8,128)(2,1)S(1)} %pad_maximum_fusion.4.refs_0_, bf16[64,192]{1,0:T(8,128)(2,1)S(1)} %collective-permute-done.5.refs_1_, bf16[64,192]{1,0:T(8,128)(2,1)S(1)} %collective-permute-done.6.refs_2_, ...), custom_call_target="tpu_custom_call" | custom-call | flops 1000000 | bytes 1000000 | tf_op jit(solution)/shard_map/pallas_call | solution.py:385
  37.4 0.1 collective-permute-start.8
  37.5 1.2 %collective-permute-done.8 = bf16[112,192]{1,0:T(8,128)(2,1)S(1)} collective-permute-done((bf16[112,192]{1,0:T(8,128)(2,1)S(1)}, bf16[112,192]{1,0:T(8,128)(2,1)S(1)}, u32[]{:S(2)}, u32[]{:S(2)}) %collective-permute-start.8) | collective-permute-done | bytes 43040 | tf_op jit(solution)/shard_map/ppermute | solution.py:436
  38.7 0.1 collective-permute-start.11
  38.8 2.9 %collective-permute-start.10 = (bf16[112,192]{1,0:T(8,128)(2,1)S(1)}, bf16[112,192]{1,0:T(8,128)(2,1)S(1)}, u32[]{:S(2)}, u32[]{:S(2)}) collective-permute-start(bf16[112,192]{1,0:T(8,128)(2,1)S(1)} %add_convert_fusion.2), channel_id=1, source_target_pairs={{4,0},{0,4},{12,8},{8,12},{20,16},{16,20},{28,24},{24,28},{5,1},{1... | collective-permute-start | bytes 129032 | tf_op jit(solution)/shard_map/ppermute | solution.py:436
  41.7 0.5 collective-permute-start.9
  42.3 1.9 %collective-permute-done.11 = bf16[112,192]{1,0:T(8,128)(2,1)S(1)} collective-permute-done((bf16[112,192]{1,0:T(8,128)(2,1)S(1)}, bf16[112,192]{1,0:T(8,128)(2,1)S(1)}, u32[]{:S(2)}, u32[]{:S(2)}) %collective-permute-start.11) | collective-permute-done | bytes 43040 | tf_op jit(solution)/shard_map/ppermute | solution.py:436
  44.2 0.7 %collective-permute-done.10 = bf16[112,192]{1,0:T(8,128)(2,1)S(1)} collective-permute-done((bf16[112,192]{1,0:T(8,128)(2,1)S(1)}, bf16[112,192]{1,0:T(8,128)(2,1)S(1)}, u32[]{:S(2)}, u32[]{:S(2)}) %collective-permute-start.10) | collective-permute-done | bytes 43040 | tf_op jit(solution)/shard_map/ppermute | solution.py:436
  44.9 1.0 %collective-permute-done.9 = bf16[112,192]{1,0:T(8,128)(2,1)S(1)} collective-permute-done((bf16[112,192]{1,0:T(8,128)(2,1)S(1)}, bf16[112,192]{1,0:T(8,128)(2,1)S(1)}, u32[]{:S(2)}, u32[]{:S(2)}) %collective-permute-start.9) | collective-permute-done | bytes 43040 | tf_op jit(solution)/shard_map/ppermute | solution.py:436
  46.0 2.0 %collective-permute-start.14 = (bf16[112,192]{1,0:T(8,128)(2,1)S(1)}, bf16[112,192]{1,0:T(8,128)(2,1)S(1)}, u32[]{:S(2)}, u32[]{:S(2)}) collective-permute-start(bf16[112,192]{1,0:T(8,128)(2,1)S(1)} %add_convert_fusion.1), channel_id=1, source_target_pairs={{24,0},{28,4},{16,8},{20,12},{8,16},{12,20},{0,24},{4,28},{25,1},{... | collective-permute-start | bytes 129032 | tf_op jit(solution)/shard_map/ppermute | solution.py:436
  48.0 2.4 %collective-permute-start.12 = (bf16[112,192]{1,0:T(8,128)(2,1)S(1)}, bf16[112,192]{1,0:T(8,128)(2,1)S(1)}, u32[]{:S(2)}, u32[]{:S(2)}) collective-permute-start(bf16[112,192]{1,0:T(8,128)(2,1)S(1)} %add_convert_fusion.1), channel_id=1, source_target_pairs={{8,0},{12,4},{0,8},{4,12},{24,16},{28,20},{16,24},{20,28},{9,1},{1... | collective-permute-start | bytes 129032 | tf_op jit(solution)/shard_map/ppermute | solution.py:436
  50.4 2.0 %collective-permute-done.14 = bf16[112,192]{1,0:T(8,128)(2,1)S(1)} collective-permute-done((bf16[112,192]{1,0:T(8,128)(2,1)S(1)}, bf16[112,192]{1,0:T(8,128)(2,1)S(1)}, u32[]{:S(2)}, u32[]{:S(2)}) %collective-permute-start.14) | collective-permute-done | bytes 43040 | tf_op jit(solution)/shard_map/ppermute | solution.py:436
  52.4 1.2 %collective-permute-done.13 = bf16[112,192]{1,0:T(8,128)(2,1)S(1)} collective-permute-done((bf16[112,192]{1,0:T(8,128)(2,1)S(1)}, bf16[112,192]{1,0:T(8,128)(2,1)S(1)}, u32[]{:S(2)}, u32[]{:S(2)}) %collective-permute-start.13) | collective-permute-done | bytes 43040 | tf_op jit(solution)/shard_map/ppermute | solution.py:436
  53.8 0.7 %copy.23 = bf16[2,6,12,192]{3,0,2,1:T(2,128)(2,1)} copy(bf16[2,6,12,192]{3,2,1,0:T(8,128)(2,1)S(1)} %get-tuple-element.33) | data formatting | bytes 110592
  54.5 0.5 collective-permute-done.15.other
  55.0 0.7 %shard_map.215 = (f32[160,192]{1,0:T(8,128)}, f32[64,192]{1,0:T(8,128)}) custom-call(bf16[112,192]{1,0:T(8,128)(2,1)S(1)} %add_convert_fusion.mine, bf16[112,192]{1,0:T(8,128)(2,1)S(1)} %collective-permute-done.15.other), custom_call_target="tpu_custom_call" | custom-call | flops 1000000 | bytes 1000000 | tf_op jit(solution)/shard_map/pallas_call | solution.py:385
  (55 shorter events, 0.4 us)
Async XLA Ops:
  0.6 7.0 %copy-start.4 = (bf16[2,256,384]{2,1,0:T(8,128)(2,1)S(1)}, bf16[2,256,384]{2,1,0:T(8,128)(2,1)}, u32[]{:S(2)}) copy-start(bf16[2,256,384]{2,1,0:T(8,128)(2,1)} %constant.18.clone.refs_1_.cols) | copy-start | bytes 1179652
  0.6 20.2 %copy-start.9 = (bf16[288,384]{1,0:T(8,128)(2,1)S(1)}, bf16[288,384]{1,0:T(8,128)(2,1)}, u32[]{:S(2)}) copy-start(bf16[288,384]{1,0:T(8,128)(2,1)} %constant.23.clone.refs_10_) | copy-start | bytes 663556
  6.3 2.3 %collective-permute-start = (bf16[192,192]{1,0:T(8,128)(2,1)}, bf16[192,192]{1,0:T(8,128)(2,1)S(1)}, u32[]{:S(2)}, u32[]{:S(2)}) collective-permute-start(bf16[192,192]{1,0:T(8,128)(2,1)} %get-tuple-element.19), channel_id=1, source_target_pairs={{1,0},{0,1},{3,2},{2,3},{5,4},{4,5},{7,6},{6,7},{9,8},{8,9},{11,10... | collective-permute-start | bytes 221192 | tf_op jit(solution)/shard_map/ppermute | solution.py:412
  7.6 13.2 %copy-start.1 = (bf16[2,768,192]{1,2,0:T(8,128)(2,1)S(1)}, bf16[2,768,192]{1,2,0:T(8,128)(2,1)}, u32[]{:S(2)}) copy-start(bf16[2,768,192]{1,2,0:T(8,128)(2,1)} %param.28) | copy-start | bytes 1769476
  7.7 13.2 %copy-start.2 = (bf16[2,192,576]{2,1,0:T(8,128)(2,1)S(1)}, bf16[2,192,576]{2,1,0:T(8,128)(2,1)}, u32[]{:S(2)}) copy-start(bf16[2,192,576]{2,1,0:T(8,128)(2,1)} %refs_5_.4) | copy-start | bytes 1327108
  7.7 13.2 %copy-start.3 = (bf16[2,192,192]{2,1,0:T(8,128)(2,1)S(1)}, bf16[2,192,192]{2,1,0:T(8,128)(2,1)}, u32[]{:S(2)}) copy-start(bf16[2,192,192]{2,1,0:T(8,128)(2,1)} %refs_6_.5) | copy-start | bytes 442372
  7.7 13.2 %copy-start.11 = (bf16[256,144]{1,0:T(8,128)(2,1)S(1)}, bf16[256,144]{1,0:T(8,128)(2,1)}, u32[]{:S(2)}) copy-start(bf16[256,144]{1,0:T(8,128)(2,1)} %constant.24.clone.refs_11_) | copy-start | bytes 221188
  8.6 12.3 %copy-start = (bf16[2,192,768]{2,1,0:T(8,128)(2,1)S(1)}, bf16[2,192,768]{2,1,0:T(8,128)(2,1)}, u32[]{:S(2)}) copy-start(bf16[2,192,768]{2,1,0:T(8,128)(2,1)} %refs_7_.5) | copy-start | bytes 1769476
  8.6 7.8 %collective-permute-start.1 = (bf16[96,192]{1,0:T(8,128)(2,1)S(1)}, bf16[96,192]{1,0:T(8,128)(2,1)S(1)}, u32[]{:S(2)}, u32[]{:S(2)}) collective-permute-start(bf16[96,192]{1,0:T(8,128)(2,1)S(1)} %pad_maximum_fusion.1), channel_id=1, source_target_pairs={{4,0},{8,4},{12,8},{16,12},{20,16},{24,20},{28,24},{0,28},{5,1},{9... | collective-permute-start | bytes 110600 | tf_op jit(solution)/shard_map/ppermute | solution.py:412
  14.3 4.5 %collective-permute-start.2 = (bf16[96,192]{1,0:T(8,128)(2,1)S(1)}, bf16[96,192]{1,0:T(8,128)(2,1)S(1)}, u32[]{:S(2)}, u32[]{:S(2)}) collective-permute-start(bf16[96,192]{1,0:T(8,128)(2,1)S(1)} %pad_maximum_fusion.2), channel_id=1, source_target_pairs={{2,0},{0,2},{3,1},{1,3},{6,4},{4,6},{7,5},{5,7},{10,8},{8,10},{11,... | collective-permute-start | bytes 110600 | tf_op jit(solution)/shard_map/ppermute | solution.py:412
  15.8 5.0 %collective-permute-start.3 = (bf16[96,192]{1,0:T(8,128)(2,1)S(1)}, bf16[96,192]{1,0:T(8,128)(2,1)S(1)}, u32[]{:S(2)}, u32[]{:S(2)}) collective-permute-start(bf16[96,192]{1,0:T(8,128)(2,1)S(1)} %pad_maximum_fusion.3), channel_id=1, source_target_pairs={{6,0},{4,2},{10,4},{8,6},{14,8},{12,10},{18,12},{16,14},{22,16},{2... | collective-permute-start | bytes 110600 | tf_op jit(solution)/shard_map/ppermute | solution.py:412
  16.4 4.6 %copy-start.16 = (f32[2,2,192]{2,1,0:T(2,128)S(1)}, f32[2,2,192]{2,1,0:T(2,128)}, u32[]{:S(2)}) copy-start(f32[2,2,192]{2,1,0:T(2,128)} %refs_4_.4) | copy-start | bytes 9220
  20.9 13.8 %copy-start.7 = (bf16[3,144,192]{2,1,0:T(8,128)(2,1)S(1)}, bf16[3,144,192]{2,1,0:T(8,128)(2,1)}, u32[]{:S(2)}) copy-start(bf16[3,144,192]{2,1,0:T(8,128)(2,1)} %get-tuple-element.24.refs_11_) | copy-start | bytes 497668
  20.9 13.8 %copy-start.8 = (bf16[144,768]{1,0:T(8,128)(2,1)S(1)}, bf16[144,768]{1,0:T(8,128)(2,1)}, u32[]{:S(2)}) copy-start(bf16[144,768]{1,0:T(8,128)(2,1)} %get-tuple-element.27.refs_14_) | copy-start | bytes 663556
  21.0 13.8 %copy-start.10 = (f32[144,192]{1,0:T(8,128)S(1)}, f32[144,192]{1,0:T(8,128)}, u32[]{:S(2)}) copy-start(f32[144,192]{1,0:T(8,128)} %get-tuple-element.26.refs_13_) | copy-start | bytes 331780
  21.0 13.8 %copy-start.13 = (bf16[144,256]{1,0:T(8,128)(2,1)S(1)}, bf16[144,256]{1,0:T(8,128)(2,1)}, u32[]{:S(2)}) copy-start(bf16[144,256]{1,0:T(8,128)(2,1)} %constant.25.clone.refs_15_) | copy-start | bytes 221188
  21.0 13.8 %copy-start.14 = (bf16[144,256]{1,0:T(8,128)(2,1)S(1)}, bf16[144,256]{1,0:T(8,128)(2,1)}, u32[]{:S(2)}) copy-start(bf16[144,256]{1,0:T(8,128)(2,1)} %get-tuple-element.22.refs_9_) | copy-start | bytes 221188
  21.0 13.8 %copy-start.15 = (bf16[144,192]{1,0:T(8,128)(2,1)S(1)}, bf16[144,192]{1,0:T(8,128)(2,1)}, u32[]{:S(2)}) copy-start(bf16[144,192]{1,0:T(8,128)(2,1)} %get-tuple-element.23.refs_10_) | copy-start | bytes 165892
  25.1 9.7 %copy-start.6 = (bf16[864,144]{1,0:T(8,128)(2,1)S(1)}, bf16[864,144]{1,0:T(8,128)(2,1)}, u32[]{:S(2)}) copy-start(bf16[864,144]{1,0:T(8,128)(2,1)} %get-tuple-element.25.refs_12_) | copy-start | bytes 746500
  25.1 1.3 %collective-permute-start.4 = (bf16[128,192]{1,0:T(8,128)(2,1)S(1)}, bf16[128,192]{1,0:T(8,128)(2,1)S(1)}, u32[]{:S(2)}, u32[]{:S(2)}) collective-permute-start(bf16[128,192]{1,0:T(8,128)(2,1)S(1)} %get-tuple-element.21), channel_id=1, source_target_pairs={{1,0},{0,1},{3,2},{2,3},{5,4},{4,5},{7,6},{6,7},{9,8},{8,9},{11,10... | collective-permute-start | bytes 147464 | tf_op jit(solution)/shard_map/ppermute | solution.py:412
  26.5 6.7 %collective-permute-start.5 = (bf16[64,192]{1,0:T(8,128)(2,1)S(1)}, bf16[64,192]{1,0:T(8,128)(2,1)S(1)}, u32[]{:S(2)}, u32[]{:S(2)}) collective-permute-start(bf16[64,192]{1,0:T(8,128)(2,1)S(1)} %pad_maximum_fusion.5), channel_id=1, source_target_pairs={{28,0},{0,4},{4,8},{8,12},{12,16},{16,20},{20,24},{24,28},{29,1},{... | collective-permute-start | bytes 73736 | tf_op jit(solution)/shard_map/ppermute | solution.py:412
  26.5 8.3 %copy-start.12 = (bf16[192,144]{1,0:T(8,128)(2,1)S(1)}, bf16[192,144]{1,0:T(8,128)(2,1)}, u32[]{:S(2)}) copy-start(bf16[192,144]{1,0:T(8,128)(2,1)} %constant.26.clone.refs_16_) | copy-start | bytes 165892
  26.6 6.6 %collective-permute-start.6 = (bf16[64,192]{1,0:T(8,128)(2,1)S(1)}, bf16[64,192]{1,0:T(8,128)(2,1)S(1)}, u32[]{:S(2)}, u32[]{:S(2)}) collective-permute-start(bf16[64,192]{1,0:T(8,128)(2,1)S(1)} %pad_maximum_fusion.6), channel_id=1, source_target_pairs={{2,0},{0,2},{3,1},{1,3},{6,4},{4,6},{7,5},{5,7},{10,8},{8,10},{11,... | collective-permute-start | bytes 73736 | tf_op jit(solution)/shard_map/ppermute | solution.py:412
  27.2 7.6 %collective-permute-start.7 = (bf16[64,192]{1,0:T(8,128)(2,1)S(1)}, bf16[64,192]{1,0:T(8,128)(2,1)S(1)}, u32[]{:S(2)}, u32[]{:S(2)}) collective-permute-start(bf16[64,192]{1,0:T(8,128)(2,1)S(1)} %pad_maximum_fusion.7), channel_id=1, source_target_pairs={{30,0},{28,2},{2,4},{0,6},{6,8},{4,10},{10,12},{8,14},{14,16},{12,... | collective-permute-start | bytes 73736 | tf_op jit(solution)/shard_map/ppermute | solution.py:412
  37.4 1.3 %collective-permute-start.8 = (bf16[112,192]{1,0:T(8,128)(2,1)S(1)}, bf16[112,192]{1,0:T(8,128)(2,1)S(1)}, u32[]{:S(2)}, u32[]{:S(2)}) collective-permute-start(bf16[112,192]{1,0:T(8,128)(2,1)S(1)} %get-tuple-element.30), channel_id=1, source_target_pairs={{1,0},{0,1},{3,2},{2,3},{5,4},{4,5},{7,6},{6,7},{9,8},{8,9},{11,10... | collective-permute-start | bytes 129032 | tf_op jit(solution)/shard_map/ppermute | solution.py:436
  38.7 5.4 %collective-permute-start.11 = (bf16[112,192]{1,0:T(8,128)(2,1)S(1)}, bf16[112,192]{1,0:T(8,128)(2,1)S(1)}, u32[]{:S(2)}, u32[]{:S(2)}) collective-permute-start(bf16[112,192]{1,0:T(8,128)(2,1)S(1)} %add_convert_fusion.2), channel_id=1, source_target_pairs={{6,0},{4,2},{2,4},{0,6},{14,8},{12,10},{10,12},{8,14},{22,16},{20,... | collective-permute-start | bytes 129032 | tf_op jit(solution)/shard_map/ppermute | solution.py:436
  38.8 6.1 %collective-permute-start.10 = (bf16[112,192]{1,0:T(8,128)(2,1)S(1)}, bf16[112,192]{1,0:T(8,128)(2,1)S(1)}, u32[]{:S(2)}, u32[]{:S(2)}) collective-permute-start(bf16[112,192]{1,0:T(8,128)(2,1)S(1)} %add_convert_fusion.2), channel_id=1, source_target_pairs={{4,0},{0,4},{12,8},{8,12},{20,16},{16,20},{28,24},{24,28},{5,1},{1... | collective-permute-start | bytes 129032 | tf_op jit(solution)/shard_map/ppermute | solution.py:436
  41.7 4.2 %collective-permute-start.9 = (bf16[112,192]{1,0:T(8,128)(2,1)S(1)}, bf16[112,192]{1,0:T(8,128)(2,1)S(1)}, u32[]{:S(2)}, u32[]{:S(2)}) collective-permute-start(bf16[112,192]{1,0:T(8,128)(2,1)S(1)} %add_convert_fusion.2), channel_id=1, source_target_pairs={{2,0},{0,2},{3,1},{1,3},{6,4},{4,6},{7,5},{5,7},{10,8},{8,10},{11,... | collective-permute-start | bytes 129032 | tf_op jit(solution)/shard_map/ppermute | solution.py:436
  46.0 6.5 %collective-permute-start.14 = (bf16[112,192]{1,0:T(8,128)(2,1)S(1)}, bf16[112,192]{1,0:T(8,128)(2,1)S(1)}, u32[]{:S(2)}, u32[]{:S(2)}) collective-permute-start(bf16[112,192]{1,0:T(8,128)(2,1)S(1)} %add_convert_fusion.1), channel_id=1, source_target_pairs={{24,0},{28,4},{16,8},{20,12},{8,16},{12,20},{0,24},{4,28},{25,1},{... | collective-permute-start | bytes 129032 | tf_op jit(solution)/shard_map/ppermute | solution.py:436
  48.0 5.7 %collective-permute-start.13 = (bf16[112,192]{1,0:T(8,128)(2,1)S(1)}, bf16[112,192]{1,0:T(8,128)(2,1)S(1)}, u32[]{:S(2)}, u32[]{:S(2)}) collective-permute-start(bf16[112,192]{1,0:T(8,128)(2,1)S(1)} %add_convert_fusion.1), channel_id=1, source_target_pairs={{16,0},{20,4},{24,8},{28,12},{0,16},{4,20},{8,24},{12,28},{17,1},{... | collective-permute-start | bytes 129032 | tf_op jit(solution)/shard_map/ppermute | solution.py:436
  48.0 5.7 %collective-permute-start.12 = (bf16[112,192]{1,0:T(8,128)(2,1)S(1)}, bf16[112,192]{1,0:T(8,128)(2,1)S(1)}, u32[]{:S(2)}, u32[]{:S(2)}) collective-permute-start(bf16[112,192]{1,0:T(8,128)(2,1)S(1)} %add_convert_fusion.1), channel_id=1, source_target_pairs={{8,0},{12,4},{0,8},{4,12},{24,16},{28,20},{16,24},{20,28},{9,1},{1... | collective-permute-start | bytes 129032 | tf_op jit(solution)/shard_map/ppermute | solution.py:436
  53.7 1.3 %collective-permute-start.15 = (bf16[112,192]{1,0:T(8,128)(2,1)S(1)}, bf16[112,192]{1,0:T(8,128)(2,1)S(1)}, u32[]{:S(2)}, u32[]{:S(2)}) collective-permute-start(bf16[112,192]{1,0:T(8,128)(2,1)S(1)} %add_convert_fusion.mine), channel_id=1, source_target_pairs={{1,0},{0,1},{3,2},{2,3},{5,4},{4,5},{7,6},{6,7},{9,8},{8,9},{11,10... | collective-permute-start | bytes 129032 | tf_op jit(solution)/shard_map/ppermute | solution.py:436
  (1 other events, 1.3 us)

commit v4 on v3

--- a/solution.py
+++ b/solution.py
@@ -356,7 +356,7 @@
 def third_kernel(*refs):
     parts, rest = refs[:4], refs[4:]
     gains, wqkv, wproj, wup, wdown, patch, x_i, qkv_i, prob, resid, slope, into, out_of = rest[:13]
-    grad_o, mine_o, other_o, stack, terms = rest[13:]
+    grad_o, chunks_o, stack, terms = rest[13:]
     for n in range(4):
         stack[n * 64 : n * 64 + 64, :] = parts[n][...]
     dflat = dot(into[...], stack[...]).astype(HALF)
@@ -372,9 +372,12 @@
         for a in range(6):
             grad_o[z, a] = moved[(z * 6 + a) * 16 : (z * 6 + a) * 16 + 12]
     terms[...] = dot_tn(patch[...], grad)
-    place = lax.axis_index("section") % 2
-    mine_o[...] = terms[pl.ds(pl.multiple_of(place * 112, 16), 112), :].astype(HALF)
-    other_o[...] = terms[pl.ds(pl.multiple_of(112 - place * 112, 16), 112), :].astype(HALF)
+    count = chunks_o.shape[1]
+    for n in range(chunks_o.shape[0]):
+        if n * count < 224:
+            chunks_o[n] = terms[n * count : (n + 1) * count, :].astype(HALF)
+        else:
+            chunks_o[n] = jnp.zeros(chunks_o.shape[1:], HALF)
 
 
 vmem = pl.BlockSpec(memory_space=pltpu.VMEM)
@@ -436,33 +439,17 @@
     return lax.ppermute(block, tuple(axes), pairs)
 
 
-def add_up(mine, other):
-    total = (mine.astype(FULL) + swap(other, {"section": 1}).astype(FULL)).astype(HALF)
-    bits = []
-    for name in ("section", "lat", "lon"):
-        size = lax.axis_size(name)
-        if size & (size - 1) or size < 2:
-            raise ValueError("axis size")
-        bits += [(name, 1 << n) for n in range(name == "section", size.bit_length() - 1)]
-    for n in range(0, len(bits), 2):
-        pair = [{name: bit} for name, bit in bits[n : n + 2]]
-        if len(pair) == 1:
-            total = total.astype(FULL) + swap(total, pair[0]).astype(FULL)
-        else:
-            one, two = pair
-            three = dict(one)
-            for name, bit in two.items():
-                three[name] = three.get(name, 0) | bit
-            near, far, last = (swap(total, step).astype(FULL) for step in (one, two, three))
-            total = (total.astype(FULL) + near) + (far + last)
-        total = total.astype(HALF)
-    return total, swap(total, {"section": 1})
-
-
-def last_kernel(scale, mine, other, upper_o, surface_o, both, sems):
-    place = lax.axis_index("section") % 2
-    both[pl.ds(pl.multiple_of(place * 112, 16), 112), :] = mine[...].astype(FULL) * scale
-    both[pl.ds(pl.multiple_of(112 - place * 112, 16), 112), :] = other[...].astype(FULL) * scale
+def add_up(chunks):
+    axes = ("lon", "lat", "section")
+    mine = lax.all_to_all(chunks, axes, 0, 0, tiled=True)
+    mine = jnp.sum(mine.astype(FULL), 0, keepdims=True).astype(HALF)
+    return lax.all_to_all(jnp.broadcast_to(mine, chunks.shape), axes, 0, 0, tiled=True)
+
+
+def last_kernel(scale, chunks, upper_o, surface_o, both, sems):
+    count = chunks.shape[1]
+    for n in range(224 // count):
+        both[n * count : (n + 1) * count, :] = chunks[n].astype(FULL) * scale
     copies = [
         pltpu.make_async_copy(both.at[pl.ds(0, 160)], upper_o, sems.at[0]),
         pltpu.make_async_copy(both.at[pl.ds(160, 64)], surface_o, sems.at[1]),
@@ -545,9 +532,10 @@
         *exchange(keep, send, 1), *weights, bias,
         jnp.asarray(into), jnp.asarray(octants_out(32, 0, False, inner_row)),
     )
-    latent_grad, mine, other = call(
+    devices = sections * bands * lax.axis_size("lon")
+    latent_grad, chunks = call(
         third_kernel,
-        [shape((2, 6, 12, WIDTH)), shape((112, WIDTH)), shape((112, WIDTH))],
+        [shape((2, 6, 12, WIDTH)), shape((devices, -(-224 // devices), WIDTH))],
         [pltpu.VMEM((8 * 32, WIDTH), HALF), pltpu.VMEM((256, WIDTH), FULL)],
         *exchange(keep, send, -1), *weights, patch, x, qkv, prob, resid, slope,
         jnp.asarray(octants_in(32, 0, True)), jnp.asarray(inner_to_padded()),
@@ -557,7 +545,7 @@
         functools.partial(last_kernel, scale),
         [shape((160, WIDTH), FULL), shape((64, WIDTH), FULL)],
         [pltpu.VMEM((224, WIDTH), FULL), pltpu.SemaphoreType.DMA((2,))],
-        *add_up(mine, other),
+        add_up(chunks),
         out=hbm,
     )
     return (latent_grad, upper_grad, surface_grad)

time: 55.9 us -> 61.2 us (1.095)
  blocking collectives: 0 us -> 11.3 us
  starting transfers between devices: 17.9 us -> 12.4 us
  waiting for transfers between devices: 21.1 us -> 20 us
  local copies, waits for them, and re-layouts: 1.63 us -> 2.3 us
    all_to_all x0 -> x1, blocking collectives: none -> 11.3 us  [add_up(): mine = lax.all_to_all(chunks, axes, 0, 0, tiled=True)]
    ppermute x8 -> x0, waiting for transfers between devices: 8.64 us -> none  [swap(): return lax.ppermute(block, tuple(axes), pairs)]
    ppermute x8 -> x0, starting transfers between devices: 8.14 us -> none  [swap(): return lax.ppermute(block, tuple(axes), pairs)]
    all_to_all x0 -> x1, waiting for transfers between devices: none -> 7.52 us  [add_up(): lax.all_to_all(jnp.broadcast_to(mine, chunks.shape), axes, 0, 0, tiled=True)]
    all_to_all x0 -> x1, starting transfers between devices: none -> 2.58 us  [add_up(): lax.all_to_all(jnp.broadcast_to(mine, chunks.shape), axes, 0, 0, tiled=True)]
    broadcast_in_dim x0 -> x1, local copies, waits for them, and re-layouts: none -> 0.67 us  [add_up(): jnp.broadcast_to(mine, chunks.shape)]
  transfers between devices with their start and end apart: 16 -> 9, of which waited for: 12 -> 6; matrix products, arithmetic and copies ran while one was open for 3% -> 3% of each run, Pallas kernels for 2% -> 1%
where the time goes in v4:
time: 61.2 us; the launch traced here: 61 us
  waiting for transfers between devices  20 us (33%)
  Pallas kernels  13.9 us (23%)
  starting transfers between devices  12.4 us (20%)
  blocking collectives  11.3 us (18%)
  local copies, waits for them, and re-layouts  2.3 us (4%)
  between operations  0.98 us (2%)
    pallas_call x5, Pallas kernels, call(): pl.pallas_call(kernel, out_shape=outs, in_specs=[spec for a in args], out...  13.9 us
    ppermute x8, waiting for transfers between devices, fetch(): return lax.ppermute(block, tuple(axes), pairs)  12.4 us
    all_to_all x1, blocking collectives, add_up(): mine = lax.all_to_all(chunks, axes, 0, 0, tiled=True)  11.3 us
    ppermute x8, starting transfers between devices, fetch(): return lax.ppermute(block, tuple(axes), pairs)  9.79 us
    all_to_all x1, waiting for transfers between devices, add_up(): lax.all_to_all(jnp.broadcast_to(mine, chunks.shape), axes, 0, 0, tiled=True)  7.52 us
    all_to_all x1, starting transfers between devices, add_up(): lax.all_to_all(jnp.broadcast_to(mine, chunks.shape), axes, 0, 0, tiled=True)  2.58 us
  transfers between devices with their start and end apart: 9, of which 6 were waited for; matrix products, arithmetic and copies ran while one was open for 3% of the time, Pallas kernels for 1%

profile of v4, /device:TPU:0, one launch (start us, length us, event | category | flops | bytes accessed | tf_op | source)
XLA Modules:
  0.0 61.0 jit_solution(6954766970482863358)
XLA Ops:
  0.6 0.0 copy-start.4
  0.6 0.0 copy-start.9
  0.7 5.6 %shard_map.211 = (bf16[192,192]{1,0:T(8,128)(2,1)}, bf16[192,192]{1,0:T(8,128)(2,1)}, bf16[144,256]{1,0:T(8,128)(2,1)}, bf16[144,192]{1,0:T(8,128)(2,1)}, bf16[3...) custom-call(f32[12,1,3312]{2,1,0:T(1,128)} %bitcast.6, ...), custom_call_target="tpu_custom_call" | custom-call | flops 1000000 | bytes 1000000 | tf_op jit(solution)/shard_map/pallas_call | solution.py:388
  6.3 0.0 copy-start.5
  6.3 0.5 collective-permute-start
  6.8 0.8 %fusion = (bf16[48,192]{1,0:T(8,128)(2,1)S(1)}, bf16[48,192]{1,0:T(8,128)(2,1)S(1)}, bf16[48,192]{1,0:T(8,128)(2,1)S(1)}, bf16[48,192]{1,0:T(8,128)(2,1)S(1)}) fusion(bf16[192,192]{1,0:T(8,128)(2,1)} %get-tuple-element.17), kind=kLoop, calls=%fused_computation.8 | loop fusion | bytes 147456 | tf_op jit(solution)/shard_map/slice | solution.py:424
  7.6 0.0 copy-start.1
  7.7 0.0 copy-start.2
  7.7 0.0 copy-start.11
  7.7 0.9 %shard_map.212.refs_9_ = f32[864,144]{1,0:T(8,128)S(1)} custom-call(f32[12,1,3312]{2,1,0:T(1,128)S(1)} %bitcast.7, bf16[2,256,384]{2,1,0:T(8,128)(2,1)S(1)} %copy-done.4), custom_call_target="tpu_custom_call" | custom-call | flops 1000000 | bytes 1000000 | tf_op jit(solution)/shard_map/pallas_call | solution.py:388
  8.6 5.6 %collective-permute-start.1 = (bf16[96,192]{1,0:T(8,128)(2,1)S(1)}, bf16[96,192]{1,0:T(8,128)(2,1)S(1)}, u32[]{:S(2)}, u32[]{:S(2)}) collective-permute-start(bf16[96,192]{1,0:T(8,128)(2,1)S(1)} %pad_maximum_fusion.1), channel_id=1, source_target_pairs={{4,0},{8,4},{12,8},{16,12},{20,16},{24,20},{28,24},{0,28},{5,1},{9... | collective-permute-start | bytes 110600 | tf_op jit(solution)/shard_map/ppermute | solution.py:415
  14.3 1.6 %collective-permute-start.2 = (bf16[96,192]{1,0:T(8,128)(2,1)S(1)}, bf16[96,192]{1,0:T(8,128)(2,1)S(1)}, u32[]{:S(2)}, u32[]{:S(2)}) collective-permute-start(bf16[96,192]{1,0:T(8,128)(2,1)S(1)} %pad_maximum_fusion.2), channel_id=1, source_target_pairs={{2,0},{0,2},{3,1},{1,3},{6,4},{4,6},{7,5},{5,7},{10,8},{8,10},{11,... | collective-permute-start | bytes 110600 | tf_op jit(solution)/shard_map/ppermute | solution.py:415
  15.8 0.5 collective-permute-start.3
  16.4 2.3 %collective-permute-done.2.refs_2_ = bf16[96,192]{1,0:T(8,128)(2,1)S(1)} collective-permute-done((bf16[96,192]{1,0:T(8,128)(2,1)S(1)}, bf16[96,192]{1,0:T(8,128)(2,1)S(1)}, u32[]{:S(2)}, u32[]{:S(2)}) %collective-permute-start.2) | collective-permute-done | bytes 36896 | tf_op jit(solution)/shard_map/ppermute | solution.py:415
  18.7 2.2 %collective-permute-done.3.refs_3_ = bf16[96,192]{1,0:T(8,128)(2,1)S(1)} collective-permute-done((bf16[96,192]{1,0:T(8,128)(2,1)S(1)}, bf16[96,192]{1,0:T(8,128)(2,1)S(1)}, u32[]{:S(2)}, u32[]{:S(2)}) %collective-permute-start.3) | collective-permute-done | bytes 36896 | tf_op jit(solution)/shard_map/ppermute | solution.py:415
  21.0 0.0 copy-start.13
  21.0 4.1 %shard_map.213 = (bf16[128,192]{1,0:T(8,128)(2,1)S(1)}, bf16[128,192]{1,0:T(8,128)(2,1)S(1)}) custom-call(bf16[96,192]{1,0:T(8,128)(2,1)S(1)} %pad_maximum_fusion.refs_0_, bf16[96,192]{1,0:T(8,128)(2,1)S(1)} %collective-permute-done.1.refs_1_, bf16[96,192]{1,0:T(8,128)(2,1)S(1)} %collective-permute-done.2.refs_2_, ...), custom_call_target="tpu_custom_call" | custom-call | flops 1000000 | bytes 1000000 | tf_op jit(solution)/shard_map/pallas_call | solution.py:388
  25.1 0.1 collective-permute-start.4
  25.2 1.2 %collective-permute-done.4 = bf16[128,192]{1,0:T(8,128)(2,1)S(1)} collective-permute-done((bf16[128,192]{1,0:T(8,128)(2,1)S(1)}, bf16[128,192]{1,0:T(8,128)(2,1)S(1)}, u32[]{:S(2)}, u32[]{:S(2)}) %collective-permute-start.4) | collective-permute-done | bytes 49184 | tf_op jit(solution)/shard_map/ppermute | solution.py:415
  26.5 0.1 collective-permute-start.5
  26.5 0.0 copy-start.12
  26.6 0.6 collective-permute-start.6
  27.2 0.8 %collective-permute-start.7 = (bf16[64,192]{1,0:T(8,128)(2,1)S(1)}, bf16[64,192]{1,0:T(8,128)(2,1)S(1)}, u32[]{:S(2)}, u32[]{:S(2)}) collective-permute-start(bf16[64,192]{1,0:T(8,128)(2,1)S(1)} %pad_maximum_fusion.7), channel_id=1, source_target_pairs={{30,0},{28,2},{2,4},{0,6},{6,8},{4,10},{10,12},{8,14},{14,16},{12,... | collective-permute-start | bytes 73736 | tf_op jit(solution)/shard_map/ppermute | solution.py:415
  28.0 5.1 %collective-permute-done.5.refs_1_ = bf16[64,192]{1,0:T(8,128)(2,1)S(1)} collective-permute-done((bf16[64,192]{1,0:T(8,128)(2,1)S(1)}, bf16[64,192]{1,0:T(8,128)(2,1)S(1)}, u32[]{:S(2)}, u32[]{:S(2)}) %collective-permute-start.5) | collective-permute-done | bytes 24608 | tf_op jit(solution)/shard_map/ppermute | solution.py:415
  33.1 1.6 %collective-permute-done.7.refs_3_ = bf16[64,192]{1,0:T(8,128)(2,1)S(1)} collective-permute-done((bf16[64,192]{1,0:T(8,128)(2,1)S(1)}, bf16[64,192]{1,0:T(8,128)(2,1)S(1)}, u32[]{:S(2)}, u32[]{:S(2)}) %collective-permute-start.7) | collective-permute-done | bytes 24608 | tf_op jit(solution)/shard_map/ppermute | solution.py:415
  34.8 2.6 %shard_map.214 = (bf16[2,6,12,192]{3,2,1,0:T(8,128)(2,1)S(1)}, bf16[32,7,192]{2,1,0:T(8,128)(2,1)S(1)}) custom-call(bf16[64,192]{1,0:T(8,128)(2,1)S(1)} %pad_maximum_fusion.4.refs_0_, bf16[64,192]{1,0:T(8,128)(2,1)S(1)} %collective-permute-done.5.refs_1_, bf16[64,192]{1,0:T(8,128)(2,1)S(1)} %collective-permute-done.6.refs_2_, ...), custom_call_target="tpu_custom_call" | custom-call | flops 1000000 | bytes 1000000 | tf_op jit(solution)/shard_map/pallas_call | solution.py:388
  37.4 11.3 %all_to_all.10 = bf16[32,7,192]{2,1,0:T(8,128)(2,1)S(1)} all-to-all(bf16[32,7,192]{2,1,0:T(8,128)(2,1)S(1)} %get-tuple-element.28), channel_id=1, replica_groups=mesh['lon'=8,'lat'=2,'section'=2] {'lon','lat','section'}, dimensions={0} | all-to-all | bytes 172032 | tf_op jit(solution)/shard_map/all_to_all | solution.py:444
  48.8 0.7 %broadcast_in_dim.2 = bf16[32,7,192]{2,1,0:T(8,128)(2,1)} broadcast(bf16[7,192]{1,0:T(8,128)(2,1)S(1)} %reduce_sum.12), dimensions={1,2} | broadcast | bytes 88704 | tf_op jit(solution)/shard_map/broadcast_in_dim | solution.py:446
  49.4 2.6 %all-to-all-start.1 = ((bf16[32,7,192]{2,1,0:T(8,128)(2,1)}), bf16[32,7,192]{2,1,0:T(8,128)(2,1)S(1)}, u32[]{:S(2)}, u32[]{:S(2)}) async-start(bf16[32,7,192]{2,1,0:T(8,128)(2,1)} %broadcast_in_dim.2), calls=%async_computation.1 | async-start | bytes 262144 | tf_op jit(solution)/shard_map/all_to_all | solution.py:446
  52.0 0.7 %copy.23 = bf16[2,6,12,192]{3,0,2,1:T(2,128)(2,1)} copy(bf16[2,6,12,192]{3,2,1,0:T(8,128)(2,1)S(1)} %get-tuple-element.31) | data formatting | bytes 110592
  52.7 7.5 %all-to-all-done.1.chunks = bf16[32,7,192]{2,1,0:T(8,128)(2,1)S(1)} async-done(((bf16[32,7,192]{2,1,0:T(8,128)(2,1)}), bf16[32,7,192]{2,1,0:T(8,128)(2,1)S(1)}, u32[]{:S(2)}, u32[]{:S(2)}) %all-to-all-start.1) | async-done | bytes 86048 | tf_op jit(solution)/shard_map/all_to_all | solution.py:446
  60.2 0.7 %shard_map.215 = (f32[160,192]{1,0:T(8,128)}, f32[64,192]{1,0:T(8,128)}) custom-call(bf16[32,7,192]{2,1,0:T(8,128)(2,1)S(1)} %all-to-all-done.1.chunks), custom_call_target="tpu_custom_call" | custom-call | flops 1000000 | bytes 1000000 | tf_op jit(solution)/shard_map/pallas_call | solution.py:388
  (41 shorter events, 0.2 us)
Async XLA Ops:
  0.6 7.0 %copy-start.4 = (bf16[2,256,384]{2,1,0:T(8,128)(2,1)S(1)}, bf16[2,256,384]{2,1,0:T(8,128)(2,1)}, u32[]{:S(2)}) copy-start(bf16[2,256,384]{2,1,0:T(8,128)(2,1)} %constant.21.clone.refs_1_.cols) | copy-start | bytes 1179652
  0.6 20.2 %copy-start.9 = (bf16[288,384]{1,0:T(8,128)(2,1)S(1)}, bf16[288,384]{1,0:T(8,128)(2,1)}, u32[]{:S(2)}) copy-start(bf16[288,384]{1,0:T(8,128)(2,1)} %constant.26.clone.refs_10_) | copy-start | bytes 663556
  6.3 1.3 %copy-start.5 = (f32[2,1,1,6,3312]{4,2,3,1,0:T(1,128)S(1)}, f32[2,1,1,6,3312]{4,2,3,1,0:T(1,128)}, u32[]{:S(2)}) copy-start(f32[2,1,1,6,3312]{4,2,3,1,0:T(1,128)} %param.29) | copy-start | bytes 476932
  6.3 2.3 %collective-permute-start = (bf16[192,192]{1,0:T(8,128)(2,1)}, bf16[192,192]{1,0:T(8,128)(2,1)S(1)}, u32[]{:S(2)}, u32[]{:S(2)}) collective-permute-start(bf16[192,192]{1,0:T(8,128)(2,1)} %get-tuple-element.18), channel_id=1, source_target_pairs={{1,0},{0,1},{3,2},{2,3},{5,4},{4,5},{7,6},{6,7},{9,8},{8,9},{11,10... | collective-permute-start | bytes 221192 | tf_op jit(solution)/shard_map/ppermute | solution.py:415
  7.6 13.2 %copy-start.1 = (bf16[2,768,192]{1,2,0:T(8,128)(2,1)S(1)}, bf16[2,768,192]{1,2,0:T(8,128)(2,1)}, u32[]{:S(2)}) copy-start(bf16[2,768,192]{1,2,0:T(8,128)(2,1)} %param.28) | copy-start | bytes 1769476
  7.7 13.2 %copy-start.2 = (bf16[2,192,576]{2,1,0:T(8,128)(2,1)S(1)}, bf16[2,192,576]{2,1,0:T(8,128)(2,1)}, u32[]{:S(2)}) copy-start(bf16[2,192,576]{2,1,0:T(8,128)(2,1)} %refs_5_.4) | copy-start | bytes 1327108
  7.7 13.2 %copy-start.3 = (bf16[2,192,192]{2,1,0:T(8,128)(2,1)S(1)}, bf16[2,192,192]{2,1,0:T(8,128)(2,1)}, u32[]{:S(2)}) copy-start(bf16[2,192,192]{2,1,0:T(8,128)(2,1)} %refs_6_.5) | copy-start | bytes 442372
  7.7 13.2 %copy-start.11 = (bf16[256,144]{1,0:T(8,128)(2,1)S(1)}, bf16[256,144]{1,0:T(8,128)(2,1)}, u32[]{:S(2)}) copy-start(bf16[256,144]{1,0:T(8,128)(2,1)} %constant.27.clone.refs_11_) | copy-start | bytes 221188
  8.6 12.3 %copy-start = (bf16[2,192,768]{2,1,0:T(8,128)(2,1)S(1)}, bf16[2,192,768]{2,1,0:T(8,128)(2,1)}, u32[]{:S(2)}) copy-start(bf16[2,192,768]{2,1,0:T(8,128)(2,1)} %refs_7_.5) | copy-start | bytes 1769476
  8.6 7.8 %collective-permute-start.1 = (bf16[96,192]{1,0:T(8,128)(2,1)S(1)}, bf16[96,192]{1,0:T(8,128)(2,1)S(1)}, u32[]{:S(2)}, u32[]{:S(2)}) collective-permute-start(bf16[96,192]{1,0:T(8,128)(2,1)S(1)} %pad_maximum_fusion.1), channel_id=1, source_target_pairs={{4,0},{8,4},{12,8},{16,12},{20,16},{24,20},{28,24},{0,28},{5,1},{9... | collective-permute-start | bytes 110600 | tf_op jit(solution)/shard_map/ppermute | solution.py:415
  14.3 4.4 %collective-permute-start.2 = (bf16[96,192]{1,0:T(8,128)(2,1)S(1)}, bf16[96,192]{1,0:T(8,128)(2,1)S(1)}, u32[]{:S(2)}, u32[]{:S(2)}) collective-permute-start(bf16[96,192]{1,0:T(8,128)(2,1)S(1)} %pad_maximum_fusion.2), channel_id=1, source_target_pairs={{2,0},{0,2},{3,1},{1,3},{6,4},{4,6},{7,5},{5,7},{10,8},{8,10},{11,... | collective-permute-start | bytes 110600 | tf_op jit(solution)/shard_map/ppermute | solution.py:415
  15.8 5.0 %collective-permute-start.3 = (bf16[96,192]{1,0:T(8,128)(2,1)S(1)}, bf16[96,192]{1,0:T(8,128)(2,1)S(1)}, u32[]{:S(2)}, u32[]{:S(2)}) collective-permute-start(bf16[96,192]{1,0:T(8,128)(2,1)S(1)} %pad_maximum_fusion.3), channel_id=1, source_target_pairs={{6,0},{4,2},{10,4},{8,6},{14,8},{12,10},{18,12},{16,14},{22,16},{2... | collective-permute-start | bytes 110600 | tf_op jit(solution)/shard_map/ppermute | solution.py:415
  16.4 4.6 %copy-start.16 = (f32[2,2,192]{2,1,0:T(2,128)S(1)}, f32[2,2,192]{2,1,0:T(2,128)}, u32[]{:S(2)}) copy-start(f32[2,2,192]{2,1,0:T(2,128)} %refs_4_.4) | copy-start | bytes 9220
  20.9 13.8 %copy-start.7 = (bf16[3,144,192]{2,1,0:T(8,128)(2,1)S(1)}, bf16[3,144,192]{2,1,0:T(8,128)(2,1)}, u32[]{:S(2)}) copy-start(bf16[3,144,192]{2,1,0:T(8,128)(2,1)} %get-tuple-element.23.refs_11_) | copy-start | bytes 497668
  20.9 13.8 %copy-start.8 = (bf16[144,768]{1,0:T(8,128)(2,1)S(1)}, bf16[144,768]{1,0:T(8,128)(2,1)}, u32[]{:S(2)}) copy-start(bf16[144,768]{1,0:T(8,128)(2,1)} %get-tuple-element.26.refs_14_) | copy-start | bytes 663556
  21.0 13.8 %copy-start.10 = (f32[144,192]{1,0:T(8,128)S(1)}, f32[144,192]{1,0:T(8,128)}, u32[]{:S(2)}) copy-start(f32[144,192]{1,0:T(8,128)} %get-tuple-element.25.refs_13_) | copy-start | bytes 331780
  21.0 13.8 %copy-start.13 = (bf16[144,256]{1,0:T(8,128)(2,1)S(1)}, bf16[144,256]{1,0:T(8,128)(2,1)}, u32[]{:S(2)}) copy-start(bf16[144,256]{1,0:T(8,128)(2,1)} %constant.28.clone.refs_15_) | copy-start | bytes 221188
  21.0 13.8 %copy-start.14 = (bf16[144,256]{1,0:T(8,128)(2,1)S(1)}, bf16[144,256]{1,0:T(8,128)(2,1)}, u32[]{:S(2)}) copy-start(bf16[144,256]{1,0:T(8,128)(2,1)} %get-tuple-element.21.refs_9_) | copy-start | bytes 221188
  21.0 13.8 %copy-start.15 = (bf16[144,192]{1,0:T(8,128)(2,1)S(1)}, bf16[144,192]{1,0:T(8,128)(2,1)}, u32[]{:S(2)}) copy-start(bf16[144,192]{1,0:T(8,128)(2,1)} %get-tuple-element.22.refs_10_) | copy-start | bytes 165892
  25.1 9.7 %copy-start.6 = (bf16[864,144]{1,0:T(8,128)(2,1)S(1)}, bf16[864,144]{1,0:T(8,128)(2,1)}, u32[]{:S(2)}) copy-start(bf16[864,144]{1,0:T(8,128)(2,1)} %get-tuple-element.24.refs_12_) | copy-start | bytes 746500
  25.1 1.3 %collective-permute-start.4 = (bf16[128,192]{1,0:T(8,128)(2,1)S(1)}, bf16[128,192]{1,0:T(8,128)(2,1)S(1)}, u32[]{:S(2)}, u32[]{:S(2)}) collective-permute-start(bf16[128,192]{1,0:T(8,128)(2,1)S(1)} %get-tuple-element.20), channel_id=1, source_target_pairs={{1,0},{0,1},{3,2},{2,3},{5,4},{4,5},{7,6},{6,7},{9,8},{8,9},{11,10... | collective-permute-start | bytes 147464 | tf_op jit(solution)/shard_map/ppermute | solution.py:415
  26.5 6.7 %collective-permute-start.5 = (bf16[64,192]{1,0:T(8,128)(2,1)S(1)}, bf16[64,192]{1,0:T(8,128)(2,1)S(1)}, u32[]{:S(2)}, u32[]{:S(2)}) collective-permute-start(bf16[64,192]{1,0:T(8,128)(2,1)S(1)} %pad_maximum_fusion.5), channel_id=1, source_target_pairs={{28,0},{0,4},{4,8},{8,12},{12,16},{16,20},{20,24},{24,28},{29,1},{... | collective-permute-start | bytes 73736 | tf_op jit(solution)/shard_map/ppermute | solution.py:415
  26.5 8.3 %copy-start.12 = (bf16[192,144]{1,0:T(8,128)(2,1)S(1)}, bf16[192,144]{1,0:T(8,128)(2,1)}, u32[]{:S(2)}) copy-start(bf16[192,144]{1,0:T(8,128)(2,1)} %constant.29.clone.refs_16_) | copy-start | bytes 165892
  26.6 6.6 %collective-permute-start.6 = (bf16[64,192]{1,0:T(8,128)(2,1)S(1)}, bf16[64,192]{1,0:T(8,128)(2,1)S(1)}, u32[]{:S(2)}, u32[]{:S(2)}) collective-permute-start(bf16[64,192]{1,0:T(8,128)(2,1)S(1)} %pad_maximum_fusion.6), channel_id=1, source_target_pairs={{2,0},{0,2},{3,1},{1,3},{6,4},{4,6},{7,5},{5,7},{10,8},{8,10},{11,... | collective-permute-start | bytes 73736 | tf_op jit(solution)/shard_map/ppermute | solution.py:415
  27.2 7.6 %collective-permute-start.7 = (bf16[64,192]{1,0:T(8,128)(2,1)S(1)}, bf16[64,192]{1,0:T(8,128)(2,1)S(1)}, u32[]{:S(2)}, u32[]{:S(2)}) collective-permute-start(bf16[64,192]{1,0:T(8,128)(2,1)S(1)} %pad_maximum_fusion.7), channel_id=1, source_target_pairs={{30,0},{28,2},{2,4},{0,6},{6,8},{4,10},{10,12},{8,14},{14,16},{12,... | collective-permute-start | bytes 73736 | tf_op jit(solution)/shard_map/ppermute | solution.py:415
  49.4 10.8 %all-to-all-start.1 = ((bf16[32,7,192]{2,1,0:T(8,128)(2,1)}), bf16[32,7,192]{2,1,0:T(8,128)(2,1)S(1)}, u32[]{:S(2)}, u32[]{:S(2)}) async-start(bf16[32,7,192]{2,1,0:T(8,128)(2,1)} %broadcast_in_dim.2), calls=%async_computation.1 | async-start | bytes 262144 | tf_op jit(solution)/shard_map/all_to_all | solution.py:446

commit v5 on v3

--- a/solution.py
+++ b/solution.py
@@ -31,20 +31,6 @@
     return array.astype(ml_dtypes.bfloat16)
 
 
-def patch_select():
-    sel = np.zeros((512, 512), np.float32)
-    for c in range(4):
-        for b in range(4):
-            base = c * 128 + b * 32
-            for z in range(2):
-                for a in range(2):
-                    for v in range(5):
-                        sel[base + (z * 2 + a) * 5 + v, z * 256 + v * 32 + a * 16 + b * 4 + c] = 1
-            for v in range(4):
-                sel[base + 20 + v, 160 + v * 16 + b * 4 + c] = 1
-    return as_half(sel)
-
-
 def cells():
     return [(z, a, o) for z in range(2) for a in range(6) for o in range(12)]
 
@@ -63,31 +49,81 @@
     return as_half(move)
 
 
-def octants_out(pitch, first, flip, source):
-    move = np.zeros((8 * pitch, CELLS), np.float32)
+def pair_out():
+    move = np.zeros((512, 3 * CELLS), np.float32)
     for z, a, o in cells():
         part, place = octant_of(z, a, o)
-        move[(7 - part if flip else part) * pitch + first + place, source(z, a, o)] = 1
+        for n in range(3):
+            slot = (7 - part) % 4 * 2 + (7 - part) // 4
+            move[slot * 64 + n * 18 + place, n * CELLS + inner_row(z, a, o)] = 1
     return as_half(move)
 
 
-def octants_in(pitch, first, flip):
-    move = np.zeros((CELLS, 8 * pitch), np.float32)
+def pair_in():
+    move = np.zeros((3 * CELLS, 512), np.float32)
     for z, a, o in cells():
         part, place = octant_of(z, a, o)
-        part = 7 - part if flip else part
-        block = (part % 4) * 2 + part // 4
-        move[inner_row(z, a, o), block * pitch + first + place] = 1
+        for n in range(3):
+            move[n * CELLS + inner_row(z, a, o), part * 64 + n * 18 + place] = 1
     return as_half(move)
 
 
-def bias_columns():
-    move = np.zeros((2, 256, 384), np.float32)
+def single_place(place):
+    return place, 1 + place // 9, 18 + place % 9
+
+
+def single_out():
+    move = np.zeros((256, 3 * CELLS), np.float32)
+    for z, a, o in cells():
+        part, place = octant_of(z, a, o)
+        first, group, last = single_place(place)
+        slot = part % 4 * 2 + part // 4
+        move[slot * 32 + first, inner_row(z, a, o)] = 1
+        move[slot * 32 + last, group * CELLS + inner_row(z, a, o)] = 1
+    return as_half(move)
+
+
+def single_in():
+    move = np.zeros((3 * CELLS, 256), np.float32)
+    for z, a, o in cells():
+        part, place = octant_of(z, a, o)
+        first, group, last = single_place(place)
+        move[inner_row(z, a, o), (7 - part) * 32 + first] = 1
+        move[group * CELLS + inner_row(z, a, o), (7 - part) * 32 + last] = 1
+    return as_half(move)
+
+
+def whole_part(v, size):
+    return jnp.floor((v + 0.5) * (1.0 / size))
+
+
+def one_hot(target, lanes):
+    lane = lax.broadcasted_iota(jnp.int32, (1, lanes), 1).astype(FULL)
+    return jnp.where(lane == target, 1.0, 0.0).astype(HALF)
+
+
+def fill_columns(cols):
+    row = lax.broadcasted_iota(jnp.int32, (256, 1), 0).astype(FULL)
+    a = whole_part(row, 23)
+    k = row - 23.0 * a
     for z in range(2):
-        for a in range(6):
-            for k in range(23):
-                move[z, a * 23 + k, (22 - k) * 12 + z * 6 + a] = 1
-    return as_half(move)
+        target = (22.0 - k) * 12.0 + (z * 6.0) + a
+        cols[z] = one_hot(jnp.where(row < 138.0, target, -1.0), 384)
+
+
+def fill_select(select):
+    row = lax.broadcasted_iota(jnp.int32, (128, 1), 0).astype(FULL)
+    b = whole_part(row, 32)
+    slot = row - 32.0 * b
+    layer = whole_part(slot, 5)
+    z = whole_part(layer, 2)
+    upper = z * 256.0 + (slot - 5.0 * layer) * 32.0 + (layer - 2.0 * z) * 16.0
+    surface = 160.0 + (slot - 20.0) * 16.0
+    target = jnp.where(slot < 20.0, upper, surface) + b * 4.0
+    for c in range(4):
+        select[c * 128 : c * 128 + 128, :] = one_hot(
+            jnp.where(slot < 24.0, target + float(c), -1.0), 512
+        )
 
 
 def dot(a, b):
@@ -149,9 +185,7 @@
     row = lax.broadcasted_iota(jnp.int32, (CELLS, 1), 0).astype(FULL)
     lane = lax.broadcasted_iota(jnp.int32, (1, CELLS), 1).astype(FULL)
 
-    def part(v, size):
-        return jnp.floor((v + 0.5) * (1.0 / size))
-
+    part = whole_part
     even = part(row, 12) - 2.0 * part(part(row, 12), 2) == 0.0
     table = jnp.where(even, pltpu.roll(table, 384 - 12, 1), table)
     if edges is not None:
@@ -269,78 +303,114 @@
 
 def first_kernel(*refs):
     names = (
-        "tbl", "cols", "upper", "surface", "select", "to_inner", "uembed", "sembed", "gains",
-        "wqkv", "wproj", "wup", "wdown", "cot", "out_first", "out_cot",
+        "tbl", "upper", "surface", "to_inner", "uembed", "sembed", "gains",
+        "wqkv", "wproj", "wup", "wdown", "cot", "out",
     )
     count = len(names)
-    source, rest = refs[:count], refs[count:]
-    keep_o, send_o, patch_o, x_o, qkv_o, prob, resid_o, slope_o = rest[:8]
-    local, rest = rest[8 : 8 + count], rest[8 + count :]
-    ff, ft, emb, cots, table, xs, bias, sems = rest
+    source, refs = refs[:count], refs[count:]
+    results = ("patch", "x", "qkv", "prob", "resid", "slope", "block0", "block1", "block2", "block3")
+    target, refs = refs[: len(results)], refs[len(results) :]
+    local, refs = refs[:count], refs[count:]
+    patch_s, x_s, qkv_s, prob, resid_s, slope_s, blocks = refs[:7]
+    ff, ft, emb, cots, table, xs, bias, cols, select, sems = refs[7:]
     copies = {}
     for n, name in enumerate(names):
-        start = source[n].at[0] if name[0] == "w" else source[n]
-        if name == "uembed":
-            target = emb.at[pl.ds(0, 160)]
+        start, end = source[n], local[n]
+        if name[0] == "w":
+            start = start.at[0]
+        elif name == "tbl":
+            start = start.at[pl.ds(0, HEADS)]
+        elif name == "uembed":
+            end = emb.at[pl.ds(0, 160)]
         elif name == "sembed":
-            target = emb.at[pl.ds(160, 64)]
-        else:
-            target = local[n]
-        copies[name] = pltpu.make_async_copy(start, target, sems.at[n])
+            end = emb.at[pl.ds(160, 64)]
+        copies[name] = pltpu.make_async_copy(start, end, sems.at[n])
         copies[name].start()
     have = dict(zip(names, local))
+    sent = []
 
     def wait(*which):
         for name in which:
             copies[name].wait()
 
+    def send(name, held):
+        n = results.index(name)
+        sent.append(pltpu.make_async_copy(held, target[n], sems.at[count + n]))
+        sent[-1].start()
+
     emb[224:256, :] = jnp.zeros((32, WIDTH), HALF)
-    wait("tbl", "cols")
+    fill_columns(cols)
+    fill_select(select)
+    wait("tbl")
     table_rows(have["tbl"], 0, table)
-    build_bias(table, have["cols"], xs, bias, None)
-    wait("upper", "surface", "select", "to_inner", "uembed", "sembed", "gains", "wqkv")
+    build_bias(table, cols, xs, bias, None)
+    wait("upper", "surface", "to_inner", "uembed", "sembed", "gains", "wqkv")
     section = lax.axis_index("section")
-    patch = gather_patches(have["upper"], have["surface"], section, have["select"], ff, ft)
+    patch = gather_patches(have["upper"], have["surface"], section, select, ff, ft)
     patch = dot(have["to_inner"][...], patch).astype(HALF)
-    patch_o[...] = patch
+    patch_s[...] = patch
+    send("patch", patch_s)
     latent = dot(patch, emb[...]).astype(HALF)
-    x_o[...] = latent
+    x_s[...] = latent
+    send("x", x_s)
     x = latent.astype(FULL)
     gains = have["gains"].at[0]
-    wait("wproj", "wup", "wdown", "cot", "out_first", "out_cot")
+    wait("wproj", "wup", "wdown", "cot", "out")
     cot = have["cot"]
+    gap = jnp.zeros((2, 64), FULL)
     for a in range(6):
         for o in range(12):
-            cots[(a * 12 + o) * 2 : (a * 12 + o) * 2 + 2, :] = cot[a, o].astype(FULL)
+            pair = cot[a, o].astype(FULL)
+            cots[0, pl.ds(o * 12 + a, 2, stride=6), :] = pair[:, :128]
+            cots[1, pl.ds(o * 12 + a, 2, stride=6), :] = jnp.concatenate((gap, pair[:, 128:]), 1)
     qkv, resid = forward_half(x, gains, have["wqkv"], have["wproj"], bias, prob)
+    send("prob", prob)
     for n in range(3):
-        qkv_o[n] = qkv[n]
-    resid_o[...] = resid
+        qkv_s[n] = qkv[n]
+    send("qkv", qkv_s)
+    resid_s[...] = resid
+    send("resid", resid_s)
     unit, spread = normalise(resid)
     normed = (unit * gains[1:2, :]).astype(HALF)
     upward = dot(normed, have["wup"][...])
     below, slope = gelu_parts(upward)
-    slope_o[...] = slope.astype(HALF)
+    slope_s[...] = slope.astype(HALF)
+    send("slope", slope_s)
     active = (upward * below).astype(HALF)
     result = (resid + dot_nt(active, have["wdown"][...])).astype(HALF)
-    moved = dot(have["out_first"][...], result)
-    moved = (moved + dot(have["out_cot"][...], cots[...].astype(HALF))).astype(HALF)
-    keep_o[...] = moved[:192]
-    send_o[...] = moved[192:]
-
-
-def bias_kernel(tbl, cols, bias, table, xs):
+    last = jnp.concatenate((result[:, 128:], jnp.zeros((CELLS, 64), HALF)), 1)
+    last = last + cots[1].astype(HALF)
+    both = jnp.concatenate((result[:, :128], cots[0].astype(HALF), last), 0)
+    moved = dot(have["out"][...], both).astype(HALF)
+    for n in range(4):
+        blocks[n] = moved[n * 128 : n * 128 + 128]
+        send("block" + str(n), blocks.at[n])
+    for copy in sent:
+        copy.wait()
+
+
+def bias_kernel(tbl, bias, table, xs, cols):
+    fill_columns(cols)
     table_rows(tbl, 1, table)
     build_bias(table, cols, xs, bias, (flag("section"), flag("lat")))
 
 
+def stacked(parts, stack):
+    pitch = stack.shape[0] // 8
+    for n in range(4):
+        stack[n * pitch : (n + 1) * pitch, :] = parts[n][0:pitch, :]
+    stack[4 * pitch :, :] = parts[4][...]
+
+
 def second_kernel(*refs):
-    parts, rest = refs[:4], refs[4:]
-    gains, wqkv, wproj, wup, wdown, bias, into, out_of, keep_o, send_o, stack, prob = rest
-    for n in range(4):
-        stack[n * 96 : n * 96 + 96, :] = parts[n][...]
+    parts, rest = refs[:5], refs[5:]
+    gains, wqkv, wproj, wup, wdown, bias, into, out_of = rest[:8]
+    blocks, stack, prob = rest[8:12], rest[12], rest[13]
+    stacked(parts, stack)
     both = dot(into[...], stack[...])
-    x, dflat = both[:CELLS], both[CELLS:].astype(HALF)
+    last = both[2 * CELLS :]
+    x = jnp.concatenate((both[:CELLS], last[:, :64]), 1)
+    dflat = jnp.concatenate((both[CELLS : 2 * CELLS], last[:, 64:]), 1).astype(HALF)
     gains, wqkv, wproj, wup, wdown = (w.at[1] for w in (gains, wqkv, wproj, wup, wdown))
     qkv, resid = forward_half(x, gains, wqkv, wproj, bias, prob)
     unit, spread = normalise(resid)
@@ -348,18 +418,23 @@
     upward = dot(normed, wup[...])
     slope = gelu_parts(upward)[1]
     dx = backward(dflat, x, qkv, prob, resid, slope, gains, wqkv, wproj, wup, wdown)
-    moved = dot(out_of[...], dx.astype(HALF)).astype(HALF)
-    keep_o[...] = moved[:128]
-    send_o[...] = moved[128:]
+    dx = dx.astype(HALF)
+    gap = jnp.zeros((CELLS, 64), HALF)
+    left = jnp.concatenate((dx[:, 128:], gap), 1)
+    right = jnp.concatenate((gap, dx[:, 128:]), 1)
+    moved = dot(out_of[...], jnp.concatenate((dx[:, :128], left, right), 0)).astype(HALF)
+    for n in range(4):
+        blocks[n][...] = moved[n * 64 : n * 64 + 64]
 
 
 def third_kernel(*refs):
-    parts, rest = refs[:4], refs[4:]
+    parts, rest = refs[:5], refs[5:]
     gains, wqkv, wproj, wup, wdown, patch, x_i, qkv_i, prob, resid, slope, into, out_of = rest[:13]
     grad_o, mine_o, other_o, stack, terms = rest[13:]
-    for n in range(4):
-        stack[n * 64 : n * 64 + 64, :] = parts[n][...]
-    dflat = dot(into[...], stack[...]).astype(HALF)
+    stacked(parts, stack)
+    moved = dot(into[...], stack[...])
+    last = moved[CELLS : 2 * CELLS, :64] + moved[2 * CELLS :, 64:]
+    dflat = jnp.concatenate((moved[:CELLS], last), 1).astype(HALF)
     qkv = tuple(qkv_i[n] for n in range(3))
     gains, wqkv, wproj, wup, wdown = (w.at[0] for w in (gains, wqkv, wproj, wup, wdown))
     dx = backward(
@@ -367,14 +442,16 @@
         gains, wqkv, wproj, wup, wdown,
     )
     grad = dx.astype(HALF)
+    total = dot_tn(patch[...], grad)
+    terms[0:224, :] = total[:224, :128]
+    terms[224:336, :] = jnp.concatenate((total[:112, 128:], total[112:224, 128:]), 1)
+    place = lax.axis_index("section") % 2
+    mine_o[...] = terms[pl.ds(pl.multiple_of(place * 168, 8), 168), :].astype(HALF)
+    other_o[...] = terms[pl.ds(pl.multiple_of(168 - place * 168, 8), 168), :].astype(HALF)
     moved = dot(out_of[...], grad).astype(HALF)
     for z in range(2):
         for a in range(6):
             grad_o[z, a] = moved[(z * 6 + a) * 16 : (z * 6 + a) * 16 + 12]
-    terms[...] = dot_tn(patch[...], grad)
-    place = lax.axis_index("section") % 2
-    mine_o[...] = terms[pl.ds(pl.multiple_of(place * 112, 16), 112), :].astype(HALF)
-    other_o[...] = terms[pl.ds(pl.multiple_of(112 - place * 112, 16), 112), :].astype(HALF)
 
 
 vmem = pl.BlockSpec(memory_space=pltpu.VMEM)
@@ -412,15 +489,11 @@
     return lax.ppermute(block, tuple(axes), pairs)
 
 
-def exchange(keep, send, way):
-    pitch = keep.shape[0] // 4
-    got = fetch(send, {"section": way})
-    blocks = []
-    for n in range(4):
-        rows = slice(n * pitch, (n + 1) * pitch)
-        block = jnp.concatenate((keep[rows], got[rows]), 0)
-        blocks.append(fetch(block, {"lat": way * (n // 2), "lon": way * (n % 2)}))
-    return blocks
+def exchange(blocks, way):
+    moved = [fetch(b, {"lat": way * (n // 2), "lon": way * (n % 2)}) for n, b in enumerate(blocks)]
+    half = blocks[0].shape[0] // 2
+    second = jnp.concatenate([block[half:] for block in moved], 0)
+    return (*moved, fetch(second, {"section": way}))
 
 
 def swap(block, flips):
@@ -459,10 +532,14 @@
     return total, swap(total, {"section": 1})
 
 
-def last_kernel(scale, mine, other, upper_o, surface_o, both, sems):
+def last_kernel(scale, mine, other, upper_o, surface_o, halves, both, sems):
     place = lax.axis_index("section") % 2
-    both[pl.ds(pl.multiple_of(place * 112, 16), 112), :] = mine[...].astype(FULL) * scale
-    both[pl.ds(pl.multiple_of(112 - place * 112, 16), 112), :] = other[...].astype(FULL) * scale
+    halves[pl.ds(pl.multiple_of(place * 168, 8), 168), :] = mine[...].astype(FULL) * scale
+    halves[pl.ds(pl.multiple_of(168 - place * 168, 8), 168), :] = other[...].astype(FULL) * scale
+    both[:, 0:128] = halves[0:224, :]
+    last = halves[224:336, :]
+    both[0:112, 128:192] = last[:, :64]
+    both[112:224, 128:192] = last[:, 64:]
     copies = [
         pltpu.make_async_copy(both.at[pl.ds(0, 160)], upper_o, sems.at[0]),
         pltpu.make_async_copy(both.at[pl.ds(160, 64)], surface_o, sems.at[1]),
@@ -491,72 +568,75 @@
     positions = earth_bias.shape[-1]
     table = earth_bias.transpose(0, 1, 3, 2, 4).reshape(2 * HEADS, 1, positions)
     weights = (norm_gains, qkv_weight, proj_weight, up_weight, down_weight.transpose(0, 2, 1))
-    cols = jnp.asarray(bias_columns())
-
-    def from_cot(z, a, o):
-        return (a * 12 + o) * 2 + z
-
     operands = (
-        table, cols, upper_fields, surface_fields, jnp.asarray(patch_select()),
-        jnp.asarray(natural_to_inner()), upper_embed, surface_embed, *weights,
-        out_grad.transpose(1, 2, 0, 3),
-        jnp.asarray(octants_out(48, 0, True, inner_row)),
-        jnp.asarray(octants_out(48, 18, True, from_cot)),
+        table, upper_fields, surface_fields, jnp.asarray(natural_to_inner()), upper_embed,
+        surface_embed, *weights, out_grad.transpose(1, 2, 0, 3), jnp.asarray(pair_out()),
     )
     local = [
-        pltpu.VMEM(v.shape[1:] if 9 <= n < 13 else v.shape, v.dtype) for n, v in enumerate(operands)
+        pltpu.VMEM(v.shape[1:] if 7 <= n < 11 else v.shape, v.dtype) for n, v in enumerate(operands)
     ]
-    local[6] = local[7] = pltpu.VMEM((16, 128), HALF)
+    local[0] = pltpu.VMEM((HEADS, 1, positions), FULL)
+    local[4] = local[5] = pltpu.VMEM((16, 128), HALF)
     scratch_bias = [pltpu.VMEM((8, 3328), FULL), pltpu.VMEM((4, CELLS, 128), FULL)]
-    keep, send, patch, x, qkv, prob, resid, slope = call(
+    scratch_cols = pltpu.VMEM((2, 256, 384), HALF)
+    held = [
+        shape((CELLS, 256)),
+        shape((CELLS, WIDTH)),
+        shape((3, CELLS, WIDTH)),
+        shape((HEADS * CELLS, CELLS)),
+        shape((CELLS, WIDTH), FULL),
+        shape((CELLS, 4 * WIDTH)),
+    ]
+    patch, x, qkv, prob, resid, slope, *blocks = call(
         first_kernel,
-        [
-            shape((192, WIDTH)),
-            shape((192, WIDTH)),
-            shape((CELLS, 256)),
-            shape((CELLS, WIDTH)),
-            shape((3, CELLS, WIDTH)),
-            shape((HEADS * CELLS, CELLS)),
-            shape((CELLS, WIDTH), FULL),
-            shape((CELLS, 4 * WIDTH)),
-        ],
+        held + [shape((128, 128))] * 4,
         local
+        + [pltpu.VMEM(v.shape, v.dtype) for v in held]
         + [
+            pltpu.VMEM((4, 128, 128), HALF),
             pltpu.VMEM((576, 128), FULL),
             pltpu.VMEM((288, 128), FULL),
             pltpu.VMEM((256, WIDTH), HALF),
-            pltpu.VMEM((CELLS, WIDTH), FULL),
+            pltpu.VMEM((2, CELLS, 128), FULL),
         ]
         + scratch_bias
         + [
             pltpu.VMEM((HEADS * CELLS, CELLS), FULL),
-            pltpu.SemaphoreType.DMA((len(operands),)),
+            scratch_cols,
+            pltpu.VMEM((512, 512), HALF),
+            pltpu.SemaphoreType.DMA((len(operands) + 10,)),
         ],
         *operands,
         spec=hbm,
+        out=hbm,
         room=60,
     )
-    bias = call(bias_kernel, shape((HEADS * CELLS, CELLS), FULL), scratch_bias, table, cols)
-    into = np.concatenate((octants_in(48, 0, False), octants_in(48, 18, False)), 0)
-    keep, send = call(
+    bias = call(
+        bias_kernel, shape((HEADS * CELLS, CELLS), FULL), [*scratch_bias, scratch_cols], table
+    )
+    blocks = call(
         second_kernel,
-        [shape((128, WIDTH))] * 2,
-        [pltpu.VMEM((8 * 48, WIDTH), HALF), pltpu.VMEM((HEADS * CELLS, CELLS), HALF)],
-        *exchange(keep, send, 1), *weights, bias,
-        jnp.asarray(into), jnp.asarray(octants_out(32, 0, False, inner_row)),
+        [shape((64, 128))] * 4,
+        [pltpu.VMEM((512, 128), HALF), pltpu.VMEM((HEADS * CELLS, CELLS), HALF)],
+        *exchange(blocks, 1), *weights, bias,
+        jnp.asarray(pair_in()), jnp.asarray(single_out()),
     )
     latent_grad, mine, other = call(
         third_kernel,
-        [shape((2, 6, 12, WIDTH)), shape((112, WIDTH)), shape((112, WIDTH))],
-        [pltpu.VMEM((8 * 32, WIDTH), HALF), pltpu.VMEM((256, WIDTH), FULL)],
-        *exchange(keep, send, -1), *weights, patch, x, qkv, prob, resid, slope,
-        jnp.asarray(octants_in(32, 0, True)), jnp.asarray(inner_to_padded()),
+        [shape((2, 6, 12, WIDTH)), shape((168, 128)), shape((168, 128))],
+        [pltpu.VMEM((256, 128), HALF), pltpu.VMEM((336, 128), FULL)],
+        *exchange(blocks, -1), *weights, patch, x, qkv, prob, resid, slope,
+        jnp.asarray(single_in()), jnp.asarray(inner_to_padded()),
     )
     scale = float(levels * sections * rows * bands * columns * lax.axis_size("lon")) ** (-0.5)
     upper_grad, surface_grad = call(
         functools.partial(last_kernel, scale),
         [shape((160, WIDTH), FULL), shape((64, WIDTH), FULL)],
-        [pltpu.VMEM((224, WIDTH), FULL), pltpu.SemaphoreType.DMA((2,))],
+        [
+            pltpu.VMEM((336, 128), FULL),
+            pltpu.VMEM((224, WIDTH), FULL),
+            pltpu.SemaphoreType.DMA((2,)),
+        ],
         *add_up(mine, other),
         out=hbm,
     )

time: 55.9 us -> 56.9 us (1.018)
  local copies, waits for them, and re-layouts: 1.63 us -> 2.89 us
  waiting for transfers between devices: 21.1 us -> 20.2 us
  Pallas kernels: 13.9 us -> 14.7 us
    unnamed x35 -> x39, local copies, waits for them, and re-layouts: 0.81 us -> 2.15 us
    ppermute x8, waiting for transfers between devices: 12.4 us -> 11.3 us  [fetch(): return lax.ppermute(block, tuple(axes), pairs)]
    pallas_call x5, Pallas kernels: 13.9 us -> 14.7 us  [call(): pl.pallas_call(kernel, out_shape=outs, in_specs=[spec for a in args], out...]
  transfers between devices with their start and end apart: 16 -> 16, of which waited for: 12 -> 13; matrix products, arithmetic and copies ran while one was open for 3% -> 3% of each run, Pallas kernels for 2% -> 2%
where the time goes in v5:
time: 56.9 us; the launch traced here: 56.7 us
  waiting for transfers between devices  20.2 us (36%)
  starting transfers between devices  17.8 us (31%)
  Pallas kernels  14.7 us (26%)
  local copies, waits for them, and re-layouts  2.89 us (5%)
  between operations  0.93 us (2%)
    pallas_call x5, Pallas kernels, call(): pl.pallas_call(kernel, out_shape=outs, in_specs=[spec for a in args], out...  14.7 us
    ppermute x8, waiting for transfers between devices, fetch(): return lax.ppermute(block, tuple(axes), pairs)  11.3 us
    ppermute x8, starting transfers between devices, fetch(): return lax.ppermute(block, tuple(axes), pairs)  9.51 us
    ppermute x8, waiting for transfers between devices, swap(): return lax.ppermute(block, tuple(axes), pairs)  8.94 us
    ppermute x8, starting transfers between devices, swap(): return lax.ppermute(block, tuple(axes), pairs)  8.28 us
    unnamed x39, local copies, waits for them, and re-layouts  2.15 us
  transfers between devices with their start and end apart: 16, of which 13 were waited for; matrix products, arithmetic and copies ran while one was open for 3% of the time, Pallas kernels for 2%

profile of v5, /device:TPU:0, one launch (start us, length us, event | category | flops | bytes accessed | tf_op | source)
XLA Modules:
  0.0 56.7 jit_solution(17997277222061318095)
XLA Ops:
  0.7 5.7 %shard_map.184 = (bf16[144,256]{1,0:T(8,128)(2,1)}, bf16[144,192]{1,0:T(8,128)(2,1)}, bf16[3,144,192]{2,1,0:T(8,128)(2,1)}, bf16[864,144]{1,0:T(8,128)(2,1)}, f3...) custom-call(f32[12,1,3312]{2,1,0:T(1,128)} %bitcast.6, ...), custom_call_target="tpu_custom_call" | custom-call | flops 1000000 | bytes 1000000 | tf_op jit(solution)/shard_map/pallas_call | solution.py:462
  6.4 6.1 %collective-permute-start = (bf16[128,128]{1,0:T(8,128)(2,1)}, bf16[128,128]{1,0:T(8,128)(2,1)S(1)}, u32[]{:S(2)}, u32[]{:S(2)}) collective-permute-start(bf16[128,128]{1,0:T(8,128)(2,1)} %get-tuple-element.23), channel_id=1, source_target_pairs={{4,0},{8,4},{12,8},{16,12},{20,16},{24,20},{28,24},{0,28},{5,1},{9... | collective-permute-start | bytes 98312 | tf_op jit(solution)/shard_map/ppermute | solution.py:489
  12.4 1.5 %collective-permute-start.1 = (bf16[128,128]{1,0:T(8,128)(2,1)}, bf16[128,128]{1,0:T(8,128)(2,1)S(1)}, u32[]{:S(2)}, u32[]{:S(2)}) collective-permute-start(bf16[128,128]{1,0:T(8,128)(2,1)} %get-tuple-element.24), channel_id=1, source_target_pairs={{2,0},{0,2},{3,1},{1,3},{6,4},{4,6},{7,5},{5,7},{10,8},{8,10},{11,... | collective-permute-start | bytes 98312 | tf_op jit(solution)/shard_map/ppermute | solution.py:489
  13.9 0.5 collective-permute-start.2
  14.4 0.7 %slice.24 = bf16[64,128]{1,0:T(8,128)(2,1)S(1)} slice(bf16[128,128]{1,0:T(8,128)(2,1)} %get-tuple-element.22.refs_0_), slice={[64:128], [0:128]} | slice | bytes 32768 | tf_op jit(solution)/shard_map/slice | solution.py:495
  15.1 0.6 %copy-done.14 = bf16[128,128]{1,0:T(8,128)(2,1)} copy-done((bf16[128,128]{1,0:T(8,128)(2,1)}, bf16[128,128]{1,0:T(8,128)(2,1)S(1)}, u32[]{:S(2)}) %copy-start.14) | copy-done | bytes 32792
  15.7 0.8 %collective-permute-done.1.refs_2_ = bf16[128,128]{1,0:T(8,128)(2,1)S(1)} collective-permute-done((bf16[128,128]{1,0:T(8,128)(2,1)}, bf16[128,128]{1,0:T(8,128)(2,1)S(1)}, u32[]{:S(2)}, u32[]{:S(2)}) %collective-permute-start.1) | collective-permute-done | bytes 32800 | tf_op jit(solution)/shard_map/ppermute | solution.py:489
  16.6 2.4 %collective-permute-done.2.refs_3_ = bf16[128,128]{1,0:T(8,128)(2,1)S(1)} collective-permute-done((bf16[128,128]{1,0:T(8,128)(2,1)}, bf16[128,128]{1,0:T(8,128)(2,1)S(1)}, u32[]{:S(2)}, u32[]{:S(2)}) %collective-permute-start.2) | collective-permute-done | bytes 32800 | tf_op jit(solution)/shard_map/ppermute | solution.py:489
  19.1 0.9 %shard_map.185.refs_10_ = f32[864,144]{1,0:T(8,128)S(1)} custom-call(f32[12,1,3312]{2,1,0:T(1,128)S(1)} %bitcast.7), custom_call_target="tpu_custom_call" | custom-call | flops 1000000 | bytes 1000000 | tf_op jit(solution)/shard_map/pallas_call | solution.py:462
  20.0 0.3 collective-permute-done.3.refs_4_
  20.4 0.7 %copy-done.15 = bf16[128,128]{1,0:T(8,128)(2,1)S(1)} copy-done((bf16[128,128]{1,0:T(8,128)(2,1)S(1)}, bf16[128,128]{1,0:T(8,128)(2,1)}, u32[]{:S(2)}) %copy-start.15) | copy-done | bytes 32792
  21.2 4.7 %shard_map.186 = (bf16[64,128]{1,0:T(8,128)(2,1)S(1)}, bf16[64,128]{1,0:T(8,128)(2,1)S(1)}, bf16[64,128]{1,0:T(8,128)(2,1)S(1)}, bf16[64,128]{1,0:T(8,128)(2,1)S(1)}) custom-call(bf16[128,128]{1,0:T(8,128)(2,1)S(1)} %copy-done.13, bf16[128,128]{1,0:T(8,128)(2,1)S(1)} %copy-done.15, bf16[128,128]{1,0:T(8,128)(2,1)S(1)} %collective-permute-done.1.refs_2_, ...), custom_call_target="tpu_custom_call" | custom-call | flops 1000000 | bytes 1000000 | tf_op jit(solution)/shard_map/pallas_call | solution.py:462
  26.0 0.6 %collective-permute-start.5 = (bf16[64,128]{1,0:T(8,128)(2,1)S(1)}, bf16[64,128]{1,0:T(8,128)(2,1)S(1)}, u32[]{:S(2)}, u32[]{:S(2)}) collective-permute-start(bf16[64,128]{1,0:T(8,128)(2,1)S(1)} %get-tuple-element.28), channel_id=1, source_target_pairs={{2,0},{0,2},{3,1},{1,3},{6,4},{4,6},{7,5},{5,7},{10,8},{8,10},{11,... | collective-permute-start | bytes 49160 | tf_op jit(solution)/shard_map/ppermute | solution.py:489
  26.6 0.7 %collective-permute-start.6 = (bf16[64,128]{1,0:T(8,128)(2,1)S(1)}, bf16[64,128]{1,0:T(8,128)(2,1)S(1)}, u32[]{:S(2)}, u32[]{:S(2)}) collective-permute-start(bf16[64,128]{1,0:T(8,128)(2,1)S(1)} %get-tuple-element.29), channel_id=1, source_target_pairs={{30,0},{28,2},{2,4},{0,6},{6,8},{4,10},{10,12},{8,14},{14,16},{12,... | collective-permute-start | bytes 49160 | tf_op jit(solution)/shard_map/ppermute | solution.py:489
  27.3 5.1 %collective-permute-done.4.refs_1_ = bf16[64,128]{1,0:T(8,128)(2,1)S(1)} collective-permute-done((bf16[64,128]{1,0:T(8,128)(2,1)S(1)}, bf16[64,128]{1,0:T(8,128)(2,1)S(1)}, u32[]{:S(2)}, u32[]{:S(2)}) %collective-permute-start.4) | collective-permute-done | bytes 16416 | tf_op jit(solution)/shard_map/ppermute | solution.py:489
  32.4 1.5 %collective-permute-done.6.refs_3_ = bf16[64,128]{1,0:T(8,128)(2,1)S(1)} collective-permute-done((bf16[64,128]{1,0:T(8,128)(2,1)S(1)}, bf16[64,128]{1,0:T(8,128)(2,1)S(1)}, u32[]{:S(2)}, u32[]{:S(2)}) %collective-permute-start.6) | collective-permute-done | bytes 16416 | tf_op jit(solution)/shard_map/ppermute | solution.py:489
  33.9 1.2 %collective-permute-done.7.refs_4_ = bf16[128,128]{1,0:T(8,128)(2,1)S(1)} collective-permute-done((bf16[128,128]{1,0:T(8,128)(2,1)S(1)}, bf16[128,128]{1,0:T(8,128)(2,1)S(1)}, u32[]{:S(2)}, u32[]{:S(2)}) %collective-permute-start.7) | collective-permute-done | bytes 32800 | tf_op jit(solution)/shard_map/ppermute | solution.py:489
  35.2 2.6 %shard_map.187 = (bf16[2,6,12,192]{3,2,1,0:T(8,128)(2,1)S(1)}, bf16[168,128]{1,0:T(8,128)(2,1)S(1)}, bf16[168,128]{1,0:T(8,128)(2,1)S(1)}) custom-call(bf16[64,128]{1,0:T(8,128)(2,1)S(1)} %get-tuple-element.26.refs_0_, bf16[64,128]{1,0:T(8,128)(2,1)S(1)} %collective-permute-done.4.refs_1_, bf16[64,128]{1,0:T(8,128)(2,1)S(1)} %collective-permute-done.5.refs_2_, ...), custom_call_target="tpu_custom_call" | custom-call | flops 1000000 | bytes 1000000 | tf_op jit(solution)/shard_map/pallas_call | solution.py:462
  37.8 0.2 collective-permute-start.8
  38.0 1.1 %collective-permute-done.8 = bf16[168,128]{1,0:T(8,128)(2,1)S(1)} collective-permute-done((bf16[168,128]{1,0:T(8,128)(2,1)S(1)}, bf16[168,128]{1,0:T(8,128)(2,1)S(1)}, u32[]{:S(2)}, u32[]{:S(2)}) %collective-permute-start.8) | collective-permute-done | bytes 43040 | tf_op jit(solution)/shard_map/ppermute | solution.py:509
  39.2 2.9 %collective-permute-start.11 = (bf16[168,128]{1,0:T(8,128)(2,1)S(1)}, bf16[168,128]{1,0:T(8,128)(2,1)S(1)}, u32[]{:S(2)}, u32[]{:S(2)}) collective-permute-start(bf16[168,128]{1,0:T(8,128)(2,1)S(1)} %add_convert_fusion.2), channel_id=1, source_target_pairs={{6,0},{4,2},{2,4},{0,6},{14,8},{12,10},{10,12},{8,14},{22,16},{20,... | collective-permute-start | bytes 129032 | tf_op jit(solution)/shard_map/ppermute | solution.py:509
  42.1 0.5 collective-permute-start.9
  42.7 1.0 %collective-permute-done.10 = bf16[168,128]{1,0:T(8,128)(2,1)S(1)} collective-permute-done((bf16[168,128]{1,0:T(8,128)(2,1)S(1)}, bf16[168,128]{1,0:T(8,128)(2,1)S(1)}, u32[]{:S(2)}, u32[]{:S(2)}) %collective-permute-start.10) | collective-permute-done | bytes 43040 | tf_op jit(solution)/shard_map/ppermute | solution.py:509
  43.7 0.7 %collective-permute-done.11 = bf16[168,128]{1,0:T(8,128)(2,1)S(1)} collective-permute-done((bf16[168,128]{1,0:T(8,128)(2,1)S(1)}, bf16[168,128]{1,0:T(8,128)(2,1)S(1)}, u32[]{:S(2)}, u32[]{:S(2)}) %collective-permute-start.11) | collective-permute-done | bytes 43040 | tf_op jit(solution)/shard_map/ppermute | solution.py:509
  44.3 1.8 %collective-permute-done.9 = bf16[168,128]{1,0:T(8,128)(2,1)S(1)} collective-permute-done((bf16[168,128]{1,0:T(8,128)(2,1)S(1)}, bf16[168,128]{1,0:T(8,128)(2,1)S(1)}, u32[]{:S(2)}, u32[]{:S(2)}) %collective-permute-start.9) | collective-permute-done | bytes 43040 | tf_op jit(solution)/shard_map/ppermute | solution.py:509
  46.3 2.4 %collective-permute-start.13 = (bf16[168,128]{1,0:T(8,128)(2,1)S(1)}, bf16[168,128]{1,0:T(8,128)(2,1)S(1)}, u32[]{:S(2)}, u32[]{:S(2)}) collective-permute-start(bf16[168,128]{1,0:T(8,128)(2,1)S(1)} %add_convert_fusion.1), channel_id=1, source_target_pairs={{16,0},{20,4},{24,8},{28,12},{0,16},{4,20},{8,24},{12,28},{17,1},{... | collective-permute-start | bytes 129032 | tf_op jit(solution)/shard_map/ppermute | solution.py:509
  48.7 1.9 %collective-permute-start.14 = (bf16[168,128]{1,0:T(8,128)(2,1)S(1)}, bf16[168,128]{1,0:T(8,128)(2,1)S(1)}, u32[]{:S(2)}, u32[]{:S(2)}) collective-permute-start(bf16[168,128]{1,0:T(8,128)(2,1)S(1)} %add_convert_fusion.1), channel_id=1, source_target_pairs={{24,0},{28,4},{16,8},{20,12},{8,16},{12,20},{0,24},{4,28},{25,1},{... | collective-permute-start | bytes 129032 | tf_op jit(solution)/shard_map/ppermute | solution.py:509
  50.6 0.6 %collective-permute-done.13 = bf16[168,128]{1,0:T(8,128)(2,1)S(1)} collective-permute-done((bf16[168,128]{1,0:T(8,128)(2,1)S(1)}, bf16[168,128]{1,0:T(8,128)(2,1)S(1)}, u32[]{:S(2)}, u32[]{:S(2)}) %collective-permute-start.13) | collective-permute-done | bytes 43040 | tf_op jit(solution)/shard_map/ppermute | solution.py:509
  51.3 3.3 %collective-permute-done.14 = bf16[168,128]{1,0:T(8,128)(2,1)S(1)} collective-permute-done((bf16[168,128]{1,0:T(8,128)(2,1)S(1)}, bf16[168,128]{1,0:T(8,128)(2,1)S(1)}, u32[]{:S(2)}, u32[]{:S(2)}) %collective-permute-start.14) | collective-permute-done | bytes 43040 | tf_op jit(solution)/shard_map/ppermute | solution.py:509
  54.6 0.7 %copy.20 = bf16[2,6,12,192]{3,0,2,1:T(2,128)(2,1)} copy(bf16[2,6,12,192]{3,2,1,0:T(8,128)(2,1)S(1)} %get-tuple-element.41) | data formatting | bytes 110592
  55.4 0.5 collective-permute-done.15.other
  55.9 0.8 %shard_map.188 = (f32[160,192]{1,0:T(8,128)}, f32[64,192]{1,0:T(8,128)}) custom-call(bf16[168,128]{1,0:T(8,128)(2,1)S(1)} %add_convert_fusion.mine, bf16[168,128]{1,0:T(8,128)(2,1)S(1)} %collective-permute-done.15.other), custom_call_target="tpu_custom_call" | custom-call | flops 1000000 | bytes 1000000 | tf_op jit(solution)/shard_map/pallas_call | solution.py:462
  (58 shorter events, 0.5 us)
Async XLA Ops:
  0.6 18.4 %copy-start.4 = (f32[2,1,1,6,3312]{4,2,3,1,0:T(1,128)S(1)}, f32[2,1,1,6,3312]{4,2,3,1,0:T(1,128)}, u32[]{:S(2)}) copy-start(f32[2,1,1,6,3312]{4,2,3,1,0:T(1,128)} %param.26) | copy-start | bytes 476932
  0.6 19.7 %copy-start.2 = (bf16[2,192,576]{2,1,0:T(8,128)(2,1)S(1)}, bf16[2,192,576]{2,1,0:T(8,128)(2,1)}, u32[]{:S(2)}) copy-start(bf16[2,192,576]{2,1,0:T(8,128)(2,1)} %refs_6_.5) | copy-start | bytes 1327108
  0.7 19.7 %copy-start.3 = (bf16[2,192,192]{2,1,0:T(8,128)(2,1)S(1)}, bf16[2,192,192]{2,1,0:T(8,128)(2,1)}, u32[]{:S(2)}) copy-start(bf16[2,192,192]{2,1,0:T(8,128)(2,1)} %refs_7_.5) | copy-start | bytes 442372
  0.7 19.7 %copy-start.6 = (bf16[432,512]{1,0:T(8,128)(2,1)S(1)}, bf16[432,512]{1,0:T(8,128)(2,1)}, u32[]{:S(2)}) copy-start(bf16[432,512]{1,0:T(8,128)(2,1)} %constant.14.clone.refs_11_) | copy-start | bytes 1327108
  0.7 19.6 %copy-start.7 = (bf16[256,432]{1,0:T(8,128)(2,1)S(1)}, bf16[256,432]{1,0:T(8,128)(2,1)}, u32[]{:S(2)}) copy-start(bf16[256,432]{1,0:T(8,128)(2,1)} %constant.15.clone.refs_12_) | copy-start | bytes 663556
  6.4 8.8 %collective-permute-start = (bf16[128,128]{1,0:T(8,128)(2,1)}, bf16[128,128]{1,0:T(8,128)(2,1)S(1)}, u32[]{:S(2)}, u32[]{:S(2)}) collective-permute-start(bf16[128,128]{1,0:T(8,128)(2,1)} %get-tuple-element.23), channel_id=1, source_target_pairs={{4,0},{8,4},{12,8},{16,12},{20,16},{24,20},{28,24},{0,28},{5,1},{9... | collective-permute-start | bytes 98312 | tf_op jit(solution)/shard_map/ppermute | solution.py:489
  12.4 4.1 %collective-permute-start.1 = (bf16[128,128]{1,0:T(8,128)(2,1)}, bf16[128,128]{1,0:T(8,128)(2,1)S(1)}, u32[]{:S(2)}, u32[]{:S(2)}) collective-permute-start(bf16[128,128]{1,0:T(8,128)(2,1)} %get-tuple-element.24), channel_id=1, source_target_pairs={{2,0},{0,2},{3,1},{1,3},{6,4},{4,6},{7,5},{5,7},{10,8},{8,10},{11,... | collective-permute-start | bytes 98312 | tf_op jit(solution)/shard_map/ppermute | solution.py:489
  13.9 5.0 %collective-permute-start.2 = (bf16[128,128]{1,0:T(8,128)(2,1)}, bf16[128,128]{1,0:T(8,128)(2,1)S(1)}, u32[]{:S(2)}, u32[]{:S(2)}) collective-permute-start(bf16[128,128]{1,0:T(8,128)(2,1)} %get-tuple-element.25), channel_id=1, source_target_pairs={{6,0},{4,2},{10,4},{8,6},{14,8},{12,10},{18,12},{16,14},{22,16},{2... | collective-permute-start | bytes 98312 | tf_op jit(solution)/shard_map/ppermute | solution.py:489
  16.6 3.8 %copy-start.13 = (bf16[128,128]{1,0:T(8,128)(2,1)S(1)}, bf16[128,128]{1,0:T(8,128)(2,1)}, u32[]{:S(2)}) copy-start(bf16[128,128]{1,0:T(8,128)(2,1)} %get-tuple-element.22.refs_0_) | copy-start | bytes 98308
  16.6 2.4 %slice-start = ((bf16[128,128]{1,0:T(8,128)(2,1)}), bf16[64,128]{1,0:T(8,128)(2,1)S(1)}, s32[]{:S(2)}) async-start(bf16[128,128]{1,0:T(8,128)(2,1)} %copy-done.14), calls=%async_computation | async-start | bytes 32768 | tf_op jit(solution)/shard_map/slice | solution.py:495
  19.0 1.4 %copy-start = (bf16[2,192,768]{2,1,0:T(8,128)(2,1)S(1)}, bf16[2,192,768]{2,1,0:T(8,128)(2,1)}, u32[]{:S(2)}) copy-start(bf16[2,192,768]{2,1,0:T(8,128)(2,1)} %refs_8_.5) | copy-start | bytes 1769476
  19.0 1.3 %collective-permute-start.3 = (bf16[256,128]{1,0:T(8,128)(2,1)S(1)}, bf16[256,128]{1,0:T(8,128)(2,1)S(1)}, u32[]{:S(2)}, u32[]{:S(2)}) collective-permute-start(bf16[256,128]{1,0:T(8,128)(2,1)S(1)} %pad_maximum_fusion), channel_id=1, source_target_pairs={{1,0},{0,1},{3,2},{2,3},{5,4},{4,5},{7,6},{6,7},{9,8},{8,9},{11,10... | collective-permute-start | bytes 196616 | tf_op jit(solution)/shard_map/ppermute | solution.py:489
  21.1 14.0 %copy-start.5 = (bf16[864,144]{1,0:T(8,128)(2,1)S(1)}, bf16[864,144]{1,0:T(8,128)(2,1)}, u32[]{:S(2)}) copy-start(bf16[864,144]{1,0:T(8,128)(2,1)} %get-tuple-element.33.refs_13_) | copy-start | bytes 746500
  21.1 14.0 %copy-start.8 = (bf16[432,256]{1,0:T(8,128)(2,1)S(1)}, bf16[432,256]{1,0:T(8,128)(2,1)}, u32[]{:S(2)}) copy-start(bf16[432,256]{1,0:T(8,128)(2,1)} %constant.16.clone.refs_16_) | copy-start | bytes 663556
  21.1 14.0 %copy-start.9 = (bf16[3,144,192]{2,1,0:T(8,128)(2,1)S(1)}, bf16[3,144,192]{2,1,0:T(8,128)(2,1)}, u32[]{:S(2)}) copy-start(bf16[3,144,192]{2,1,0:T(8,128)(2,1)} %get-tuple-element.32.refs_12_) | copy-start | bytes 497668
  21.1 14.0 %copy-start.10 = (bf16[144,768]{1,0:T(8,128)(2,1)S(1)}, bf16[144,768]{1,0:T(8,128)(2,1)}, u32[]{:S(2)}) copy-start(bf16[144,768]{1,0:T(8,128)(2,1)} %get-tuple-element.35.refs_15_) | copy-start | bytes 663556
  21.1 14.0 %copy-start.12 = (bf16[192,144]{1,0:T(8,128)(2,1)S(1)}, bf16[192,144]{1,0:T(8,128)(2,1)}, u32[]{:S(2)}) copy-start(bf16[192,144]{1,0:T(8,128)(2,1)} %constant.17.clone.refs_17_) | copy-start | bytes 165892
  21.2 14.0 %copy-start.16 = (bf16[144,256]{1,0:T(8,128)(2,1)S(1)}, bf16[144,256]{1,0:T(8,128)(2,1)}, u32[]{:S(2)}) copy-start(bf16[144,256]{1,0:T(8,128)(2,1)} %get-tuple-element.30.refs_10_) | copy-start | bytes 221188
  21.2 14.0 %copy-start.17 = (bf16[144,192]{1,0:T(8,128)(2,1)S(1)}, bf16[144,192]{1,0:T(8,128)(2,1)}, u32[]{:S(2)}) copy-start(bf16[144,192]{1,0:T(8,128)(2,1)} %get-tuple-element.31.refs_11_) | copy-start | bytes 165892
  25.9 9.3 %copy-start.11 = (f32[144,192]{1,0:T(8,128)S(1)}, f32[144,192]{1,0:T(8,128)}, u32[]{:S(2)}) copy-start(f32[144,192]{1,0:T(8,128)} %get-tuple-element.34.refs_14_) | copy-start | bytes 331780
  25.9 6.5 %collective-permute-start.4 = (bf16[64,128]{1,0:T(8,128)(2,1)S(1)}, bf16[64,128]{1,0:T(8,128)(2,1)S(1)}, u32[]{:S(2)}, u32[]{:S(2)}) collective-permute-start(bf16[64,128]{1,0:T(8,128)(2,1)S(1)} %get-tuple-element.27), channel_id=1, source_target_pairs={{28,0},{0,4},{4,8},{8,12},{12,16},{16,20},{20,24},{24,28},{29,1},{... | collective-permute-start | bytes 49160 | tf_op jit(solution)/shard_map/ppermute | solution.py:489
  26.0 6.4 %collective-permute-start.5 = (bf16[64,128]{1,0:T(8,128)(2,1)S(1)}, bf16[64,128]{1,0:T(8,128)(2,1)S(1)}, u32[]{:S(2)}, u32[]{:S(2)}) collective-permute-start(bf16[64,128]{1,0:T(8,128)(2,1)S(1)} %get-tuple-element.28), channel_id=1, source_target_pairs={{2,0},{0,2},{3,1},{1,3},{6,4},{4,6},{7,5},{5,7},{10,8},{8,10},{11,... | collective-permute-start | bytes 49160 | tf_op jit(solution)/shard_map/ppermute | solution.py:489
  26.6 7.3 %collective-permute-start.6 = (bf16[64,128]{1,0:T(8,128)(2,1)S(1)}, bf16[64,128]{1,0:T(8,128)(2,1)S(1)}, u32[]{:S(2)}, u32[]{:S(2)}) collective-permute-start(bf16[64,128]{1,0:T(8,128)(2,1)S(1)} %get-tuple-element.29), channel_id=1, source_target_pairs={{30,0},{28,2},{2,4},{0,6},{6,8},{4,10},{10,12},{8,14},{14,16},{12,... | collective-permute-start | bytes 49160 | tf_op jit(solution)/shard_map/ppermute | solution.py:489
  33.9 1.2 %collective-permute-start.7 = (bf16[128,128]{1,0:T(8,128)(2,1)S(1)}, bf16[128,128]{1,0:T(8,128)(2,1)S(1)}, u32[]{:S(2)}, u32[]{:S(2)}) collective-permute-start(bf16[128,128]{1,0:T(8,128)(2,1)S(1)} %pad_maximum_fusion.1), channel_id=1, source_target_pairs={{1,0},{0,1},{3,2},{2,3},{5,4},{4,5},{7,6},{6,7},{9,8},{8,9},{11,10... | collective-permute-start | bytes 98312 | tf_op jit(solution)/shard_map/ppermute | solution.py:489
  37.8 1.3 %collective-permute-start.8 = (bf16[168,128]{1,0:T(8,128)(2,1)S(1)}, bf16[168,128]{1,0:T(8,128)(2,1)S(1)}, u32[]{:S(2)}, u32[]{:S(2)}) collective-permute-start(bf16[168,128]{1,0:T(8,128)(2,1)S(1)} %get-tuple-element.38), channel_id=1, source_target_pairs={{1,0},{0,1},{3,2},{2,3},{5,4},{4,5},{7,6},{6,7},{9,8},{8,9},{11,10... | collective-permute-start | bytes 129032 | tf_op jit(solution)/shard_map/ppermute | solution.py:509
  39.1 4.6 %collective-permute-start.10 = (bf16[168,128]{1,0:T(8,128)(2,1)S(1)}, bf16[168,128]{1,0:T(8,128)(2,1)S(1)}, u32[]{:S(2)}, u32[]{:S(2)}) collective-permute-start(bf16[168,128]{1,0:T(8,128)(2,1)S(1)} %add_convert_fusion.2), channel_id=1, source_target_pairs={{4,0},{0,4},{12,8},{8,12},{20,16},{16,20},{28,24},{24,28},{5,1},{1... | collective-permute-start | bytes 129032 | tf_op jit(solution)/shard_map/ppermute | solution.py:509
  39.2 5.1 %collective-permute-start.11 = (bf16[168,128]{1,0:T(8,128)(2,1)S(1)}, bf16[168,128]{1,0:T(8,128)(2,1)S(1)}, u32[]{:S(2)}, u32[]{:S(2)}) collective-permute-start(bf16[168,128]{1,0:T(8,128)(2,1)S(1)} %add_convert_fusion.2), channel_id=1, source_target_pairs={{6,0},{4,2},{2,4},{0,6},{14,8},{12,10},{10,12},{8,14},{22,16},{20,... | collective-permute-start | bytes 129032 | tf_op jit(solution)/shard_map/ppermute | solution.py:509
  42.1 4.0 %collective-permute-start.9 = (bf16[168,128]{1,0:T(8,128)(2,1)S(1)}, bf16[168,128]{1,0:T(8,128)(2,1)S(1)}, u32[]{:S(2)}, u32[]{:S(2)}) collective-permute-start(bf16[168,128]{1,0:T(8,128)(2,1)S(1)} %add_convert_fusion.2), channel_id=1, source_target_pairs={{2,0},{0,2},{3,1},{1,3},{6,4},{4,6},{7,5},{5,7},{10,8},{8,10},{11,... | collective-permute-start | bytes 129032 | tf_op jit(solution)/shard_map/ppermute | solution.py:509
  46.2 4.5 %collective-permute-start.12 = (bf16[168,128]{1,0:T(8,128)(2,1)S(1)}, bf16[168,128]{1,0:T(8,128)(2,1)S(1)}, u32[]{:S(2)}, u32[]{:S(2)}) collective-permute-start(bf16[168,128]{1,0:T(8,128)(2,1)S(1)} %add_convert_fusion.1), channel_id=1, source_target_pairs={{8,0},{12,4},{0,8},{4,12},{24,16},{28,20},{16,24},{20,28},{9,1},{1... | collective-permute-start | bytes 129032 | tf_op jit(solution)/shard_map/ppermute | solution.py:509
  46.3 5.0 %collective-permute-start.13 = (bf16[168,128]{1,0:T(8,128)(2,1)S(1)}, bf16[168,128]{1,0:T(8,128)(2,1)S(1)}, u32[]{:S(2)}, u32[]{:S(2)}) collective-permute-start(bf16[168,128]{1,0:T(8,128)(2,1)S(1)} %add_convert_fusion.1), channel_id=1, source_target_pairs={{16,0},{20,4},{24,8},{28,12},{0,16},{4,20},{8,24},{12,28},{17,1},{... | collective-permute-start | bytes 129032 | tf_op jit(solution)/shard_map/ppermute | solution.py:509
  48.7 5.8 %collective-permute-start.14 = (bf16[168,128]{1,0:T(8,128)(2,1)S(1)}, bf16[168,128]{1,0:T(8,128)(2,1)S(1)}, u32[]{:S(2)}, u32[]{:S(2)}) collective-permute-start(bf16[168,128]{1,0:T(8,128)(2,1)S(1)} %add_convert_fusion.1), channel_id=1, source_target_pairs={{24,0},{28,4},{16,8},{20,12},{8,16},{12,20},{0,24},{4,28},{25,1},{... | collective-permute-start | bytes 129032 | tf_op jit(solution)/shard_map/ppermute | solution.py:509
  54.6 1.3 %collective-permute-start.15 = (bf16[168,128]{1,0:T(8,128)(2,1)S(1)}, bf16[168,128]{1,0:T(8,128)(2,1)S(1)}, u32[]{:S(2)}, u32[]{:S(2)}) collective-permute-start(bf16[168,128]{1,0:T(8,128)(2,1)S(1)} %add_convert_fusion.mine), channel_id=1, source_target_pairs={{1,0},{0,1},{3,2},{2,3},{5,4},{4,5},{7,6},{6,7},{9,8},{8,9},{11,10... | collective-permute-start | bytes 129032 | tf_op jit(solution)/shard_map/ppermute | solution.py:509
  (4 other events, 4.2 us)

commit v6 on v5

--- a/solution.py
+++ b/solution.py
@@ -49,47 +49,21 @@
     return as_half(move)
 
 
-def pair_out():
-    move = np.zeros((512, 3 * CELLS), np.float32)
+def octants_out(pitch, first, flip, source):
+    move = np.zeros((8 * pitch, CELLS), np.float32)
     for z, a, o in cells():
         part, place = octant_of(z, a, o)
-        for n in range(3):
-            slot = (7 - part) % 4 * 2 + (7 - part) // 4
-            move[slot * 64 + n * 18 + place, n * CELLS + inner_row(z, a, o)] = 1
+        part = 7 - part if flip else part
+        move[(part % 4 * 2 + part // 4) * pitch + first + place, source(z, a, o)] = 1
     return as_half(move)
 
 
-def pair_in():
-    move = np.zeros((3 * CELLS, 512), np.float32)
+def octants_in(pitch, first, flip):
+    move = np.zeros((CELLS, 8 * pitch), np.float32)
     for z, a, o in cells():
         part, place = octant_of(z, a, o)
-        for n in range(3):
-            move[n * CELLS + inner_row(z, a, o), part * 64 + n * 18 + place] = 1
-    return as_half(move)
-
-
-def single_place(place):
-    return place, 1 + place // 9, 18 + place % 9
-
-
-def single_out():
-    move = np.zeros((256, 3 * CELLS), np.float32)
-    for z, a, o in cells():
-        part, place = octant_of(z, a, o)
-        first, group, last = single_place(place)
-        slot = part % 4 * 2 + part // 4
-        move[slot * 32 + first, inner_row(z, a, o)] = 1
-        move[slot * 32 + last, group * CELLS + inner_row(z, a, o)] = 1
-    return as_half(move)
-
-
-def single_in():
-    move = np.zeros((3 * CELLS, 256), np.float32)
-    for z, a, o in cells():
-        part, place = octant_of(z, a, o)
-        first, group, last = single_place(place)
-        move[inner_row(z, a, o), (7 - part) * 32 + first] = 1
-        move[group * CELLS + inner_row(z, a, o), (7 - part) * 32 + last] = 1
+        part = 7 - part if flip else part
+        move[inner_row(z, a, o), part * pitch + first + place] = 1
     return as_half(move)
 
 
@@ -304,11 +278,11 @@
 def first_kernel(*refs):
     names = (
         "tbl", "upper", "surface", "to_inner", "uembed", "sembed", "gains",
-        "wqkv", "wproj", "wup", "wdown", "cot", "out",
+        "wqkv", "wproj", "wup", "wdown", "cot", "out_first", "out_cot",
     )
     count = len(names)
     source, refs = refs[:count], refs[count:]
-    results = ("patch", "x", "qkv", "prob", "resid", "slope", "block0", "block1", "block2", "block3")
+    results = ("patch", "x", "qkv", "prob", "resid", "slope", "keep", "give", "one", "two", "three")
     target, refs = refs[: len(results)], refs[len(results) :]
     local, refs = refs[:count], refs[count:]
     patch_s, x_s, qkv_s, prob, resid_s, slope_s, blocks = refs[:7]
@@ -335,7 +309,7 @@
 
     def send(name, held):
         n = results.index(name)
-        sent.append(pltpu.make_async_copy(held, target[n], sems.at[count + n]))
+        sent.append(pltpu.make_async_copy(held, target[n], sems.at[len(names) + n]))
         sent[-1].start()
 
     emb[224:256, :] = jnp.zeros((32, WIDTH), HALF)
@@ -355,14 +329,12 @@
     send("x", x_s)
     x = latent.astype(FULL)
     gains = have["gains"].at[0]
-    wait("wproj", "wup", "wdown", "cot", "out")
+    wait("wproj", "wup", "wdown", "cot", "out_first", "out_cot")
     cot = have["cot"]
-    gap = jnp.zeros((2, 64), FULL)
     for a in range(6):
         for o in range(12):
-            pair = cot[a, o].astype(FULL)
-            cots[0, pl.ds(o * 12 + a, 2, stride=6), :] = pair[:, :128]
-            cots[1, pl.ds(o * 12 + a, 2, stride=6), :] = jnp.concatenate((gap, pair[:, 128:]), 1)
+            cots[(a * 12 + o) * 2 : (a * 12 + o) * 2 + 2, :] = cot[a, o].astype(FULL)
+    ready = dot(have["out_cot"][...], cots[...].astype(HALF))
     qkv, resid = forward_half(x, gains, have["wqkv"], have["wproj"], bias, prob)
     send("prob", prob)
     for n in range(3):
@@ -378,39 +350,35 @@
     send("slope", slope_s)
     active = (upward * below).astype(HALF)
     result = (resid + dot_nt(active, have["wdown"][...])).astype(HALF)
-    last = jnp.concatenate((result[:, 128:], jnp.zeros((CELLS, 64), HALF)), 1)
-    last = last + cots[1].astype(HALF)
-    both = jnp.concatenate((result[:, :128], cots[0].astype(HALF), last), 0)
-    moved = dot(have["out"][...], both).astype(HALF)
-    for n in range(4):
-        blocks[n] = moved[n * 128 : n * 128 + 128]
-        send("block" + str(n), blocks.at[n])
+    blocks[...] = (dot(have["out_first"][...], result) + ready).astype(HALF)
+    for name, first, count in (("give", 48, 48), ("one", 96, 96), ("two", 192, 96), ("three", 288, 96), ("keep", 0, 48)):
+        send(name, blocks.at[pl.ds(first, count)])
     for copy in sent:
         copy.wait()
 
 
-def bias_kernel(tbl, bias, table, xs, cols):
+def bias_kernel(tbl, bias, done, table, xs, cols):
+    done[...] = jnp.zeros_like(done)
     fill_columns(cols)
     table_rows(tbl, 1, table)
     build_bias(table, cols, xs, bias, (flag("section"), flag("lat")))
 
 
 def stacked(parts, stack):
-    pitch = stack.shape[0] // 8
-    for n in range(4):
-        stack[n * pitch : (n + 1) * pitch, :] = parts[n][0:pitch, :]
-    stack[4 * pitch :, :] = parts[4][...]
+    keep, one, two, three, own, others = parts
+    pitch = keep.shape[0]
+    for n, part in enumerate((keep, one, two, three, own)):
+        stack[n * pitch : (n + 1) * pitch, :] = part[0:pitch, :]
+    stack[5 * pitch :, :] = others[...]
 
 
 def second_kernel(*refs):
-    parts, rest = refs[:5], refs[5:]
+    parts, rest = refs[:6], refs[6:]
     gains, wqkv, wproj, wup, wdown, bias, into, out_of = rest[:8]
-    blocks, stack, prob = rest[8:12], rest[12], rest[13]
+    keep, give, one, two, three, stack, prob = rest[8:]
     stacked(parts, stack)
     both = dot(into[...], stack[...])
-    last = both[2 * CELLS :]
-    x = jnp.concatenate((both[:CELLS], last[:, :64]), 1)
-    dflat = jnp.concatenate((both[CELLS : 2 * CELLS], last[:, 64:]), 1).astype(HALF)
+    x, dflat = both[:CELLS], both[CELLS:].astype(HALF)
     gains, wqkv, wproj, wup, wdown = (w.at[1] for w in (gains, wqkv, wproj, wup, wdown))
     qkv, resid = forward_half(x, gains, wqkv, wproj, bias, prob)
     unit, spread = normalise(resid)
@@ -418,23 +386,19 @@
     upward = dot(normed, wup[...])
     slope = gelu_parts(upward)[1]
     dx = backward(dflat, x, qkv, prob, resid, slope, gains, wqkv, wproj, wup, wdown)
-    dx = dx.astype(HALF)
-    gap = jnp.zeros((CELLS, 64), HALF)
-    left = jnp.concatenate((dx[:, 128:], gap), 1)
-    right = jnp.concatenate((gap, dx[:, 128:]), 1)
-    moved = dot(out_of[...], jnp.concatenate((dx[:, :128], left, right), 0)).astype(HALF)
-    for n in range(4):
-        blocks[n][...] = moved[n * 64 : n * 64 + 64]
+    moved = dot(out_of[...], dx.astype(HALF)).astype(HALF)
+    keep[...] = moved[:32]
+    give[...] = moved[32:64]
+    for n, block in enumerate((one, two, three)):
+        block[...] = moved[n * 64 + 64 : n * 64 + 128]
 
 
 def third_kernel(*refs):
-    parts, rest = refs[:5], refs[5:]
+    parts, rest = refs[:6], refs[6:]
     gains, wqkv, wproj, wup, wdown, patch, x_i, qkv_i, prob, resid, slope, into, out_of = rest[:13]
-    grad_o, mine_o, other_o, stack, terms = rest[13:]
+    grad_o, terms_o, stack = rest[13:]
     stacked(parts, stack)
-    moved = dot(into[...], stack[...])
-    last = moved[CELLS : 2 * CELLS, :64] + moved[2 * CELLS :, 64:]
-    dflat = jnp.concatenate((moved[:CELLS], last), 1).astype(HALF)
+    dflat = dot(into[...], stack[...]).astype(HALF)
     qkv = tuple(qkv_i[n] for n in range(3))
     gains, wqkv, wproj, wup, wdown = (w.at[0] for w in (gains, wqkv, wproj, wup, wdown))
     dx = backward(
@@ -443,11 +407,9 @@
     )
     grad = dx.astype(HALF)
     total = dot_tn(patch[...], grad)
-    terms[0:224, :] = total[:224, :128]
-    terms[224:336, :] = jnp.concatenate((total[:112, 128:], total[112:224, 128:]), 1)
-    place = lax.axis_index("section") % 2
-    mine_o[...] = terms[pl.ds(pl.multiple_of(place * 168, 8), 168), :].astype(HALF)
-    other_o[...] = terms[pl.ds(pl.multiple_of(168 - place * 168, 8), 168), :].astype(HALF)
+    terms_o[0:224, :] = total[:224, :128].astype(HALF)
+    last = jnp.concatenate((total[:112, 128:], total[112:224, 128:]), 1)
+    terms_o[224:336, :] = last.astype(HALF)
     moved = dot(out_of[...], grad).astype(HALF)
     for z in range(2):
         for a in range(6):
@@ -489,28 +451,32 @@
     return lax.ppermute(block, tuple(axes), pairs)
 
 
-def exchange(blocks, way):
-    moved = [fetch(b, {"lat": way * (n // 2), "lon": way * (n % 2)}) for n, b in enumerate(blocks)]
-    half = blocks[0].shape[0] // 2
-    second = jnp.concatenate([block[half:] for block in moved], 0)
-    return (*moved, fetch(second, {"section": way}))
+def exchange(keep, give, others, way, wait=None):
+    own = fetch(give, {"section": way})
+    moved = [
+        fetch(b, {"lat": way * (n // 2), "lon": way * (n % 2)}) for n, b in enumerate(others, 1)
+    ]
+    second = jnp.concatenate([block[keep.shape[0] :] for block in moved], 0)
+    if wait is not None:
+        second = second + wait[0, 0].astype(HALF)
+    return (keep, *moved, own, fetch(second, {"section": way}))
 
 
 def swap(block, flips):
-    names = ("lon", "lat", "section")
-    axes = [name for name in names if flips.get(name, 0)]
+    axes = ("lon", "lat", "section")
     sizes = [lax.axis_size(name) for name in axes]
     pairs = []
     for place in np.ndindex(*sizes):
-        source = [p ^ flips[name] for p, name in zip(place, axes)]
-        pairs.append(
-            (int(np.ravel_multi_index(source, sizes)), int(np.ravel_multi_index(place, sizes)))
-        )
-    return lax.ppermute(block, tuple(axes), pairs)
-
-
-def add_up(mine, other):
-    total = (mine.astype(FULL) + swap(other, {"section": 1}).astype(FULL)).astype(HALF)
+        source = [p ^ flips.get(name, 0) for p, name in zip(place, axes)]
+        if place[2] % 2:
+            pairs.append(
+                (int(np.ravel_multi_index(source, sizes)), int(np.ravel_multi_index(place, sizes)))
+            )
+    return lax.ppermute(block, axes, pairs)
+
+
+def add_up(terms):
+    total = (terms.astype(FULL) + swap(terms, {"section": 1}).astype(FULL)).astype(HALF)
     bits = []
     for name in ("section", "lat", "lon"):
         size = lax.axis_size(name)
@@ -529,17 +495,16 @@
             near, far, last = (swap(total, step).astype(FULL) for step in (one, two, three))
             total = (total.astype(FULL) + near) + (far + last)
         total = total.astype(HALF)
-    return total, swap(total, {"section": 1})
-
-
-def last_kernel(scale, mine, other, upper_o, surface_o, halves, both, sems):
-    place = lax.axis_index("section") % 2
-    halves[pl.ds(pl.multiple_of(place * 168, 8), 168), :] = mine[...].astype(FULL) * scale
-    halves[pl.ds(pl.multiple_of(168 - place * 168, 8), 168), :] = other[...].astype(FULL) * scale
-    both[:, 0:128] = halves[0:224, :]
-    last = halves[224:336, :]
-    both[0:112, 128:192] = last[:, :64]
-    both[112:224, 128:192] = last[:, 64:]
+    sections = range(0, lax.axis_size("section"), 2)
+    return total, lax.ppermute(total, "section", [(i + 1, i) for i in sections])
+
+
+def last_kernel(scale, own, given, upper_o, surface_o, both, sems):
+    odd = lax.axis_index("section") % 2 == 1
+    total = jnp.where(odd, own[...].astype(FULL), given[...].astype(FULL)) * scale
+    both[:, 0:128] = total[:224]
+    both[0:112, 128:192] = total[224:, :64]
+    both[112:224, 128:192] = total[224:, 64:]
     copies = [
         pltpu.make_async_copy(both.at[pl.ds(0, 160)], upper_o, sems.at[0]),
         pltpu.make_async_copy(both.at[pl.ds(160, 64)], surface_o, sems.at[1]),
@@ -568,9 +533,14 @@
     positions = earth_bias.shape[-1]
     table = earth_bias.transpose(0, 1, 3, 2, 4).reshape(2 * HEADS, 1, positions)
     weights = (norm_gains, qkv_weight, proj_weight, up_weight, down_weight.transpose(0, 2, 1))
+    def from_cot(z, a, o):
+        return (a * 12 + o) * 2 + z
+
     operands = (
         table, upper_fields, surface_fields, jnp.asarray(natural_to_inner()), upper_embed,
-        surface_embed, *weights, out_grad.transpose(1, 2, 0, 3), jnp.asarray(pair_out()),
+        surface_embed, *weights, out_grad.transpose(1, 2, 0, 3),
+        jnp.asarray(octants_out(48, 0, True, inner_row)),
+        jnp.asarray(octants_out(48, 18, True, from_cot)),
     )
     local = [
         pltpu.VMEM(v.shape[1:] if 7 <= n < 11 else v.shape, v.dtype) for n, v in enumerate(operands)
@@ -587,57 +557,60 @@
         shape((CELLS, WIDTH), FULL),
         shape((CELLS, 4 * WIDTH)),
     ]
-    patch, x, qkv, prob, resid, slope, *blocks = call(
+    patch, x, qkv, prob, resid, slope, keep, give, *others = call(
         first_kernel,
-        held + [shape((128, 128))] * 4,
+        held + [shape((48, WIDTH))] * 2 + [shape((96, WIDTH))] * 3,
         local
         + [pltpu.VMEM(v.shape, v.dtype) for v in held]
         + [
-            pltpu.VMEM((4, 128, 128), HALF),
+            pltpu.VMEM((384, WIDTH), HALF),
             pltpu.VMEM((576, 128), FULL),
             pltpu.VMEM((288, 128), FULL),
             pltpu.VMEM((256, WIDTH), HALF),
-            pltpu.VMEM((2, CELLS, 128), FULL),
+            pltpu.VMEM((CELLS, WIDTH), FULL),
         ]
         + scratch_bias
         + [
             pltpu.VMEM((HEADS * CELLS, CELLS), FULL),
             scratch_cols,
             pltpu.VMEM((512, 512), HALF),
-            pltpu.SemaphoreType.DMA((len(operands) + 10,)),
+            pltpu.SemaphoreType.DMA((len(operands) + 11,)),
         ],
         *operands,
         spec=hbm,
         out=hbm,
         room=60,
     )
-    bias = call(
-        bias_kernel, shape((HEADS * CELLS, CELLS), FULL), [*scratch_bias, scratch_cols], table
-    )
-    blocks = call(
+    bias, done = call(
+        bias_kernel,
+        [shape((HEADS * CELLS, CELLS), FULL), shape((8, 128), FULL)],
+        [*scratch_bias, scratch_cols],
+        table,
+    )
+    into = np.concatenate((octants_in(48, 0, False), octants_in(48, 18, False)), 0)
+    keep, give, *others = call(
         second_kernel,
-        [shape((64, 128))] * 4,
-        [pltpu.VMEM((512, 128), HALF), pltpu.VMEM((HEADS * CELLS, CELLS), HALF)],
-        *exchange(blocks, 1), *weights, bias,
-        jnp.asarray(pair_in()), jnp.asarray(single_out()),
-    )
-    latent_grad, mine, other = call(
+        [shape((32, WIDTH))] * 2 + [shape((64, WIDTH))] * 3,
+        [pltpu.VMEM((384, WIDTH), HALF), pltpu.VMEM((HEADS * CELLS, CELLS), HALF)],
+        *exchange(keep, give, others, 1, done), *weights, bias,
+        jnp.asarray(into), jnp.asarray(octants_out(32, 0, False, inner_row)),
+    )
+    latent_grad, terms = call(
         third_kernel,
-        [shape((2, 6, 12, WIDTH)), shape((168, 128)), shape((168, 128))],
-        [pltpu.VMEM((256, 128), HALF), pltpu.VMEM((336, 128), FULL)],
-        *exchange(blocks, -1), *weights, patch, x, qkv, prob, resid, slope,
-        jnp.asarray(single_in()), jnp.asarray(inner_to_padded()),
+        [shape((2, 6, 12, WIDTH)), shape((336, 128))],
+        [pltpu.VMEM((256, WIDTH), HALF)],
+        *exchange(keep, give, others, -1), *weights, patch, x, qkv, prob, resid, slope,
+        jnp.asarray(octants_in(32, 0, True)), jnp.asarray(inner_to_padded()),
     )
     scale = float(levels * sections * rows * bands * columns * lax.axis_size("lon")) ** (-0.5)
     upper_grad, surface_grad = call(
         functools.partial(last_kernel, scale),
         [shape((160, WIDTH), FULL), shape((64, WIDTH), FULL)],
         [
-            pltpu.VMEM((336, 128), FULL),
             pltpu.VMEM((224, WIDTH), FULL),
             pltpu.SemaphoreType.DMA((2,)),
         ],
-        *add_up(mine, other),
+        *add_up(terms),
         out=hbm,
     )
     return (latent_grad, upper_grad, surface_grad)

time: 56.9 us -> 67.1 us (1.18)
  waiting for transfers between devices: 20.2 us -> 31.5 us
  local copies, waits for them, and re-layouts: 2.89 us -> 1.36 us
  Pallas kernels: 14.7 us -> 14 us
    ppermute x8, waiting for transfers between devices: 8.94 us -> 19.8 us  [the longest x1 18.9 us: add_up(): lax.ppermute(total, 'section', [(i + 1, i) for i in sections])]
    unnamed x39 -> x37, local copies, waits for them, and re-layouts: 2.15 us -> 0.83 us
    ppermute x8 -> x10, starting transfers between devices: 9.51 us -> 10.5 us  [fetch(): return lax.ppermute(block, tuple(axes), pairs)]
    ppermute x8, starting transfers between devices: 8.28 us -> 7.55 us  [the longest x7 6.26 us: swap(): return lax.ppermute(block, axes, pairs)]
    pallas_call x5, Pallas kernels: 14.7 us -> 14 us  [call(): pl.pallas_call(kernel, out_shape=outs, in_specs=[spec for a in args], out...]
    ppermute x8 -> x10, waiting for transfers between devices: 11.3 us -> 11.7 us  [fetch(): return lax.ppermute(block, tuple(axes), pairs)]
  transfers between devices with their start and end apart: 16 -> 18, of which waited for: 13 -> 8; matrix products, arithmetic and copies ran while one was open for 3% -> 2% of each run, Pallas kernels for 2% -> 1%
where the time goes in v6:
time: 67.1 us; the launch traced here: 66.8 us
  waiting for transfers between devices  31.5 us (47%)
  starting transfers between devices  18.1 us (27%)
  Pallas kernels  14 us (21%)
  local copies, waits for them, and re-layouts  1.36 us (2%)
  between operations  1.05 us (2%)
  other arithmetic  0.74 us (1%)
    ppermute x1, waiting for transfers between devices, add_up(): lax.ppermute(total, 'section', [(i + 1, i) for i in sections])  18.9 us
    pallas_call x5, Pallas kernels, call(): pl.pallas_call(kernel, out_shape=outs, in_specs=[spec for a in args], out...  14 us
    ppermute x10, waiting for transfers between devices, fetch(): return lax.ppermute(block, tuple(axes), pairs)  11.7 us
    ppermute x10, starting transfers between devices, fetch(): return lax.ppermute(block, tuple(axes), pairs)  10.5 us
    ppermute x7, starting transfers between devices, swap(): return lax.ppermute(block, axes, pairs)  6.26 us
  transfers between devices with their start and end apart: 18, of which 8 were waited for; matrix products, arithmetic and copies ran while one was open for 2% of the time, Pallas kernels for 1%

profile of v6, /device:TPU:0, one launch (start us, length us, event | category | flops | bytes accessed | tf_op | source)
XLA Modules:
  0.0 66.8 jit_solution(12998106715045218510)
XLA Ops:
  0.7 5.6 %shard_map.193 = (bf16[144,256]{1,0:T(8,128)(2,1)}, bf16[144,192]{1,0:T(8,128)(2,1)}, bf16[3,144,192]{2,1,0:T(8,128)(2,1)}, bf16[864,144]{1,0:T(8,128)(2,1)}, f3...) custom-call(f32[12,1,3312]{2,1,0:T(1,128)} %bitcast.7, ...), custom_call_target="tpu_custom_call" | custom-call | flops 1000000 | bytes 1000000 | tf_op jit(solution)/shard_map/pallas_call | solution.py:424
  6.3 6.1 %collective-permute-start = (bf16[96,192]{1,0:T(8,128)(2,1)}, bf16[96,192]{1,0:T(8,128)(2,1)S(1)}, u32[]{:S(2)}, u32[]{:S(2)}) collective-permute-start(bf16[96,192]{1,0:T(8,128)(2,1)} %get-tuple-element.26), channel_id=1, source_target_pairs={{4,0},{8,4},{12,8},{16,12},{20,16},{24,20},{28,24},{0,28},{5,1},{9... | collective-permute-start | bytes 110600 | tf_op jit(solution)/shard_map/ppermute | solution.py:451
  12.4 1.5 %collective-permute-start.1 = (bf16[96,192]{1,0:T(8,128)(2,1)}, bf16[96,192]{1,0:T(8,128)(2,1)S(1)}, u32[]{:S(2)}, u32[]{:S(2)}) collective-permute-start(bf16[96,192]{1,0:T(8,128)(2,1)} %get-tuple-element.27), channel_id=1, source_target_pairs={{2,0},{0,2},{3,1},{1,3},{6,4},{4,6},{7,5},{5,7},{10,8},{8,10},{11,... | collective-permute-start | bytes 110600 | tf_op jit(solution)/shard_map/ppermute | solution.py:451
  13.9 0.5 collective-permute-start.2
  14.4 0.9 %shard_map.194 = (f32[864,144]{1,0:T(8,128)S(1)}, f32[8,128]{1,0:T(8,128)S(1)}) custom-call(f32[12,1,3312]{2,1,0:T(1,128)S(1)} %bitcast.8), custom_call_target="tpu_custom_call" | custom-call | flops 1000000 | bytes 1000000 | tf_op jit(solution)/shard_map/pallas_call | solution.py:424
  15.3 0.5 slice.25
  15.8 0.9 %collective-permute-done.1.refs_2_ = bf16[96,192]{1,0:T(8,128)(2,1)S(1)} collective-permute-done((bf16[96,192]{1,0:T(8,128)(2,1)}, bf16[96,192]{1,0:T(8,128)(2,1)S(1)}, u32[]{:S(2)}, u32[]{:S(2)}) %collective-permute-start.1) | collective-permute-done | bytes 36896 | tf_op jit(solution)/shard_map/ppermute | solution.py:451
  16.7 2.4 %collective-permute-done.2.refs_3_ = bf16[96,192]{1,0:T(8,128)(2,1)S(1)} collective-permute-done((bf16[96,192]{1,0:T(8,128)(2,1)}, bf16[96,192]{1,0:T(8,128)(2,1)S(1)}, u32[]{:S(2)}, u32[]{:S(2)}) %collective-permute-start.2) | collective-permute-done | bytes 36896 | tf_op jit(solution)/shard_map/ppermute | solution.py:451
  19.1 0.6 maximum_add_fusion
  19.8 0.5 collective-permute-start.3
  20.3 0.8 %collective-permute-done.3.refs_4_ = bf16[48,192]{1,0:T(8,128)(2,1)S(1)} collective-permute-done((bf16[48,192]{1,0:T(8,128)(2,1)S(1)}, bf16[48,192]{1,0:T(8,128)(2,1)S(1)}, u32[]{:S(2)}, u32[]{:S(2)}) %collective-permute-start.3) | collective-permute-done | bytes 18464 | tf_op jit(solution)/shard_map/ppermute | solution.py:451
  21.3 4.1 %shard_map.195 = (bf16[32,192]{1,0:T(8,128)(2,1)S(1)}, bf16[32,192]{1,0:T(8,128)(2,1)S(1)}, bf16[64,192]{1,0:T(8,128)(2,1)S(1)}, bf16[64,192]{1,0:T(8,128)(2,1)S(1)}, bf16[64,192]{1,0:T(8,128)(2,1)S(1)}) custom-call(bf16[48,192]{1,0:T(8,128)(2,1)S(1)} %copy-done.16, bf16[96,192]{1,0:T(8,128)(2,1)S(1)} %collective-permute-done.refs_1_, ...), custom_call_target="tpu_custom_call" | custom-call | flops 1000000 | bytes 1000000 | tf_op jit(solution)/shard_map/pallas_call | solution.py:424
  25.5 0.6 collective-permute-start.6
  26.1 0.7 %collective-permute-start.7 = (bf16[64,192]{1,0:T(8,128)(2,1)S(1)}, bf16[64,192]{1,0:T(8,128)(2,1)S(1)}, u32[]{:S(2)}, u32[]{:S(2)}) collective-permute-start(bf16[64,192]{1,0:T(8,128)(2,1)S(1)} %get-tuple-element.35), channel_id=1, source_target_pairs={{30,0},{28,2},{2,4},{0,6},{6,8},{4,10},{10,12},{8,14},{14,16},{12,... | collective-permute-start | bytes 73736 | tf_op jit(solution)/shard_map/ppermute | solution.py:451
  26.8 5.3 %collective-permute-done.5.refs_1_ = bf16[64,192]{1,0:T(8,128)(2,1)S(1)} collective-permute-done((bf16[64,192]{1,0:T(8,128)(2,1)S(1)}, bf16[64,192]{1,0:T(8,128)(2,1)S(1)}, u32[]{:S(2)}, u32[]{:S(2)}) %collective-permute-start.5) | collective-permute-done | bytes 24608 | tf_op jit(solution)/shard_map/ppermute | solution.py:451
  32.1 1.5 %collective-permute-done.7.refs_3_ = bf16[64,192]{1,0:T(8,128)(2,1)S(1)} collective-permute-done((bf16[64,192]{1,0:T(8,128)(2,1)S(1)}, bf16[64,192]{1,0:T(8,128)(2,1)S(1)}, u32[]{:S(2)}, u32[]{:S(2)}) %collective-permute-start.7) | collective-permute-done | bytes 24608 | tf_op jit(solution)/shard_map/ppermute | solution.py:451
  33.6 0.1 collective-permute-start.9
  33.7 0.5 collective-permute-start.8
  34.2 0.8 %collective-permute-done.8.refs_4_ = bf16[32,192]{1,0:T(8,128)(2,1)S(1)} collective-permute-done((bf16[32,192]{1,0:T(8,128)(2,1)S(1)}, bf16[32,192]{1,0:T(8,128)(2,1)S(1)}, u32[]{:S(2)}, u32[]{:S(2)}) %collective-permute-start.8) | collective-permute-done | bytes 12320 | tf_op jit(solution)/shard_map/ppermute | solution.py:451
  35.1 2.6 %shard_map.196 = (bf16[2,6,12,192]{3,2,1,0:T(8,128)(2,1)S(1)}, bf16[336,128]{1,0:T(8,128)(2,1)S(1)}) custom-call(bf16[32,192]{1,0:T(8,128)(2,1)S(1)} %get-tuple-element.32.refs_0_, bf16[64,192]{1,0:T(8,128)(2,1)S(1)} %collective-permute-done.5.refs_1_, bf16[64,192]{1,0:T(8,128)(2,1)S(1)} %collective-permute-done.6.refs_2_, ...), custom_call_target="tpu_custom_call" | custom-call | flops 1000000 | bytes 1000000 | tf_op jit(solution)/shard_map/pallas_call | solution.py:424
  37.7 2.3 %collective-permute-start.10 = (bf16[336,128]{1,0:T(8,128)(2,1)S(1)}, bf16[336,128]{1,0:T(8,128)(2,1)S(1)}, u32[]{:S(2)}, u32[]{:S(2)}) collective-permute-start(bf16[336,128]{1,0:T(8,128)(2,1)S(1)} %get-tuple-element.44), channel_id=1, source_target_pairs={{0,1},{2,3},{4,5},{6,7},{8,9},{10,11},{12,13},{14,15},{16,17},{18,... | collective-permute-start | bytes 258056 | tf_op jit(solution)/shard_map/ppermute | solution.py:475
  39.9 0.9 %collective-permute-done.10 = bf16[336,128]{1,0:T(8,128)(2,1)S(1)} collective-permute-done((bf16[336,128]{1,0:T(8,128)(2,1)S(1)}, bf16[336,128]{1,0:T(8,128)(2,1)S(1)}, u32[]{:S(2)}, u32[]{:S(2)}) %collective-permute-start.10) | collective-permute-done | bytes 86048 | tf_op jit(solution)/shard_map/ppermute | solution.py:475
  40.9 0.7 collective-permute-start.13
  41.6 0.7 collective-permute-start.12
  42.2 0.7 collective-permute-start.11
  43.0 0.7 collective-permute-start.16
  43.7 0.7 collective-permute-start.15
  44.3 0.7 collective-permute-start.14
  45.1 1.3 %collective-permute-start.17 = (bf16[336,128]{1,0:T(8,128)(2,1)S(1)}, bf16[336,128]{1,0:T(8,128)(2,1)S(1)}, u32[]{:S(2)}, u32[]{:S(2)}) collective-permute-start(bf16[336,128]{1,0:T(8,128)(2,1)S(1)} %add_convert_fusion.own), channel_id=1, source_target_pairs={{1,0},{3,2},{5,4},{7,6},{9,8},{11,10},{13,12},{15,14},{17,16},{19,... | collective-permute-start | bytes 258056 | tf_op jit(solution)/shard_map/ppermute | solution.py:499
  46.4 0.7 %copy.21 = bf16[2,6,12,192]{3,0,2,1:T(2,128)(2,1)} copy(bf16[2,6,12,192]{3,2,1,0:T(8,128)(2,1)S(1)} %get-tuple-element.47) | data formatting | bytes 110592
  47.1 18.9 %collective-permute-done.17.given = bf16[336,128]{1,0:T(8,128)(2,1)S(1)} collective-permute-done((bf16[336,128]{1,0:T(8,128)(2,1)S(1)}, bf16[336,128]{1,0:T(8,128)(2,1)S(1)}, u32[]{:S(2)}, u32[]{:S(2)}) %collective-permute-start.17) | collective-permute-done | bytes 86048 | tf_op jit(solution)/shard_map/ppermute | solution.py:499
  66.0 0.8 %shard_map.197 = (f32[160,192]{1,0:T(8,128)}, f32[64,192]{1,0:T(8,128)}) custom-call(bf16[336,128]{1,0:T(8,128)(2,1)S(1)} %add_convert_fusion.own, bf16[336,128]{1,0:T(8,128)(2,1)S(1)} %collective-permute-done.17.given), custom_call_target="tpu_custom_call" | custom-call | flops 1000000 | bytes 1000000 | tf_op jit(solution)/shard_map/pallas_call | solution.py:424
  (59 shorter events, 0.4 us)
Async XLA Ops:
  0.6 13.7 %copy-start.4 = (f32[2,1,1,6,3312]{4,2,3,1,0:T(1,128)S(1)}, f32[2,1,1,6,3312]{4,2,3,1,0:T(1,128)}, u32[]{:S(2)}) copy-start(f32[2,1,1,6,3312]{4,2,3,1,0:T(1,128)} %param.27) | copy-start | bytes 476932
  0.6 20.5 %copy-start = (bf16[2,192,768]{2,1,0:T(8,128)(2,1)S(1)}, bf16[2,192,768]{2,1,0:T(8,128)(2,1)}, u32[]{:S(2)}) copy-start(bf16[2,192,768]{2,1,0:T(8,128)(2,1)} %refs_9_.5) | copy-start | bytes 1769476
  0.7 20.5 %copy-start.1 = (bf16[2,768,192]{1,2,0:T(8,128)(2,1)S(1)}, bf16[2,768,192]{1,2,0:T(8,128)(2,1)}, u32[]{:S(2)}) copy-start(bf16[2,768,192]{1,2,0:T(8,128)(2,1)} %param.26) | copy-start | bytes 1769476
  0.7 20.5 %copy-start.2 = (bf16[2,192,576]{2,1,0:T(8,128)(2,1)S(1)}, bf16[2,192,576]{2,1,0:T(8,128)(2,1)}, u32[]{:S(2)}) copy-start(bf16[2,192,576]{2,1,0:T(8,128)(2,1)} %refs_7_.5) | copy-start | bytes 1327108
  0.7 20.5 %copy-start.10 = (bf16[256,144]{1,0:T(8,128)(2,1)S(1)}, bf16[256,144]{1,0:T(8,128)(2,1)}, u32[]{:S(2)}) copy-start(bf16[256,144]{1,0:T(8,128)(2,1)} %constant.18.clone.refs_13_) | copy-start | bytes 221188
  6.3 9.5 %collective-permute-start = (bf16[96,192]{1,0:T(8,128)(2,1)}, bf16[96,192]{1,0:T(8,128)(2,1)S(1)}, u32[]{:S(2)}, u32[]{:S(2)}) collective-permute-start(bf16[96,192]{1,0:T(8,128)(2,1)} %get-tuple-element.26), channel_id=1, source_target_pairs={{4,0},{8,4},{12,8},{16,12},{20,16},{24,20},{28,24},{0,28},{5,1},{9... | collective-permute-start | bytes 110600 | tf_op jit(solution)/shard_map/ppermute | solution.py:451
  12.4 4.3 %collective-permute-start.1 = (bf16[96,192]{1,0:T(8,128)(2,1)}, bf16[96,192]{1,0:T(8,128)(2,1)S(1)}, u32[]{:S(2)}, u32[]{:S(2)}) collective-permute-start(bf16[96,192]{1,0:T(8,128)(2,1)} %get-tuple-element.27), channel_id=1, source_target_pairs={{2,0},{0,2},{3,1},{1,3},{6,4},{4,6},{7,5},{5,7},{10,8},{8,10},{11,... | collective-permute-start | bytes 110600 | tf_op jit(solution)/shard_map/ppermute | solution.py:451
  13.9 7.3 %copy-start.6 = (bf16[288,384]{1,0:T(8,128)(2,1)S(1)}, bf16[288,384]{1,0:T(8,128)(2,1)}, u32[]{:S(2)}) copy-start(bf16[288,384]{1,0:T(8,128)(2,1)} %constant.17.clone.refs_12_) | copy-start | bytes 663556
  13.9 5.2 %collective-permute-start.2 = (bf16[96,192]{1,0:T(8,128)(2,1)}, bf16[96,192]{1,0:T(8,128)(2,1)S(1)}, u32[]{:S(2)}, u32[]{:S(2)}) collective-permute-start(bf16[96,192]{1,0:T(8,128)(2,1)} %get-tuple-element.28), channel_id=1, source_target_pairs={{6,0},{4,2},{10,4},{8,6},{14,8},{12,10},{18,12},{16,14},{22,16},{2... | collective-permute-start | bytes 110600 | tf_op jit(solution)/shard_map/ppermute | solution.py:451
  19.7 1.4 %collective-permute-start.4 = (bf16[144,192]{1,0:T(8,128)(2,1)S(1)}, bf16[144,192]{1,0:T(8,128)(2,1)S(1)}, u32[]{:S(2)}, u32[]{:S(2)}) collective-permute-start(bf16[144,192]{1,0:T(8,128)(2,1)S(1)} %maximum_add_fusion), channel_id=1, source_target_pairs={{1,0},{0,1},{3,2},{2,3},{5,4},{4,5},{7,6},{6,7},{9,8},{8,9},{11,10... | collective-permute-start | bytes 165896 | tf_op jit(solution)/shard_map/ppermute | solution.py:451
  19.8 1.3 %collective-permute-start.3 = (bf16[48,192]{1,0:T(8,128)(2,1)S(1)}, bf16[48,192]{1,0:T(8,128)(2,1)S(1)}, u32[]{:S(2)}, u32[]{:S(2)}) collective-permute-start(bf16[48,192]{1,0:T(8,128)(2,1)S(1)} %copy-done.17), channel_id=1, source_target_pairs={{1,0},{0,1},{3,2},{2,3},{5,4},{4,5},{7,6},{6,7},{9,8},{8,9},{11,10... | collective-permute-start | bytes 55304 | tf_op jit(solution)/shard_map/ppermute | solution.py:451
  21.2 13.8 %copy-start.5 = (bf16[864,144]{1,0:T(8,128)(2,1)S(1)}, bf16[864,144]{1,0:T(8,128)(2,1)}, u32[]{:S(2)}) copy-start(bf16[864,144]{1,0:T(8,128)(2,1)} %get-tuple-element.40.refs_14_) | copy-start | bytes 746500
  21.2 13.8 %copy-start.7 = (bf16[3,144,192]{2,1,0:T(8,128)(2,1)S(1)}, bf16[3,144,192]{2,1,0:T(8,128)(2,1)}, u32[]{:S(2)}) copy-start(bf16[3,144,192]{2,1,0:T(8,128)(2,1)} %get-tuple-element.39.refs_13_) | copy-start | bytes 497668
  21.2 13.8 %copy-start.8 = (bf16[144,768]{1,0:T(8,128)(2,1)S(1)}, bf16[144,768]{1,0:T(8,128)(2,1)}, u32[]{:S(2)}) copy-start(bf16[144,768]{1,0:T(8,128)(2,1)} %get-tuple-element.42.refs_16_) | copy-start | bytes 663556
  21.2 13.8 %copy-start.11 = (bf16[192,144]{1,0:T(8,128)(2,1)S(1)}, bf16[192,144]{1,0:T(8,128)(2,1)}, u32[]{:S(2)}) copy-start(bf16[192,144]{1,0:T(8,128)(2,1)} %constant.20.clone.refs_18_) | copy-start | bytes 165892
  21.3 13.8 %copy-start.12 = (bf16[144,256]{1,0:T(8,128)(2,1)S(1)}, bf16[144,256]{1,0:T(8,128)(2,1)}, u32[]{:S(2)}) copy-start(bf16[144,256]{1,0:T(8,128)(2,1)} %constant.19.clone.refs_17_) | copy-start | bytes 221188
  21.3 13.8 %copy-start.13 = (bf16[144,256]{1,0:T(8,128)(2,1)S(1)}, bf16[144,256]{1,0:T(8,128)(2,1)}, u32[]{:S(2)}) copy-start(bf16[144,256]{1,0:T(8,128)(2,1)} %get-tuple-element.37.refs_11_) | copy-start | bytes 221188
  21.3 13.8 %copy-start.14 = (bf16[144,192]{1,0:T(8,128)(2,1)S(1)}, bf16[144,192]{1,0:T(8,128)(2,1)}, u32[]{:S(2)}) copy-start(bf16[144,192]{1,0:T(8,128)(2,1)} %get-tuple-element.38.refs_12_) | copy-start | bytes 165892
  25.4 9.7 %copy-start.9 = (f32[144,192]{1,0:T(8,128)S(1)}, f32[144,192]{1,0:T(8,128)}, u32[]{:S(2)}) copy-start(f32[144,192]{1,0:T(8,128)} %get-tuple-element.41.refs_15_) | copy-start | bytes 331780
  25.4 6.7 %collective-permute-start.5 = (bf16[64,192]{1,0:T(8,128)(2,1)S(1)}, bf16[64,192]{1,0:T(8,128)(2,1)S(1)}, u32[]{:S(2)}, u32[]{:S(2)}) collective-permute-start(bf16[64,192]{1,0:T(8,128)(2,1)S(1)} %get-tuple-element.33), channel_id=1, source_target_pairs={{28,0},{0,4},{4,8},{8,12},{12,16},{16,20},{20,24},{24,28},{29,1},{... | collective-permute-start | bytes 73736 | tf_op jit(solution)/shard_map/ppermute | solution.py:451
  25.5 6.6 %collective-permute-start.6 = (bf16[64,192]{1,0:T(8,128)(2,1)S(1)}, bf16[64,192]{1,0:T(8,128)(2,1)S(1)}, u32[]{:S(2)}, u32[]{:S(2)}) collective-permute-start(bf16[64,192]{1,0:T(8,128)(2,1)S(1)} %get-tuple-element.34), channel_id=1, source_target_pairs={{2,0},{0,2},{3,1},{1,3},{6,4},{4,6},{7,5},{5,7},{10,8},{8,10},{11,... | collective-permute-start | bytes 73736 | tf_op jit(solution)/shard_map/ppermute | solution.py:451
  26.1 7.5 %collective-permute-start.7 = (bf16[64,192]{1,0:T(8,128)(2,1)S(1)}, bf16[64,192]{1,0:T(8,128)(2,1)S(1)}, u32[]{:S(2)}, u32[]{:S(2)}) collective-permute-start(bf16[64,192]{1,0:T(8,128)(2,1)S(1)} %get-tuple-element.35), channel_id=1, source_target_pairs={{30,0},{28,2},{2,4},{0,6},{6,8},{4,10},{10,12},{8,14},{14,16},{12,... | collective-permute-start | bytes 73736 | tf_op jit(solution)/shard_map/ppermute | solution.py:451
  33.6 1.4 %collective-permute-start.9 = (bf16[96,192]{1,0:T(8,128)(2,1)S(1)}, bf16[96,192]{1,0:T(8,128)(2,1)S(1)}, u32[]{:S(2)}, u32[]{:S(2)}) collective-permute-start(bf16[96,192]{1,0:T(8,128)(2,1)S(1)} %pad_maximum_fusion), channel_id=1, source_target_pairs={{1,0},{0,1},{3,2},{2,3},{5,4},{4,5},{7,6},{6,7},{9,8},{8,9},{11,10... | collective-permute-start | bytes 110600 | tf_op jit(solution)/shard_map/ppermute | solution.py:451
  33.7 1.3 %collective-permute-start.8 = (bf16[32,192]{1,0:T(8,128)(2,1)S(1)}, bf16[32,192]{1,0:T(8,128)(2,1)S(1)}, u32[]{:S(2)}, u32[]{:S(2)}) collective-permute-start(bf16[32,192]{1,0:T(8,128)(2,1)S(1)} %get-tuple-element.36), channel_id=1, source_target_pairs={{1,0},{0,1},{3,2},{2,3},{5,4},{4,5},{7,6},{6,7},{9,8},{8,9},{11,10... | collective-permute-start | bytes 36872 | tf_op jit(solution)/shard_map/ppermute | solution.py:451
  37.7 3.2 %collective-permute-start.10 = (bf16[336,128]{1,0:T(8,128)(2,1)S(1)}, bf16[336,128]{1,0:T(8,128)(2,1)S(1)}, u32[]{:S(2)}, u32[]{:S(2)}) collective-permute-start(bf16[336,128]{1,0:T(8,128)(2,1)S(1)} %get-tuple-element.44), channel_id=1, source_target_pairs={{0,1},{2,3},{4,5},{6,7},{8,9},{10,11},{12,13},{14,15},{16,17},{18,... | collective-permute-start | bytes 258056 | tf_op jit(solution)/shard_map/ppermute | solution.py:475
  40.9 2.0 %collective-permute-start.13 = (bf16[336,128]{1,0:T(8,128)(2,1)S(1)}, bf16[336,128]{1,0:T(8,128)(2,1)S(1)}, u32[]{:S(2)}, u32[]{:S(2)}) collective-permute-start(bf16[336,128]{1,0:T(8,128)(2,1)S(1)} %add_convert_fusion.2), channel_id=1, source_target_pairs={{7,1},{5,3},{3,5},{1,7},{15,9},{13,11},{11,13},{9,15},{23,17},{21,... | collective-permute-start | bytes 258056 | tf_op jit(solution)/shard_map/ppermute | solution.py:475
  41.6 1.4 %collective-permute-start.12 = (bf16[336,128]{1,0:T(8,128)(2,1)S(1)}, bf16[336,128]{1,0:T(8,128)(2,1)S(1)}, u32[]{:S(2)}, u32[]{:S(2)}) collective-permute-start(bf16[336,128]{1,0:T(8,128)(2,1)S(1)} %add_convert_fusion.2), channel_id=1, source_target_pairs={{5,1},{7,3},{1,5},{3,7},{13,9},{15,11},{9,13},{11,15},{21,17},{23,... | collective-permute-start | bytes 258056 | tf_op jit(solution)/shard_map/ppermute | solution.py:475
  42.2 0.7 %collective-permute-start.11 = (bf16[336,128]{1,0:T(8,128)(2,1)S(1)}, bf16[336,128]{1,0:T(8,128)(2,1)S(1)}, u32[]{:S(2)}, u32[]{:S(2)}) collective-permute-start(bf16[336,128]{1,0:T(8,128)(2,1)S(1)} %add_convert_fusion.2), channel_id=1, source_target_pairs={{3,1},{1,3},{7,5},{5,7},{11,9},{9,11},{15,13},{13,15},{19,17},{17,... | collective-permute-start | bytes 258056 | tf_op jit(solution)/shard_map/ppermute | solution.py:475
  43.0 2.0 %collective-permute-start.16 = (bf16[336,128]{1,0:T(8,128)(2,1)S(1)}, bf16[336,128]{1,0:T(8,128)(2,1)S(1)}, u32[]{:S(2)}, u32[]{:S(2)}) collective-permute-start(bf16[336,128]{1,0:T(8,128)(2,1)S(1)} %add_convert_fusion.1), channel_id=1, source_target_pairs={{25,1},{27,3},{29,5},{31,7},{17,9},{19,11},{21,13},{23,15},{9,17},... | collective-permute-start | bytes 258056 | tf_op jit(solution)/shard_map/ppermute | solution.py:475
  43.7 1.4 %collective-permute-start.15 = (bf16[336,128]{1,0:T(8,128)(2,1)S(1)}, bf16[336,128]{1,0:T(8,128)(2,1)S(1)}, u32[]{:S(2)}, u32[]{:S(2)}) collective-permute-start(bf16[336,128]{1,0:T(8,128)(2,1)S(1)} %add_convert_fusion.1), channel_id=1, source_target_pairs={{17,1},{19,3},{21,5},{23,7},{25,9},{27,11},{29,13},{31,15},{1,17},... | collective-permute-start | bytes 258056 | tf_op jit(solution)/shard_map/ppermute | solution.py:475
  44.3 0.7 %collective-permute-start.14 = (bf16[336,128]{1,0:T(8,128)(2,1)S(1)}, bf16[336,128]{1,0:T(8,128)(2,1)S(1)}, u32[]{:S(2)}, u32[]{:S(2)}) collective-permute-start(bf16[336,128]{1,0:T(8,128)(2,1)S(1)} %add_convert_fusion.1), channel_id=1, source_target_pairs={{9,1},{11,3},{13,5},{15,7},{1,9},{3,11},{5,13},{7,15},{25,17},{27,... | collective-permute-start | bytes 258056 | tf_op jit(solution)/shard_map/ppermute | solution.py:475
  45.1 20.9 %collective-permute-start.17 = (bf16[336,128]{1,0:T(8,128)(2,1)S(1)}, bf16[336,128]{1,0:T(8,128)(2,1)S(1)}, u32[]{:S(2)}, u32[]{:S(2)}) collective-permute-start(bf16[336,128]{1,0:T(8,128)(2,1)S(1)} %add_convert_fusion.own), channel_id=1, source_target_pairs={{1,0},{3,2},{5,4},{7,6},{9,8},{11,10},{13,12},{15,14},{17,16},{19,... | collective-permute-start | bytes 258056 | tf_op jit(solution)/shard_map/ppermute | solution.py:499
  (4 other events, 11.6 us)

commit v7 on v6

--- a/solution.py
+++ b/solution.py
@@ -53,8 +53,7 @@
     move = np.zeros((8 * pitch, CELLS), np.float32)
     for z, a, o in cells():
         part, place = octant_of(z, a, o)
-        part = 7 - part if flip else part
-        move[(part % 4 * 2 + part // 4) * pitch + first + place, source(z, a, o)] = 1
+        move[(7 - part if flip else part) * pitch + first + place, source(z, a, o)] = 1
     return as_half(move)
 
 
@@ -63,7 +62,8 @@
     for z, a, o in cells():
         part, place = octant_of(z, a, o)
         part = 7 - part if flip else part
-        move[inner_row(z, a, o), part * pitch + first + place] = 1
+        block = (part % 4) * 2 + part // 4
+        move[inner_row(z, a, o), block * pitch + first + place] = 1
     return as_half(move)
 
 
@@ -282,7 +282,7 @@
     )
     count = len(names)
     source, refs = refs[:count], refs[count:]
-    results = ("patch", "x", "qkv", "prob", "resid", "slope", "keep", "give", "one", "two", "three")
+    results = ("patch", "x", "qkv", "prob", "resid", "slope", "send", "keep0", "keep1", "keep2", "keep3")
     target, refs = refs[: len(results)], refs[len(results) :]
     local, refs = refs[:count], refs[count:]
     patch_s, x_s, qkv_s, prob, resid_s, slope_s, blocks = refs[:7]
@@ -351,32 +351,25 @@
     active = (upward * below).astype(HALF)
     result = (resid + dot_nt(active, have["wdown"][...])).astype(HALF)
     blocks[...] = (dot(have["out_first"][...], result) + ready).astype(HALF)
-    for name, first, count in (("give", 48, 48), ("one", 96, 96), ("two", 192, 96), ("three", 288, 96), ("keep", 0, 48)):
-        send(name, blocks.at[pl.ds(first, count)])
+    send("send", blocks.at[pl.ds(192, 192)])
+    for n in range(4):
+        send("keep" + str(n), blocks.at[pl.ds(n * 48, 48)])
     for copy in sent:
         copy.wait()
 
 
-def bias_kernel(tbl, bias, done, table, xs, cols):
-    done[...] = jnp.zeros_like(done)
+def second_bias(tbl, after, bias, table, xs, cols):
     fill_columns(cols)
     table_rows(tbl, 1, table)
     build_bias(table, cols, xs, bias, (flag("section"), flag("lat")))
 
 
-def stacked(parts, stack):
-    keep, one, two, three, own, others = parts
-    pitch = keep.shape[0]
-    for n, part in enumerate((keep, one, two, three, own)):
-        stack[n * pitch : (n + 1) * pitch, :] = part[0:pitch, :]
-    stack[5 * pitch :, :] = others[...]
-
-
 def second_kernel(*refs):
-    parts, rest = refs[:6], refs[6:]
-    gains, wqkv, wproj, wup, wdown, bias, into, out_of = rest[:8]
-    keep, give, one, two, three, stack, prob = rest[8:]
-    stacked(parts, stack)
+    parts, rest = refs[:4], refs[4:]
+    gains, wqkv, wproj, wup, wdown, bias, into, out_of, send_o = rest[:9]
+    keep, stack, prob = rest[9:13], rest[13], rest[14]
+    for n in range(4):
+        stack[n * 96 : n * 96 + 96, :] = parts[n][...]
     both = dot(into[...], stack[...])
     x, dflat = both[:CELLS], both[CELLS:].astype(HALF)
     gains, wqkv, wproj, wup, wdown = (w.at[1] for w in (gains, wqkv, wproj, wup, wdown))
@@ -387,17 +380,17 @@
     slope = gelu_parts(upward)[1]
     dx = backward(dflat, x, qkv, prob, resid, slope, gains, wqkv, wproj, wup, wdown)
     moved = dot(out_of[...], dx.astype(HALF)).astype(HALF)
-    keep[...] = moved[:32]
-    give[...] = moved[32:64]
-    for n, block in enumerate((one, two, three)):
-        block[...] = moved[n * 64 + 64 : n * 64 + 128]
+    send_o[...] = moved[128:]
+    for n in range(4):
+        keep[n][...] = moved[n * 32 : n * 32 + 32]
 
 
 def third_kernel(*refs):
-    parts, rest = refs[:6], refs[6:]
+    parts, rest = refs[:4], refs[4:]
     gains, wqkv, wproj, wup, wdown, patch, x_i, qkv_i, prob, resid, slope, into, out_of = rest[:13]
-    grad_o, terms_o, stack = rest[13:]
-    stacked(parts, stack)
+    grad_o, mine_o, other_o, stack, terms = rest[13:]
+    for n in range(4):
+        stack[n * 64 : n * 64 + 64, :] = parts[n][...]
     dflat = dot(into[...], stack[...]).astype(HALF)
     qkv = tuple(qkv_i[n] for n in range(3))
     gains, wqkv, wproj, wup, wdown = (w.at[0] for w in (gains, wqkv, wproj, wup, wdown))
@@ -406,21 +399,23 @@
         gains, wqkv, wproj, wup, wdown,
     )
     grad = dx.astype(HALF)
-    total = dot_tn(patch[...], grad)
-    terms_o[0:224, :] = total[:224, :128].astype(HALF)
-    last = jnp.concatenate((total[:112, 128:], total[112:224, 128:]), 1)
-    terms_o[224:336, :] = last.astype(HALF)
     moved = dot(out_of[...], grad).astype(HALF)
     for z in range(2):
         for a in range(6):
             grad_o[z, a] = moved[(z * 6 + a) * 16 : (z * 6 + a) * 16 + 12]
+    total = dot_tn(patch[...], grad)
+    terms[0:224, :] = total[:224, :128]
+    terms[224:336, :] = jnp.concatenate((total[:112, 128:], total[112:224, 128:]), 1)
+    place = lax.axis_index("section") % 2
+    mine_o[...] = terms[pl.ds(pl.multiple_of(place * 168, 8), 168), :].astype(HALF)
+    other_o[...] = terms[pl.ds(pl.multiple_of(168 - place * 168, 8), 168), :].astype(HALF)
 
 
 vmem = pl.BlockSpec(memory_space=pltpu.VMEM)
 hbm = pl.BlockSpec(memory_space=pltpu.HBM)
 
 
-def call(kernel, outs, scratch, *args, spec=vmem, out=vmem, room=30):
+def call(kernel, outs, scratch, *args, spec=vmem, out=vmem, room=30, size=1):
     return pl.pallas_call(
         kernel,
         out_shape=outs,
@@ -428,7 +423,7 @@
         out_specs=jax.tree.map(lambda _: out, outs),
         scratch_shapes=scratch,
         compiler_params=pltpu.CompilerParams(vmem_limit_bytes=room * 2**20),
-        cost_estimate=pl.CostEstimate(flops=1000000, bytes_accessed=1000000, transcendentals=0),
+        cost_estimate=pl.CostEstimate(flops=1000000, bytes_accessed=size * 1000000, transcendentals=0),
     )(*args)
 
 
@@ -451,32 +446,30 @@
     return lax.ppermute(block, tuple(axes), pairs)
 
 
-def exchange(keep, give, others, way, wait=None):
-    own = fetch(give, {"section": way})
-    moved = [
-        fetch(b, {"lat": way * (n // 2), "lon": way * (n % 2)}) for n, b in enumerate(others, 1)
-    ]
-    second = jnp.concatenate([block[keep.shape[0] :] for block in moved], 0)
-    if wait is not None:
-        second = second + wait[0, 0].astype(HALF)
-    return (keep, *moved, own, fetch(second, {"section": way}))
+def exchange(keep, got, way):
+    pitch = got.shape[0] // 4
+    blocks = []
+    for n in range(4):
+        block = jnp.concatenate((keep[n], got[n * pitch : (n + 1) * pitch]), 0)
+        blocks.append(fetch(block, {"lat": way * (n // 2), "lon": way * (n % 2)}))
+    return blocks
 
 
 def swap(block, flips):
-    axes = ("lon", "lat", "section")
+    names = ("lon", "lat", "section")
+    axes = [name for name in names if flips.get(name, 0)]
     sizes = [lax.axis_size(name) for name in axes]
     pairs = []
     for place in np.ndindex(*sizes):
-        source = [p ^ flips.get(name, 0) for p, name in zip(place, axes)]
-        if place[2] % 2:
-            pairs.append(
-                (int(np.ravel_multi_index(source, sizes)), int(np.ravel_multi_index(place, sizes)))
-            )
-    return lax.ppermute(block, axes, pairs)
-
-
-def add_up(terms):
-    total = (terms.astype(FULL) + swap(terms, {"section": 1}).astype(FULL)).astype(HALF)
+        source = [p ^ flips[name] for p, name in zip(place, axes)]
+        pairs.append(
+            (int(np.ravel_multi_index(source, sizes)), int(np.ravel_multi_index(place, sizes)))
+        )
+    return lax.ppermute(block, tuple(axes), pairs)
+
+
+def add_up(mine, other):
+    total = (mine.astype(FULL) + swap(other, {"section": 1}).astype(FULL)).astype(HALF)
     bits = []
     for name in ("section", "lat", "lon"):
         size = lax.axis_size(name)
@@ -495,16 +488,17 @@
             near, far, last = (swap(total, step).astype(FULL) for step in (one, two, three))
             total = (total.astype(FULL) + near) + (far + last)
         total = total.astype(HALF)
-    sections = range(0, lax.axis_size("section"), 2)
-    return total, lax.ppermute(total, "section", [(i + 1, i) for i in sections])
-
-
-def last_kernel(scale, own, given, upper_o, surface_o, both, sems):
-    odd = lax.axis_index("section") % 2 == 1
-    total = jnp.where(odd, own[...].astype(FULL), given[...].astype(FULL)) * scale
-    both[:, 0:128] = total[:224]
-    both[0:112, 128:192] = total[224:, :64]
-    both[112:224, 128:192] = total[224:, 64:]
+    return total, swap(total, {"section": 1})
+
+
+def last_kernel(scale, mine, other, upper_o, surface_o, halves, both, sems):
+    place = lax.axis_index("section") % 2
+    halves[pl.ds(pl.multiple_of(place * 168, 8), 168), :] = mine[...].astype(FULL) * scale
+    halves[pl.ds(pl.multiple_of(168 - place * 168, 8), 168), :] = other[...].astype(FULL) * scale
+    both[:, 0:128] = halves[0:224, :]
+    last = halves[224:336, :]
+    both[0:112, 128:192] = last[:, :64]
+    both[112:224, 128:192] = last[:, 64:]
     copies = [
         pltpu.make_async_copy(both.at[pl.ds(0, 160)], upper_o, sems.at[0]),
         pltpu.make_async_copy(both.at[pl.ds(160, 64)], surface_o, sems.at[1]),
@@ -533,6 +527,7 @@
     positions = earth_bias.shape[-1]
     table = earth_bias.transpose(0, 1, 3, 2, 4).reshape(2 * HEADS, 1, positions)
     weights = (norm_gains, qkv_weight, proj_weight, up_weight, down_weight.transpose(0, 2, 1))
+
     def from_cot(z, a, o):
         return (a * 12 + o) * 2 + z
 
@@ -557,9 +552,9 @@
         shape((CELLS, WIDTH), FULL),
         shape((CELLS, 4 * WIDTH)),
     ]
-    patch, x, qkv, prob, resid, slope, keep, give, *others = call(
+    patch, x, qkv, prob, resid, slope, send, *keep = call(
         first_kernel,
-        held + [shape((48, WIDTH))] * 2 + [shape((96, WIDTH))] * 3,
+        held + [shape((192, WIDTH))] + [shape((48, WIDTH))] * 4,
         local
         + [pltpu.VMEM(v.shape, v.dtype) for v in held]
         + [
@@ -581,25 +576,22 @@
         out=hbm,
         room=60,
     )
-    bias, done = call(
-        bias_kernel,
-        [shape((HEADS * CELLS, CELLS), FULL), shape((8, 128), FULL)],
-        [*scratch_bias, scratch_cols],
-        table,
-    )
+    bias_shape = shape((HEADS * CELLS, CELLS), FULL)
+    got = fetch(send, {"section": 1})
+    bias = call(second_bias, bias_shape, [*scratch_bias, scratch_cols], table, got)
     into = np.concatenate((octants_in(48, 0, False), octants_in(48, 18, False)), 0)
-    keep, give, *others = call(
+    send, *keep = call(
         second_kernel,
-        [shape((32, WIDTH))] * 2 + [shape((64, WIDTH))] * 3,
-        [pltpu.VMEM((384, WIDTH), HALF), pltpu.VMEM((HEADS * CELLS, CELLS), HALF)],
-        *exchange(keep, give, others, 1, done), *weights, bias,
+        [shape((128, WIDTH))] + [shape((32, WIDTH))] * 4,
+        [pltpu.VMEM((8 * 48, WIDTH), HALF), pltpu.VMEM((HEADS * CELLS, CELLS), HALF)],
+        *exchange(keep, got, 1), *weights, bias,
         jnp.asarray(into), jnp.asarray(octants_out(32, 0, False, inner_row)),
     )
-    latent_grad, terms = call(
+    latent_grad, mine, other = call(
         third_kernel,
-        [shape((2, 6, 12, WIDTH)), shape((336, 128))],
-        [pltpu.VMEM((256, WIDTH), HALF)],
-        *exchange(keep, give, others, -1), *weights, patch, x, qkv, prob, resid, slope,
+        [shape((2, 6, 12, WIDTH)), shape((168, 128)), shape((168, 128))],
+        [pltpu.VMEM((8 * 32, WIDTH), HALF), pltpu.VMEM((336, 128), FULL)],
+        *exchange(keep, fetch(send, {"section": -1}), -1), *weights, patch, x, qkv, prob, resid, slope,
         jnp.asarray(octants_in(32, 0, True)), jnp.asarray(inner_to_padded()),
     )
     scale = float(levels * sections * rows * bands * columns * lax.axis_size("lon")) ** (-0.5)
@@ -607,10 +599,11 @@
         functools.partial(last_kernel, scale),
         [shape((160, WIDTH), FULL), shape((64, WIDTH), FULL)],
         [
+            pltpu.VMEM((336, 128), FULL),
             pltpu.VMEM((224, WIDTH), FULL),
             pltpu.SemaphoreType.DMA((2,)),
         ],
-        *add_up(terms),
+        *add_up(mine, other),
         out=hbm,
     )
     return (latent_grad, upper_grad, surface_grad)

time: 67.1 us -> 56.4 us (0.84)
  waiting for transfers between devices: 31.5 us -> 19.5 us
  other arithmetic: 0.74 us -> 2.42 us
    ppermute x8, waiting for transfers between devices: 19.8 us -> 7.69 us  [swap(): return lax.ppermute(block, tuple(axes), pairs)]
    concatenate x1 -> x8, other arithmetic: 0.01 us -> 2.35 us  [exchange(): block = jnp.concatenate((keep[n], got[n * pitch:(n + 1) * pitch]), 0)]
    ppermute x10 -> x8, starting transfers between devices: 10.5 us -> 10.1 us  [fetch(): return lax.ppermute(block, tuple(axes), pairs)]
    ppermute x10 -> x8, waiting for transfers between devices: 11.7 us -> 11.8 us  [fetch(): return lax.ppermute(block, tuple(axes), pairs)]
  transfers between devices with their start and end apart: 18 -> 16, of which waited for: 8 -> 13; matrix products, arithmetic and copies ran while one was open for 2% -> 5% of each run, Pallas kernels for 1% -> 2%
where the time goes in v7:
time: 56.4 us; the launch traced here: 56.1 us
  waiting for transfers between devices  19.5 us (35%)
  starting transfers between devices  18.3 us (32%)
  Pallas kernels  14.1 us (25%)
  other arithmetic  2.42 us (4%)
  between operations  0.98 us (2%)
  local copies, waits for them, and re-layouts  0.81 us (1%)
    pallas_call x5, Pallas kernels, call(): pl.pallas_call(kernel, out_shape=outs, in_specs=[spec for a in args], out...  14.1 us
    ppermute x8, waiting for transfers between devices, fetch(): return lax.ppermute(block, tuple(axes), pairs)  11.8 us
    ppermute x8, starting transfers between devices, fetch(): return lax.ppermute(block, tuple(axes), pairs)  10.1 us
    ppermute x8, starting transfers between devices, swap(): return lax.ppermute(block, tuple(axes), pairs)  8.14 us
    ppermute x8, waiting for transfers between devices, swap(): return lax.ppermute(block, tuple(axes), pairs)  7.69 us
    concatenate x8, other arithmetic, exchange(): block = jnp.concatenate((keep[n], got[n * pitch:(n + 1) * pitch]), 0)  2.35 us
  transfers between devices with their start and end apart: 16, of which 13 were waited for; matrix products, arithmetic and copies ran while one was open for 5% of the time, Pallas kernels for 2%

profile of v7, /device:TPU:0, one launch (start us, length us, event | category | flops | bytes accessed | tf_op | source)
XLA Modules:
  0.0 56.1 jit_solution(11176187079140989290)
XLA Ops:
  0.7 5.6 %shard_map.193 = (bf16[144,256]{1,0:T(8,128)(2,1)}, bf16[144,192]{1,0:T(8,128)(2,1)}, bf16[3,144,192]{2,1,0:T(8,128)(2,1)}, bf16[864,144]{1,0:T(8,128)(2,1)}, f3...) custom-call(f32[12,1,3312]{2,1,0:T(1,128)} %bitcast.6, ...), custom_call_target="tpu_custom_call" | custom-call | flops 1000000 | bytes 1000000 | tf_op jit(solution)/shard_map/pallas_call | solution.py:419
  6.3 0.5 collective-permute-start
  6.8 1.2 %collective-permute-done.after = bf16[192,192]{1,0:T(8,128)(2,1)S(1)} collective-permute-done((bf16[192,192]{1,0:T(8,128)(2,1)}, bf16[192,192]{1,0:T(8,128)(2,1)S(1)}, u32[]{:S(2)}, u32[]{:S(2)}) %collective-permute-start) | collective-permute-done | bytes 73760 | tf_op jit(solution)/shard_map/ppermute | solution.py:446
  8.0 6.0 %collective-permute-start.1 = (bf16[96,192]{1,0:T(8,128)(2,1)S(1)}, bf16[96,192]{1,0:T(8,128)(2,1)S(1)}, u32[]{:S(2)}, u32[]{:S(2)}) collective-permute-start(bf16[96,192]{1,0:T(8,128)(2,1)S(1)} %pad_maximum_fusion.1), channel_id=1, source_target_pairs={{4,0},{8,4},{12,8},{16,12},{20,16},{24,20},{28,24},{0,28},{5,1},{9... | collective-permute-start | bytes 110600 | tf_op jit(solution)/shard_map/ppermute | solution.py:446
  14.0 0.7 %pad_maximum_fusion.2 = bf16[96,192]{1,0:T(8,128)(2,1)S(1)} fusion(bf16[48,192]{1,0:T(8,128)(2,1)S(1)} %get-tuple-element.49, bf16[48,192]{1,0:T(8,128)(2,1)} %get-tuple-element.27), kind=kLoop, calls=%fused_computation.5 | loop fusion | flops 73728 | bytes 73728 | tf_op jit(solution)/shard_map/concatenate | solution.py:453
  14.7 1.6 %collective-permute-start.2 = (bf16[96,192]{1,0:T(8,128)(2,1)S(1)}, bf16[96,192]{1,0:T(8,128)(2,1)S(1)}, u32[]{:S(2)}, u32[]{:S(2)}) collective-permute-start(bf16[96,192]{1,0:T(8,128)(2,1)S(1)} %pad_maximum_fusion.2), channel_id=1, source_target_pairs={{2,0},{0,2},{3,1},{1,3},{6,4},{4,6},{7,5},{5,7},{10,8},{8,10},{11,... | collective-permute-start | bytes 110600 | tf_op jit(solution)/shard_map/ppermute | solution.py:446
  16.3 0.7 %pad_maximum_fusion.3 = bf16[96,192]{1,0:T(8,128)(2,1)S(1)} fusion(bf16[48,192]{1,0:T(8,128)(2,1)S(1)} %get-tuple-element.48, bf16[48,192]{1,0:T(8,128)(2,1)} %get-tuple-element.28), kind=kLoop, calls=%fused_computation.6 | loop fusion | flops 73728 | bytes 73728 | tf_op jit(solution)/shard_map/concatenate | solution.py:453
  17.0 0.5 collective-permute-start.3
  17.6 0.8 %pad_maximum_fusion.refs_0_ = bf16[96,192]{1,0:T(8,128)(2,1)S(1)} fusion(bf16[48,192]{1,0:T(8,128)(2,1)S(1)} %get-tuple-element.51, bf16[48,192]{1,0:T(8,128)(2,1)} %get-tuple-element.24), kind=kLoop, calls=%fused_computation.3 | loop fusion | flops 73728 | bytes 73728 | tf_op jit(solution)/shard_map/concatenate | solution.py:453
  18.4 0.9 %shard_map.194.refs_9_ = f32[864,144]{1,0:T(8,128)S(1)} custom-call(f32[12,1,3312]{2,1,0:T(1,128)S(1)} %bitcast.7, bf16[192,192]{1,0:T(8,128)(2,1)S(1)} %collective-permute-done.after), custom_call_target="tpu_custom_call" | custom-call | flops 1000000 | bytes 1000000 | tf_op jit(solution)/shard_map/pallas_call | solution.py:419
  19.4 2.7 %collective-permute-done.3.refs_3_ = bf16[96,192]{1,0:T(8,128)(2,1)S(1)} collective-permute-done((bf16[96,192]{1,0:T(8,128)(2,1)S(1)}, bf16[96,192]{1,0:T(8,128)(2,1)S(1)}, u32[]{:S(2)}, u32[]{:S(2)}) %collective-permute-start.3) | collective-permute-done | bytes 36896 | tf_op jit(solution)/shard_map/ppermute | solution.py:446
  22.2 4.1 %shard_map.195 = (bf16[128,192]{1,0:T(8,128)(2,1)S(1)}, bf16[32,192]{1,0:T(8,128)(2,1)S(1)}, bf16[32,192]{1,0:T(8,128)(2,1)S(1)}, bf16[32,192]{1,0:T(8,128)(2,1)S(1)}, bf16[32,192]{1,0:T(8,128)(2,1)S(1)}) custom-call(bf16[96,192]{1,0:T(8,128)(2,1)S(1)} %pad_maximum_fusion.refs_0_, bf16[96,192]{1,0:T(8,128)(2,1)S(1)} %collective-permute-done.1.refs_1_, ...), custom_call_target="tpu_custom_call" | custom-call | flops 1000000 | bytes 1000000 | tf_op jit(solution)/shard_map/pallas_call | solution.py:419
  26.4 1.2 %collective-permute-done.4 = bf16[128,192]{1,0:T(8,128)(2,1)S(1)} collective-permute-done((bf16[128,192]{1,0:T(8,128)(2,1)S(1)}, bf16[128,192]{1,0:T(8,128)(2,1)S(1)}, u32[]{:S(2)}, u32[]{:S(2)}) %collective-permute-start.4) | collective-permute-done | bytes 49184 | tf_op jit(solution)/shard_map/ppermute | solution.py:446
  27.8 0.6 %collective-permute-start.6 = (bf16[64,192]{1,0:T(8,128)(2,1)S(1)}, bf16[64,192]{1,0:T(8,128)(2,1)S(1)}, u32[]{:S(2)}, u32[]{:S(2)}) collective-permute-start(bf16[64,192]{1,0:T(8,128)(2,1)S(1)} %pad_maximum_fusion.6), channel_id=1, source_target_pairs={{2,0},{0,2},{3,1},{1,3},{6,4},{4,6},{7,5},{5,7},{10,8},{8,10},{11,... | collective-permute-start | bytes 73736 | tf_op jit(solution)/shard_map/ppermute | solution.py:446
  28.4 0.8 %collective-permute-start.7 = (bf16[64,192]{1,0:T(8,128)(2,1)S(1)}, bf16[64,192]{1,0:T(8,128)(2,1)S(1)}, u32[]{:S(2)}, u32[]{:S(2)}) collective-permute-start(bf16[64,192]{1,0:T(8,128)(2,1)S(1)} %pad_maximum_fusion.7), channel_id=1, source_target_pairs={{30,0},{28,2},{2,4},{0,6},{6,8},{4,10},{10,12},{8,14},{14,16},{12,... | collective-permute-start | bytes 73736 | tf_op jit(solution)/shard_map/ppermute | solution.py:446
  29.2 5.1 %collective-permute-done.5.refs_1_ = bf16[64,192]{1,0:T(8,128)(2,1)S(1)} collective-permute-done((bf16[64,192]{1,0:T(8,128)(2,1)S(1)}, bf16[64,192]{1,0:T(8,128)(2,1)S(1)}, u32[]{:S(2)}, u32[]{:S(2)}) %collective-permute-start.5) | collective-permute-done | bytes 24608 | tf_op jit(solution)/shard_map/ppermute | solution.py:446
  34.3 1.6 %collective-permute-done.7.refs_3_ = bf16[64,192]{1,0:T(8,128)(2,1)S(1)} collective-permute-done((bf16[64,192]{1,0:T(8,128)(2,1)S(1)}, bf16[64,192]{1,0:T(8,128)(2,1)S(1)}, u32[]{:S(2)}, u32[]{:S(2)}) %collective-permute-start.7) | collective-permute-done | bytes 24608 | tf_op jit(solution)/shard_map/ppermute | solution.py:446
  36.0 2.6 %shard_map.196 = (bf16[2,6,12,192]{3,2,1,0:T(8,128)(2,1)S(1)}, bf16[168,128]{1,0:T(8,128)(2,1)S(1)}, bf16[168,128]{1,0:T(8,128)(2,1)S(1)}) custom-call(bf16[64,192]{1,0:T(8,128)(2,1)S(1)} %pad_maximum_fusion.4.refs_0_, bf16[64,192]{1,0:T(8,128)(2,1)S(1)} %collective-permute-done.5.refs_1_, bf16[64,192]{1,0:T(8,128)(2,1)S(1)} %collective-permute-done.6.refs_2_, ...), custom_call_target="tpu_custom_call" | custom-call | flops 1000000 | bytes 1000000 | tf_op jit(solution)/shard_map/pallas_call | solution.py:419
  38.6 0.1 collective-permute-start.8
  38.7 1.2 %collective-permute-done.8 = bf16[168,128]{1,0:T(8,128)(2,1)S(1)} collective-permute-done((bf16[168,128]{1,0:T(8,128)(2,1)S(1)}, bf16[168,128]{1,0:T(8,128)(2,1)S(1)}, u32[]{:S(2)}, u32[]{:S(2)}) %collective-permute-start.8) | collective-permute-done | bytes 43040 | tf_op jit(solution)/shard_map/ppermute | solution.py:468
  40.0 2.9 %collective-permute-start.10 = (bf16[168,128]{1,0:T(8,128)(2,1)S(1)}, bf16[168,128]{1,0:T(8,128)(2,1)S(1)}, u32[]{:S(2)}, u32[]{:S(2)}) collective-permute-start(bf16[168,128]{1,0:T(8,128)(2,1)S(1)} %add_convert_fusion.2), channel_id=1, source_target_pairs={{4,0},{0,4},{12,8},{8,12},{20,16},{16,20},{28,24},{24,28},{5,1},{1... | collective-permute-start | bytes 129032 | tf_op jit(solution)/shard_map/ppermute | solution.py:468
  42.9 0.6 collective-permute-start.9
  43.5 1.6 %collective-permute-done.11 = bf16[168,128]{1,0:T(8,128)(2,1)S(1)} collective-permute-done((bf16[168,128]{1,0:T(8,128)(2,1)S(1)}, bf16[168,128]{1,0:T(8,128)(2,1)S(1)}, u32[]{:S(2)}, u32[]{:S(2)}) %collective-permute-start.11) | collective-permute-done | bytes 43040 | tf_op jit(solution)/shard_map/ppermute | solution.py:468
  45.1 0.4 collective-permute-done.10
  45.5 1.5 %collective-permute-done.9 = bf16[168,128]{1,0:T(8,128)(2,1)S(1)} collective-permute-done((bf16[168,128]{1,0:T(8,128)(2,1)S(1)}, bf16[168,128]{1,0:T(8,128)(2,1)S(1)}, u32[]{:S(2)}, u32[]{:S(2)}) %collective-permute-start.9) | collective-permute-done | bytes 43040 | tf_op jit(solution)/shard_map/ppermute | solution.py:468
  47.0 2.0 %collective-permute-start.14 = (bf16[168,128]{1,0:T(8,128)(2,1)S(1)}, bf16[168,128]{1,0:T(8,128)(2,1)S(1)}, u32[]{:S(2)}, u32[]{:S(2)}) collective-permute-start(bf16[168,128]{1,0:T(8,128)(2,1)S(1)} %add_convert_fusion.1), channel_id=1, source_target_pairs={{24,0},{28,4},{16,8},{20,12},{8,16},{12,20},{0,24},{4,28},{25,1},{... | collective-permute-start | bytes 129032 | tf_op jit(solution)/shard_map/ppermute | solution.py:468
  49.0 2.4 %collective-permute-start.12 = (bf16[168,128]{1,0:T(8,128)(2,1)S(1)}, bf16[168,128]{1,0:T(8,128)(2,1)S(1)}, u32[]{:S(2)}, u32[]{:S(2)}) collective-permute-start(bf16[168,128]{1,0:T(8,128)(2,1)S(1)} %add_convert_fusion.1), channel_id=1, source_target_pairs={{8,0},{12,4},{0,8},{4,12},{24,16},{28,20},{16,24},{20,28},{9,1},{1... | collective-permute-start | bytes 129032 | tf_op jit(solution)/shard_map/ppermute | solution.py:468
  51.4 1.6 %collective-permute-done.14 = bf16[168,128]{1,0:T(8,128)(2,1)S(1)} collective-permute-done((bf16[168,128]{1,0:T(8,128)(2,1)S(1)}, bf16[168,128]{1,0:T(8,128)(2,1)S(1)}, u32[]{:S(2)}, u32[]{:S(2)}) %collective-permute-start.14) | collective-permute-done | bytes 43040 | tf_op jit(solution)/shard_map/ppermute | solution.py:468
  53.0 0.9 %collective-permute-done.13 = bf16[168,128]{1,0:T(8,128)(2,1)S(1)} collective-permute-done((bf16[168,128]{1,0:T(8,128)(2,1)S(1)}, bf16[168,128]{1,0:T(8,128)(2,1)S(1)}, u32[]{:S(2)}, u32[]{:S(2)}) %collective-permute-start.13) | collective-permute-done | bytes 43040 | tf_op jit(solution)/shard_map/ppermute | solution.py:468
  54.1 0.7 %copy.21 = bf16[2,6,12,192]{3,0,2,1:T(2,128)(2,1)} copy(bf16[2,6,12,192]{3,2,1,0:T(8,128)(2,1)S(1)} %get-tuple-element.45) | data formatting | bytes 110592
  54.8 0.5 collective-permute-done.15.other
  55.3 0.8 %shard_map.197 = (f32[160,192]{1,0:T(8,128)}, f32[64,192]{1,0:T(8,128)}) custom-call(bf16[168,128]{1,0:T(8,128)(2,1)S(1)} %add_convert_fusion.mine, bf16[168,128]{1,0:T(8,128)(2,1)S(1)} %collective-permute-done.15.other), custom_call_target="tpu_custom_call" | custom-call | flops 1000000 | bytes 1000000 | tf_op jit(solution)/shard_map/pallas_call | solution.py:419
  (53 shorter events, 0.6 us)
Async XLA Ops:
  0.6 17.7 %copy-start.4 = (f32[2,1,1,6,3312]{4,2,3,1,0:T(1,128)S(1)}, f32[2,1,1,6,3312]{4,2,3,1,0:T(1,128)}, u32[]{:S(2)}) copy-start(f32[2,1,1,6,3312]{4,2,3,1,0:T(1,128)} %param.27) | copy-start | bytes 476932
  0.6 21.4 %copy-start.3 = (bf16[2,192,192]{2,1,0:T(8,128)(2,1)S(1)}, bf16[2,192,192]{2,1,0:T(8,128)(2,1)}, u32[]{:S(2)}) copy-start(bf16[2,192,192]{2,1,0:T(8,128)(2,1)} %refs_6_.5) | copy-start | bytes 442372
  0.7 21.4 %copy-start.8 = (bf16[288,384]{1,0:T(8,128)(2,1)S(1)}, bf16[288,384]{1,0:T(8,128)(2,1)}, u32[]{:S(2)}) copy-start(bf16[288,384]{1,0:T(8,128)(2,1)} %constant.17.clone.refs_10_) | copy-start | bytes 663556
  0.7 21.4 %copy-start.10 = (bf16[256,144]{1,0:T(8,128)(2,1)S(1)}, bf16[256,144]{1,0:T(8,128)(2,1)}, u32[]{:S(2)}) copy-start(bf16[256,144]{1,0:T(8,128)(2,1)} %constant.18.clone.refs_11_) | copy-start | bytes 221188
  6.3 1.7 %collective-permute-start = (bf16[192,192]{1,0:T(8,128)(2,1)}, bf16[192,192]{1,0:T(8,128)(2,1)S(1)}, u32[]{:S(2)}, u32[]{:S(2)}) collective-permute-start(bf16[192,192]{1,0:T(8,128)(2,1)} %get-tuple-element.25), channel_id=1, source_target_pairs={{1,0},{0,1},{3,2},{2,3},{5,4},{4,5},{7,6},{6,7},{9,8},{8,9},{11,10... | collective-permute-start | bytes 221192 | tf_op jit(solution)/shard_map/ppermute | solution.py:446
  8.0 14.1 %copy-start.2 = (bf16[2,192,576]{2,1,0:T(8,128)(2,1)S(1)}, bf16[2,192,576]{2,1,0:T(8,128)(2,1)}, u32[]{:S(2)}) copy-start(bf16[2,192,576]{2,1,0:T(8,128)(2,1)} %refs_5_.5) | copy-start | bytes 1327108
  8.0 11.3 %collective-permute-start.1 = (bf16[96,192]{1,0:T(8,128)(2,1)S(1)}, bf16[96,192]{1,0:T(8,128)(2,1)S(1)}, u32[]{:S(2)}, u32[]{:S(2)}) collective-permute-start(bf16[96,192]{1,0:T(8,128)(2,1)S(1)} %pad_maximum_fusion.1), channel_id=1, source_target_pairs={{4,0},{8,4},{12,8},{16,12},{20,16},{24,20},{28,24},{0,28},{5,1},{9... | collective-permute-start | bytes 110600 | tf_op jit(solution)/shard_map/ppermute | solution.py:446
  14.7 4.7 %collective-permute-start.2 = (bf16[96,192]{1,0:T(8,128)(2,1)S(1)}, bf16[96,192]{1,0:T(8,128)(2,1)S(1)}, u32[]{:S(2)}, u32[]{:S(2)}) collective-permute-start(bf16[96,192]{1,0:T(8,128)(2,1)S(1)} %pad_maximum_fusion.2), channel_id=1, source_target_pairs={{2,0},{0,2},{3,1},{1,3},{6,4},{4,6},{7,5},{5,7},{10,8},{8,10},{11,... | collective-permute-start | bytes 110600 | tf_op jit(solution)/shard_map/ppermute | solution.py:446
  17.0 5.0 %collective-permute-start.3 = (bf16[96,192]{1,0:T(8,128)(2,1)S(1)}, bf16[96,192]{1,0:T(8,128)(2,1)S(1)}, u32[]{:S(2)}, u32[]{:S(2)}) collective-permute-start(bf16[96,192]{1,0:T(8,128)(2,1)S(1)} %pad_maximum_fusion.3), channel_id=1, source_target_pairs={{6,0},{4,2},{10,4},{8,6},{14,8},{12,10},{18,12},{16,14},{22,16},{2... | collective-permute-start | bytes 110600 | tf_op jit(solution)/shard_map/ppermute | solution.py:446
  17.5 4.5 %copy-start.1 = (bf16[2,768,192]{1,2,0:T(8,128)(2,1)S(1)}, bf16[2,768,192]{1,2,0:T(8,128)(2,1)}, u32[]{:S(2)}) copy-start(bf16[2,768,192]{1,2,0:T(8,128)(2,1)} %param.26) | copy-start | bytes 1769476
  18.4 3.7 %copy-start = (bf16[2,192,768]{2,1,0:T(8,128)(2,1)S(1)}, bf16[2,192,768]{2,1,0:T(8,128)(2,1)}, u32[]{:S(2)}) copy-start(bf16[2,192,768]{2,1,0:T(8,128)(2,1)} %refs_7_.5) | copy-start | bytes 1769476
  18.4 3.7 %copy-start.15 = (f32[2,2,192]{2,1,0:T(2,128)S(1)}, f32[2,2,192]{2,1,0:T(2,128)}, u32[]{:S(2)}) copy-start(f32[2,2,192]{2,1,0:T(2,128)} %refs_4_.5) | copy-start | bytes 9220
  22.1 13.8 %copy-start.5 = (bf16[864,144]{1,0:T(8,128)(2,1)S(1)}, bf16[864,144]{1,0:T(8,128)(2,1)}, u32[]{:S(2)}) copy-start(bf16[864,144]{1,0:T(8,128)(2,1)} %get-tuple-element.37.refs_12_) | copy-start | bytes 746500
  22.1 13.8 %copy-start.7 = (bf16[144,768]{1,0:T(8,128)(2,1)S(1)}, bf16[144,768]{1,0:T(8,128)(2,1)}, u32[]{:S(2)}) copy-start(bf16[144,768]{1,0:T(8,128)(2,1)} %get-tuple-element.39.refs_14_) | copy-start | bytes 663556
  22.1 13.8 %copy-start.11 = (bf16[192,144]{1,0:T(8,128)(2,1)S(1)}, bf16[192,144]{1,0:T(8,128)(2,1)}, u32[]{:S(2)}) copy-start(bf16[192,144]{1,0:T(8,128)(2,1)} %constant.20.clone.refs_16_) | copy-start | bytes 165892
  22.1 13.8 %copy-start.12 = (bf16[144,256]{1,0:T(8,128)(2,1)S(1)}, bf16[144,256]{1,0:T(8,128)(2,1)}, u32[]{:S(2)}) copy-start(bf16[144,256]{1,0:T(8,128)(2,1)} %constant.19.clone.refs_15_) | copy-start | bytes 221188
  22.2 13.8 %copy-start.13 = (bf16[144,256]{1,0:T(8,128)(2,1)S(1)}, bf16[144,256]{1,0:T(8,128)(2,1)}, u32[]{:S(2)}) copy-start(bf16[144,256]{1,0:T(8,128)(2,1)} %get-tuple-element.34.refs_9_) | copy-start | bytes 221188
  22.2 13.8 %copy-start.14 = (bf16[144,192]{1,0:T(8,128)(2,1)S(1)}, bf16[144,192]{1,0:T(8,128)(2,1)}, u32[]{:S(2)}) copy-start(bf16[144,192]{1,0:T(8,128)(2,1)} %get-tuple-element.35.refs_10_) | copy-start | bytes 165892
  26.3 9.7 %copy-start.6 = (bf16[3,144,192]{2,1,0:T(8,128)(2,1)S(1)}, bf16[3,144,192]{2,1,0:T(8,128)(2,1)}, u32[]{:S(2)}) copy-start(bf16[3,144,192]{2,1,0:T(8,128)(2,1)} %get-tuple-element.36.refs_11_) | copy-start | bytes 497668
  26.3 1.3 %collective-permute-start.4 = (bf16[128,192]{1,0:T(8,128)(2,1)S(1)}, bf16[128,192]{1,0:T(8,128)(2,1)S(1)}, u32[]{:S(2)}, u32[]{:S(2)}) collective-permute-start(bf16[128,192]{1,0:T(8,128)(2,1)S(1)} %get-tuple-element.30), channel_id=1, source_target_pairs={{1,0},{0,1},{3,2},{2,3},{5,4},{4,5},{7,6},{6,7},{9,8},{8,9},{11,10... | collective-permute-start | bytes 147464 | tf_op jit(solution)/shard_map/ppermute | solution.py:446
  27.6 8.3 %copy-start.9 = (f32[144,192]{1,0:T(8,128)S(1)}, f32[144,192]{1,0:T(8,128)}, u32[]{:S(2)}) copy-start(f32[144,192]{1,0:T(8,128)} %get-tuple-element.38.refs_13_) | copy-start | bytes 331780
  27.7 6.7 %collective-permute-start.5 = (bf16[64,192]{1,0:T(8,128)(2,1)S(1)}, bf16[64,192]{1,0:T(8,128)(2,1)S(1)}, u32[]{:S(2)}, u32[]{:S(2)}) collective-permute-start(bf16[64,192]{1,0:T(8,128)(2,1)S(1)} %pad_maximum_fusion.5), channel_id=1, source_target_pairs={{28,0},{0,4},{4,8},{8,12},{12,16},{16,20},{20,24},{24,28},{29,1},{... | collective-permute-start | bytes 73736 | tf_op jit(solution)/shard_map/ppermute | solution.py:446
  27.8 6.6 %collective-permute-start.6 = (bf16[64,192]{1,0:T(8,128)(2,1)S(1)}, bf16[64,192]{1,0:T(8,128)(2,1)S(1)}, u32[]{:S(2)}, u32[]{:S(2)}) collective-permute-start(bf16[64,192]{1,0:T(8,128)(2,1)S(1)} %pad_maximum_fusion.6), channel_id=1, source_target_pairs={{2,0},{0,2},{3,1},{1,3},{6,4},{4,6},{7,5},{5,7},{10,8},{8,10},{11,... | collective-permute-start | bytes 73736 | tf_op jit(solution)/shard_map/ppermute | solution.py:446
  28.4 7.6 %collective-permute-start.7 = (bf16[64,192]{1,0:T(8,128)(2,1)S(1)}, bf16[64,192]{1,0:T(8,128)(2,1)S(1)}, u32[]{:S(2)}, u32[]{:S(2)}) collective-permute-start(bf16[64,192]{1,0:T(8,128)(2,1)S(1)} %pad_maximum_fusion.7), channel_id=1, source_target_pairs={{30,0},{28,2},{2,4},{0,6},{6,8},{4,10},{10,12},{8,14},{14,16},{12,... | collective-permute-start | bytes 73736 | tf_op jit(solution)/shard_map/ppermute | solution.py:446
  38.6 1.3 %collective-permute-start.8 = (bf16[168,128]{1,0:T(8,128)(2,1)S(1)}, bf16[168,128]{1,0:T(8,128)(2,1)S(1)}, u32[]{:S(2)}, u32[]{:S(2)}) collective-permute-start(bf16[168,128]{1,0:T(8,128)(2,1)S(1)} %get-tuple-element.42), channel_id=1, source_target_pairs={{1,0},{0,1},{3,2},{2,3},{5,4},{4,5},{7,6},{6,7},{9,8},{8,9},{11,10... | collective-permute-start | bytes 129032 | tf_op jit(solution)/shard_map/ppermute | solution.py:468
  39.9 5.2 %collective-permute-start.11 = (bf16[168,128]{1,0:T(8,128)(2,1)S(1)}, bf16[168,128]{1,0:T(8,128)(2,1)S(1)}, u32[]{:S(2)}, u32[]{:S(2)}) collective-permute-start(bf16[168,128]{1,0:T(8,128)(2,1)S(1)} %add_convert_fusion.2), channel_id=1, source_target_pairs={{6,0},{4,2},{2,4},{0,6},{14,8},{12,10},{10,12},{8,14},{22,16},{20,... | collective-permute-start | bytes 129032 | tf_op jit(solution)/shard_map/ppermute | solution.py:468
  40.0 5.5 %collective-permute-start.10 = (bf16[168,128]{1,0:T(8,128)(2,1)S(1)}, bf16[168,128]{1,0:T(8,128)(2,1)S(1)}, u32[]{:S(2)}, u32[]{:S(2)}) collective-permute-start(bf16[168,128]{1,0:T(8,128)(2,1)S(1)} %add_convert_fusion.2), channel_id=1, source_target_pairs={{4,0},{0,4},{12,8},{8,12},{20,16},{16,20},{28,24},{24,28},{5,1},{1... | collective-permute-start | bytes 129032 | tf_op jit(solution)/shard_map/ppermute | solution.py:468
  42.9 4.0 %collective-permute-start.9 = (bf16[168,128]{1,0:T(8,128)(2,1)S(1)}, bf16[168,128]{1,0:T(8,128)(2,1)S(1)}, u32[]{:S(2)}, u32[]{:S(2)}) collective-permute-start(bf16[168,128]{1,0:T(8,128)(2,1)S(1)} %add_convert_fusion.2), channel_id=1, source_target_pairs={{2,0},{0,2},{3,1},{1,3},{6,4},{4,6},{7,5},{5,7},{10,8},{8,10},{11,... | collective-permute-start | bytes 129032 | tf_op jit(solution)/shard_map/ppermute | solution.py:468
  47.0 6.0 %collective-permute-start.14 = (bf16[168,128]{1,0:T(8,128)(2,1)S(1)}, bf16[168,128]{1,0:T(8,128)(2,1)S(1)}, u32[]{:S(2)}, u32[]{:S(2)}) collective-permute-start(bf16[168,128]{1,0:T(8,128)(2,1)S(1)} %add_convert_fusion.1), channel_id=1, source_target_pairs={{24,0},{28,4},{16,8},{20,12},{8,16},{12,20},{0,24},{4,28},{25,1},{... | collective-permute-start | bytes 129032 | tf_op jit(solution)/shard_map/ppermute | solution.py:468
  49.0 4.9 %collective-permute-start.13 = (bf16[168,128]{1,0:T(8,128)(2,1)S(1)}, bf16[168,128]{1,0:T(8,128)(2,1)S(1)}, u32[]{:S(2)}, u32[]{:S(2)}) collective-permute-start(bf16[168,128]{1,0:T(8,128)(2,1)S(1)} %add_convert_fusion.1), channel_id=1, source_target_pairs={{16,0},{20,4},{24,8},{28,12},{0,16},{4,20},{8,24},{12,28},{17,1},{... | collective-permute-start | bytes 129032 | tf_op jit(solution)/shard_map/ppermute | solution.py:468
  49.0 4.9 %collective-permute-start.12 = (bf16[168,128]{1,0:T(8,128)(2,1)S(1)}, bf16[168,128]{1,0:T(8,128)(2,1)S(1)}, u32[]{:S(2)}, u32[]{:S(2)}) collective-permute-start(bf16[168,128]{1,0:T(8,128)(2,1)S(1)} %add_convert_fusion.1), channel_id=1, source_target_pairs={{8,0},{12,4},{0,8},{4,12},{24,16},{28,20},{16,24},{20,28},{9,1},{1... | collective-permute-start | bytes 129032 | tf_op jit(solution)/shard_map/ppermute | solution.py:468
  54.0 1.3 %collective-permute-start.15 = (bf16[168,128]{1,0:T(8,128)(2,1)S(1)}, bf16[168,128]{1,0:T(8,128)(2,1)S(1)}, u32[]{:S(2)}, u32[]{:S(2)}) collective-permute-start(bf16[168,128]{1,0:T(8,128)(2,1)S(1)} %add_convert_fusion.mine), channel_id=1, source_target_pairs={{1,0},{0,1},{3,2},{2,3},{5,4},{4,5},{7,6},{6,7},{9,8},{8,9},{11,10... | collective-permute-start | bytes 129032 | tf_op jit(solution)/shard_map/ppermute | solution.py:468
  (1 other events, 1.7 us)

commit v8 on v7

--- a/solution.py
+++ b/solution.py
@@ -282,11 +282,10 @@
     )
     count = len(names)
     source, refs = refs[:count], refs[count:]
-    results = ("patch", "x", "qkv", "prob", "resid", "slope", "send", "keep0", "keep1", "keep2", "keep3")
-    target, refs = refs[: len(results)], refs[len(results) :]
+    patch_o, x_o, qkv_o, prob, resid_o, slope_o, send_o, *keep_o = refs[:11]
+    refs = refs[11:]
     local, refs = refs[:count], refs[count:]
-    patch_s, x_s, qkv_s, prob, resid_s, slope_s, blocks = refs[:7]
-    ff, ft, emb, cots, table, xs, bias, cols, select, sems = refs[7:]
+    ff, ft, emb, cots, table, xs, bias, cols, select, sems = refs
     copies = {}
     for n, name in enumerate(names):
         start, end = source[n], local[n]
@@ -301,16 +300,10 @@
         copies[name] = pltpu.make_async_copy(start, end, sems.at[n])
         copies[name].start()
     have = dict(zip(names, local))
-    sent = []
 
     def wait(*which):
         for name in which:
             copies[name].wait()
-
-    def send(name, held):
-        n = results.index(name)
-        sent.append(pltpu.make_async_copy(held, target[n], sems.at[len(names) + n]))
-        sent[-1].start()
 
     emb[224:256, :] = jnp.zeros((32, WIDTH), HALF)
     fill_columns(cols)
@@ -322,11 +315,9 @@
     section = lax.axis_index("section")
     patch = gather_patches(have["upper"], have["surface"], section, select, ff, ft)
     patch = dot(have["to_inner"][...], patch).astype(HALF)
-    patch_s[...] = patch
-    send("patch", patch_s)
+    patch_o[...] = patch
     latent = dot(patch, emb[...]).astype(HALF)
-    x_s[...] = latent
-    send("x", x_s)
+    x_o[...] = latent
     x = latent.astype(FULL)
     gains = have["gains"].at[0]
     wait("wproj", "wup", "wdown", "cot", "out_first", "out_cot")
@@ -336,26 +327,20 @@
             cots[(a * 12 + o) * 2 : (a * 12 + o) * 2 + 2, :] = cot[a, o].astype(FULL)
     ready = dot(have["out_cot"][...], cots[...].astype(HALF))
     qkv, resid = forward_half(x, gains, have["wqkv"], have["wproj"], bias, prob)
-    send("prob", prob)
     for n in range(3):
-        qkv_s[n] = qkv[n]
-    send("qkv", qkv_s)
-    resid_s[...] = resid
-    send("resid", resid_s)
+        qkv_o[n] = qkv[n]
+    resid_o[...] = resid
     unit, spread = normalise(resid)
     normed = (unit * gains[1:2, :]).astype(HALF)
     upward = dot(normed, have["wup"][...])
     below, slope = gelu_parts(upward)
-    slope_s[...] = slope.astype(HALF)
-    send("slope", slope_s)
+    slope_o[...] = slope.astype(HALF)
     active = (upward * below).astype(HALF)
     result = (resid + dot_nt(active, have["wdown"][...])).astype(HALF)
-    blocks[...] = (dot(have["out_first"][...], result) + ready).astype(HALF)
-    send("send", blocks.at[pl.ds(192, 192)])
+    moved = (dot(have["out_first"][...], result) + ready).astype(HALF)
+    send_o[...] = moved[192:]
     for n in range(4):
-        send("keep" + str(n), blocks.at[pl.ds(n * 48, 48)])
-    for copy in sent:
-        copy.wait()
+        keep_o[n][...] = moved[n * 48 : n * 48 + 48]
 
 
 def second_bias(tbl, after, bias, table, xs, cols):
@@ -556,9 +541,7 @@
         first_kernel,
         held + [shape((192, WIDTH))] + [shape((48, WIDTH))] * 4,
         local
-        + [pltpu.VMEM(v.shape, v.dtype) for v in held]
         + [
-            pltpu.VMEM((384, WIDTH), HALF),
             pltpu.VMEM((576, 128), FULL),
             pltpu.VMEM((288, 128), FULL),
             pltpu.VMEM((256, WIDTH), HALF),
@@ -569,12 +552,10 @@
             pltpu.VMEM((HEADS * CELLS, CELLS), FULL),
             scratch_cols,
             pltpu.VMEM((512, 512), HALF),
-            pltpu.SemaphoreType.DMA((len(operands) + 11,)),
+            pltpu.SemaphoreType.DMA((len(operands),)),
         ],
-        *operands,
+        *(pltpu.with_memory_space_constraint(v, pltpu.HBM) for v in operands),
         spec=hbm,
-        out=hbm,
-        room=60,
     )
     bias_shape = shape((HEADS * CELLS, CELLS), FULL)
     got = fetch(send, {"section": 1})

time: 56.4 us -> 53.6 us (0.950)
  other arithmetic: 2.42 us -> 0.15 us
  Pallas kernels: 14.1 us -> 13.3 us
  waiting for transfers between devices: 19.5 us -> 20.1 us
    concatenate x8, other arithmetic: 2.35 us -> 0.08 us  [exchange(): block = jnp.concatenate((keep[n], got[n * pitch:(n + 1) * pitch]), 0)]
    pallas_call x5, Pallas kernels: 14.1 us -> 13.3 us  [call(): pl.pallas_call(kernel, out_shape=outs, in_specs=[spec for a in args], out...]
    ppermute x8, waiting for transfers between devices: 11.8 us -> 12.4 us  [fetch(): return lax.ppermute(block, tuple(axes), pairs)]
  transfers between devices with their start and end apart: 16 -> 16, of which waited for: 13 -> 13; matrix products, arithmetic and copies ran while one was open for 5% -> 1% of each run, Pallas kernels for 2% -> 2%
where the time goes in v8:
time: 53.6 us; the launch traced here: 53.5 us
  waiting for transfers between devices  20.1 us (38%)
  starting transfers between devices  18.3 us (34%)
  Pallas kernels  13.3 us (25%)
  between operations  0.87 us (2%)
  local copies, waits for them, and re-layouts  0.77 us (1%)
    pallas_call x5, Pallas kernels, call(): pl.pallas_call(kernel, out_shape=outs, in_specs=[spec for a in args], out...  13.3 us
    ppermute x8, waiting for transfers between devices, fetch(): return lax.ppermute(block, tuple(axes), pairs)  12.4 us
    ppermute x8, starting transfers between devices, fetch(): return lax.ppermute(block, tuple(axes), pairs)  10.1 us
    ppermute x8, starting transfers between devices, swap(): return lax.ppermute(block, tuple(axes), pairs)  8.14 us
    ppermute x8, waiting for transfers between devices, swap(): return lax.ppermute(block, tuple(axes), pairs)  7.69 us
  transfers between devices with their start and end apart: 16, of which 13 were waited for; matrix products, arithmetic and copies ran while one was open for 1% of the time, Pallas kernels for 2%

profile of v8, /device:TPU:0, one launch (start us, length us, event | category | flops | bytes accessed | tf_op | source)
XLA Modules:
  0.0 53.5 jit_solution(15998959507011734023)
XLA Ops:
  0.7 4.8 %shard_map.193 = (bf16[144,256]{1,0:T(8,128)(2,1)S(1)}, bf16[144,192]{1,0:T(8,128)(2,1)S(1)}, bf16[3,144,192]{2,1,0:T(8,128)(2,1)S(1)}, bf16[864,144]{1,0:T(8,12...) custom-call(f32[12,1,3312]{2,1,0:T(1,128)} %bitcast.6, ...), custom_call_target="tpu_custom_call" | custom-call | flops 1000000 | bytes 1000000 | tf_op jit(solution)/shard_map/pallas_call | solution.py:404
  5.5 0.5 collective-permute-start
  6.0 0.9 %collective-permute-done.after = bf16[192,192]{1,0:T(8,128)(2,1)S(1)} collective-permute-done((bf16[192,192]{1,0:T(8,128)(2,1)S(1)}, bf16[192,192]{1,0:T(8,128)(2,1)S(1)}, u32[]{:S(2)}, u32[]{:S(2)}) %collective-permute-start) | collective-permute-done | bytes 73760 | tf_op jit(solution)/shard_map/ppermute | solution.py:431
  7.0 6.0 %collective-permute-start.1 = (bf16[96,192]{1,0:T(8,128)(2,1)S(1)}, bf16[96,192]{1,0:T(8,128)(2,1)S(1)}, u32[]{:S(2)}, u32[]{:S(2)}) collective-permute-start(bf16[96,192]{1,0:T(8,128)(2,1)S(1)} %pad_maximum_fusion.1), channel_id=1, source_target_pairs={{4,0},{8,4},{12,8},{16,12},{20,16},{24,20},{28,24},{0,28},{5,1},{9... | collective-permute-start | bytes 110600 | tf_op jit(solution)/shard_map/ppermute | solution.py:431
  13.0 1.6 %collective-permute-start.2 = (bf16[96,192]{1,0:T(8,128)(2,1)S(1)}, bf16[96,192]{1,0:T(8,128)(2,1)S(1)}, u32[]{:S(2)}, u32[]{:S(2)}) collective-permute-start(bf16[96,192]{1,0:T(8,128)(2,1)S(1)} %pad_maximum_fusion.2), channel_id=1, source_target_pairs={{2,0},{0,2},{3,1},{1,3},{6,4},{4,6},{7,5},{5,7},{10,8},{8,10},{11,... | collective-permute-start | bytes 110600 | tf_op jit(solution)/shard_map/ppermute | solution.py:431
  14.5 0.5 collective-permute-start.3
  15.1 0.9 %shard_map.194.refs_9_ = f32[864,144]{1,0:T(8,128)S(1)} custom-call(f32[12,1,3312]{2,1,0:T(1,128)S(1)} %bitcast.7, bf16[192,192]{1,0:T(8,128)(2,1)S(1)} %collective-permute-done.after), custom_call_target="tpu_custom_call" | custom-call | flops 1000000 | bytes 1000000 | tf_op jit(solution)/shard_map/pallas_call | solution.py:404
  16.1 1.1 %collective-permute-done.2.refs_2_ = bf16[96,192]{1,0:T(8,128)(2,1)S(1)} collective-permute-done((bf16[96,192]{1,0:T(8,128)(2,1)S(1)}, bf16[96,192]{1,0:T(8,128)(2,1)S(1)}, u32[]{:S(2)}, u32[]{:S(2)}) %collective-permute-start.2) | collective-permute-done | bytes 36896 | tf_op jit(solution)/shard_map/ppermute | solution.py:431
  17.1 2.5 %collective-permute-done.3.refs_3_ = bf16[96,192]{1,0:T(8,128)(2,1)S(1)} collective-permute-done((bf16[96,192]{1,0:T(8,128)(2,1)S(1)}, bf16[96,192]{1,0:T(8,128)(2,1)S(1)}, u32[]{:S(2)}, u32[]{:S(2)}) %collective-permute-start.3) | collective-permute-done | bytes 36896 | tf_op jit(solution)/shard_map/ppermute | solution.py:431
  19.6 4.1 %shard_map.195 = (bf16[128,192]{1,0:T(8,128)(2,1)S(1)}, bf16[32,192]{1,0:T(8,128)(2,1)S(1)}, bf16[32,192]{1,0:T(8,128)(2,1)S(1)}, bf16[32,192]{1,0:T(8,128)(2,1)S(1)}, bf16[32,192]{1,0:T(8,128)(2,1)S(1)}) custom-call(bf16[96,192]{1,0:T(8,128)(2,1)S(1)} %pad_maximum_fusion.refs_0_, bf16[96,192]{1,0:T(8,128)(2,1)S(1)} %collective-permute-done.1.refs_1_, ...), custom_call_target="tpu_custom_call" | custom-call | flops 1000000 | bytes 1000000 | tf_op jit(solution)/shard_map/pallas_call | solution.py:404
  23.8 0.1 collective-permute-start.4
  23.9 1.2 %collective-permute-done.4 = bf16[128,192]{1,0:T(8,128)(2,1)S(1)} collective-permute-done((bf16[128,192]{1,0:T(8,128)(2,1)S(1)}, bf16[128,192]{1,0:T(8,128)(2,1)S(1)}, u32[]{:S(2)}, u32[]{:S(2)}) %collective-permute-start.4) | collective-permute-done | bytes 49184 | tf_op jit(solution)/shard_map/ppermute | solution.py:431
  25.2 0.6 %collective-permute-start.6 = (bf16[64,192]{1,0:T(8,128)(2,1)S(1)}, bf16[64,192]{1,0:T(8,128)(2,1)S(1)}, u32[]{:S(2)}, u32[]{:S(2)}) collective-permute-start(bf16[64,192]{1,0:T(8,128)(2,1)S(1)} %pad_maximum_fusion.6), channel_id=1, source_target_pairs={{2,0},{0,2},{3,1},{1,3},{6,4},{4,6},{7,5},{5,7},{10,8},{8,10},{11,... | collective-permute-start | bytes 73736 | tf_op jit(solution)/shard_map/ppermute | solution.py:431
  25.8 0.8 %collective-permute-start.7 = (bf16[64,192]{1,0:T(8,128)(2,1)S(1)}, bf16[64,192]{1,0:T(8,128)(2,1)S(1)}, u32[]{:S(2)}, u32[]{:S(2)}) collective-permute-start(bf16[64,192]{1,0:T(8,128)(2,1)S(1)} %pad_maximum_fusion.7), channel_id=1, source_target_pairs={{30,0},{28,2},{2,4},{0,6},{6,8},{4,10},{10,12},{8,14},{14,16},{12,... | collective-permute-start | bytes 73736 | tf_op jit(solution)/shard_map/ppermute | solution.py:431
  26.7 5.1 %collective-permute-done.5.refs_1_ = bf16[64,192]{1,0:T(8,128)(2,1)S(1)} collective-permute-done((bf16[64,192]{1,0:T(8,128)(2,1)S(1)}, bf16[64,192]{1,0:T(8,128)(2,1)S(1)}, u32[]{:S(2)}, u32[]{:S(2)}) %collective-permute-start.5) | collective-permute-done | bytes 24608 | tf_op jit(solution)/shard_map/ppermute | solution.py:431
  31.8 1.6 %collective-permute-done.7.refs_3_ = bf16[64,192]{1,0:T(8,128)(2,1)S(1)} collective-permute-done((bf16[64,192]{1,0:T(8,128)(2,1)S(1)}, bf16[64,192]{1,0:T(8,128)(2,1)S(1)}, u32[]{:S(2)}, u32[]{:S(2)}) %collective-permute-start.7) | collective-permute-done | bytes 24608 | tf_op jit(solution)/shard_map/ppermute | solution.py:431
  33.4 2.6 %shard_map.196 = (bf16[2,6,12,192]{3,2,1,0:T(8,128)(2,1)S(1)}, bf16[168,128]{1,0:T(8,128)(2,1)S(1)}, bf16[168,128]{1,0:T(8,128)(2,1)S(1)}) custom-call(bf16[64,192]{1,0:T(8,128)(2,1)S(1)} %pad_maximum_fusion.4.refs_0_, bf16[64,192]{1,0:T(8,128)(2,1)S(1)} %collective-permute-done.5.refs_1_, bf16[64,192]{1,0:T(8,128)(2,1)S(1)} %collective-permute-done.6.refs_2_, ...), custom_call_target="tpu_custom_call" | custom-call | flops 1000000 | bytes 1000000 | tf_op jit(solution)/shard_map/pallas_call | solution.py:404
  36.0 0.1 collective-permute-start.8
  36.1 1.2 %collective-permute-done.8 = bf16[168,128]{1,0:T(8,128)(2,1)S(1)} collective-permute-done((bf16[168,128]{1,0:T(8,128)(2,1)S(1)}, bf16[168,128]{1,0:T(8,128)(2,1)S(1)}, u32[]{:S(2)}, u32[]{:S(2)}) %collective-permute-start.8) | collective-permute-done | bytes 43040 | tf_op jit(solution)/shard_map/ppermute | solution.py:453
  37.3 0.1 collective-permute-start.11
  37.4 2.9 %collective-permute-start.10 = (bf16[168,128]{1,0:T(8,128)(2,1)S(1)}, bf16[168,128]{1,0:T(8,128)(2,1)S(1)}, u32[]{:S(2)}, u32[]{:S(2)}) collective-permute-start(bf16[168,128]{1,0:T(8,128)(2,1)S(1)} %add_convert_fusion.2), channel_id=1, source_target_pairs={{4,0},{0,4},{12,8},{8,12},{20,16},{16,20},{28,24},{24,28},{5,1},{1... | collective-permute-start | bytes 129032 | tf_op jit(solution)/shard_map/ppermute | solution.py:453
  40.3 0.5 %collective-permute-start.9 = (bf16[168,128]{1,0:T(8,128)(2,1)S(1)}, bf16[168,128]{1,0:T(8,128)(2,1)S(1)}, u32[]{:S(2)}, u32[]{:S(2)}) collective-permute-start(bf16[168,128]{1,0:T(8,128)(2,1)S(1)} %add_convert_fusion.2), channel_id=1, source_target_pairs={{2,0},{0,2},{3,1},{1,3},{6,4},{4,6},{7,5},{5,7},{10,8},{8,10},{11,... | collective-permute-start | bytes 129032 | tf_op jit(solution)/shard_map/ppermute | solution.py:453
  40.9 1.6 %collective-permute-done.11 = bf16[168,128]{1,0:T(8,128)(2,1)S(1)} collective-permute-done((bf16[168,128]{1,0:T(8,128)(2,1)S(1)}, bf16[168,128]{1,0:T(8,128)(2,1)S(1)}, u32[]{:S(2)}, u32[]{:S(2)}) %collective-permute-start.11) | collective-permute-done | bytes 43040 | tf_op jit(solution)/shard_map/ppermute | solution.py:453
  42.5 0.4 collective-permute-done.10
  42.9 1.5 %collective-permute-done.9 = bf16[168,128]{1,0:T(8,128)(2,1)S(1)} collective-permute-done((bf16[168,128]{1,0:T(8,128)(2,1)S(1)}, bf16[168,128]{1,0:T(8,128)(2,1)S(1)}, u32[]{:S(2)}, u32[]{:S(2)}) %collective-permute-start.9) | collective-permute-done | bytes 43040 | tf_op jit(solution)/shard_map/ppermute | solution.py:453
  44.4 2.0 %collective-permute-start.14 = (bf16[168,128]{1,0:T(8,128)(2,1)S(1)}, bf16[168,128]{1,0:T(8,128)(2,1)S(1)}, u32[]{:S(2)}, u32[]{:S(2)}) collective-permute-start(bf16[168,128]{1,0:T(8,128)(2,1)S(1)} %add_convert_fusion.1), channel_id=1, source_target_pairs={{24,0},{28,4},{16,8},{20,12},{8,16},{12,20},{0,24},{4,28},{25,1},{... | collective-permute-start | bytes 129032 | tf_op jit(solution)/shard_map/ppermute | solution.py:453
  46.4 2.4 %collective-permute-start.12 = (bf16[168,128]{1,0:T(8,128)(2,1)S(1)}, bf16[168,128]{1,0:T(8,128)(2,1)S(1)}, u32[]{:S(2)}, u32[]{:S(2)}) collective-permute-start(bf16[168,128]{1,0:T(8,128)(2,1)S(1)} %add_convert_fusion.1), channel_id=1, source_target_pairs={{8,0},{12,4},{0,8},{4,12},{24,16},{28,20},{16,24},{20,28},{9,1},{1... | collective-permute-start | bytes 129032 | tf_op jit(solution)/shard_map/ppermute | solution.py:453
  48.8 1.6 %collective-permute-done.14 = bf16[168,128]{1,0:T(8,128)(2,1)S(1)} collective-permute-done((bf16[168,128]{1,0:T(8,128)(2,1)S(1)}, bf16[168,128]{1,0:T(8,128)(2,1)S(1)}, u32[]{:S(2)}, u32[]{:S(2)}) %collective-permute-start.14) | collective-permute-done | bytes 43040 | tf_op jit(solution)/shard_map/ppermute | solution.py:453
  50.4 0.9 %collective-permute-done.13 = bf16[168,128]{1,0:T(8,128)(2,1)S(1)} collective-permute-done((bf16[168,128]{1,0:T(8,128)(2,1)S(1)}, bf16[168,128]{1,0:T(8,128)(2,1)S(1)}, u32[]{:S(2)}, u32[]{:S(2)}) %collective-permute-start.13) | collective-permute-done | bytes 43040 | tf_op jit(solution)/shard_map/ppermute | solution.py:453
  51.5 0.7 %copy.21 = bf16[2,6,12,192]{3,0,2,1:T(2,128)(2,1)} copy(bf16[2,6,12,192]{3,2,1,0:T(8,128)(2,1)S(1)} %get-tuple-element.45) | data formatting | bytes 110592
  52.2 0.5 collective-permute-done.15.other
  52.7 0.8 %shard_map.197 = (f32[160,192]{1,0:T(8,128)}, f32[64,192]{1,0:T(8,128)}) custom-call(bf16[168,128]{1,0:T(8,128)(2,1)S(1)} %add_convert_fusion.mine, bf16[168,128]{1,0:T(8,128)(2,1)S(1)} %collective-permute-done.15.other), custom_call_target="tpu_custom_call" | custom-call | flops 1000000 | bytes 1000000 | tf_op jit(solution)/shard_map/pallas_call | solution.py:404
  (39 shorter events, 0.4 us)
Async XLA Ops:
  0.6 14.5 %copy-start.4 = (f32[2,1,1,6,3312]{4,2,3,1,0:T(1,128)S(1)}, f32[2,1,1,6,3312]{4,2,3,1,0:T(1,128)}, u32[]{:S(2)}) copy-start(f32[2,1,1,6,3312]{4,2,3,1,0:T(1,128)} %param.27) | copy-start | bytes 476932
  0.6 18.9 %copy-start.3 = (bf16[2,192,192]{2,1,0:T(8,128)(2,1)S(1)}, bf16[2,192,192]{2,1,0:T(8,128)(2,1)}, u32[]{:S(2)}) copy-start(bf16[2,192,192]{2,1,0:T(8,128)(2,1)} %refs_6_.5) | copy-start | bytes 442372
  0.7 18.9 %copy-start.5 = (bf16[288,384]{1,0:T(8,128)(2,1)S(1)}, bf16[288,384]{1,0:T(8,128)(2,1)}, u32[]{:S(2)}) copy-start(bf16[288,384]{1,0:T(8,128)(2,1)} %constant.17.clone.refs_10_) | copy-start | bytes 663556
  0.7 18.9 %copy-start.6 = (bf16[256,144]{1,0:T(8,128)(2,1)S(1)}, bf16[256,144]{1,0:T(8,128)(2,1)}, u32[]{:S(2)}) copy-start(bf16[256,144]{1,0:T(8,128)(2,1)} %constant.18.clone.refs_11_) | copy-start | bytes 221188
  5.5 1.5 %collective-permute-start = (bf16[192,192]{1,0:T(8,128)(2,1)S(1)}, bf16[192,192]{1,0:T(8,128)(2,1)S(1)}, u32[]{:S(2)}, u32[]{:S(2)}) collective-permute-start(bf16[192,192]{1,0:T(8,128)(2,1)S(1)} %get-tuple-element.25), channel_id=1, source_target_pairs={{1,0},{0,1},{3,2},{2,3},{5,4},{4,5},{7,6},{6,7},{9,8},{8,9},{11,10... | collective-permute-start | bytes 221192 | tf_op jit(solution)/shard_map/ppermute | solution.py:431
  7.0 12.6 %copy-start.2 = (bf16[2,192,576]{2,1,0:T(8,128)(2,1)S(1)}, bf16[2,192,576]{2,1,0:T(8,128)(2,1)}, u32[]{:S(2)}) copy-start(bf16[2,192,576]{2,1,0:T(8,128)(2,1)} %refs_5_.5) | copy-start | bytes 1327108
  7.0 9.1 %collective-permute-start.1 = (bf16[96,192]{1,0:T(8,128)(2,1)S(1)}, bf16[96,192]{1,0:T(8,128)(2,1)S(1)}, u32[]{:S(2)}, u32[]{:S(2)}) collective-permute-start(bf16[96,192]{1,0:T(8,128)(2,1)S(1)} %pad_maximum_fusion.1), channel_id=1, source_target_pairs={{4,0},{8,4},{12,8},{16,12},{20,16},{24,20},{28,24},{0,28},{5,1},{9... | collective-permute-start | bytes 110600 | tf_op jit(solution)/shard_map/ppermute | solution.py:431
  13.0 4.2 %collective-permute-start.2 = (bf16[96,192]{1,0:T(8,128)(2,1)S(1)}, bf16[96,192]{1,0:T(8,128)(2,1)S(1)}, u32[]{:S(2)}, u32[]{:S(2)}) collective-permute-start(bf16[96,192]{1,0:T(8,128)(2,1)S(1)} %pad_maximum_fusion.2), channel_id=1, source_target_pairs={{2,0},{0,2},{3,1},{1,3},{6,4},{4,6},{7,5},{5,7},{10,8},{8,10},{11,... | collective-permute-start | bytes 110600 | tf_op jit(solution)/shard_map/ppermute | solution.py:431
  14.5 5.0 %collective-permute-start.3 = (bf16[96,192]{1,0:T(8,128)(2,1)S(1)}, bf16[96,192]{1,0:T(8,128)(2,1)S(1)}, u32[]{:S(2)}, u32[]{:S(2)}) collective-permute-start(bf16[96,192]{1,0:T(8,128)(2,1)S(1)} %pad_maximum_fusion.3), channel_id=1, source_target_pairs={{6,0},{4,2},{10,4},{8,6},{14,8},{12,10},{18,12},{16,14},{22,16},{2... | collective-permute-start | bytes 110600 | tf_op jit(solution)/shard_map/ppermute | solution.py:431
  15.1 4.5 %copy-start.1 = (bf16[2,768,192]{1,2,0:T(8,128)(2,1)S(1)}, bf16[2,768,192]{1,2,0:T(8,128)(2,1)}, u32[]{:S(2)}) copy-start(bf16[2,768,192]{1,2,0:T(8,128)(2,1)} %param.26) | copy-start | bytes 1769476
  15.1 4.5 %copy-start = (bf16[2,192,768]{2,1,0:T(8,128)(2,1)S(1)}, bf16[2,192,768]{2,1,0:T(8,128)(2,1)}, u32[]{:S(2)}) copy-start(bf16[2,192,768]{2,1,0:T(8,128)(2,1)} %refs_7_.5) | copy-start | bytes 1769476
  15.1 4.5 %copy-start.9 = (f32[2,2,192]{2,1,0:T(2,128)S(1)}, f32[2,2,192]{2,1,0:T(2,128)}, u32[]{:S(2)}) copy-start(f32[2,2,192]{2,1,0:T(2,128)} %refs_4_.5) | copy-start | bytes 9220
  23.8 1.3 %collective-permute-start.4 = (bf16[128,192]{1,0:T(8,128)(2,1)S(1)}, bf16[128,192]{1,0:T(8,128)(2,1)S(1)}, u32[]{:S(2)}, u32[]{:S(2)}) collective-permute-start(bf16[128,192]{1,0:T(8,128)(2,1)S(1)} %get-tuple-element.30), channel_id=1, source_target_pairs={{1,0},{0,1},{3,2},{2,3},{5,4},{4,5},{7,6},{6,7},{9,8},{8,9},{11,10... | collective-permute-start | bytes 147464 | tf_op jit(solution)/shard_map/ppermute | solution.py:431
  25.1 6.7 %collective-permute-start.5 = (bf16[64,192]{1,0:T(8,128)(2,1)S(1)}, bf16[64,192]{1,0:T(8,128)(2,1)S(1)}, u32[]{:S(2)}, u32[]{:S(2)}) collective-permute-start(bf16[64,192]{1,0:T(8,128)(2,1)S(1)} %pad_maximum_fusion.5), channel_id=1, source_target_pairs={{28,0},{0,4},{4,8},{8,12},{12,16},{16,20},{20,24},{24,28},{29,1},{... | collective-permute-start | bytes 73736 | tf_op jit(solution)/shard_map/ppermute | solution.py:431
  25.2 8.2 %copy-start.7 = (bf16[192,144]{1,0:T(8,128)(2,1)S(1)}, bf16[192,144]{1,0:T(8,128)(2,1)}, u32[]{:S(2)}) copy-start(bf16[192,144]{1,0:T(8,128)(2,1)} %constant.20.clone.refs_16_) | copy-start | bytes 165892
  25.2 6.6 %collective-permute-start.6 = (bf16[64,192]{1,0:T(8,128)(2,1)S(1)}, bf16[64,192]{1,0:T(8,128)(2,1)S(1)}, u32[]{:S(2)}, u32[]{:S(2)}) collective-permute-start(bf16[64,192]{1,0:T(8,128)(2,1)S(1)} %pad_maximum_fusion.6), channel_id=1, source_target_pairs={{2,0},{0,2},{3,1},{1,3},{6,4},{4,6},{7,5},{5,7},{10,8},{8,10},{11,... | collective-permute-start | bytes 73736 | tf_op jit(solution)/shard_map/ppermute | solution.py:431
  25.8 7.6 %copy-start.8 = (bf16[144,256]{1,0:T(8,128)(2,1)S(1)}, bf16[144,256]{1,0:T(8,128)(2,1)}, u32[]{:S(2)}) copy-start(bf16[144,256]{1,0:T(8,128)(2,1)} %constant.19.clone.refs_15_) | copy-start | bytes 221188
  25.8 7.6 %collective-permute-start.7 = (bf16[64,192]{1,0:T(8,128)(2,1)S(1)}, bf16[64,192]{1,0:T(8,128)(2,1)S(1)}, u32[]{:S(2)}, u32[]{:S(2)}) collective-permute-start(bf16[64,192]{1,0:T(8,128)(2,1)S(1)} %pad_maximum_fusion.7), channel_id=1, source_target_pairs={{30,0},{28,2},{2,4},{0,6},{6,8},{4,10},{10,12},{8,14},{14,16},{12,... | collective-permute-start | bytes 73736 | tf_op jit(solution)/shard_map/ppermute | solution.py:431
  36.0 1.3 %collective-permute-start.8 = (bf16[168,128]{1,0:T(8,128)(2,1)S(1)}, bf16[168,128]{1,0:T(8,128)(2,1)S(1)}, u32[]{:S(2)}, u32[]{:S(2)}) collective-permute-start(bf16[168,128]{1,0:T(8,128)(2,1)S(1)} %get-tuple-element.42), channel_id=1, source_target_pairs={{1,0},{0,1},{3,2},{2,3},{5,4},{4,5},{7,6},{6,7},{9,8},{8,9},{11,10... | collective-permute-start | bytes 129032 | tf_op jit(solution)/shard_map/ppermute | solution.py:453
  37.3 5.1 %collective-permute-start.11 = (bf16[168,128]{1,0:T(8,128)(2,1)S(1)}, bf16[168,128]{1,0:T(8,128)(2,1)S(1)}, u32[]{:S(2)}, u32[]{:S(2)}) collective-permute-start(bf16[168,128]{1,0:T(8,128)(2,1)S(1)} %add_convert_fusion.2), channel_id=1, source_target_pairs={{6,0},{4,2},{2,4},{0,6},{14,8},{12,10},{10,12},{8,14},{22,16},{20,... | collective-permute-start | bytes 129032 | tf_op jit(solution)/shard_map/ppermute | solution.py:453
  37.4 5.5 %collective-permute-start.10 = (bf16[168,128]{1,0:T(8,128)(2,1)S(1)}, bf16[168,128]{1,0:T(8,128)(2,1)S(1)}, u32[]{:S(2)}, u32[]{:S(2)}) collective-permute-start(bf16[168,128]{1,0:T(8,128)(2,1)S(1)} %add_convert_fusion.2), channel_id=1, source_target_pairs={{4,0},{0,4},{12,8},{8,12},{20,16},{16,20},{28,24},{24,28},{5,1},{1... | collective-permute-start | bytes 129032 | tf_op jit(solution)/shard_map/ppermute | solution.py:453
  40.3 4.0 %collective-permute-start.9 = (bf16[168,128]{1,0:T(8,128)(2,1)S(1)}, bf16[168,128]{1,0:T(8,128)(2,1)S(1)}, u32[]{:S(2)}, u32[]{:S(2)}) collective-permute-start(bf16[168,128]{1,0:T(8,128)(2,1)S(1)} %add_convert_fusion.2), channel_id=1, source_target_pairs={{2,0},{0,2},{3,1},{1,3},{6,4},{4,6},{7,5},{5,7},{10,8},{8,10},{11,... | collective-permute-start | bytes 129032 | tf_op jit(solution)/shard_map/ppermute | solution.py:453
  44.4 6.0 %collective-permute-start.14 = (bf16[168,128]{1,0:T(8,128)(2,1)S(1)}, bf16[168,128]{1,0:T(8,128)(2,1)S(1)}, u32[]{:S(2)}, u32[]{:S(2)}) collective-permute-start(bf16[168,128]{1,0:T(8,128)(2,1)S(1)} %add_convert_fusion.1), channel_id=1, source_target_pairs={{24,0},{28,4},{16,8},{20,12},{8,16},{12,20},{0,24},{4,28},{25,1},{... | collective-permute-start | bytes 129032 | tf_op jit(solution)/shard_map/ppermute | solution.py:453
  46.4 4.9 %collective-permute-start.13 = (bf16[168,128]{1,0:T(8,128)(2,1)S(1)}, bf16[168,128]{1,0:T(8,128)(2,1)S(1)}, u32[]{:S(2)}, u32[]{:S(2)}) collective-permute-start(bf16[168,128]{1,0:T(8,128)(2,1)S(1)} %add_convert_fusion.1), channel_id=1, source_target_pairs={{16,0},{20,4},{24,8},{28,12},{0,16},{4,20},{8,24},{12,28},{17,1},{... | collective-permute-start | bytes 129032 | tf_op jit(solution)/shard_map/ppermute | solution.py:453
  46.4 4.9 %collective-permute-start.12 = (bf16[168,128]{1,0:T(8,128)(2,1)S(1)}, bf16[168,128]{1,0:T(8,128)(2,1)S(1)}, u32[]{:S(2)}, u32[]{:S(2)}) collective-permute-start(bf16[168,128]{1,0:T(8,128)(2,1)S(1)} %add_convert_fusion.1), channel_id=1, source_target_pairs={{8,0},{12,4},{0,8},{4,12},{24,16},{28,20},{16,24},{20,28},{9,1},{1... | collective-permute-start | bytes 129032 | tf_op jit(solution)/shard_map/ppermute | solution.py:453
  51.4 1.3 %collective-permute-start.15 = (bf16[168,128]{1,0:T(8,128)(2,1)S(1)}, bf16[168,128]{1,0:T(8,128)(2,1)S(1)}, u32[]{:S(2)}, u32[]{:S(2)}) collective-permute-start(bf16[168,128]{1,0:T(8,128)(2,1)S(1)} %add_convert_fusion.mine), channel_id=1, source_target_pairs={{1,0},{0,1},{3,2},{2,3},{5,4},{4,5},{7,6},{6,7},{9,8},{8,9},{11,10... | collective-permute-start | bytes 129032 | tf_op jit(solution)/shard_map/ppermute | solution.py:453

commit v9 on v8

--- a/solution.py
+++ b/solution.py
@@ -179,33 +179,38 @@
             bias[h * CELLS + j * 24 : h * CELLS + j * 24 + 24, :] = moved[h * 24 : h * 24 + 24, :]
 
 
+def by_head(rows):
+    return jnp.concatenate([rows * head_mask(h) for h in range(HEADS)], 0)
+
+
 def attend(q, k, v, bias, prob):
+    scores = dot_nt(by_head(q), k)
+    for h in range(HEADS):
+        rows = slice(h * CELLS, (h + 1) * CELLS)
+        score = scores[rows] * HEAD ** (-0.5) + bias[rows, :]
+        expo = jnp.exp(score - jnp.max(score, -1, keepdims=True))
+        prob[rows, :] = (expo * (1.0 / jnp.sum(expo, -1, keepdims=True))).astype(HALF)
     mixed = jnp.zeros((CELLS, WIDTH), FULL)
     for h in range(HEADS):
-        rows = slice(h * CELLS, (h + 1) * CELLS)
-        score = dot_nt(q * head_mask(h), k) * HEAD ** (-0.5) + bias[rows, :]
-        expo = jnp.exp(score - jnp.max(score, -1, keepdims=True))
-        weights = (expo * (1.0 / jnp.sum(expo, -1, keepdims=True))).astype(HALF)
-        prob[rows, :] = weights
-        mixed = jnp.where(head_lanes(h), dot(weights, v), mixed)
+        term = dot(prob[h * CELLS : (h + 1) * CELLS, :], v)
+        mixed = jnp.where(head_lanes(h), term, mixed)
     return mixed.astype(HALF)
 
 
 def attend_back(dmixed, q, k, v, prob):
-    dq = jnp.zeros((CELLS, WIDTH), FULL)
-    dk = jnp.zeros((CELLS, WIDTH), FULL)
-    dv = jnp.zeros((CELLS, WIDTH), FULL)
+    dheads = by_head(dmixed)
+    dweights = dot_nt(dheads, v)
+    dv = dot_tn(prob[...], dheads)
+    dscores = []
     for h in range(HEADS):
         rows = slice(h * CELLS, (h + 1) * CELLS)
-        weights = prob[rows, :]
-        dhead = dmixed * head_mask(h)
-        full = weights.astype(FULL)
-        dweights = dot_nt(dhead, v)
-        inner = jnp.sum(dweights * full, -1, keepdims=True)
-        dscore = (full * (dweights - inner) * HEAD ** (-0.5)).astype(HALF)
-        dv = dv + dot_tn(weights, dhead)
-        dq = jnp.where(head_lanes(h), dot(dscore, k), dq)
-        dk = dk + dot_tn(dscore, q * head_mask(h))
+        full = prob[rows, :].astype(FULL)
+        inner = jnp.sum(dweights[rows] * full, -1, keepdims=True)
+        dscores.append((full * (dweights[rows] - inner) * HEAD ** (-0.5)).astype(HALF))
+    dk = dot_tn(jnp.concatenate(dscores, 0), by_head(q))
+    dq = jnp.zeros((CELLS, WIDTH), FULL)
+    for h in range(HEADS):
+        dq = jnp.where(head_lanes(h), dot(dscores[h], k), dq)
     return dq.astype(HALF), dk.astype(HALF), dv.astype(HALF)
 
 
@@ -308,10 +313,9 @@
     emb[224:256, :] = jnp.zeros((32, WIDTH), HALF)
     fill_columns(cols)
     fill_select(select)
-    wait("tbl")
+    wait("tbl", "upper", "surface", "to_inner", "uembed", "sembed", "gains", "wqkv")
     table_rows(have["tbl"], 0, table)
     build_bias(table, cols, xs, bias, None)
-    wait("upper", "surface", "to_inner", "uembed", "sembed", "gains", "wqkv")
     section = lax.axis_index("section")
     patch = gather_patches(have["upper"], have["surface"], section, select, ff, ft)
     patch = dot(have["to_inner"][...], patch).astype(HALF)

time: 53.6 us -> 52.4 us (0.978)
  Pallas kernels: 13.3 us -> 12 us
    pallas_call x5, Pallas kernels: 13.3 us -> 12 us  [call(): pl.pallas_call(kernel, out_shape=outs, in_specs=[spec for a in args], out...]
where the time goes in v9:
time: 52.4 us; the launch traced here: 52.2 us
  waiting for transfers between devices  20.1 us (38%)
  starting transfers between devices  18.3 us (35%)
  Pallas kernels  12 us (23%)
  between operations  0.87 us (2%)
  local copies, waits for them, and re-layouts  0.77 us (1%)
    ppermute x8, waiting for transfers between devices, fetch(): return lax.ppermute(block, tuple(axes), pairs)  12.4 us
    pallas_call x5, Pallas kernels, call(): pl.pallas_call(kernel, out_shape=outs, in_specs=[spec for a in args], out...  12 us
    ppermute x8, starting transfers between devices, fetch(): return lax.ppermute(block, tuple(axes), pairs)  10.1 us
    ppermute x8, starting transfers between devices, swap(): return lax.ppermute(block, tuple(axes), pairs)  8.14 us
    ppermute x8, waiting for transfers between devices, swap(): return lax.ppermute(block, tuple(axes), pairs)  7.69 us
  transfers between devices with their start and end apart: 16, of which 13 were waited for; matrix products, arithmetic and copies ran while one was open for 1% of the time, Pallas kernels for 2%

profile of v9, /device:TPU:0, one launch (start us, length us, event | category | flops | bytes accessed | tf_op | source)
XLA Modules:
  0.0 52.2 jit_solution(10504147851011490542)
XLA Ops:
  0.7 4.6 %shard_map.193 = (bf16[144,256]{1,0:T(8,128)(2,1)S(1)}, bf16[144,192]{1,0:T(8,128)(2,1)S(1)}, bf16[3,144,192]{2,1,0:T(8,128)(2,1)S(1)}, bf16[864,144]{1,0:T(8,12...) custom-call(f32[12,1,3312]{2,1,0:T(1,128)} %bitcast.6, ...), custom_call_target="tpu_custom_call" | custom-call | flops 1000000 | bytes 1000000 | tf_op jit(solution)/shard_map/pallas_call | solution.py:408
  5.3 0.5 collective-permute-start
  5.8 0.9 %collective-permute-done.after = bf16[192,192]{1,0:T(8,128)(2,1)S(1)} collective-permute-done((bf16[192,192]{1,0:T(8,128)(2,1)S(1)}, bf16[192,192]{1,0:T(8,128)(2,1)S(1)}, u32[]{:S(2)}, u32[]{:S(2)}) %collective-permute-start) | collective-permute-done | bytes 73760 | tf_op jit(solution)/shard_map/ppermute | solution.py:435
  6.8 6.0 %collective-permute-start.1 = (bf16[96,192]{1,0:T(8,128)(2,1)S(1)}, bf16[96,192]{1,0:T(8,128)(2,1)S(1)}, u32[]{:S(2)}, u32[]{:S(2)}) collective-permute-start(bf16[96,192]{1,0:T(8,128)(2,1)S(1)} %pad_maximum_fusion.1), channel_id=1, source_target_pairs={{4,0},{8,4},{12,8},{16,12},{20,16},{24,20},{28,24},{0,28},{5,1},{9... | collective-permute-start | bytes 110600 | tf_op jit(solution)/shard_map/ppermute | solution.py:435
  12.8 1.6 %collective-permute-start.2 = (bf16[96,192]{1,0:T(8,128)(2,1)S(1)}, bf16[96,192]{1,0:T(8,128)(2,1)S(1)}, u32[]{:S(2)}, u32[]{:S(2)}) collective-permute-start(bf16[96,192]{1,0:T(8,128)(2,1)S(1)} %pad_maximum_fusion.2), channel_id=1, source_target_pairs={{2,0},{0,2},{3,1},{1,3},{6,4},{4,6},{7,5},{5,7},{10,8},{8,10},{11,... | collective-permute-start | bytes 110600 | tf_op jit(solution)/shard_map/ppermute | solution.py:435
  14.3 0.5 %collective-permute-start.3 = (bf16[96,192]{1,0:T(8,128)(2,1)S(1)}, bf16[96,192]{1,0:T(8,128)(2,1)S(1)}, u32[]{:S(2)}, u32[]{:S(2)}) collective-permute-start(bf16[96,192]{1,0:T(8,128)(2,1)S(1)} %pad_maximum_fusion.3), channel_id=1, source_target_pairs={{6,0},{4,2},{10,4},{8,6},{14,8},{12,10},{18,12},{16,14},{22,16},{2... | collective-permute-start | bytes 110600 | tf_op jit(solution)/shard_map/ppermute | solution.py:435
  14.9 0.9 %shard_map.194.refs_9_ = f32[864,144]{1,0:T(8,128)S(1)} custom-call(f32[12,1,3312]{2,1,0:T(1,128)S(1)} %bitcast.7, bf16[192,192]{1,0:T(8,128)(2,1)S(1)} %collective-permute-done.after), custom_call_target="tpu_custom_call" | custom-call | flops 1000000 | bytes 1000000 | tf_op jit(solution)/shard_map/pallas_call | solution.py:408
  15.8 1.1 %collective-permute-done.2.refs_2_ = bf16[96,192]{1,0:T(8,128)(2,1)S(1)} collective-permute-done((bf16[96,192]{1,0:T(8,128)(2,1)S(1)}, bf16[96,192]{1,0:T(8,128)(2,1)S(1)}, u32[]{:S(2)}, u32[]{:S(2)}) %collective-permute-start.2) | collective-permute-done | bytes 36896 | tf_op jit(solution)/shard_map/ppermute | solution.py:435
  16.9 2.5 %collective-permute-done.3.refs_3_ = bf16[96,192]{1,0:T(8,128)(2,1)S(1)} collective-permute-done((bf16[96,192]{1,0:T(8,128)(2,1)S(1)}, bf16[96,192]{1,0:T(8,128)(2,1)S(1)}, u32[]{:S(2)}, u32[]{:S(2)}) %collective-permute-start.3) | collective-permute-done | bytes 36896 | tf_op jit(solution)/shard_map/ppermute | solution.py:435
  19.4 3.6 %shard_map.195 = (bf16[128,192]{1,0:T(8,128)(2,1)S(1)}, bf16[32,192]{1,0:T(8,128)(2,1)S(1)}, bf16[32,192]{1,0:T(8,128)(2,1)S(1)}, bf16[32,192]{1,0:T(8,128)(2,1)S(1)}, bf16[32,192]{1,0:T(8,128)(2,1)S(1)}) custom-call(bf16[96,192]{1,0:T(8,128)(2,1)S(1)} %pad_maximum_fusion.refs_0_, bf16[96,192]{1,0:T(8,128)(2,1)S(1)} %collective-permute-done.1.refs_1_, ...), custom_call_target="tpu_custom_call" | custom-call | flops 1000000 | bytes 1000000 | tf_op jit(solution)/shard_map/pallas_call | solution.py:408
  23.0 0.1 collective-permute-start.4
  23.1 1.2 %collective-permute-done.4 = bf16[128,192]{1,0:T(8,128)(2,1)S(1)} collective-permute-done((bf16[128,192]{1,0:T(8,128)(2,1)S(1)}, bf16[128,192]{1,0:T(8,128)(2,1)S(1)}, u32[]{:S(2)}, u32[]{:S(2)}) %collective-permute-start.4) | collective-permute-done | bytes 49184 | tf_op jit(solution)/shard_map/ppermute | solution.py:435
  24.4 0.6 %collective-permute-start.6 = (bf16[64,192]{1,0:T(8,128)(2,1)S(1)}, bf16[64,192]{1,0:T(8,128)(2,1)S(1)}, u32[]{:S(2)}, u32[]{:S(2)}) collective-permute-start(bf16[64,192]{1,0:T(8,128)(2,1)S(1)} %pad_maximum_fusion.6), channel_id=1, source_target_pairs={{2,0},{0,2},{3,1},{1,3},{6,4},{4,6},{7,5},{5,7},{10,8},{8,10},{11,... | collective-permute-start | bytes 73736 | tf_op jit(solution)/shard_map/ppermute | solution.py:435
  25.0 0.8 %collective-permute-start.7 = (bf16[64,192]{1,0:T(8,128)(2,1)S(1)}, bf16[64,192]{1,0:T(8,128)(2,1)S(1)}, u32[]{:S(2)}, u32[]{:S(2)}) collective-permute-start(bf16[64,192]{1,0:T(8,128)(2,1)S(1)} %pad_maximum_fusion.7), channel_id=1, source_target_pairs={{30,0},{28,2},{2,4},{0,6},{6,8},{4,10},{10,12},{8,14},{14,16},{12,... | collective-permute-start | bytes 73736 | tf_op jit(solution)/shard_map/ppermute | solution.py:435
  25.9 5.1 %collective-permute-done.5.refs_1_ = bf16[64,192]{1,0:T(8,128)(2,1)S(1)} collective-permute-done((bf16[64,192]{1,0:T(8,128)(2,1)S(1)}, bf16[64,192]{1,0:T(8,128)(2,1)S(1)}, u32[]{:S(2)}, u32[]{:S(2)}) %collective-permute-start.5) | collective-permute-done | bytes 24608 | tf_op jit(solution)/shard_map/ppermute | solution.py:435
  31.0 1.6 %collective-permute-done.7.refs_3_ = bf16[64,192]{1,0:T(8,128)(2,1)S(1)} collective-permute-done((bf16[64,192]{1,0:T(8,128)(2,1)S(1)}, bf16[64,192]{1,0:T(8,128)(2,1)S(1)}, u32[]{:S(2)}, u32[]{:S(2)}) %collective-permute-start.7) | collective-permute-done | bytes 24608 | tf_op jit(solution)/shard_map/ppermute | solution.py:435
  32.6 2.1 %shard_map.196 = (bf16[2,6,12,192]{3,2,1,0:T(8,128)(2,1)S(1)}, bf16[168,128]{1,0:T(8,128)(2,1)S(1)}, bf16[168,128]{1,0:T(8,128)(2,1)S(1)}) custom-call(bf16[64,192]{1,0:T(8,128)(2,1)S(1)} %pad_maximum_fusion.4.refs_0_, bf16[64,192]{1,0:T(8,128)(2,1)S(1)} %collective-permute-done.5.refs_1_, bf16[64,192]{1,0:T(8,128)(2,1)S(1)} %collective-permute-done.6.refs_2_, ...), custom_call_target="tpu_custom_call" | custom-call | flops 1000000 | bytes 1000000 | tf_op jit(solution)/shard_map/pallas_call | solution.py:408
  34.8 0.1 collective-permute-start.8
  34.8 1.2 %collective-permute-done.8 = bf16[168,128]{1,0:T(8,128)(2,1)S(1)} collective-permute-done((bf16[168,128]{1,0:T(8,128)(2,1)S(1)}, bf16[168,128]{1,0:T(8,128)(2,1)S(1)}, u32[]{:S(2)}, u32[]{:S(2)}) %collective-permute-start.8) | collective-permute-done | bytes 43040 | tf_op jit(solution)/shard_map/ppermute | solution.py:457
  36.1 0.1 collective-permute-start.11
  36.1 2.9 %collective-permute-start.10 = (bf16[168,128]{1,0:T(8,128)(2,1)S(1)}, bf16[168,128]{1,0:T(8,128)(2,1)S(1)}, u32[]{:S(2)}, u32[]{:S(2)}) collective-permute-start(bf16[168,128]{1,0:T(8,128)(2,1)S(1)} %add_convert_fusion.2), channel_id=1, source_target_pairs={{4,0},{0,4},{12,8},{8,12},{20,16},{16,20},{28,24},{24,28},{5,1},{1... | collective-permute-start | bytes 129032 | tf_op jit(solution)/shard_map/ppermute | solution.py:457
  39.1 0.5 %collective-permute-start.9 = (bf16[168,128]{1,0:T(8,128)(2,1)S(1)}, bf16[168,128]{1,0:T(8,128)(2,1)S(1)}, u32[]{:S(2)}, u32[]{:S(2)}) collective-permute-start(bf16[168,128]{1,0:T(8,128)(2,1)S(1)} %add_convert_fusion.2), channel_id=1, source_target_pairs={{2,0},{0,2},{3,1},{1,3},{6,4},{4,6},{7,5},{5,7},{10,8},{8,10},{11,... | collective-permute-start | bytes 129032 | tf_op jit(solution)/shard_map/ppermute | solution.py:457
  39.6 1.6 %collective-permute-done.11 = bf16[168,128]{1,0:T(8,128)(2,1)S(1)} collective-permute-done((bf16[168,128]{1,0:T(8,128)(2,1)S(1)}, bf16[168,128]{1,0:T(8,128)(2,1)S(1)}, u32[]{:S(2)}, u32[]{:S(2)}) %collective-permute-start.11) | collective-permute-done | bytes 43040 | tf_op jit(solution)/shard_map/ppermute | solution.py:457
  41.2 0.4 collective-permute-done.10
  41.6 1.5 %collective-permute-done.9 = bf16[168,128]{1,0:T(8,128)(2,1)S(1)} collective-permute-done((bf16[168,128]{1,0:T(8,128)(2,1)S(1)}, bf16[168,128]{1,0:T(8,128)(2,1)S(1)}, u32[]{:S(2)}, u32[]{:S(2)}) %collective-permute-start.9) | collective-permute-done | bytes 43040 | tf_op jit(solution)/shard_map/ppermute | solution.py:457
  43.1 2.0 %collective-permute-start.14 = (bf16[168,128]{1,0:T(8,128)(2,1)S(1)}, bf16[168,128]{1,0:T(8,128)(2,1)S(1)}, u32[]{:S(2)}, u32[]{:S(2)}) collective-permute-start(bf16[168,128]{1,0:T(8,128)(2,1)S(1)} %add_convert_fusion.1), channel_id=1, source_target_pairs={{24,0},{28,4},{16,8},{20,12},{8,16},{12,20},{0,24},{4,28},{25,1},{... | collective-permute-start | bytes 129032 | tf_op jit(solution)/shard_map/ppermute | solution.py:457
  45.1 2.4 %collective-permute-start.12 = (bf16[168,128]{1,0:T(8,128)(2,1)S(1)}, bf16[168,128]{1,0:T(8,128)(2,1)S(1)}, u32[]{:S(2)}, u32[]{:S(2)}) collective-permute-start(bf16[168,128]{1,0:T(8,128)(2,1)S(1)} %add_convert_fusion.1), channel_id=1, source_target_pairs={{8,0},{12,4},{0,8},{4,12},{24,16},{28,20},{16,24},{20,28},{9,1},{1... | collective-permute-start | bytes 129032 | tf_op jit(solution)/shard_map/ppermute | solution.py:457
  47.6 1.6 %collective-permute-done.14 = bf16[168,128]{1,0:T(8,128)(2,1)S(1)} collective-permute-done((bf16[168,128]{1,0:T(8,128)(2,1)S(1)}, bf16[168,128]{1,0:T(8,128)(2,1)S(1)}, u32[]{:S(2)}, u32[]{:S(2)}) %collective-permute-start.14) | collective-permute-done | bytes 43040 | tf_op jit(solution)/shard_map/ppermute | solution.py:457
  49.2 0.9 %collective-permute-done.13 = bf16[168,128]{1,0:T(8,128)(2,1)S(1)} collective-permute-done((bf16[168,128]{1,0:T(8,128)(2,1)S(1)}, bf16[168,128]{1,0:T(8,128)(2,1)S(1)}, u32[]{:S(2)}, u32[]{:S(2)}) %collective-permute-start.13) | collective-permute-done | bytes 43040 | tf_op jit(solution)/shard_map/ppermute | solution.py:457
  50.2 0.7 %copy.21 = bf16[2,6,12,192]{3,0,2,1:T(2,128)(2,1)} copy(bf16[2,6,12,192]{3,2,1,0:T(8,128)(2,1)S(1)} %get-tuple-element.45) | data formatting | bytes 110592
  50.9 0.5 collective-permute-done.15.other
  51.4 0.8 %shard_map.197 = (f32[160,192]{1,0:T(8,128)}, f32[64,192]{1,0:T(8,128)}) custom-call(bf16[168,128]{1,0:T(8,128)(2,1)S(1)} %add_convert_fusion.mine, bf16[168,128]{1,0:T(8,128)(2,1)S(1)} %collective-permute-done.15.other), custom_call_target="tpu_custom_call" | custom-call | flops 1000000 | bytes 1000000 | tf_op jit(solution)/shard_map/pallas_call | solution.py:408
  (39 shorter events, 0.4 us)
Async XLA Ops:
  0.6 14.2 %copy-start.4 = (f32[2,1,1,6,3312]{4,2,3,1,0:T(1,128)S(1)}, f32[2,1,1,6,3312]{4,2,3,1,0:T(1,128)}, u32[]{:S(2)}) copy-start(f32[2,1,1,6,3312]{4,2,3,1,0:T(1,128)} %param.27) | copy-start | bytes 476932
  0.6 18.7 %copy-start.3 = (bf16[2,192,192]{2,1,0:T(8,128)(2,1)S(1)}, bf16[2,192,192]{2,1,0:T(8,128)(2,1)}, u32[]{:S(2)}) copy-start(bf16[2,192,192]{2,1,0:T(8,128)(2,1)} %refs_6_.5) | copy-start | bytes 442372
  0.7 18.7 %copy-start.5 = (bf16[288,384]{1,0:T(8,128)(2,1)S(1)}, bf16[288,384]{1,0:T(8,128)(2,1)}, u32[]{:S(2)}) copy-start(bf16[288,384]{1,0:T(8,128)(2,1)} %constant.17.clone.refs_10_) | copy-start | bytes 663556
  0.7 18.7 %copy-start.6 = (bf16[256,144]{1,0:T(8,128)(2,1)S(1)}, bf16[256,144]{1,0:T(8,128)(2,1)}, u32[]{:S(2)}) copy-start(bf16[256,144]{1,0:T(8,128)(2,1)} %constant.18.clone.refs_11_) | copy-start | bytes 221188
  5.3 1.5 %collective-permute-start = (bf16[192,192]{1,0:T(8,128)(2,1)S(1)}, bf16[192,192]{1,0:T(8,128)(2,1)S(1)}, u32[]{:S(2)}, u32[]{:S(2)}) collective-permute-start(bf16[192,192]{1,0:T(8,128)(2,1)S(1)} %get-tuple-element.25), channel_id=1, source_target_pairs={{1,0},{0,1},{3,2},{2,3},{5,4},{4,5},{7,6},{6,7},{9,8},{8,9},{11,10... | collective-permute-start | bytes 221192 | tf_op jit(solution)/shard_map/ppermute | solution.py:435
  6.8 12.6 %copy-start.2 = (bf16[2,192,576]{2,1,0:T(8,128)(2,1)S(1)}, bf16[2,192,576]{2,1,0:T(8,128)(2,1)}, u32[]{:S(2)}) copy-start(bf16[2,192,576]{2,1,0:T(8,128)(2,1)} %refs_5_.5) | copy-start | bytes 1327108
  6.8 9.0 %collective-permute-start.1 = (bf16[96,192]{1,0:T(8,128)(2,1)S(1)}, bf16[96,192]{1,0:T(8,128)(2,1)S(1)}, u32[]{:S(2)}, u32[]{:S(2)}) collective-permute-start(bf16[96,192]{1,0:T(8,128)(2,1)S(1)} %pad_maximum_fusion.1), channel_id=1, source_target_pairs={{4,0},{8,4},{12,8},{16,12},{20,16},{24,20},{28,24},{0,28},{5,1},{9... | collective-permute-start | bytes 110600 | tf_op jit(solution)/shard_map/ppermute | solution.py:435
  12.8 4.2 %collective-permute-start.2 = (bf16[96,192]{1,0:T(8,128)(2,1)S(1)}, bf16[96,192]{1,0:T(8,128)(2,1)S(1)}, u32[]{:S(2)}, u32[]{:S(2)}) collective-permute-start(bf16[96,192]{1,0:T(8,128)(2,1)S(1)} %pad_maximum_fusion.2), channel_id=1, source_target_pairs={{2,0},{0,2},{3,1},{1,3},{6,4},{4,6},{7,5},{5,7},{10,8},{8,10},{11,... | collective-permute-start | bytes 110600 | tf_op jit(solution)/shard_map/ppermute | solution.py:435
  14.3 5.0 %collective-permute-start.3 = (bf16[96,192]{1,0:T(8,128)(2,1)S(1)}, bf16[96,192]{1,0:T(8,128)(2,1)S(1)}, u32[]{:S(2)}, u32[]{:S(2)}) collective-permute-start(bf16[96,192]{1,0:T(8,128)(2,1)S(1)} %pad_maximum_fusion.3), channel_id=1, source_target_pairs={{6,0},{4,2},{10,4},{8,6},{14,8},{12,10},{18,12},{16,14},{22,16},{2... | collective-permute-start | bytes 110600 | tf_op jit(solution)/shard_map/ppermute | solution.py:435
  14.9 4.5 %copy-start.1 = (bf16[2,768,192]{1,2,0:T(8,128)(2,1)S(1)}, bf16[2,768,192]{1,2,0:T(8,128)(2,1)}, u32[]{:S(2)}) copy-start(bf16[2,768,192]{1,2,0:T(8,128)(2,1)} %param.26) | copy-start | bytes 1769476
  14.9 4.5 %copy-start = (bf16[2,192,768]{2,1,0:T(8,128)(2,1)S(1)}, bf16[2,192,768]{2,1,0:T(8,128)(2,1)}, u32[]{:S(2)}) copy-start(bf16[2,192,768]{2,1,0:T(8,128)(2,1)} %refs_7_.5) | copy-start | bytes 1769476
  14.9 4.5 %copy-start.9 = (f32[2,2,192]{2,1,0:T(2,128)S(1)}, f32[2,2,192]{2,1,0:T(2,128)}, u32[]{:S(2)}) copy-start(f32[2,2,192]{2,1,0:T(2,128)} %refs_4_.5) | copy-start | bytes 9220
  23.0 1.3 %collective-permute-start.4 = (bf16[128,192]{1,0:T(8,128)(2,1)S(1)}, bf16[128,192]{1,0:T(8,128)(2,1)S(1)}, u32[]{:S(2)}, u32[]{:S(2)}) collective-permute-start(bf16[128,192]{1,0:T(8,128)(2,1)S(1)} %get-tuple-element.30), channel_id=1, source_target_pairs={{1,0},{0,1},{3,2},{2,3},{5,4},{4,5},{7,6},{6,7},{9,8},{8,9},{11,10... | collective-permute-start | bytes 147464 | tf_op jit(solution)/shard_map/ppermute | solution.py:435
  24.3 6.7 %collective-permute-start.5 = (bf16[64,192]{1,0:T(8,128)(2,1)S(1)}, bf16[64,192]{1,0:T(8,128)(2,1)S(1)}, u32[]{:S(2)}, u32[]{:S(2)}) collective-permute-start(bf16[64,192]{1,0:T(8,128)(2,1)S(1)} %pad_maximum_fusion.5), channel_id=1, source_target_pairs={{28,0},{0,4},{4,8},{8,12},{12,16},{16,20},{20,24},{24,28},{29,1},{... | collective-permute-start | bytes 73736 | tf_op jit(solution)/shard_map/ppermute | solution.py:435
  24.4 8.2 %copy-start.7 = (bf16[192,144]{1,0:T(8,128)(2,1)S(1)}, bf16[192,144]{1,0:T(8,128)(2,1)}, u32[]{:S(2)}) copy-start(bf16[192,144]{1,0:T(8,128)(2,1)} %constant.20.clone.refs_16_) | copy-start | bytes 165892
  24.4 6.6 %collective-permute-start.6 = (bf16[64,192]{1,0:T(8,128)(2,1)S(1)}, bf16[64,192]{1,0:T(8,128)(2,1)S(1)}, u32[]{:S(2)}, u32[]{:S(2)}) collective-permute-start(bf16[64,192]{1,0:T(8,128)(2,1)S(1)} %pad_maximum_fusion.6), channel_id=1, source_target_pairs={{2,0},{0,2},{3,1},{1,3},{6,4},{4,6},{7,5},{5,7},{10,8},{8,10},{11,... | collective-permute-start | bytes 73736 | tf_op jit(solution)/shard_map/ppermute | solution.py:435
  25.0 7.6 %copy-start.8 = (bf16[144,256]{1,0:T(8,128)(2,1)S(1)}, bf16[144,256]{1,0:T(8,128)(2,1)}, u32[]{:S(2)}) copy-start(bf16[144,256]{1,0:T(8,128)(2,1)} %constant.19.clone.refs_15_) | copy-start | bytes 221188
  25.0 7.6 %collective-permute-start.7 = (bf16[64,192]{1,0:T(8,128)(2,1)S(1)}, bf16[64,192]{1,0:T(8,128)(2,1)S(1)}, u32[]{:S(2)}, u32[]{:S(2)}) collective-permute-start(bf16[64,192]{1,0:T(8,128)(2,1)S(1)} %pad_maximum_fusion.7), channel_id=1, source_target_pairs={{30,0},{28,2},{2,4},{0,6},{6,8},{4,10},{10,12},{8,14},{14,16},{12,... | collective-permute-start | bytes 73736 | tf_op jit(solution)/shard_map/ppermute | solution.py:435
  34.8 1.3 %collective-permute-start.8 = (bf16[168,128]{1,0:T(8,128)(2,1)S(1)}, bf16[168,128]{1,0:T(8,128)(2,1)S(1)}, u32[]{:S(2)}, u32[]{:S(2)}) collective-permute-start(bf16[168,128]{1,0:T(8,128)(2,1)S(1)} %get-tuple-element.42), channel_id=1, source_target_pairs={{1,0},{0,1},{3,2},{2,3},{5,4},{4,5},{7,6},{6,7},{9,8},{8,9},{11,10... | collective-permute-start | bytes 129032 | tf_op jit(solution)/shard_map/ppermute | solution.py:457
  36.1 5.1 %collective-permute-start.11 = (bf16[168,128]{1,0:T(8,128)(2,1)S(1)}, bf16[168,128]{1,0:T(8,128)(2,1)S(1)}, u32[]{:S(2)}, u32[]{:S(2)}) collective-permute-start(bf16[168,128]{1,0:T(8,128)(2,1)S(1)} %add_convert_fusion.2), channel_id=1, source_target_pairs={{6,0},{4,2},{2,4},{0,6},{14,8},{12,10},{10,12},{8,14},{22,16},{20,... | collective-permute-start | bytes 129032 | tf_op jit(solution)/shard_map/ppermute | solution.py:457
  36.1 5.5 %collective-permute-start.10 = (bf16[168,128]{1,0:T(8,128)(2,1)S(1)}, bf16[168,128]{1,0:T(8,128)(2,1)S(1)}, u32[]{:S(2)}, u32[]{:S(2)}) collective-permute-start(bf16[168,128]{1,0:T(8,128)(2,1)S(1)} %add_convert_fusion.2), channel_id=1, source_target_pairs={{4,0},{0,4},{12,8},{8,12},{20,16},{16,20},{28,24},{24,28},{5,1},{1... | collective-permute-start | bytes 129032 | tf_op jit(solution)/shard_map/ppermute | solution.py:457
  39.1 4.0 %collective-permute-start.9 = (bf16[168,128]{1,0:T(8,128)(2,1)S(1)}, bf16[168,128]{1,0:T(8,128)(2,1)S(1)}, u32[]{:S(2)}, u32[]{:S(2)}) collective-permute-start(bf16[168,128]{1,0:T(8,128)(2,1)S(1)} %add_convert_fusion.2), channel_id=1, source_target_pairs={{2,0},{0,2},{3,1},{1,3},{6,4},{4,6},{7,5},{5,7},{10,8},{8,10},{11,... | collective-permute-start | bytes 129032 | tf_op jit(solution)/shard_map/ppermute | solution.py:457
  43.1 6.0 %collective-permute-start.14 = (bf16[168,128]{1,0:T(8,128)(2,1)S(1)}, bf16[168,128]{1,0:T(8,128)(2,1)S(1)}, u32[]{:S(2)}, u32[]{:S(2)}) collective-permute-start(bf16[168,128]{1,0:T(8,128)(2,1)S(1)} %add_convert_fusion.1), channel_id=1, source_target_pairs={{24,0},{28,4},{16,8},{20,12},{8,16},{12,20},{0,24},{4,28},{25,1},{... | collective-permute-start | bytes 129032 | tf_op jit(solution)/shard_map/ppermute | solution.py:457
  45.1 4.9 %collective-permute-start.13 = (bf16[168,128]{1,0:T(8,128)(2,1)S(1)}, bf16[168,128]{1,0:T(8,128)(2,1)S(1)}, u32[]{:S(2)}, u32[]{:S(2)}) collective-permute-start(bf16[168,128]{1,0:T(8,128)(2,1)S(1)} %add_convert_fusion.1), channel_id=1, source_target_pairs={{16,0},{20,4},{24,8},{28,12},{0,16},{4,20},{8,24},{12,28},{17,1},{... | collective-permute-start | bytes 129032 | tf_op jit(solution)/shard_map/ppermute | solution.py:457
  45.1 4.9 %collective-permute-start.12 = (bf16[168,128]{1,0:T(8,128)(2,1)S(1)}, bf16[168,128]{1,0:T(8,128)(2,1)S(1)}, u32[]{:S(2)}, u32[]{:S(2)}) collective-permute-start(bf16[168,128]{1,0:T(8,128)(2,1)S(1)} %add_convert_fusion.1), channel_id=1, source_target_pairs={{8,0},{12,4},{0,8},{4,12},{24,16},{28,20},{16,24},{20,28},{9,1},{1... | collective-permute-start | bytes 129032 | tf_op jit(solution)/shard_map/ppermute | solution.py:457
  50.1 1.3 %collective-permute-start.15 = (bf16[168,128]{1,0:T(8,128)(2,1)S(1)}, bf16[168,128]{1,0:T(8,128)(2,1)S(1)}, u32[]{:S(2)}, u32[]{:S(2)}) collective-permute-start(bf16[168,128]{1,0:T(8,128)(2,1)S(1)} %add_convert_fusion.mine), channel_id=1, source_target_pairs={{1,0},{0,1},{3,2},{2,3},{5,4},{4,5},{7,6},{6,7},{9,8},{8,9},{11,10... | collective-permute-start | bytes 129032 | tf_op jit(solution)/shard_map/ppermute | solution.py:457

commit v10 on v9

--- a/solution.py
+++ b/solution.py
@@ -357,8 +357,8 @@
     parts, rest = refs[:4], refs[4:]
     gains, wqkv, wproj, wup, wdown, bias, into, out_of, send_o = rest[:9]
     keep, stack, prob = rest[9:13], rest[13], rest[14]
-    for n in range(4):
-        stack[n * 96 : n * 96 + 96, :] = parts[n][...]
+    for n, part in zip(order, parts):
+        stack[n * 96 : n * 96 + 96, :] = part[...]
     both = dot(into[...], stack[...])
     x, dflat = both[:CELLS], both[CELLS:].astype(HALF)
     gains, wqkv, wproj, wup, wdown = (w.at[1] for w in (gains, wqkv, wproj, wup, wdown))
@@ -378,8 +378,8 @@
     parts, rest = refs[:4], refs[4:]
     gains, wqkv, wproj, wup, wdown, patch, x_i, qkv_i, prob, resid, slope, into, out_of = rest[:13]
     grad_o, mine_o, other_o, stack, terms = rest[13:]
-    for n in range(4):
-        stack[n * 64 : n * 64 + 64, :] = parts[n][...]
+    for n, part in zip(order, parts):
+        stack[n * 64 : n * 64 + 64, :] = part[...]
     dflat = dot(into[...], stack[...]).astype(HALF)
     qkv = tuple(qkv_i[n] for n in range(3))
     gains, wqkv, wproj, wup, wdown = (w.at[0] for w in (gains, wqkv, wproj, wup, wdown))
@@ -435,10 +435,13 @@
     return lax.ppermute(block, tuple(axes), pairs)
 
 
+order = (3, 1, 2, 0)
+
+
 def exchange(keep, got, way):
     pitch = got.shape[0] // 4
     blocks = []
-    for n in range(4):
+    for n in order:
         block = jnp.concatenate((keep[n], got[n * pitch : (n + 1) * pitch]), 0)
         blocks.append(fetch(block, {"lat": way * (n // 2), "lon": way * (n % 2)}))
     return blocks

time: 52.4 us -> 51.3 us (0.979)
  waiting for transfers between devices: 20.1 us -> 17.4 us
  starting transfers between devices: 18.3 us -> 20 us
    ppermute x8, waiting for transfers between devices: 12.4 us -> 9.77 us  [fetch(): return lax.ppermute(block, tuple(axes), pairs)]
    ppermute x8, starting transfers between devices: 10.1 us -> 11.8 us  [fetch(): return lax.ppermute(block, tuple(axes), pairs)]
where the time goes in v10:
time: 51.3 us; the launch traced here: 51.2 us
  starting transfers between devices  20 us (39%)
  waiting for transfers between devices  17.4 us (34%)
  Pallas kernels  12 us (23%)
  between operations  0.85 us (2%)
  local copies, waits for them, and re-layouts  0.77 us (2%)
    pallas_call x5, Pallas kernels, call(): pl.pallas_call(kernel, out_shape=outs, in_specs=[spec for a in args], out...  12 us
    ppermute x8, starting transfers between devices, fetch(): return lax.ppermute(block, tuple(axes), pairs)  11.8 us
    ppermute x8, waiting for transfers between devices, fetch(): return lax.ppermute(block, tuple(axes), pairs)  9.77 us
    ppermute x8, starting transfers between devices, swap(): return lax.ppermute(block, tuple(axes), pairs)  8.14 us
    ppermute x8, waiting for transfers between devices, swap(): return lax.ppermute(block, tuple(axes), pairs)  7.63 us
  transfers between devices with their start and end apart: 16, of which 13 were waited for; matrix products, arithmetic and copies ran while one was open for 1% of the time, Pallas kernels for 2%

profile of v10, /device:TPU:0, one launch (start us, length us, event | category | flops | bytes accessed | tf_op | source)
XLA Modules:
  0.0 51.2 jit_solution(10763806027720576535)
XLA Ops:
  0.7 4.6 %shard_map.193 = (bf16[144,256]{1,0:T(8,128)(2,1)S(1)}, bf16[144,192]{1,0:T(8,128)(2,1)S(1)}, bf16[3,144,192]{2,1,0:T(8,128)(2,1)S(1)}, bf16[864,144]{1,0:T(8,12...) custom-call(f32[12,1,3312]{2,1,0:T(1,128)} %bitcast.6, ...), custom_call_target="tpu_custom_call" | custom-call | flops 1000000 | bytes 1000000 | tf_op jit(solution)/shard_map/pallas_call | solution.py:408
  5.3 0.5 %collective-permute-start = (bf16[192,192]{1,0:T(8,128)(2,1)S(1)}, bf16[192,192]{1,0:T(8,128)(2,1)S(1)}, u32[]{:S(2)}, u32[]{:S(2)}) collective-permute-start(bf16[192,192]{1,0:T(8,128)(2,1)S(1)} %get-tuple-element.25), channel_id=1, source_target_pairs={{1,0},{0,1},{3,2},{2,3},{5,4},{4,5},{7,6},{6,7},{9,8},{8,9},{11,10... | collective-permute-start | bytes 221192 | tf_op jit(solution)/shard_map/ppermute | solution.py:435
  5.8 0.9 %collective-permute-done.after = bf16[192,192]{1,0:T(8,128)(2,1)S(1)} collective-permute-done((bf16[192,192]{1,0:T(8,128)(2,1)S(1)}, bf16[192,192]{1,0:T(8,128)(2,1)S(1)}, u32[]{:S(2)}, u32[]{:S(2)}) %collective-permute-start) | collective-permute-done | bytes 73760 | tf_op jit(solution)/shard_map/ppermute | solution.py:435
  6.8 6.9 %collective-permute-start.1 = (bf16[96,192]{1,0:T(8,128)(2,1)S(1)}, bf16[96,192]{1,0:T(8,128)(2,1)S(1)}, u32[]{:S(2)}, u32[]{:S(2)}) collective-permute-start(bf16[96,192]{1,0:T(8,128)(2,1)S(1)} %pad_maximum_fusion), channel_id=1, source_target_pairs={{6,0},{4,2},{10,4},{8,6},{14,8},{12,10},{18,12},{16,14},{22,16},{2... | collective-permute-start | bytes 110600 | tf_op jit(solution)/shard_map/ppermute | solution.py:435
  13.7 0.6 %collective-permute-start.2 = (bf16[96,192]{1,0:T(8,128)(2,1)S(1)}, bf16[96,192]{1,0:T(8,128)(2,1)S(1)}, u32[]{:S(2)}, u32[]{:S(2)}) collective-permute-start(bf16[96,192]{1,0:T(8,128)(2,1)S(1)} %pad_maximum_fusion.1), channel_id=1, source_target_pairs={{4,0},{8,4},{12,8},{16,12},{20,16},{24,20},{28,24},{0,28},{5,1},{9... | collective-permute-start | bytes 110600 | tf_op jit(solution)/shard_map/ppermute | solution.py:435
  14.3 0.6 %collective-permute-start.3 = (bf16[96,192]{1,0:T(8,128)(2,1)S(1)}, bf16[96,192]{1,0:T(8,128)(2,1)S(1)}, u32[]{:S(2)}, u32[]{:S(2)}) collective-permute-start(bf16[96,192]{1,0:T(8,128)(2,1)S(1)} %pad_maximum_fusion.2), channel_id=1, source_target_pairs={{2,0},{0,2},{3,1},{1,3},{6,4},{4,6},{7,5},{5,7},{10,8},{8,10},{11,... | collective-permute-start | bytes 110600 | tf_op jit(solution)/shard_map/ppermute | solution.py:435
  14.9 0.9 %shard_map.194.refs_9_ = f32[864,144]{1,0:T(8,128)S(1)} custom-call(f32[12,1,3312]{2,1,0:T(1,128)S(1)} %bitcast.7, bf16[192,192]{1,0:T(8,128)(2,1)S(1)} %collective-permute-done.after), custom_call_target="tpu_custom_call" | custom-call | flops 1000000 | bytes 1000000 | tf_op jit(solution)/shard_map/pallas_call | solution.py:408
  15.8 2.0 %collective-permute-done.2.refs_1_ = bf16[96,192]{1,0:T(8,128)(2,1)S(1)} collective-permute-done((bf16[96,192]{1,0:T(8,128)(2,1)S(1)}, bf16[96,192]{1,0:T(8,128)(2,1)S(1)}, u32[]{:S(2)}, u32[]{:S(2)}) %collective-permute-start.2) | collective-permute-done | bytes 36896 | tf_op jit(solution)/shard_map/ppermute | solution.py:435
  17.8 0.6 %collective-permute-done.3.refs_2_ = bf16[96,192]{1,0:T(8,128)(2,1)S(1)} collective-permute-done((bf16[96,192]{1,0:T(8,128)(2,1)S(1)}, bf16[96,192]{1,0:T(8,128)(2,1)S(1)}, u32[]{:S(2)}, u32[]{:S(2)}) %collective-permute-start.3) | collective-permute-done | bytes 36896 | tf_op jit(solution)/shard_map/ppermute | solution.py:435
  18.5 3.6 %shard_map.195 = (bf16[128,192]{1,0:T(8,128)(2,1)S(1)}, bf16[32,192]{1,0:T(8,128)(2,1)S(1)}, bf16[32,192]{1,0:T(8,128)(2,1)S(1)}, bf16[32,192]{1,0:T(8,128)(2,1)S(1)}, bf16[32,192]{1,0:T(8,128)(2,1)S(1)}) custom-call(bf16[96,192]{1,0:T(8,128)(2,1)S(1)} %collective-permute-done.1.refs_0_, bf16[96,192]{1,0:T(8,128)(2,1)S(1)} %collective-permute-done.2.refs_1_, ...), custom_call_target="tpu_custom_call" | custom-call | flops 1000000 | bytes 1000000 | tf_op jit(solution)/shard_map/pallas_call | solution.py:408
  22.1 0.1 collective-permute-start.4
  22.1 1.2 %collective-permute-done.4 = bf16[128,192]{1,0:T(8,128)(2,1)S(1)} collective-permute-done((bf16[128,192]{1,0:T(8,128)(2,1)S(1)}, bf16[128,192]{1,0:T(8,128)(2,1)S(1)}, u32[]{:S(2)}, u32[]{:S(2)}) %collective-permute-start.4) | collective-permute-done | bytes 49184 | tf_op jit(solution)/shard_map/ppermute | solution.py:435
  23.4 1.5 %collective-permute-start.5 = (bf16[64,192]{1,0:T(8,128)(2,1)S(1)}, bf16[64,192]{1,0:T(8,128)(2,1)S(1)}, u32[]{:S(2)}, u32[]{:S(2)}) collective-permute-start(bf16[64,192]{1,0:T(8,128)(2,1)S(1)} %pad_maximum_fusion.4), channel_id=1, source_target_pairs={{30,0},{28,2},{2,4},{0,6},{6,8},{4,10},{10,12},{8,14},{14,16},{12,... | collective-permute-start | bytes 73736 | tf_op jit(solution)/shard_map/ppermute | solution.py:435
  24.9 0.1 collective-permute-start.6
  25.1 1.5 %collective-permute-start.7 = (bf16[64,192]{1,0:T(8,128)(2,1)S(1)}, bf16[64,192]{1,0:T(8,128)(2,1)S(1)}, u32[]{:S(2)}, u32[]{:S(2)}) collective-permute-start(bf16[64,192]{1,0:T(8,128)(2,1)S(1)} %pad_maximum_fusion.6), channel_id=1, source_target_pairs={{2,0},{0,2},{3,1},{1,3},{6,4},{4,6},{7,5},{5,7},{10,8},{8,10},{11,... | collective-permute-start | bytes 73736 | tf_op jit(solution)/shard_map/ppermute | solution.py:435
  26.6 4.3 %collective-permute-done.5.refs_0_ = bf16[64,192]{1,0:T(8,128)(2,1)S(1)} collective-permute-done((bf16[64,192]{1,0:T(8,128)(2,1)S(1)}, bf16[64,192]{1,0:T(8,128)(2,1)S(1)}, u32[]{:S(2)}, u32[]{:S(2)}) %collective-permute-start.5) | collective-permute-done | bytes 24608 | tf_op jit(solution)/shard_map/ppermute | solution.py:435
  31.0 0.7 %collective-permute-done.6.refs_1_ = bf16[64,192]{1,0:T(8,128)(2,1)S(1)} collective-permute-done((bf16[64,192]{1,0:T(8,128)(2,1)S(1)}, bf16[64,192]{1,0:T(8,128)(2,1)S(1)}, u32[]{:S(2)}, u32[]{:S(2)}) %collective-permute-start.6) | collective-permute-done | bytes 24608 | tf_op jit(solution)/shard_map/ppermute | solution.py:435
  31.6 2.1 %shard_map.196 = (bf16[2,6,12,192]{3,2,1,0:T(8,128)(2,1)S(1)}, bf16[168,128]{1,0:T(8,128)(2,1)S(1)}, bf16[168,128]{1,0:T(8,128)(2,1)S(1)}) custom-call(bf16[64,192]{1,0:T(8,128)(2,1)S(1)} %collective-permute-done.5.refs_0_, bf16[64,192]{1,0:T(8,128)(2,1)S(1)} %collective-permute-done.6.refs_1_, bf16[64,192]{1,0:T(8,128)(2,1)S(1)} %collective-permute-done.7.refs_2_, ...), custom_call_target="tpu_custom_call" | custom-call | flops 1000000 | bytes 1000000 | tf_op jit(solution)/shard_map/pallas_call | solution.py:408
  33.8 0.1 collective-permute-start.8
  33.8 1.2 %collective-permute-done.8 = bf16[168,128]{1,0:T(8,128)(2,1)S(1)} collective-permute-done((bf16[168,128]{1,0:T(8,128)(2,1)S(1)}, bf16[168,128]{1,0:T(8,128)(2,1)S(1)}, u32[]{:S(2)}, u32[]{:S(2)}) %collective-permute-start.8) | collective-permute-done | bytes 43040 | tf_op jit(solution)/shard_map/ppermute | solution.py:460
  35.1 2.9 %collective-permute-start.10 = (bf16[168,128]{1,0:T(8,128)(2,1)S(1)}, bf16[168,128]{1,0:T(8,128)(2,1)S(1)}, u32[]{:S(2)}, u32[]{:S(2)}) collective-permute-start(bf16[168,128]{1,0:T(8,128)(2,1)S(1)} %add_convert_fusion.2), channel_id=1, source_target_pairs={{4,0},{0,4},{12,8},{8,12},{20,16},{16,20},{28,24},{24,28},{5,1},{1... | collective-permute-start | bytes 129032 | tf_op jit(solution)/shard_map/ppermute | solution.py:460
  38.1 0.5 %collective-permute-start.9 = (bf16[168,128]{1,0:T(8,128)(2,1)S(1)}, bf16[168,128]{1,0:T(8,128)(2,1)S(1)}, u32[]{:S(2)}, u32[]{:S(2)}) collective-permute-start(bf16[168,128]{1,0:T(8,128)(2,1)S(1)} %add_convert_fusion.2), channel_id=1, source_target_pairs={{2,0},{0,2},{3,1},{1,3},{6,4},{4,6},{7,5},{5,7},{10,8},{8,10},{11,... | collective-permute-start | bytes 129032 | tf_op jit(solution)/shard_map/ppermute | solution.py:460
  38.6 1.6 %collective-permute-done.11 = bf16[168,128]{1,0:T(8,128)(2,1)S(1)} collective-permute-done((bf16[168,128]{1,0:T(8,128)(2,1)S(1)}, bf16[168,128]{1,0:T(8,128)(2,1)S(1)}, u32[]{:S(2)}, u32[]{:S(2)}) %collective-permute-start.11) | collective-permute-done | bytes 43040 | tf_op jit(solution)/shard_map/ppermute | solution.py:460
  40.2 0.4 collective-permute-done.10
  40.6 1.5 %collective-permute-done.9 = bf16[168,128]{1,0:T(8,128)(2,1)S(1)} collective-permute-done((bf16[168,128]{1,0:T(8,128)(2,1)S(1)}, bf16[168,128]{1,0:T(8,128)(2,1)S(1)}, u32[]{:S(2)}, u32[]{:S(2)}) %collective-permute-start.9) | collective-permute-done | bytes 43040 | tf_op jit(solution)/shard_map/ppermute | solution.py:460
  42.1 1.2 %collective-permute-start.14 = (bf16[168,128]{1,0:T(8,128)(2,1)S(1)}, bf16[168,128]{1,0:T(8,128)(2,1)S(1)}, u32[]{:S(2)}, u32[]{:S(2)}) collective-permute-start(bf16[168,128]{1,0:T(8,128)(2,1)S(1)} %add_convert_fusion.1), channel_id=1, source_target_pairs={{24,0},{28,4},{16,8},{20,12},{8,16},{12,20},{0,24},{4,28},{25,1},{... | collective-permute-start | bytes 129032 | tf_op jit(solution)/shard_map/ppermute | solution.py:460
  43.3 3.2 %collective-permute-start.12 = (bf16[168,128]{1,0:T(8,128)(2,1)S(1)}, bf16[168,128]{1,0:T(8,128)(2,1)S(1)}, u32[]{:S(2)}, u32[]{:S(2)}) collective-permute-start(bf16[168,128]{1,0:T(8,128)(2,1)S(1)} %add_convert_fusion.1), channel_id=1, source_target_pairs={{8,0},{12,4},{0,8},{4,12},{24,16},{28,20},{16,24},{20,28},{9,1},{1... | collective-permute-start | bytes 129032 | tf_op jit(solution)/shard_map/ppermute | solution.py:460
  46.6 1.5 %collective-permute-done.14 = bf16[168,128]{1,0:T(8,128)(2,1)S(1)} collective-permute-done((bf16[168,128]{1,0:T(8,128)(2,1)S(1)}, bf16[168,128]{1,0:T(8,128)(2,1)S(1)}, u32[]{:S(2)}, u32[]{:S(2)}) %collective-permute-start.14) | collective-permute-done | bytes 43040 | tf_op jit(solution)/shard_map/ppermute | solution.py:460
  48.0 1.0 %collective-permute-done.13 = bf16[168,128]{1,0:T(8,128)(2,1)S(1)} collective-permute-done((bf16[168,128]{1,0:T(8,128)(2,1)S(1)}, bf16[168,128]{1,0:T(8,128)(2,1)S(1)}, u32[]{:S(2)}, u32[]{:S(2)}) %collective-permute-start.13) | collective-permute-done | bytes 43040 | tf_op jit(solution)/shard_map/ppermute | solution.py:460
  49.1 0.7 %copy.21 = bf16[2,6,12,192]{3,0,2,1:T(2,128)(2,1)} copy(bf16[2,6,12,192]{3,2,1,0:T(8,128)(2,1)S(1)} %get-tuple-element.45) | data formatting | bytes 110592
  49.8 0.5 collective-permute-done.15.other
  50.3 0.8 %shard_map.197 = (f32[160,192]{1,0:T(8,128)}, f32[64,192]{1,0:T(8,128)}) custom-call(bf16[168,128]{1,0:T(8,128)(2,1)S(1)} %add_convert_fusion.mine, bf16[168,128]{1,0:T(8,128)(2,1)S(1)} %collective-permute-done.15.other), custom_call_target="tpu_custom_call" | custom-call | flops 1000000 | bytes 1000000 | tf_op jit(solution)/shard_map/pallas_call | solution.py:408
  (39 shorter events, 0.4 us)
Async XLA Ops:
  0.6 14.2 %copy-start.4 = (f32[2,1,1,6,3312]{4,2,3,1,0:T(1,128)S(1)}, f32[2,1,1,6,3312]{4,2,3,1,0:T(1,128)}, u32[]{:S(2)}) copy-start(f32[2,1,1,6,3312]{4,2,3,1,0:T(1,128)} %param.27) | copy-start | bytes 476932
  0.6 17.8 %copy-start.3 = (bf16[2,192,192]{2,1,0:T(8,128)(2,1)S(1)}, bf16[2,192,192]{2,1,0:T(8,128)(2,1)}, u32[]{:S(2)}) copy-start(bf16[2,192,192]{2,1,0:T(8,128)(2,1)} %refs_6_.5) | copy-start | bytes 442372
  0.7 17.8 %copy-start.5 = (bf16[288,384]{1,0:T(8,128)(2,1)S(1)}, bf16[288,384]{1,0:T(8,128)(2,1)}, u32[]{:S(2)}) copy-start(bf16[288,384]{1,0:T(8,128)(2,1)} %constant.17.clone.refs_10_) | copy-start | bytes 663556
  0.7 17.8 %copy-start.6 = (bf16[256,144]{1,0:T(8,128)(2,1)S(1)}, bf16[256,144]{1,0:T(8,128)(2,1)}, u32[]{:S(2)}) copy-start(bf16[256,144]{1,0:T(8,128)(2,1)} %constant.18.clone.refs_11_) | copy-start | bytes 221188
  5.3 1.5 %collective-permute-start = (bf16[192,192]{1,0:T(8,128)(2,1)S(1)}, bf16[192,192]{1,0:T(8,128)(2,1)S(1)}, u32[]{:S(2)}, u32[]{:S(2)}) collective-permute-start(bf16[192,192]{1,0:T(8,128)(2,1)S(1)} %get-tuple-element.25), channel_id=1, source_target_pairs={{1,0},{0,1},{3,2},{2,3},{5,4},{4,5},{7,6},{6,7},{9,8},{8,9},{11,10... | collective-permute-start | bytes 221192 | tf_op jit(solution)/shard_map/ppermute | solution.py:435
  6.8 11.7 %copy-start.2 = (bf16[2,192,576]{2,1,0:T(8,128)(2,1)S(1)}, bf16[2,192,576]{2,1,0:T(8,128)(2,1)}, u32[]{:S(2)}) copy-start(bf16[2,192,576]{2,1,0:T(8,128)(2,1)} %refs_5_.5) | copy-start | bytes 1327108
  6.8 9.0 %collective-permute-start.1 = (bf16[96,192]{1,0:T(8,128)(2,1)S(1)}, bf16[96,192]{1,0:T(8,128)(2,1)S(1)}, u32[]{:S(2)}, u32[]{:S(2)}) collective-permute-start(bf16[96,192]{1,0:T(8,128)(2,1)S(1)} %pad_maximum_fusion), channel_id=1, source_target_pairs={{6,0},{4,2},{10,4},{8,6},{14,8},{12,10},{18,12},{16,14},{22,16},{2... | collective-permute-start | bytes 110600 | tf_op jit(solution)/shard_map/ppermute | solution.py:435
  13.7 4.1 %collective-permute-start.2 = (bf16[96,192]{1,0:T(8,128)(2,1)S(1)}, bf16[96,192]{1,0:T(8,128)(2,1)S(1)}, u32[]{:S(2)}, u32[]{:S(2)}) collective-permute-start(bf16[96,192]{1,0:T(8,128)(2,1)S(1)} %pad_maximum_fusion.1), channel_id=1, source_target_pairs={{4,0},{8,4},{12,8},{16,12},{20,16},{24,20},{28,24},{0,28},{5,1},{9... | collective-permute-start | bytes 110600 | tf_op jit(solution)/shard_map/ppermute | solution.py:435
  14.3 4.2 %collective-permute-start.3 = (bf16[96,192]{1,0:T(8,128)(2,1)S(1)}, bf16[96,192]{1,0:T(8,128)(2,1)S(1)}, u32[]{:S(2)}, u32[]{:S(2)}) collective-permute-start(bf16[96,192]{1,0:T(8,128)(2,1)S(1)} %pad_maximum_fusion.2), channel_id=1, source_target_pairs={{2,0},{0,2},{3,1},{1,3},{6,4},{4,6},{7,5},{5,7},{10,8},{8,10},{11,... | collective-permute-start | bytes 110600 | tf_op jit(solution)/shard_map/ppermute | solution.py:435
  14.9 3.6 %copy-start.1 = (bf16[2,768,192]{1,2,0:T(8,128)(2,1)S(1)}, bf16[2,768,192]{1,2,0:T(8,128)(2,1)}, u32[]{:S(2)}) copy-start(bf16[2,768,192]{1,2,0:T(8,128)(2,1)} %param.26) | copy-start | bytes 1769476
  14.9 3.6 %copy-start = (bf16[2,192,768]{2,1,0:T(8,128)(2,1)S(1)}, bf16[2,192,768]{2,1,0:T(8,128)(2,1)}, u32[]{:S(2)}) copy-start(bf16[2,192,768]{2,1,0:T(8,128)(2,1)} %refs_7_.5) | copy-start | bytes 1769476
  14.9 3.6 %copy-start.9 = (f32[2,2,192]{2,1,0:T(2,128)S(1)}, f32[2,2,192]{2,1,0:T(2,128)}, u32[]{:S(2)}) copy-start(f32[2,2,192]{2,1,0:T(2,128)} %refs_4_.5) | copy-start | bytes 9220
  22.1 1.3 %collective-permute-start.4 = (bf16[128,192]{1,0:T(8,128)(2,1)S(1)}, bf16[128,192]{1,0:T(8,128)(2,1)S(1)}, u32[]{:S(2)}, u32[]{:S(2)}) collective-permute-start(bf16[128,192]{1,0:T(8,128)(2,1)S(1)} %get-tuple-element.30), channel_id=1, source_target_pairs={{1,0},{0,1},{3,2},{2,3},{5,4},{4,5},{7,6},{6,7},{9,8},{8,9},{11,10... | collective-permute-start | bytes 147464 | tf_op jit(solution)/shard_map/ppermute | solution.py:435
  23.4 7.6 %collective-permute-start.5 = (bf16[64,192]{1,0:T(8,128)(2,1)S(1)}, bf16[64,192]{1,0:T(8,128)(2,1)S(1)}, u32[]{:S(2)}, u32[]{:S(2)}) collective-permute-start(bf16[64,192]{1,0:T(8,128)(2,1)S(1)} %pad_maximum_fusion.4), channel_id=1, source_target_pairs={{30,0},{28,2},{2,4},{0,6},{6,8},{4,10},{10,12},{8,14},{14,16},{12,... | collective-permute-start | bytes 73736 | tf_op jit(solution)/shard_map/ppermute | solution.py:435
  24.9 6.7 %copy-start.7 = (bf16[192,144]{1,0:T(8,128)(2,1)S(1)}, bf16[192,144]{1,0:T(8,128)(2,1)}, u32[]{:S(2)}) copy-start(bf16[192,144]{1,0:T(8,128)(2,1)} %constant.20.clone.refs_16_) | copy-start | bytes 165892
  24.9 6.7 %collective-permute-start.6 = (bf16[64,192]{1,0:T(8,128)(2,1)S(1)}, bf16[64,192]{1,0:T(8,128)(2,1)S(1)}, u32[]{:S(2)}, u32[]{:S(2)}) collective-permute-start(bf16[64,192]{1,0:T(8,128)(2,1)S(1)} %pad_maximum_fusion.5), channel_id=1, source_target_pairs={{28,0},{0,4},{4,8},{8,12},{12,16},{16,20},{20,24},{24,28},{29,1},{... | collective-permute-start | bytes 73736 | tf_op jit(solution)/shard_map/ppermute | solution.py:435
  25.1 6.6 %copy-start.8 = (bf16[144,256]{1,0:T(8,128)(2,1)S(1)}, bf16[144,256]{1,0:T(8,128)(2,1)}, u32[]{:S(2)}) copy-start(bf16[144,256]{1,0:T(8,128)(2,1)} %constant.19.clone.refs_15_) | copy-start | bytes 221188
  25.1 6.5 %collective-permute-start.7 = (bf16[64,192]{1,0:T(8,128)(2,1)S(1)}, bf16[64,192]{1,0:T(8,128)(2,1)S(1)}, u32[]{:S(2)}, u32[]{:S(2)}) collective-permute-start(bf16[64,192]{1,0:T(8,128)(2,1)S(1)} %pad_maximum_fusion.6), channel_id=1, source_target_pairs={{2,0},{0,2},{3,1},{1,3},{6,4},{4,6},{7,5},{5,7},{10,8},{8,10},{11,... | collective-permute-start | bytes 73736 | tf_op jit(solution)/shard_map/ppermute | solution.py:435
  33.8 1.3 %collective-permute-start.8 = (bf16[168,128]{1,0:T(8,128)(2,1)S(1)}, bf16[168,128]{1,0:T(8,128)(2,1)S(1)}, u32[]{:S(2)}, u32[]{:S(2)}) collective-permute-start(bf16[168,128]{1,0:T(8,128)(2,1)S(1)} %get-tuple-element.42), channel_id=1, source_target_pairs={{1,0},{0,1},{3,2},{2,3},{5,4},{4,5},{7,6},{6,7},{9,8},{8,9},{11,10... | collective-permute-start | bytes 129032 | tf_op jit(solution)/shard_map/ppermute | solution.py:460
  35.1 5.1 %collective-permute-start.11 = (bf16[168,128]{1,0:T(8,128)(2,1)S(1)}, bf16[168,128]{1,0:T(8,128)(2,1)S(1)}, u32[]{:S(2)}, u32[]{:S(2)}) collective-permute-start(bf16[168,128]{1,0:T(8,128)(2,1)S(1)} %add_convert_fusion.2), channel_id=1, source_target_pairs={{6,0},{4,2},{2,4},{0,6},{14,8},{12,10},{10,12},{8,14},{22,16},{20,... | collective-permute-start | bytes 129032 | tf_op jit(solution)/shard_map/ppermute | solution.py:460
  35.1 5.5 %collective-permute-start.10 = (bf16[168,128]{1,0:T(8,128)(2,1)S(1)}, bf16[168,128]{1,0:T(8,128)(2,1)S(1)}, u32[]{:S(2)}, u32[]{:S(2)}) collective-permute-start(bf16[168,128]{1,0:T(8,128)(2,1)S(1)} %add_convert_fusion.2), channel_id=1, source_target_pairs={{4,0},{0,4},{12,8},{8,12},{20,16},{16,20},{28,24},{24,28},{5,1},{1... | collective-permute-start | bytes 129032 | tf_op jit(solution)/shard_map/ppermute | solution.py:460
  38.1 4.0 %collective-permute-start.9 = (bf16[168,128]{1,0:T(8,128)(2,1)S(1)}, bf16[168,128]{1,0:T(8,128)(2,1)S(1)}, u32[]{:S(2)}, u32[]{:S(2)}) collective-permute-start(bf16[168,128]{1,0:T(8,128)(2,1)S(1)} %add_convert_fusion.2), channel_id=1, source_target_pairs={{2,0},{0,2},{3,1},{1,3},{6,4},{4,6},{7,5},{5,7},{10,8},{8,10},{11,... | collective-permute-start | bytes 129032 | tf_op jit(solution)/shard_map/ppermute | solution.py:460
  42.1 5.9 %collective-permute-start.14 = (bf16[168,128]{1,0:T(8,128)(2,1)S(1)}, bf16[168,128]{1,0:T(8,128)(2,1)S(1)}, u32[]{:S(2)}, u32[]{:S(2)}) collective-permute-start(bf16[168,128]{1,0:T(8,128)(2,1)S(1)} %add_convert_fusion.1), channel_id=1, source_target_pairs={{24,0},{28,4},{16,8},{20,12},{8,16},{12,20},{0,24},{4,28},{25,1},{... | collective-permute-start | bytes 129032 | tf_op jit(solution)/shard_map/ppermute | solution.py:460
  43.3 5.7 %collective-permute-start.13 = (bf16[168,128]{1,0:T(8,128)(2,1)S(1)}, bf16[168,128]{1,0:T(8,128)(2,1)S(1)}, u32[]{:S(2)}, u32[]{:S(2)}) collective-permute-start(bf16[168,128]{1,0:T(8,128)(2,1)S(1)} %add_convert_fusion.1), channel_id=1, source_target_pairs={{16,0},{20,4},{24,8},{28,12},{0,16},{4,20},{8,24},{12,28},{17,1},{... | collective-permute-start | bytes 129032 | tf_op jit(solution)/shard_map/ppermute | solution.py:460
  43.3 5.7 %collective-permute-start.12 = (bf16[168,128]{1,0:T(8,128)(2,1)S(1)}, bf16[168,128]{1,0:T(8,128)(2,1)S(1)}, u32[]{:S(2)}, u32[]{:S(2)}) collective-permute-start(bf16[168,128]{1,0:T(8,128)(2,1)S(1)} %add_convert_fusion.1), channel_id=1, source_target_pairs={{8,0},{12,4},{0,8},{4,12},{24,16},{28,20},{16,24},{20,28},{9,1},{1... | collective-permute-start | bytes 129032 | tf_op jit(solution)/shard_map/ppermute | solution.py:460
  49.1 1.3 %collective-permute-start.15 = (bf16[168,128]{1,0:T(8,128)(2,1)S(1)}, bf16[168,128]{1,0:T(8,128)(2,1)S(1)}, u32[]{:S(2)}, u32[]{:S(2)}) collective-permute-start(bf16[168,128]{1,0:T(8,128)(2,1)S(1)} %add_convert_fusion.mine), channel_id=1, source_target_pairs={{1,0},{0,1},{3,2},{2,3},{5,4},{4,5},{7,6},{6,7},{9,8},{8,9},{11,10... | collective-permute-start | bytes 129032 | tf_op jit(solution)/shard_map/ppermute | solution.py:460

commit v11 on v10

--- a/solution.py
+++ b/solution.py
@@ -197,17 +197,17 @@
     return mixed.astype(HALF)
 
 
-def attend_back(dmixed, q, k, v, prob):
+def attend_back(dmixed, qheads, k, v, prob, turned):
     dheads = by_head(dmixed)
     dweights = dot_nt(dheads, v)
-    dv = dot_tn(prob[...], dheads)
+    dv = dot_tn(prob[...], dheads) if turned is None else dot(turned[...], dheads)
     dscores = []
     for h in range(HEADS):
         rows = slice(h * CELLS, (h + 1) * CELLS)
         full = prob[rows, :].astype(FULL)
         inner = jnp.sum(dweights[rows] * full, -1, keepdims=True)
         dscores.append((full * (dweights[rows] - inner) * HEAD ** (-0.5)).astype(HALF))
-    dk = dot_tn(jnp.concatenate(dscores, 0), by_head(q))
+    dk = dot_tn(jnp.concatenate(dscores, 0), qheads)
     dq = jnp.zeros((CELLS, WIDTH), FULL)
     for h in range(HEADS):
         dq = jnp.where(head_lanes(h), dot(dscores[h], k), dq)
@@ -226,23 +226,21 @@
     qkv = dot(hidden, wqkv[...]).astype(HALF)
     q, k, v = (qkv[:, n * WIDTH : (n + 1) * WIDTH] for n in range(3))
     mixed = attend(q, k, v, bias, prob)
-    return (q, k, v), x + dot(mixed, wproj[...])
-
-
-def backward(dflat, x, qkv, prob, resid, slope, gains, wqkv, wproj, wup, wdown):
-    q, k, v = qkv
+    return (unit, spread), (q, k, v), x + dot(mixed, wproj[...])
+
+
+def backward(dflat, norms, heads, prob, turned, slope, gains, wqkv, wproj, wup, wdown):
+    qheads, k, v = heads
     dactive = dot(dflat, wdown[...])
     dupward = (dactive * slope).astype(HALF)
     dnormed = dot_nt(dupward, wup[...])
-    unit, spread = normalise(resid)
-    dresid = dflat.astype(FULL) + normalise_back(dnormed, unit, spread, gains[1:2, :])
+    dresid = dflat.astype(FULL) + normalise_back(dnormed, *norms[1], gains[1:2, :])
     dmixed = dot_nt(dresid.astype(HALF), wproj[...]).astype(HALF)
-    dq, dk, dv = attend_back(dmixed, q, k, v, prob)
+    dq, dk, dv = attend_back(dmixed, qheads, k, v, prob, turned)
     dhidden = dot_nt(dq, wqkv[:, :WIDTH])
     dhidden = dhidden + dot_nt(dk, wqkv[:, WIDTH : 2 * WIDTH])
     dhidden = dhidden + dot_nt(dv, wqkv[:, 2 * WIDTH :])
-    unit, spread = normalise(x)
-    return dresid + normalise_back(dhidden, unit, spread, gains[0:1, :])
+    return dresid + normalise_back(dhidden, *norms[0], gains[0:1, :])
 
 
 def gather_patches(upper, surface, section, select, ff, ft):
@@ -287,8 +285,8 @@
     )
     count = len(names)
     source, refs = refs[:count], refs[count:]
-    patch_o, x_o, qkv_o, prob, resid_o, slope_o, send_o, *keep_o = refs[:11]
-    refs = refs[11:]
+    patch_o, x_o, qkv_o, prob, resid_o, send_o, *keep_o = refs[:10]
+    refs = refs[10:]
     local, refs = refs[:count], refs[count:]
     ff, ft, emb, cots, table, xs, bias, cols, select, sems = refs
     copies = {}
@@ -330,16 +328,14 @@
         for o in range(12):
             cots[(a * 12 + o) * 2 : (a * 12 + o) * 2 + 2, :] = cot[a, o].astype(FULL)
     ready = dot(have["out_cot"][...], cots[...].astype(HALF))
-    qkv, resid = forward_half(x, gains, have["wqkv"], have["wproj"], bias, prob)
+    _, qkv, resid = forward_half(x, gains, have["wqkv"], have["wproj"], bias, prob)
     for n in range(3):
         qkv_o[n] = qkv[n]
     resid_o[...] = resid
     unit, spread = normalise(resid)
     normed = (unit * gains[1:2, :]).astype(HALF)
     upward = dot(normed, have["wup"][...])
-    below, slope = gelu_parts(upward)
-    slope_o[...] = slope.astype(HALF)
-    active = (upward * below).astype(HALF)
+    active = (upward * gelu_parts(upward)[0]).astype(HALF)
     result = (resid + dot_nt(active, have["wdown"][...])).astype(HALF)
     moved = (dot(have["out_first"][...], result) + ready).astype(HALF)
     send_o[...] = moved[192:]
@@ -351,6 +347,18 @@
     fill_columns(cols)
     table_rows(tbl, 1, table)
     build_bias(table, cols, xs, bias, (flag("section"), flag("lat")))
+
+
+def between_kernel(after, x, qkv, prob, resid, gains, wup, *results):
+    slope_o, unit_o, spread_o, heads_o, turned_o = results
+    for n, values in enumerate((x[...].astype(FULL), resid[...])):
+        unit, spread = normalise(values)
+        unit_o[n] = unit
+        spread_o[n] = spread
+    upward = dot((unit * gains[0, 1:2, :]).astype(HALF), wup[0])
+    slope_o[...] = gelu_parts(upward)[1].astype(HALF)
+    heads_o[...] = by_head(qkv[0])
+    turned_o[...] = prob[...].astype(FULL).T.astype(HALF)
 
 
 def second_kernel(*refs):
@@ -362,12 +370,14 @@
     both = dot(into[...], stack[...])
     x, dflat = both[:CELLS], both[CELLS:].astype(HALF)
     gains, wqkv, wproj, wup, wdown = (w.at[1] for w in (gains, wqkv, wproj, wup, wdown))
-    qkv, resid = forward_half(x, gains, wqkv, wproj, bias, prob)
-    unit, spread = normalise(resid)
-    normed = (unit * gains[1:2, :]).astype(HALF)
-    upward = dot(normed, wup[...])
+    first, (q, k, v), resid = forward_half(x, gains, wqkv, wproj, bias, prob)
+    last = normalise(resid)
+    upward = dot((last[0] * gains[1:2, :]).astype(HALF), wup[...])
     slope = gelu_parts(upward)[1]
-    dx = backward(dflat, x, qkv, prob, resid, slope, gains, wqkv, wproj, wup, wdown)
+    heads = (by_head(q), k, v)
+    dx = backward(
+        dflat, (first, last), heads, prob, None, slope, gains, wqkv, wproj, wup, wdown
+    )
     moved = dot(out_of[...], dx.astype(HALF)).astype(HALF)
     send_o[...] = moved[128:]
     for n in range(4):
@@ -376,15 +386,15 @@
 
 def third_kernel(*refs):
     parts, rest = refs[:4], refs[4:]
-    gains, wqkv, wproj, wup, wdown, patch, x_i, qkv_i, prob, resid, slope, into, out_of = rest[:13]
-    grad_o, mine_o, other_o, stack, terms = rest[13:]
+    gains, wqkv, wproj, wup, wdown, patch, qkv_i, prob, slope, unit, spread, heads, turned = rest[:13]
+    into, out_of, grad_o, mine_o, other_o, stack, terms = rest[13:]
     for n, part in zip(order, parts):
         stack[n * 64 : n * 64 + 64, :] = part[...]
     dflat = dot(into[...], stack[...]).astype(HALF)
-    qkv = tuple(qkv_i[n] for n in range(3))
     gains, wqkv, wproj, wup, wdown = (w.at[0] for w in (gains, wqkv, wproj, wup, wdown))
+    norms = tuple((unit[n], spread[n]) for n in range(2))
     dx = backward(
-        dflat, x_i[...].astype(FULL), qkv, prob, resid[...], slope[...].astype(FULL),
+        dflat, norms, (heads[...], qkv_i[1], qkv_i[2]), prob, turned, slope[...].astype(FULL),
         gains, wqkv, wproj, wup, wdown,
     )
     grad = dx.astype(HALF)
@@ -542,9 +552,8 @@
         shape((3, CELLS, WIDTH)),
         shape((HEADS * CELLS, CELLS)),
         shape((CELLS, WIDTH), FULL),
-        shape((CELLS, 4 * WIDTH)),
     ]
-    patch, x, qkv, prob, resid, slope, send, *keep = call(
+    patch, x, qkv, prob, resid, send, *keep = call(
         first_kernel,
         held + [shape((192, WIDTH))] + [shape((48, WIDTH))] * 4,
         local
@@ -567,6 +576,18 @@
     bias_shape = shape((HEADS * CELLS, CELLS), FULL)
     got = fetch(send, {"section": 1})
     bias = call(second_bias, bias_shape, [*scratch_bias, scratch_cols], table, got)
+    slope, unit, spread, heads, turned = call(
+        between_kernel,
+        [
+            shape((CELLS, 4 * WIDTH)),
+            shape((2, CELLS, WIDTH), FULL),
+            shape((2, CELLS, 1), FULL),
+            shape((HEADS * CELLS, WIDTH)),
+            shape((CELLS, HEADS * CELLS)),
+        ],
+        [],
+        got, x, qkv, prob, resid, norm_gains, up_weight,
+    )
     into = np.concatenate((octants_in(48, 0, False), octants_in(48, 18, False)), 0)
     send, *keep = call(
         second_kernel,
@@ -579,7 +600,8 @@
         third_kernel,
         [shape((2, 6, 12, WIDTH)), shape((168, 128)), shape((168, 128))],
         [pltpu.VMEM((8 * 32, WIDTH), HALF), pltpu.VMEM((336, 128), FULL)],
-        *exchange(keep, fetch(send, {"section": -1}), -1), *weights, patch, x, qkv, prob, resid, slope,
+        *exchange(keep, fetch(send, {"section": -1}), -1), *weights, patch, qkv, prob,
+        slope, unit, spread, heads, turned,
         jnp.asarray(octants_in(32, 0, True)), jnp.asarray(inner_to_padded()),
     )
     scale = float(levels * sections * rows * bands * columns * lax.axis_size("lon")) ** (-0.5)

time: 51.3 us -> 51.2 us (level)
  waiting for transfers between devices: 17.4 us -> 16.8 us
    ppermute x8, waiting for transfers between devices: 9.77 us -> 9.2 us  [fetch(): return lax.ppermute(block, tuple(axes), pairs)]
    pallas_call x5 -> x6, Pallas kernels: 12 us -> 12.5 us  [call(): pl.pallas_call(kernel, out_shape=outs, in_specs=[spec for a in args], out...]
  transfers between devices with their start and end apart: 16 -> 16, of which waited for: 13 -> 13; matrix products, arithmetic and copies ran while one was open for 1% -> 1% of each run, Pallas kernels for 2% -> 3%
where the time goes in v11:
time: 51.2 us; the launch traced here: 51.1 us
  starting transfers between devices  20 us (39%)
  waiting for transfers between devices  16.8 us (33%)
  Pallas kernels  12.5 us (24%)
  between operations  0.86 us (2%)
  local copies, waits for them, and re-layouts  0.77 us (2%)
    pallas_call x6, Pallas kernels, call(): pl.pallas_call(kernel, out_shape=outs, in_specs=[spec for a in args], out...  12.5 us
    ppermute x8, starting transfers between devices, fetch(): return lax.ppermute(block, tuple(axes), pairs)  11.8 us
    ppermute x8, waiting for transfers between devices, fetch(): return lax.ppermute(block, tuple(axes), pairs)  9.2 us
    ppermute x8, starting transfers between devices, swap(): return lax.ppermute(block, tuple(axes), pairs)  8.14 us
    ppermute x8, waiting for transfers between devices, swap(): return lax.ppermute(block, tuple(axes), pairs)  7.63 us
  transfers between devices with their start and end apart: 16, of which 13 were waited for; matrix products, arithmetic and copies ran while one was open for 1% of the time, Pallas kernels for 3%

profile of v11, /device:TPU:0, one launch (start us, length us, event | category | flops | bytes accessed | tf_op | source)
XLA Modules:
  0.0 51.1 jit_solution(4475959630507106759)
XLA Ops:
  0.7 4.5 %shard_map.193 = (bf16[144,256]{1,0:T(8,128)(2,1)S(1)}, bf16[144,192]{1,0:T(8,128)(2,1)S(1)}, bf16[3,144,192]{2,1,0:T(8,128)(2,1)S(1)}, bf16[864,144]{1,0:T(8,12...) custom-call(f32[12,1,3312]{2,1,0:T(1,128)} %bitcast.6, ...), custom_call_target="tpu_custom_call" | custom-call | flops 1000000 | bytes 1000000 | tf_op jit(solution)/shard_map/pallas_call | solution.py:418
  5.2 0.5 %collective-permute-start = (bf16[192,192]{1,0:T(8,128)(2,1)S(1)}, bf16[192,192]{1,0:T(8,128)(2,1)S(1)}, u32[]{:S(2)}, u32[]{:S(2)}) collective-permute-start(bf16[192,192]{1,0:T(8,128)(2,1)S(1)} %get-tuple-element.29), channel_id=1, source_target_pairs={{1,0},{0,1},{3,2},{2,3},{5,4},{4,5},{7,6},{6,7},{9,8},{8,9},{11,10... | collective-permute-start | bytes 221192 | tf_op jit(solution)/shard_map/ppermute | solution.py:445
  5.8 0.9 %collective-permute-done.after = bf16[192,192]{1,0:T(8,128)(2,1)S(1)} collective-permute-done((bf16[192,192]{1,0:T(8,128)(2,1)S(1)}, bf16[192,192]{1,0:T(8,128)(2,1)S(1)}, u32[]{:S(2)}, u32[]{:S(2)}) %collective-permute-start) | collective-permute-done | bytes 73760 | tf_op jit(solution)/shard_map/ppermute | solution.py:445
  6.7 6.9 %collective-permute-start.1 = (bf16[96,192]{1,0:T(8,128)(2,1)S(1)}, bf16[96,192]{1,0:T(8,128)(2,1)S(1)}, u32[]{:S(2)}, u32[]{:S(2)}) collective-permute-start(bf16[96,192]{1,0:T(8,128)(2,1)S(1)} %pad_maximum_fusion), channel_id=1, source_target_pairs={{6,0},{4,2},{10,4},{8,6},{14,8},{12,10},{18,12},{16,14},{22,16},{2... | collective-permute-start | bytes 110600 | tf_op jit(solution)/shard_map/ppermute | solution.py:445
  13.6 0.6 %collective-permute-start.2 = (bf16[96,192]{1,0:T(8,128)(2,1)S(1)}, bf16[96,192]{1,0:T(8,128)(2,1)S(1)}, u32[]{:S(2)}, u32[]{:S(2)}) collective-permute-start(bf16[96,192]{1,0:T(8,128)(2,1)S(1)} %pad_maximum_fusion.1), channel_id=1, source_target_pairs={{4,0},{8,4},{12,8},{16,12},{20,16},{24,20},{28,24},{0,28},{5,1},{9... | collective-permute-start | bytes 110600 | tf_op jit(solution)/shard_map/ppermute | solution.py:445
  14.2 0.6 %collective-permute-start.3 = (bf16[96,192]{1,0:T(8,128)(2,1)S(1)}, bf16[96,192]{1,0:T(8,128)(2,1)S(1)}, u32[]{:S(2)}, u32[]{:S(2)}) collective-permute-start(bf16[96,192]{1,0:T(8,128)(2,1)S(1)} %pad_maximum_fusion.2), channel_id=1, source_target_pairs={{2,0},{0,2},{3,1},{1,3},{6,4},{4,6},{7,5},{5,7},{10,8},{8,10},{11,... | collective-permute-start | bytes 110600 | tf_op jit(solution)/shard_map/ppermute | solution.py:445
  14.8 0.9 %shard_map.194.refs_9_ = f32[864,144]{1,0:T(8,128)S(1)} custom-call(f32[12,1,3312]{2,1,0:T(1,128)S(1)} %bitcast.7, bf16[192,192]{1,0:T(8,128)(2,1)S(1)} %collective-permute-done.after), custom_call_target="tpu_custom_call" | custom-call | flops 1000000 | bytes 1000000 | tf_op jit(solution)/shard_map/pallas_call | solution.py:418
  15.8 2.0 %collective-permute-done.2.refs_1_ = bf16[96,192]{1,0:T(8,128)(2,1)S(1)} collective-permute-done((bf16[96,192]{1,0:T(8,128)(2,1)S(1)}, bf16[96,192]{1,0:T(8,128)(2,1)S(1)}, u32[]{:S(2)}, u32[]{:S(2)}) %collective-permute-start.2) | collective-permute-done | bytes 36896 | tf_op jit(solution)/shard_map/ppermute | solution.py:445
  17.8 0.6 %collective-permute-done.3.refs_2_ = bf16[96,192]{1,0:T(8,128)(2,1)S(1)} collective-permute-done((bf16[96,192]{1,0:T(8,128)(2,1)S(1)}, bf16[96,192]{1,0:T(8,128)(2,1)S(1)}, u32[]{:S(2)}, u32[]{:S(2)}) %collective-permute-start.3) | collective-permute-done | bytes 36896 | tf_op jit(solution)/shard_map/ppermute | solution.py:445
  18.4 3.6 %shard_map.195 = (bf16[128,192]{1,0:T(8,128)(2,1)S(1)}, bf16[32,192]{1,0:T(8,128)(2,1)S(1)}, bf16[32,192]{1,0:T(8,128)(2,1)S(1)}, bf16[32,192]{1,0:T(8,128)(2,1)S(1)}, bf16[32,192]{1,0:T(8,128)(2,1)S(1)}) custom-call(bf16[96,192]{1,0:T(8,128)(2,1)S(1)} %collective-permute-done.1.refs_0_, bf16[96,192]{1,0:T(8,128)(2,1)S(1)} %collective-permute-done.2.refs_1_, ...), custom_call_target="tpu_custom_call" | custom-call | flops 1000000 | bytes 1000000 | tf_op jit(solution)/shard_map/pallas_call | solution.py:418
  22.1 0.6 %shard_map.196 = (bf16[144,768]{1,0:T(8,128)(2,1)S(1)}, f32[2,144,192]{2,1,0:T(8,128)S(1)}, f32[2,144,1]{2,1,0:T(8,128)S(1)}, bf16[864,192]{1,0:T(8,128)(2,1)S(1)}, bf16[144,864]{1,0:T(8,128)(2,1)S(1)}) custom-call(bf16[192,192]{1,0:T(8,128)(2,1)S(1)} %collective-permute-done.after, bf16[144,192]{1,0:T(8,128)(2,1)S(1)} %get-tuple-element.41.x, ...), custom_call_target="tpu_custom_call" | custom-call | flops 1000000 | bytes 1000000 | tf_op jit(solution)/shard_map/pallas_call | solution.py:418
  22.6 0.7 %collective-permute-done.4 = bf16[128,192]{1,0:T(8,128)(2,1)S(1)} collective-permute-done((bf16[128,192]{1,0:T(8,128)(2,1)S(1)}, bf16[128,192]{1,0:T(8,128)(2,1)S(1)}, u32[]{:S(2)}, u32[]{:S(2)}) %collective-permute-start.4) | collective-permute-done | bytes 49184 | tf_op jit(solution)/shard_map/ppermute | solution.py:445
  23.3 1.5 %collective-permute-start.5 = (bf16[64,192]{1,0:T(8,128)(2,1)S(1)}, bf16[64,192]{1,0:T(8,128)(2,1)S(1)}, u32[]{:S(2)}, u32[]{:S(2)}) collective-permute-start(bf16[64,192]{1,0:T(8,128)(2,1)S(1)} %pad_maximum_fusion.4), channel_id=1, source_target_pairs={{30,0},{28,2},{2,4},{0,6},{6,8},{4,10},{10,12},{8,14},{14,16},{12,... | collective-permute-start | bytes 73736 | tf_op jit(solution)/shard_map/ppermute | solution.py:445
  24.9 0.1 collective-permute-start.6
  25.0 1.5 %collective-permute-start.7 = (bf16[64,192]{1,0:T(8,128)(2,1)S(1)}, bf16[64,192]{1,0:T(8,128)(2,1)S(1)}, u32[]{:S(2)}, u32[]{:S(2)}) collective-permute-start(bf16[64,192]{1,0:T(8,128)(2,1)S(1)} %pad_maximum_fusion.6), channel_id=1, source_target_pairs={{2,0},{0,2},{3,1},{1,3},{6,4},{4,6},{7,5},{5,7},{10,8},{8,10},{11,... | collective-permute-start | bytes 73736 | tf_op jit(solution)/shard_map/ppermute | solution.py:445
  26.5 4.3 %collective-permute-done.5.refs_0_ = bf16[64,192]{1,0:T(8,128)(2,1)S(1)} collective-permute-done((bf16[64,192]{1,0:T(8,128)(2,1)S(1)}, bf16[64,192]{1,0:T(8,128)(2,1)S(1)}, u32[]{:S(2)}, u32[]{:S(2)}) %collective-permute-start.5) | collective-permute-done | bytes 24608 | tf_op jit(solution)/shard_map/ppermute | solution.py:445
  30.9 0.7 %collective-permute-done.6.refs_1_ = bf16[64,192]{1,0:T(8,128)(2,1)S(1)} collective-permute-done((bf16[64,192]{1,0:T(8,128)(2,1)S(1)}, bf16[64,192]{1,0:T(8,128)(2,1)S(1)}, u32[]{:S(2)}, u32[]{:S(2)}) %collective-permute-start.6) | collective-permute-done | bytes 24608 | tf_op jit(solution)/shard_map/ppermute | solution.py:445
  31.5 2.1 %shard_map.197 = (bf16[2,6,12,192]{3,2,1,0:T(8,128)(2,1)S(1)}, bf16[168,128]{1,0:T(8,128)(2,1)S(1)}, bf16[168,128]{1,0:T(8,128)(2,1)S(1)}) custom-call(bf16[64,192]{1,0:T(8,128)(2,1)S(1)} %collective-permute-done.5.refs_0_, bf16[64,192]{1,0:T(8,128)(2,1)S(1)} %collective-permute-done.6.refs_1_, bf16[64,192]{1,0:T(8,128)(2,1)S(1)} %collective-permute-done.7.refs_2_, ...), custom_call_target="tpu_custom_call" | custom-call | flops 1000000 | bytes 1000000 | tf_op jit(solution)/shard_map/pallas_call | solution.py:418
  33.7 0.1 collective-permute-start.8
  33.8 1.2 %collective-permute-done.8 = bf16[168,128]{1,0:T(8,128)(2,1)S(1)} collective-permute-done((bf16[168,128]{1,0:T(8,128)(2,1)S(1)}, bf16[168,128]{1,0:T(8,128)(2,1)S(1)}, u32[]{:S(2)}, u32[]{:S(2)}) %collective-permute-start.8) | collective-permute-done | bytes 43040 | tf_op jit(solution)/shard_map/ppermute | solution.py:470
  35.1 2.9 %collective-permute-start.10 = (bf16[168,128]{1,0:T(8,128)(2,1)S(1)}, bf16[168,128]{1,0:T(8,128)(2,1)S(1)}, u32[]{:S(2)}, u32[]{:S(2)}) collective-permute-start(bf16[168,128]{1,0:T(8,128)(2,1)S(1)} %add_convert_fusion.2), channel_id=1, source_target_pairs={{4,0},{0,4},{12,8},{8,12},{20,16},{16,20},{28,24},{24,28},{5,1},{1... | collective-permute-start | bytes 129032 | tf_op jit(solution)/shard_map/ppermute | solution.py:470
  38.0 0.5 %collective-permute-start.9 = (bf16[168,128]{1,0:T(8,128)(2,1)S(1)}, bf16[168,128]{1,0:T(8,128)(2,1)S(1)}, u32[]{:S(2)}, u32[]{:S(2)}) collective-permute-start(bf16[168,128]{1,0:T(8,128)(2,1)S(1)} %add_convert_fusion.2), channel_id=1, source_target_pairs={{2,0},{0,2},{3,1},{1,3},{6,4},{4,6},{7,5},{5,7},{10,8},{8,10},{11,... | collective-permute-start | bytes 129032 | tf_op jit(solution)/shard_map/ppermute | solution.py:470
  38.6 1.6 %collective-permute-done.11 = bf16[168,128]{1,0:T(8,128)(2,1)S(1)} collective-permute-done((bf16[168,128]{1,0:T(8,128)(2,1)S(1)}, bf16[168,128]{1,0:T(8,128)(2,1)S(1)}, u32[]{:S(2)}, u32[]{:S(2)}) %collective-permute-start.11) | collective-permute-done | bytes 43040 | tf_op jit(solution)/shard_map/ppermute | solution.py:470
  40.1 0.4 collective-permute-done.10
  40.6 1.5 %collective-permute-done.9 = bf16[168,128]{1,0:T(8,128)(2,1)S(1)} collective-permute-done((bf16[168,128]{1,0:T(8,128)(2,1)S(1)}, bf16[168,128]{1,0:T(8,128)(2,1)S(1)}, u32[]{:S(2)}, u32[]{:S(2)}) %collective-permute-start.9) | collective-permute-done | bytes 43040 | tf_op jit(solution)/shard_map/ppermute | solution.py:470
  42.1 1.2 %collective-permute-start.14 = (bf16[168,128]{1,0:T(8,128)(2,1)S(1)}, bf16[168,128]{1,0:T(8,128)(2,1)S(1)}, u32[]{:S(2)}, u32[]{:S(2)}) collective-permute-start(bf16[168,128]{1,0:T(8,128)(2,1)S(1)} %add_convert_fusion.1), channel_id=1, source_target_pairs={{24,0},{28,4},{16,8},{20,12},{8,16},{12,20},{0,24},{4,28},{25,1},{... | collective-permute-start | bytes 129032 | tf_op jit(solution)/shard_map/ppermute | solution.py:470
  43.3 3.3 %collective-permute-start.12 = (bf16[168,128]{1,0:T(8,128)(2,1)S(1)}, bf16[168,128]{1,0:T(8,128)(2,1)S(1)}, u32[]{:S(2)}, u32[]{:S(2)}) collective-permute-start(bf16[168,128]{1,0:T(8,128)(2,1)S(1)} %add_convert_fusion.1), channel_id=1, source_target_pairs={{8,0},{12,4},{0,8},{4,12},{24,16},{28,20},{16,24},{20,28},{9,1},{1... | collective-permute-start | bytes 129032 | tf_op jit(solution)/shard_map/ppermute | solution.py:470
  46.5 1.5 %collective-permute-done.14 = bf16[168,128]{1,0:T(8,128)(2,1)S(1)} collective-permute-done((bf16[168,128]{1,0:T(8,128)(2,1)S(1)}, bf16[168,128]{1,0:T(8,128)(2,1)S(1)}, u32[]{:S(2)}, u32[]{:S(2)}) %collective-permute-start.14) | collective-permute-done | bytes 43040 | tf_op jit(solution)/shard_map/ppermute | solution.py:470
  48.0 1.0 %collective-permute-done.13 = bf16[168,128]{1,0:T(8,128)(2,1)S(1)} collective-permute-done((bf16[168,128]{1,0:T(8,128)(2,1)S(1)}, bf16[168,128]{1,0:T(8,128)(2,1)S(1)}, u32[]{:S(2)}, u32[]{:S(2)}) %collective-permute-start.13) | collective-permute-done | bytes 43040 | tf_op jit(solution)/shard_map/ppermute | solution.py:470
  49.1 0.7 %copy.21 = bf16[2,6,12,192]{3,0,2,1:T(2,128)(2,1)} copy(bf16[2,6,12,192]{3,2,1,0:T(8,128)(2,1)S(1)} %get-tuple-element.53) | data formatting | bytes 110592
  49.8 0.5 collective-permute-done.15.other
  50.3 0.8 %shard_map.198 = (f32[160,192]{1,0:T(8,128)}, f32[64,192]{1,0:T(8,128)}) custom-call(bf16[168,128]{1,0:T(8,128)(2,1)S(1)} %add_convert_fusion.mine, bf16[168,128]{1,0:T(8,128)(2,1)S(1)} %collective-permute-done.15.other), custom_call_target="tpu_custom_call" | custom-call | flops 1000000 | bytes 1000000 | tf_op jit(solution)/shard_map/pallas_call | solution.py:418
  (40 shorter events, 0.4 us)
Async XLA Ops:
  0.6 14.2 %copy-start.4 = (f32[2,1,1,6,3312]{4,2,3,1,0:T(1,128)S(1)}, f32[2,1,1,6,3312]{4,2,3,1,0:T(1,128)}, u32[]{:S(2)}) copy-start(f32[2,1,1,6,3312]{4,2,3,1,0:T(1,128)} %param.27) | copy-start | bytes 476932
  0.6 17.7 %copy-start.3 = (bf16[2,192,192]{2,1,0:T(8,128)(2,1)S(1)}, bf16[2,192,192]{2,1,0:T(8,128)(2,1)}, u32[]{:S(2)}) copy-start(bf16[2,192,192]{2,1,0:T(8,128)(2,1)} %refs_6_.5) | copy-start | bytes 442372
  0.7 17.7 %copy-start.5 = (bf16[288,384]{1,0:T(8,128)(2,1)S(1)}, bf16[288,384]{1,0:T(8,128)(2,1)}, u32[]{:S(2)}) copy-start(bf16[288,384]{1,0:T(8,128)(2,1)} %constant.17.clone.refs_10_) | copy-start | bytes 663556
  0.7 17.7 %copy-start.6 = (bf16[256,144]{1,0:T(8,128)(2,1)S(1)}, bf16[256,144]{1,0:T(8,128)(2,1)}, u32[]{:S(2)}) copy-start(bf16[256,144]{1,0:T(8,128)(2,1)} %constant.18.clone.refs_11_) | copy-start | bytes 221188
  5.2 1.5 %collective-permute-start = (bf16[192,192]{1,0:T(8,128)(2,1)S(1)}, bf16[192,192]{1,0:T(8,128)(2,1)S(1)}, u32[]{:S(2)}, u32[]{:S(2)}) collective-permute-start(bf16[192,192]{1,0:T(8,128)(2,1)S(1)} %get-tuple-element.29), channel_id=1, source_target_pairs={{1,0},{0,1},{3,2},{2,3},{5,4},{4,5},{7,6},{6,7},{9,8},{8,9},{11,10... | collective-permute-start | bytes 221192 | tf_op jit(solution)/shard_map/ppermute | solution.py:445
  6.7 11.7 %copy-start.2 = (bf16[2,192,576]{2,1,0:T(8,128)(2,1)S(1)}, bf16[2,192,576]{2,1,0:T(8,128)(2,1)}, u32[]{:S(2)}) copy-start(bf16[2,192,576]{2,1,0:T(8,128)(2,1)} %refs_5_.5) | copy-start | bytes 1327108
  6.7 9.0 %collective-permute-start.1 = (bf16[96,192]{1,0:T(8,128)(2,1)S(1)}, bf16[96,192]{1,0:T(8,128)(2,1)S(1)}, u32[]{:S(2)}, u32[]{:S(2)}) collective-permute-start(bf16[96,192]{1,0:T(8,128)(2,1)S(1)} %pad_maximum_fusion), channel_id=1, source_target_pairs={{6,0},{4,2},{10,4},{8,6},{14,8},{12,10},{18,12},{16,14},{22,16},{2... | collective-permute-start | bytes 110600 | tf_op jit(solution)/shard_map/ppermute | solution.py:445
  13.6 4.1 %collective-permute-start.2 = (bf16[96,192]{1,0:T(8,128)(2,1)S(1)}, bf16[96,192]{1,0:T(8,128)(2,1)S(1)}, u32[]{:S(2)}, u32[]{:S(2)}) collective-permute-start(bf16[96,192]{1,0:T(8,128)(2,1)S(1)} %pad_maximum_fusion.1), channel_id=1, source_target_pairs={{4,0},{8,4},{12,8},{16,12},{20,16},{24,20},{28,24},{0,28},{5,1},{9... | collective-permute-start | bytes 110600 | tf_op jit(solution)/shard_map/ppermute | solution.py:445
  14.2 4.2 %collective-permute-start.3 = (bf16[96,192]{1,0:T(8,128)(2,1)S(1)}, bf16[96,192]{1,0:T(8,128)(2,1)S(1)}, u32[]{:S(2)}, u32[]{:S(2)}) collective-permute-start(bf16[96,192]{1,0:T(8,128)(2,1)S(1)} %pad_maximum_fusion.2), channel_id=1, source_target_pairs={{2,0},{0,2},{3,1},{1,3},{6,4},{4,6},{7,5},{5,7},{10,8},{8,10},{11,... | collective-permute-start | bytes 110600 | tf_op jit(solution)/shard_map/ppermute | solution.py:445
  14.8 3.6 %copy-start.1 = (bf16[2,768,192]{1,2,0:T(8,128)(2,1)S(1)}, bf16[2,768,192]{1,2,0:T(8,128)(2,1)}, u32[]{:S(2)}) copy-start(bf16[2,768,192]{1,2,0:T(8,128)(2,1)} %param.26) | copy-start | bytes 1769476
  14.8 3.6 %copy-start = (bf16[2,192,768]{2,1,0:T(8,128)(2,1)S(1)}, bf16[2,192,768]{2,1,0:T(8,128)(2,1)}, u32[]{:S(2)}) copy-start(bf16[2,192,768]{2,1,0:T(8,128)(2,1)} %refs_7_.5) | copy-start | bytes 1769476
  14.8 3.6 %copy-start.9 = (f32[2,2,192]{2,1,0:T(2,128)S(1)}, f32[2,2,192]{2,1,0:T(2,128)}, u32[]{:S(2)}) copy-start(f32[2,2,192]{2,1,0:T(2,128)} %refs_4_.5) | copy-start | bytes 9220
  22.0 1.3 %collective-permute-start.4 = (bf16[128,192]{1,0:T(8,128)(2,1)S(1)}, bf16[128,192]{1,0:T(8,128)(2,1)S(1)}, u32[]{:S(2)}, u32[]{:S(2)}) collective-permute-start(bf16[128,192]{1,0:T(8,128)(2,1)S(1)} %get-tuple-element.34), channel_id=1, source_target_pairs={{1,0},{0,1},{3,2},{2,3},{5,4},{4,5},{7,6},{6,7},{9,8},{8,9},{11,10... | collective-permute-start | bytes 147464 | tf_op jit(solution)/shard_map/ppermute | solution.py:445
  23.3 7.6 %collective-permute-start.5 = (bf16[64,192]{1,0:T(8,128)(2,1)S(1)}, bf16[64,192]{1,0:T(8,128)(2,1)S(1)}, u32[]{:S(2)}, u32[]{:S(2)}) collective-permute-start(bf16[64,192]{1,0:T(8,128)(2,1)S(1)} %pad_maximum_fusion.4), channel_id=1, source_target_pairs={{30,0},{28,2},{2,4},{0,6},{6,8},{4,10},{10,12},{8,14},{14,16},{12,... | collective-permute-start | bytes 73736 | tf_op jit(solution)/shard_map/ppermute | solution.py:445
  24.9 6.7 %copy-start.7 = (bf16[192,144]{1,0:T(8,128)(2,1)S(1)}, bf16[192,144]{1,0:T(8,128)(2,1)}, u32[]{:S(2)}) copy-start(bf16[192,144]{1,0:T(8,128)(2,1)} %constant.20.clone.refs_18_) | copy-start | bytes 165892
  24.9 6.7 %collective-permute-start.6 = (bf16[64,192]{1,0:T(8,128)(2,1)S(1)}, bf16[64,192]{1,0:T(8,128)(2,1)S(1)}, u32[]{:S(2)}, u32[]{:S(2)}) collective-permute-start(bf16[64,192]{1,0:T(8,128)(2,1)S(1)} %pad_maximum_fusion.5), channel_id=1, source_target_pairs={{28,0},{0,4},{4,8},{8,12},{12,16},{16,20},{20,24},{24,28},{29,1},{... | collective-permute-start | bytes 73736 | tf_op jit(solution)/shard_map/ppermute | solution.py:445
  25.0 6.6 %copy-start.8 = (bf16[144,256]{1,0:T(8,128)(2,1)S(1)}, bf16[144,256]{1,0:T(8,128)(2,1)}, u32[]{:S(2)}) copy-start(bf16[144,256]{1,0:T(8,128)(2,1)} %constant.19.clone.refs_17_) | copy-start | bytes 221188
  25.0 6.5 %collective-permute-start.7 = (bf16[64,192]{1,0:T(8,128)(2,1)S(1)}, bf16[64,192]{1,0:T(8,128)(2,1)S(1)}, u32[]{:S(2)}, u32[]{:S(2)}) collective-permute-start(bf16[64,192]{1,0:T(8,128)(2,1)S(1)} %pad_maximum_fusion.6), channel_id=1, source_target_pairs={{2,0},{0,2},{3,1},{1,3},{6,4},{4,6},{7,5},{5,7},{10,8},{8,10},{11,... | collective-permute-start | bytes 73736 | tf_op jit(solution)/shard_map/ppermute | solution.py:445
  33.7 1.3 %collective-permute-start.8 = (bf16[168,128]{1,0:T(8,128)(2,1)S(1)}, bf16[168,128]{1,0:T(8,128)(2,1)S(1)}, u32[]{:S(2)}, u32[]{:S(2)}) collective-permute-start(bf16[168,128]{1,0:T(8,128)(2,1)S(1)} %get-tuple-element.50), channel_id=1, source_target_pairs={{1,0},{0,1},{3,2},{2,3},{5,4},{4,5},{7,6},{6,7},{9,8},{8,9},{11,10... | collective-permute-start | bytes 129032 | tf_op jit(solution)/shard_map/ppermute | solution.py:470
  35.0 5.1 %collective-permute-start.11 = (bf16[168,128]{1,0:T(8,128)(2,1)S(1)}, bf16[168,128]{1,0:T(8,128)(2,1)S(1)}, u32[]{:S(2)}, u32[]{:S(2)}) collective-permute-start(bf16[168,128]{1,0:T(8,128)(2,1)S(1)} %add_convert_fusion.2), channel_id=1, source_target_pairs={{6,0},{4,2},{2,4},{0,6},{14,8},{12,10},{10,12},{8,14},{22,16},{20,... | collective-permute-start | bytes 129032 | tf_op jit(solution)/shard_map/ppermute | solution.py:470
  35.1 5.5 %collective-permute-start.10 = (bf16[168,128]{1,0:T(8,128)(2,1)S(1)}, bf16[168,128]{1,0:T(8,128)(2,1)S(1)}, u32[]{:S(2)}, u32[]{:S(2)}) collective-permute-start(bf16[168,128]{1,0:T(8,128)(2,1)S(1)} %add_convert_fusion.2), channel_id=1, source_target_pairs={{4,0},{0,4},{12,8},{8,12},{20,16},{16,20},{28,24},{24,28},{5,1},{1... | collective-permute-start | bytes 129032 | tf_op jit(solution)/shard_map/ppermute | solution.py:470
  38.0 4.0 %collective-permute-start.9 = (bf16[168,128]{1,0:T(8,128)(2,1)S(1)}, bf16[168,128]{1,0:T(8,128)(2,1)S(1)}, u32[]{:S(2)}, u32[]{:S(2)}) collective-permute-start(bf16[168,128]{1,0:T(8,128)(2,1)S(1)} %add_convert_fusion.2), channel_id=1, source_target_pairs={{2,0},{0,2},{3,1},{1,3},{6,4},{4,6},{7,5},{5,7},{10,8},{8,10},{11,... | collective-permute-start | bytes 129032 | tf_op jit(solution)/shard_map/ppermute | solution.py:470
  42.1 5.9 %collective-permute-start.14 = (bf16[168,128]{1,0:T(8,128)(2,1)S(1)}, bf16[168,128]{1,0:T(8,128)(2,1)S(1)}, u32[]{:S(2)}, u32[]{:S(2)}) collective-permute-start(bf16[168,128]{1,0:T(8,128)(2,1)S(1)} %add_convert_fusion.1), channel_id=1, source_target_pairs={{24,0},{28,4},{16,8},{20,12},{8,16},{12,20},{0,24},{4,28},{25,1},{... | collective-permute-start | bytes 129032 | tf_op jit(solution)/shard_map/ppermute | solution.py:470
  43.3 5.7 %collective-permute-start.13 = (bf16[168,128]{1,0:T(8,128)(2,1)S(1)}, bf16[168,128]{1,0:T(8,128)(2,1)S(1)}, u32[]{:S(2)}, u32[]{:S(2)}) collective-permute-start(bf16[168,128]{1,0:T(8,128)(2,1)S(1)} %add_convert_fusion.1), channel_id=1, source_target_pairs={{16,0},{20,4},{24,8},{28,12},{0,16},{4,20},{8,24},{12,28},{17,1},{... | collective-permute-start | bytes 129032 | tf_op jit(solution)/shard_map/ppermute | solution.py:470
  43.3 5.7 %collective-permute-start.12 = (bf16[168,128]{1,0:T(8,128)(2,1)S(1)}, bf16[168,128]{1,0:T(8,128)(2,1)S(1)}, u32[]{:S(2)}, u32[]{:S(2)}) collective-permute-start(bf16[168,128]{1,0:T(8,128)(2,1)S(1)} %add_convert_fusion.1), channel_id=1, source_target_pairs={{8,0},{12,4},{0,8},{4,12},{24,16},{28,20},{16,24},{20,28},{9,1},{1... | collective-permute-start | bytes 129032 | tf_op jit(solution)/shard_map/ppermute | solution.py:470
  49.0 1.3 %collective-permute-start.15 = (bf16[168,128]{1,0:T(8,128)(2,1)S(1)}, bf16[168,128]{1,0:T(8,128)(2,1)S(1)}, u32[]{:S(2)}, u32[]{:S(2)}) collective-permute-start(bf16[168,128]{1,0:T(8,128)(2,1)S(1)} %add_convert_fusion.mine), channel_id=1, source_target_pairs={{1,0},{0,1},{3,2},{2,3},{5,4},{4,5},{7,6},{6,7},{9,8},{8,9},{11,10... | collective-permute-start | bytes 129032 | tf_op jit(solution)/shard_map/ppermute | solution.py:470

commit v12 on v10

--- a/solution.py
+++ b/solution.py
@@ -49,21 +49,24 @@
     return as_half(move)
 
 
-def octants_out(pitch, first, flip, source):
-    move = np.zeros((8 * pitch, CELLS), np.float32)
-    for z, a, o in cells():
-        part, place = octant_of(z, a, o)
-        move[(7 - part if flip else part) * pitch + first + place, source(z, a, o)] = 1
-    return as_half(move)
-
-
-def octants_in(pitch, first, flip):
-    move = np.zeros((CELLS, 8 * pitch), np.float32)
+def octants_out(count, first, flip, source):
+    pitch = -(-count // 8) * 8
+    move = np.zeros((4 * pitch + 4 * count, CELLS), np.float32)
     for z, a, o in cells():
         part, place = octant_of(z, a, o)
         part = 7 - part if flip else part
-        block = (part % 4) * 2 + part // 4
-        move[inner_row(z, a, o), block * pitch + first + place] = 1
+        start = part * pitch if part < 4 else 4 * pitch + (part - 4) * count
+        move[start + first + place, source(z, a, o)] = 1
+    return as_half(move)
+
+
+def octants_in(count, first, flip):
+    pitch = -(-2 * count // 16) * 16
+    move = np.zeros((CELLS, 4 * pitch), np.float32)
+    for z, a, o in cells():
+        part, place = octant_of(z, a, o)
+        part = 7 - part if flip else part
+        move[inner_row(z, a, o), part % 4 * pitch + part // 4 * count + first + place] = 1
     return as_half(move)
 
 
@@ -341,10 +344,10 @@
     slope_o[...] = slope.astype(HALF)
     active = (upward * below).astype(HALF)
     result = (resid + dot_nt(active, have["wdown"][...])).astype(HALF)
-    moved = (dot(have["out_first"][...], result) + ready).astype(HALF)
-    send_o[...] = moved[192:]
+    moved = dot(have["out_first"][...], result) + ready
+    send_o[...] = moved[160:].astype(HALF)
     for n in range(4):
-        keep_o[n][...] = moved[n * 48 : n * 48 + 48]
+        keep_o[n][...] = moved[n * 40 : n * 40 + 36].astype(HALF)
 
 
 def second_bias(tbl, after, bias, table, xs, cols):
@@ -357,8 +360,9 @@
     parts, rest = refs[:4], refs[4:]
     gains, wqkv, wproj, wup, wdown, bias, into, out_of, send_o = rest[:9]
     keep, stack, prob = rest[9:13], rest[13], rest[14]
+    stack[...] = jnp.zeros_like(stack)
     for n, part in zip(order, parts):
-        stack[n * 96 : n * 96 + 96, :] = part[...]
+        stack[n * 80 : n * 80 + 72, :] = part[...]
     both = dot(into[...], stack[...])
     x, dflat = both[:CELLS], both[CELLS:].astype(HALF)
     gains, wqkv, wproj, wup, wdown = (w.at[1] for w in (gains, wqkv, wproj, wup, wdown))
@@ -368,18 +372,19 @@
     upward = dot(normed, wup[...])
     slope = gelu_parts(upward)[1]
     dx = backward(dflat, x, qkv, prob, resid, slope, gains, wqkv, wproj, wup, wdown)
-    moved = dot(out_of[...], dx.astype(HALF)).astype(HALF)
-    send_o[...] = moved[128:]
+    moved = dot(out_of[...], dx.astype(HALF))
+    send_o[...] = moved[96:].astype(HALF)
     for n in range(4):
-        keep[n][...] = moved[n * 32 : n * 32 + 32]
+        keep[n][...] = moved[n * 24 : n * 24 + 18].astype(HALF)
 
 
 def third_kernel(*refs):
     parts, rest = refs[:4], refs[4:]
     gains, wqkv, wproj, wup, wdown, patch, x_i, qkv_i, prob, resid, slope, into, out_of = rest[:13]
     grad_o, mine_o, other_o, stack, terms = rest[13:]
+    stack[...] = jnp.zeros_like(stack)
     for n, part in zip(order, parts):
-        stack[n * 64 : n * 64 + 64, :] = part[...]
+        stack[n * 48 : n * 48 + 36, :] = part[...]
     dflat = dot(into[...], stack[...]).astype(HALF)
     qkv = tuple(qkv_i[n] for n in range(3))
     gains, wqkv, wproj, wup, wdown = (w.at[0] for w in (gains, wqkv, wproj, wup, wdown))
@@ -526,8 +531,8 @@
     operands = (
         table, upper_fields, surface_fields, jnp.asarray(natural_to_inner()), upper_embed,
         surface_embed, *weights, out_grad.transpose(1, 2, 0, 3),
-        jnp.asarray(octants_out(48, 0, True, inner_row)),
-        jnp.asarray(octants_out(48, 18, True, from_cot)),
+        jnp.asarray(octants_out(36, 0, True, inner_row)),
+        jnp.asarray(octants_out(36, 18, True, from_cot)),
     )
     local = [
         pltpu.VMEM(v.shape[1:] if 7 <= n < 11 else v.shape, v.dtype) for n, v in enumerate(operands)
@@ -546,7 +551,7 @@
     ]
     patch, x, qkv, prob, resid, slope, send, *keep = call(
         first_kernel,
-        held + [shape((192, WIDTH))] + [shape((48, WIDTH))] * 4,
+        held + [shape((144, WIDTH))] + [shape((36, WIDTH))] * 4,
         local
         + [
             pltpu.VMEM((576, 128), FULL),
@@ -567,20 +572,20 @@
     bias_shape = shape((HEADS * CELLS, CELLS), FULL)
     got = fetch(send, {"section": 1})
     bias = call(second_bias, bias_shape, [*scratch_bias, scratch_cols], table, got)
-    into = np.concatenate((octants_in(48, 0, False), octants_in(48, 18, False)), 0)
+    into = np.concatenate((octants_in(36, 0, False), octants_in(36, 18, False)), 0)
     send, *keep = call(
         second_kernel,
-        [shape((128, WIDTH))] + [shape((32, WIDTH))] * 4,
-        [pltpu.VMEM((8 * 48, WIDTH), HALF), pltpu.VMEM((HEADS * CELLS, CELLS), HALF)],
+        [shape((72, WIDTH))] + [shape((18, WIDTH))] * 4,
+        [pltpu.VMEM((320, WIDTH), HALF), pltpu.VMEM((HEADS * CELLS, CELLS), HALF)],
         *exchange(keep, got, 1), *weights, bias,
-        jnp.asarray(into), jnp.asarray(octants_out(32, 0, False, inner_row)),
+        jnp.asarray(into), jnp.asarray(octants_out(18, 0, False, inner_row)),
     )
     latent_grad, mine, other = call(
         third_kernel,
         [shape((2, 6, 12, WIDTH)), shape((168, 128)), shape((168, 128))],
-        [pltpu.VMEM((8 * 32, WIDTH), HALF), pltpu.VMEM((336, 128), FULL)],
+        [pltpu.VMEM((192, WIDTH), HALF), pltpu.VMEM((336, 128), FULL)],
         *exchange(keep, fetch(send, {"section": -1}), -1), *weights, patch, x, qkv, prob, resid, slope,
-        jnp.asarray(octants_in(32, 0, True)), jnp.asarray(inner_to_padded()),
+        jnp.asarray(octants_in(18, 0, True)), jnp.asarray(inner_to_padded()),
     )
     scale = float(levels * sections * rows * bands * columns * lax.axis_size("lon")) ** (-0.5)
     upper_grad, surface_grad = call(

time: 51.3 us -> 51 us (level)
  transfers between devices with their start and end apart: 16 -> 16, of which waited for: 13 -> 13; matrix products, arithmetic and copies ran while one was open for 1% -> 2% of each run, Pallas kernels for 2% -> 2%
where the time goes in v12:
time: 51 us; the launch traced here: 50.8 us
  starting transfers between devices  20 us (39%)
  waiting for transfers between devices  17.1 us (34%)
  Pallas kernels  12 us (24%)
  between operations  0.86 us (2%)
  local copies, waits for them, and re-layouts  0.79 us (2%)
    pallas_call x5, Pallas kernels, call(): pl.pallas_call(kernel, out_shape=outs, in_specs=[spec for a in args], out...  12 us
    ppermute x8, starting transfers between devices, fetch(): return lax.ppermute(block, tuple(axes), pairs)  11.8 us
    ppermute x8, waiting for transfers between devices, fetch(): return lax.ppermute(block, tuple(axes), pairs)  9.42 us
    ppermute x8, starting transfers between devices, swap(): return lax.ppermute(block, tuple(axes), pairs)  8.14 us
    ppermute x8, waiting for transfers between devices, swap(): return lax.ppermute(block, tuple(axes), pairs)  7.64 us
  transfers between devices with their start and end apart: 16, of which 13 were waited for; matrix products, arithmetic and copies ran while one was open for 2% of the time, Pallas kernels for 2%

profile of v12, /device:TPU:0, one launch (start us, length us, event | category | flops | bytes accessed | tf_op | source)
XLA Modules:
  0.0 50.8 jit_solution(18036337443103343909)
XLA Ops:
  0.7 4.6 %shard_map.193 = (bf16[144,256]{1,0:T(8,128)(2,1)S(1)}, bf16[144,192]{1,0:T(8,128)(2,1)S(1)}, bf16[3,144,192]{2,1,0:T(8,128)(2,1)S(1)}, bf16[864,144]{1,0:T(8,12...) custom-call(f32[12,1,3312]{2,1,0:T(1,128)} %bitcast.6, ...), custom_call_target="tpu_custom_call" | custom-call | flops 1000000 | bytes 1000000 | tf_op jit(solution)/shard_map/pallas_call | solution.py:413
  5.3 0.5 %collective-permute-start = (bf16[144,192]{1,0:T(8,128)(2,1)S(1)}, bf16[144,192]{1,0:T(8,128)(2,1)S(1)}, u32[]{:S(2)}, u32[]{:S(2)}) collective-permute-start(bf16[144,192]{1,0:T(8,128)(2,1)S(1)} %get-tuple-element.25), channel_id=1, source_target_pairs={{1,0},{0,1},{3,2},{2,3},{5,4},{4,5},{7,6},{6,7},{9,8},{8,9},{11,10... | collective-permute-start | bytes 165896 | tf_op jit(solution)/shard_map/ppermute | solution.py:440
  5.8 0.9 %collective-permute-done.after = bf16[144,192]{1,0:T(8,128)(2,1)S(1)} collective-permute-done((bf16[144,192]{1,0:T(8,128)(2,1)S(1)}, bf16[144,192]{1,0:T(8,128)(2,1)S(1)}, u32[]{:S(2)}, u32[]{:S(2)}) %collective-permute-start) | collective-permute-done | bytes 55328 | tf_op jit(solution)/shard_map/ppermute | solution.py:440
  6.7 6.9 %collective-permute-start.1 = (bf16[72,192]{1,0:T(8,128)(2,1)S(1)}, bf16[72,192]{1,0:T(8,128)(2,1)S(1)}, u32[]{:S(2)}, u32[]{:S(2)}) collective-permute-start(bf16[72,192]{1,0:T(8,128)(2,1)S(1)} %pad_maximum_fusion), channel_id=1, source_target_pairs={{6,0},{4,2},{10,4},{8,6},{14,8},{12,10},{18,12},{16,14},{22,16},{2... | collective-permute-start | bytes 82952 | tf_op jit(solution)/shard_map/ppermute | solution.py:440
  13.7 0.5 %collective-permute-start.2 = (bf16[72,192]{1,0:T(8,128)(2,1)S(1)}, bf16[72,192]{1,0:T(8,128)(2,1)S(1)}, u32[]{:S(2)}, u32[]{:S(2)}) collective-permute-start(bf16[72,192]{1,0:T(8,128)(2,1)S(1)} %pad_maximum_fusion.1), channel_id=1, source_target_pairs={{4,0},{8,4},{12,8},{16,12},{20,16},{24,20},{28,24},{0,28},{5,1},{9... | collective-permute-start | bytes 82952 | tf_op jit(solution)/shard_map/ppermute | solution.py:440
  14.2 0.6 %collective-permute-start.3 = (bf16[72,192]{1,0:T(8,128)(2,1)S(1)}, bf16[72,192]{1,0:T(8,128)(2,1)S(1)}, u32[]{:S(2)}, u32[]{:S(2)}) collective-permute-start(bf16[72,192]{1,0:T(8,128)(2,1)S(1)} %pad_maximum_fusion.2), channel_id=1, source_target_pairs={{2,0},{0,2},{3,1},{1,3},{6,4},{4,6},{7,5},{5,7},{10,8},{8,10},{11,... | collective-permute-start | bytes 82952 | tf_op jit(solution)/shard_map/ppermute | solution.py:440
  14.9 0.9 %shard_map.194.refs_9_ = f32[864,144]{1,0:T(8,128)S(1)} custom-call(f32[12,1,3312]{2,1,0:T(1,128)S(1)} %bitcast.7, bf16[144,192]{1,0:T(8,128)(2,1)S(1)} %collective-permute-done.after), custom_call_target="tpu_custom_call" | custom-call | flops 1000000 | bytes 1000000 | tf_op jit(solution)/shard_map/pallas_call | solution.py:413
  15.8 1.9 %collective-permute-done.2.refs_1_ = bf16[72,192]{1,0:T(8,128)(2,1)S(1)} collective-permute-done((bf16[72,192]{1,0:T(8,128)(2,1)S(1)}, bf16[72,192]{1,0:T(8,128)(2,1)S(1)}, u32[]{:S(2)}, u32[]{:S(2)}) %collective-permute-start.2) | collective-permute-done | bytes 27680 | tf_op jit(solution)/shard_map/ppermute | solution.py:440
  17.7 0.6 %collective-permute-done.3.refs_2_ = bf16[72,192]{1,0:T(8,128)(2,1)S(1)} collective-permute-done((bf16[72,192]{1,0:T(8,128)(2,1)S(1)}, bf16[72,192]{1,0:T(8,128)(2,1)S(1)}, u32[]{:S(2)}, u32[]{:S(2)}) %collective-permute-start.3) | collective-permute-done | bytes 27680 | tf_op jit(solution)/shard_map/ppermute | solution.py:440
  18.3 3.6 %shard_map.195 = (bf16[72,192]{1,0:T(8,128)(2,1)S(1)}, bf16[18,192]{1,0:T(8,128)(2,1)S(1)}, bf16[18,192]{1,0:T(8,128)(2,1)S(1)}, bf16[18,192]{1,0:T(8,128)(2,1)S(1)}, bf16[18,192]{1,0:T(8,128)(2,1)S(1)}) custom-call(bf16[72,192]{1,0:T(8,128)(2,1)S(1)} %collective-permute-done.1.refs_0_, bf16[72,192]{1,0:T(8,128)(2,1)S(1)} %collective-permute-done.2.refs_1_, ...), custom_call_target="tpu_custom_call" | custom-call | flops 1000000 | bytes 1000000 | tf_op jit(solution)/shard_map/pallas_call | solution.py:413
  21.9 1.2 %collective-permute-done.4 = bf16[72,192]{1,0:T(8,128)(2,1)S(1)} collective-permute-done((bf16[72,192]{1,0:T(8,128)(2,1)S(1)}, bf16[72,192]{1,0:T(8,128)(2,1)S(1)}, u32[]{:S(2)}, u32[]{:S(2)}) %collective-permute-start.4) | collective-permute-done | bytes 27680 | tf_op jit(solution)/shard_map/ppermute | solution.py:440
  23.2 1.5 %collective-permute-start.5 = (bf16[36,192]{1,0:T(8,128)(2,1)S(1)}, bf16[36,192]{1,0:T(8,128)(2,1)S(1)}, u32[]{:S(2)}, u32[]{:S(2)}) collective-permute-start(bf16[36,192]{1,0:T(8,128)(2,1)S(1)} %pad_maximum_fusion.4), channel_id=1, source_target_pairs={{30,0},{28,2},{2,4},{0,6},{6,8},{4,10},{10,12},{8,14},{14,16},{12,... | collective-permute-start | bytes 41480 | tf_op jit(solution)/shard_map/ppermute | solution.py:440
  24.7 0.1 collective-permute-start.6
  24.9 1.5 %collective-permute-start.7 = (bf16[36,192]{1,0:T(8,128)(2,1)S(1)}, bf16[36,192]{1,0:T(8,128)(2,1)S(1)}, u32[]{:S(2)}, u32[]{:S(2)}) collective-permute-start(bf16[36,192]{1,0:T(8,128)(2,1)S(1)} %pad_maximum_fusion.6), channel_id=1, source_target_pairs={{2,0},{0,2},{3,1},{1,3},{6,4},{4,6},{7,5},{5,7},{10,8},{8,10},{11,... | collective-permute-start | bytes 41480 | tf_op jit(solution)/shard_map/ppermute | solution.py:440
  26.4 4.2 %collective-permute-done.5.refs_0_ = bf16[36,192]{1,0:T(8,128)(2,1)S(1)} collective-permute-done((bf16[36,192]{1,0:T(8,128)(2,1)S(1)}, bf16[36,192]{1,0:T(8,128)(2,1)S(1)}, u32[]{:S(2)}, u32[]{:S(2)}) %collective-permute-start.5) | collective-permute-done | bytes 13856 | tf_op jit(solution)/shard_map/ppermute | solution.py:440
  30.6 0.7 %collective-permute-done.6.refs_1_ = bf16[36,192]{1,0:T(8,128)(2,1)S(1)} collective-permute-done((bf16[36,192]{1,0:T(8,128)(2,1)S(1)}, bf16[36,192]{1,0:T(8,128)(2,1)S(1)}, u32[]{:S(2)}, u32[]{:S(2)}) %collective-permute-start.6) | collective-permute-done | bytes 13856 | tf_op jit(solution)/shard_map/ppermute | solution.py:440
  31.3 2.1 %shard_map.196 = (bf16[2,6,12,192]{3,2,1,0:T(8,128)(2,1)S(1)}, bf16[168,128]{1,0:T(8,128)(2,1)S(1)}, bf16[168,128]{1,0:T(8,128)(2,1)S(1)}) custom-call(bf16[36,192]{1,0:T(8,128)(2,1)S(1)} %collective-permute-done.5.refs_0_, bf16[36,192]{1,0:T(8,128)(2,1)S(1)} %collective-permute-done.6.refs_1_, bf16[36,192]{1,0:T(8,128)(2,1)S(1)} %collective-permute-done.7.refs_2_, ...), custom_call_target="tpu_custom_call" | custom-call | flops 1000000 | bytes 1000000 | tf_op jit(solution)/shard_map/pallas_call | solution.py:413
  33.4 0.1 collective-permute-start.8
  33.5 1.2 %collective-permute-done.8 = bf16[168,128]{1,0:T(8,128)(2,1)S(1)} collective-permute-done((bf16[168,128]{1,0:T(8,128)(2,1)S(1)}, bf16[168,128]{1,0:T(8,128)(2,1)S(1)}, u32[]{:S(2)}, u32[]{:S(2)}) %collective-permute-start.8) | collective-permute-done | bytes 43040 | tf_op jit(solution)/shard_map/ppermute | solution.py:465
  34.7 0.1 collective-permute-start.11
  34.8 3.0 %collective-permute-start.10 = (bf16[168,128]{1,0:T(8,128)(2,1)S(1)}, bf16[168,128]{1,0:T(8,128)(2,1)S(1)}, u32[]{:S(2)}, u32[]{:S(2)}) collective-permute-start(bf16[168,128]{1,0:T(8,128)(2,1)S(1)} %add_convert_fusion.2), channel_id=1, source_target_pairs={{4,0},{0,4},{12,8},{8,12},{20,16},{16,20},{28,24},{24,28},{5,1},{1... | collective-permute-start | bytes 129032 | tf_op jit(solution)/shard_map/ppermute | solution.py:465
  37.8 0.5 %collective-permute-start.9 = (bf16[168,128]{1,0:T(8,128)(2,1)S(1)}, bf16[168,128]{1,0:T(8,128)(2,1)S(1)}, u32[]{:S(2)}, u32[]{:S(2)}) collective-permute-start(bf16[168,128]{1,0:T(8,128)(2,1)S(1)} %add_convert_fusion.2), channel_id=1, source_target_pairs={{2,0},{0,2},{3,1},{1,3},{6,4},{4,6},{7,5},{5,7},{10,8},{8,10},{11,... | collective-permute-start | bytes 129032 | tf_op jit(solution)/shard_map/ppermute | solution.py:465
  38.3 1.6 %collective-permute-done.11 = bf16[168,128]{1,0:T(8,128)(2,1)S(1)} collective-permute-done((bf16[168,128]{1,0:T(8,128)(2,1)S(1)}, bf16[168,128]{1,0:T(8,128)(2,1)S(1)}, u32[]{:S(2)}, u32[]{:S(2)}) %collective-permute-start.11) | collective-permute-done | bytes 43040 | tf_op jit(solution)/shard_map/ppermute | solution.py:465
  39.8 0.4 collective-permute-done.10
  40.3 1.5 %collective-permute-done.9 = bf16[168,128]{1,0:T(8,128)(2,1)S(1)} collective-permute-done((bf16[168,128]{1,0:T(8,128)(2,1)S(1)}, bf16[168,128]{1,0:T(8,128)(2,1)S(1)}, u32[]{:S(2)}, u32[]{:S(2)}) %collective-permute-start.9) | collective-permute-done | bytes 43040 | tf_op jit(solution)/shard_map/ppermute | solution.py:465
  41.8 1.2 %collective-permute-start.14 = (bf16[168,128]{1,0:T(8,128)(2,1)S(1)}, bf16[168,128]{1,0:T(8,128)(2,1)S(1)}, u32[]{:S(2)}, u32[]{:S(2)}) collective-permute-start(bf16[168,128]{1,0:T(8,128)(2,1)S(1)} %add_convert_fusion.1), channel_id=1, source_target_pairs={{24,0},{28,4},{16,8},{20,12},{8,16},{12,20},{0,24},{4,28},{25,1},{... | collective-permute-start | bytes 129032 | tf_op jit(solution)/shard_map/ppermute | solution.py:465
  43.0 3.3 %collective-permute-start.12 = (bf16[168,128]{1,0:T(8,128)(2,1)S(1)}, bf16[168,128]{1,0:T(8,128)(2,1)S(1)}, u32[]{:S(2)}, u32[]{:S(2)}) collective-permute-start(bf16[168,128]{1,0:T(8,128)(2,1)S(1)} %add_convert_fusion.1), channel_id=1, source_target_pairs={{8,0},{12,4},{0,8},{4,12},{24,16},{28,20},{16,24},{20,28},{9,1},{1... | collective-permute-start | bytes 129032 | tf_op jit(solution)/shard_map/ppermute | solution.py:465
  46.3 1.5 %collective-permute-done.14 = bf16[168,128]{1,0:T(8,128)(2,1)S(1)} collective-permute-done((bf16[168,128]{1,0:T(8,128)(2,1)S(1)}, bf16[168,128]{1,0:T(8,128)(2,1)S(1)}, u32[]{:S(2)}, u32[]{:S(2)}) %collective-permute-start.14) | collective-permute-done | bytes 43040 | tf_op jit(solution)/shard_map/ppermute | solution.py:465
  47.7 1.0 %collective-permute-done.13 = bf16[168,128]{1,0:T(8,128)(2,1)S(1)} collective-permute-done((bf16[168,128]{1,0:T(8,128)(2,1)S(1)}, bf16[168,128]{1,0:T(8,128)(2,1)S(1)}, u32[]{:S(2)}, u32[]{:S(2)}) %collective-permute-start.13) | collective-permute-done | bytes 43040 | tf_op jit(solution)/shard_map/ppermute | solution.py:465
  48.8 0.7 %copy.21 = bf16[2,6,12,192]{3,0,2,1:T(2,128)(2,1)} copy(bf16[2,6,12,192]{3,2,1,0:T(8,128)(2,1)S(1)} %get-tuple-element.45) | data formatting | bytes 110592
  49.5 0.5 collective-permute-done.15.other
  50.0 0.8 %shard_map.197 = (f32[160,192]{1,0:T(8,128)}, f32[64,192]{1,0:T(8,128)}) custom-call(bf16[168,128]{1,0:T(8,128)(2,1)S(1)} %add_convert_fusion.mine, bf16[168,128]{1,0:T(8,128)(2,1)S(1)} %collective-permute-done.15.other), custom_call_target="tpu_custom_call" | custom-call | flops 1000000 | bytes 1000000 | tf_op jit(solution)/shard_map/pallas_call | solution.py:413
  (39 shorter events, 0.4 us)
Async XLA Ops:
  0.6 17.6 %copy-start.2 = (bf16[2,192,576]{2,1,0:T(8,128)(2,1)S(1)}, bf16[2,192,576]{2,1,0:T(8,128)(2,1)}, u32[]{:S(2)}) copy-start(bf16[2,192,576]{2,1,0:T(8,128)(2,1)} %refs_5_.5) | copy-start | bytes 1327108
  0.6 17.6 %copy-start.5 = (bf16[288,320]{1,0:T(8,128)(2,1)S(1)}, bf16[288,320]{1,0:T(8,128)(2,1)}, u32[]{:S(2)}) copy-start(bf16[288,320]{1,0:T(8,128)(2,1)} %constant.17.clone.refs_10_) | copy-start | bytes 552964
  0.7 17.6 %copy-start.7 = (bf16[168,144]{1,0:T(8,128)(2,1)S(1)}, bf16[168,144]{1,0:T(8,128)(2,1)}, u32[]{:S(2)}) copy-start(bf16[168,144]{1,0:T(8,128)(2,1)} %constant.18.clone.refs_11_) | copy-start | bytes 145156
  5.3 1.4 %collective-permute-start = (bf16[144,192]{1,0:T(8,128)(2,1)S(1)}, bf16[144,192]{1,0:T(8,128)(2,1)S(1)}, u32[]{:S(2)}, u32[]{:S(2)}) collective-permute-start(bf16[144,192]{1,0:T(8,128)(2,1)S(1)} %get-tuple-element.25), channel_id=1, source_target_pairs={{1,0},{0,1},{3,2},{2,3},{5,4},{4,5},{7,6},{6,7},{9,8},{8,9},{11,10... | collective-permute-start | bytes 165896 | tf_op jit(solution)/shard_map/ppermute | solution.py:440
  6.7 8.2 %copy-start.4 = (f32[2,1,1,6,3312]{4,2,3,1,0:T(1,128)S(1)}, f32[2,1,1,6,3312]{4,2,3,1,0:T(1,128)}, u32[]{:S(2)}) copy-start(f32[2,1,1,6,3312]{4,2,3,1,0:T(1,128)} %param.27) | copy-start | bytes 476932
  6.7 11.5 %copy-start.3 = (bf16[2,192,192]{2,1,0:T(8,128)(2,1)S(1)}, bf16[2,192,192]{2,1,0:T(8,128)(2,1)}, u32[]{:S(2)}) copy-start(bf16[2,192,192]{2,1,0:T(8,128)(2,1)} %refs_6_.5) | copy-start | bytes 442372
  6.7 9.1 %collective-permute-start.1 = (bf16[72,192]{1,0:T(8,128)(2,1)S(1)}, bf16[72,192]{1,0:T(8,128)(2,1)S(1)}, u32[]{:S(2)}, u32[]{:S(2)}) collective-permute-start(bf16[72,192]{1,0:T(8,128)(2,1)S(1)} %pad_maximum_fusion), channel_id=1, source_target_pairs={{6,0},{4,2},{10,4},{8,6},{14,8},{12,10},{18,12},{16,14},{22,16},{2... | collective-permute-start | bytes 82952 | tf_op jit(solution)/shard_map/ppermute | solution.py:440
  13.7 4.0 %collective-permute-start.2 = (bf16[72,192]{1,0:T(8,128)(2,1)S(1)}, bf16[72,192]{1,0:T(8,128)(2,1)S(1)}, u32[]{:S(2)}, u32[]{:S(2)}) collective-permute-start(bf16[72,192]{1,0:T(8,128)(2,1)S(1)} %pad_maximum_fusion.1), channel_id=1, source_target_pairs={{4,0},{8,4},{12,8},{16,12},{20,16},{24,20},{28,24},{0,28},{5,1},{9... | collective-permute-start | bytes 82952 | tf_op jit(solution)/shard_map/ppermute | solution.py:440
  14.2 4.0 %collective-permute-start.3 = (bf16[72,192]{1,0:T(8,128)(2,1)S(1)}, bf16[72,192]{1,0:T(8,128)(2,1)S(1)}, u32[]{:S(2)}, u32[]{:S(2)}) collective-permute-start(bf16[72,192]{1,0:T(8,128)(2,1)S(1)} %pad_maximum_fusion.2), channel_id=1, source_target_pairs={{2,0},{0,2},{3,1},{1,3},{6,4},{4,6},{7,5},{5,7},{10,8},{8,10},{11,... | collective-permute-start | bytes 82952 | tf_op jit(solution)/shard_map/ppermute | solution.py:440
  14.8 3.4 %copy-start = (bf16[2,192,768]{2,1,0:T(8,128)(2,1)S(1)}, bf16[2,192,768]{2,1,0:T(8,128)(2,1)}, u32[]{:S(2)}) copy-start(bf16[2,192,768]{2,1,0:T(8,128)(2,1)} %refs_7_.5) | copy-start | bytes 1769476
  14.8 3.4 %copy-start.1 = (bf16[2,768,192]{1,2,0:T(8,128)(2,1)S(1)}, bf16[2,768,192]{1,2,0:T(8,128)(2,1)}, u32[]{:S(2)}) copy-start(bf16[2,768,192]{1,2,0:T(8,128)(2,1)} %param.26) | copy-start | bytes 1769476
  14.8 3.4 %copy-start.9 = (f32[2,2,192]{2,1,0:T(2,128)S(1)}, f32[2,2,192]{2,1,0:T(2,128)}, u32[]{:S(2)}) copy-start(f32[2,2,192]{2,1,0:T(2,128)} %refs_4_.5) | copy-start | bytes 9220
  21.8 1.3 %collective-permute-start.4 = (bf16[72,192]{1,0:T(8,128)(2,1)S(1)}, bf16[72,192]{1,0:T(8,128)(2,1)S(1)}, u32[]{:S(2)}, u32[]{:S(2)}) collective-permute-start(bf16[72,192]{1,0:T(8,128)(2,1)S(1)} %get-tuple-element.30), channel_id=1, source_target_pairs={{1,0},{0,1},{3,2},{2,3},{5,4},{4,5},{7,6},{6,7},{9,8},{8,9},{11,10... | collective-permute-start | bytes 82952 | tf_op jit(solution)/shard_map/ppermute | solution.py:440
  23.1 8.1 %copy-start.6 = (bf16[192,144]{1,0:T(8,128)(2,1)S(1)}, bf16[192,144]{1,0:T(8,128)(2,1)}, u32[]{:S(2)}) copy-start(bf16[192,144]{1,0:T(8,128)(2,1)} %constant.20.clone.refs_16_) | copy-start | bytes 165892
  23.2 7.4 %collective-permute-start.5 = (bf16[36,192]{1,0:T(8,128)(2,1)S(1)}, bf16[36,192]{1,0:T(8,128)(2,1)S(1)}, u32[]{:S(2)}, u32[]{:S(2)}) collective-permute-start(bf16[36,192]{1,0:T(8,128)(2,1)S(1)} %pad_maximum_fusion.4), channel_id=1, source_target_pairs={{30,0},{28,2},{2,4},{0,6},{6,8},{4,10},{10,12},{8,14},{14,16},{12,... | collective-permute-start | bytes 41480 | tf_op jit(solution)/shard_map/ppermute | solution.py:440
  24.7 6.6 %copy-start.8 = (bf16[144,192]{1,0:T(8,128)(2,1)S(1)}, bf16[144,192]{1,0:T(8,128)(2,1)}, u32[]{:S(2)}) copy-start(bf16[144,192]{1,0:T(8,128)(2,1)} %constant.19.clone.refs_15_) | copy-start | bytes 165892
  24.7 6.5 %collective-permute-start.6 = (bf16[36,192]{1,0:T(8,128)(2,1)S(1)}, bf16[36,192]{1,0:T(8,128)(2,1)S(1)}, u32[]{:S(2)}, u32[]{:S(2)}) collective-permute-start(bf16[36,192]{1,0:T(8,128)(2,1)S(1)} %pad_maximum_fusion.5), channel_id=1, source_target_pairs={{28,0},{0,4},{4,8},{8,12},{12,16},{16,20},{20,24},{24,28},{29,1},{... | collective-permute-start | bytes 41480 | tf_op jit(solution)/shard_map/ppermute | solution.py:440
  24.9 6.4 %collective-permute-start.7 = (bf16[36,192]{1,0:T(8,128)(2,1)S(1)}, bf16[36,192]{1,0:T(8,128)(2,1)S(1)}, u32[]{:S(2)}, u32[]{:S(2)}) collective-permute-start(bf16[36,192]{1,0:T(8,128)(2,1)S(1)} %pad_maximum_fusion.6), channel_id=1, source_target_pairs={{2,0},{0,2},{3,1},{1,3},{6,4},{4,6},{7,5},{5,7},{10,8},{8,10},{11,... | collective-permute-start | bytes 41480 | tf_op jit(solution)/shard_map/ppermute | solution.py:440
  33.4 1.3 %collective-permute-start.8 = (bf16[168,128]{1,0:T(8,128)(2,1)S(1)}, bf16[168,128]{1,0:T(8,128)(2,1)S(1)}, u32[]{:S(2)}, u32[]{:S(2)}) collective-permute-start(bf16[168,128]{1,0:T(8,128)(2,1)S(1)} %get-tuple-element.42), channel_id=1, source_target_pairs={{1,0},{0,1},{3,2},{2,3},{5,4},{4,5},{7,6},{6,7},{9,8},{8,9},{11,10... | collective-permute-start | bytes 129032 | tf_op jit(solution)/shard_map/ppermute | solution.py:465
  34.7 5.1 %collective-permute-start.11 = (bf16[168,128]{1,0:T(8,128)(2,1)S(1)}, bf16[168,128]{1,0:T(8,128)(2,1)S(1)}, u32[]{:S(2)}, u32[]{:S(2)}) collective-permute-start(bf16[168,128]{1,0:T(8,128)(2,1)S(1)} %add_convert_fusion.2), channel_id=1, source_target_pairs={{6,0},{4,2},{2,4},{0,6},{14,8},{12,10},{10,12},{8,14},{22,16},{20,... | collective-permute-start | bytes 129032 | tf_op jit(solution)/shard_map/ppermute | solution.py:465
  34.8 5.5 %collective-permute-start.10 = (bf16[168,128]{1,0:T(8,128)(2,1)S(1)}, bf16[168,128]{1,0:T(8,128)(2,1)S(1)}, u32[]{:S(2)}, u32[]{:S(2)}) collective-permute-start(bf16[168,128]{1,0:T(8,128)(2,1)S(1)} %add_convert_fusion.2), channel_id=1, source_target_pairs={{4,0},{0,4},{12,8},{8,12},{20,16},{16,20},{28,24},{24,28},{5,1},{1... | collective-permute-start | bytes 129032 | tf_op jit(solution)/shard_map/ppermute | solution.py:465
  37.8 4.0 %collective-permute-start.9 = (bf16[168,128]{1,0:T(8,128)(2,1)S(1)}, bf16[168,128]{1,0:T(8,128)(2,1)S(1)}, u32[]{:S(2)}, u32[]{:S(2)}) collective-permute-start(bf16[168,128]{1,0:T(8,128)(2,1)S(1)} %add_convert_fusion.2), channel_id=1, source_target_pairs={{2,0},{0,2},{3,1},{1,3},{6,4},{4,6},{7,5},{5,7},{10,8},{8,10},{11,... | collective-permute-start | bytes 129032 | tf_op jit(solution)/shard_map/ppermute | solution.py:465
  41.8 5.9 %collective-permute-start.14 = (bf16[168,128]{1,0:T(8,128)(2,1)S(1)}, bf16[168,128]{1,0:T(8,128)(2,1)S(1)}, u32[]{:S(2)}, u32[]{:S(2)}) collective-permute-start(bf16[168,128]{1,0:T(8,128)(2,1)S(1)} %add_convert_fusion.1), channel_id=1, source_target_pairs={{24,0},{28,4},{16,8},{20,12},{8,16},{12,20},{0,24},{4,28},{25,1},{... | collective-permute-start | bytes 129032 | tf_op jit(solution)/shard_map/ppermute | solution.py:465
  43.0 5.7 %collective-permute-start.13 = (bf16[168,128]{1,0:T(8,128)(2,1)S(1)}, bf16[168,128]{1,0:T(8,128)(2,1)S(1)}, u32[]{:S(2)}, u32[]{:S(2)}) collective-permute-start(bf16[168,128]{1,0:T(8,128)(2,1)S(1)} %add_convert_fusion.1), channel_id=1, source_target_pairs={{16,0},{20,4},{24,8},{28,12},{0,16},{4,20},{8,24},{12,28},{17,1},{... | collective-permute-start | bytes 129032 | tf_op jit(solution)/shard_map/ppermute | solution.py:465
  43.0 5.7 %collective-permute-start.12 = (bf16[168,128]{1,0:T(8,128)(2,1)S(1)}, bf16[168,128]{1,0:T(8,128)(2,1)S(1)}, u32[]{:S(2)}, u32[]{:S(2)}) collective-permute-start(bf16[168,128]{1,0:T(8,128)(2,1)S(1)} %add_convert_fusion.1), channel_id=1, source_target_pairs={{8,0},{12,4},{0,8},{4,12},{24,16},{28,20},{16,24},{20,28},{9,1},{1... | collective-permute-start | bytes 129032 | tf_op jit(solution)/shard_map/ppermute | solution.py:465
  48.7 1.3 %collective-permute-start.15 = (bf16[168,128]{1,0:T(8,128)(2,1)S(1)}, bf16[168,128]{1,0:T(8,128)(2,1)S(1)}, u32[]{:S(2)}, u32[]{:S(2)}) collective-permute-start(bf16[168,128]{1,0:T(8,128)(2,1)S(1)} %add_convert_fusion.mine), channel_id=1, source_target_pairs={{1,0},{0,1},{3,2},{2,3},{5,4},{4,5},{7,6},{6,7},{9,8},{8,9},{11,10... | collective-permute-start | bytes 129032 | tf_op jit(solution)/shard_map/ppermute | solution.py:465

commit v13 on v12

--- a/solution.py
+++ b/solution.py
@@ -151,7 +151,7 @@
                         ]
     total = None
     for zu in range(2):
-        x = jnp.concatenate((xs[zu * 2], xs[zu * 2 + 1]), 1)
+        x = jnp.concatenate((xs[zu * 2, :CELLS, :], xs[zu * 2 + 1, :CELLS, :]), 1)
         high = x.astype(HALF)
         left = x - high.astype(FULL)
         mid = left.astype(HALF)
@@ -332,7 +332,7 @@
     for a in range(6):
         for o in range(12):
             cots[(a * 12 + o) * 2 : (a * 12 + o) * 2 + 2, :] = cot[a, o].astype(FULL)
-    ready = dot(have["out_cot"][...], cots[...].astype(HALF))
+    ready = dot(have["out_cot"][...], cots[:CELLS, :].astype(HALF))
     qkv, resid = forward_half(x, gains, have["wqkv"], have["wproj"], bias, prob)
     for n in range(3):
         qkv_o[n] = qkv[n]
@@ -539,7 +539,7 @@
     ]
     local[0] = pltpu.VMEM((HEADS, 1, positions), FULL)
     local[4] = local[5] = pltpu.VMEM((16, 128), HALF)
-    scratch_bias = [pltpu.VMEM((8, 3328), FULL), pltpu.VMEM((4, CELLS, 128), FULL)]
+    scratch_bias = [pltpu.VMEM((8, 3328), FULL), pltpu.VMEM((4, 192, 128), FULL)]
     scratch_cols = pltpu.VMEM((2, 256, 384), HALF)
     held = [
         shape((CELLS, 256)),
@@ -557,7 +557,7 @@
             pltpu.VMEM((576, 128), FULL),
             pltpu.VMEM((288, 128), FULL),
             pltpu.VMEM((256, WIDTH), HALF),
-            pltpu.VMEM((CELLS, WIDTH), FULL),
+            pltpu.VMEM((160, WIDTH), FULL),
         ]
         + scratch_bias
         + [

time: 51 us -> 51 us (level)
  no operation moved by 1% of the time
where the time goes in v13:
time: 51 us; the launch traced here: 50.8 us
  starting transfers between devices  19.9 us (39%)
  waiting for transfers between devices  17.1 us (34%)
  Pallas kernels  12 us (24%)
  between operations  0.86 us (2%)
  local copies, waits for them, and re-layouts  0.79 us (2%)
    pallas_call x5, Pallas kernels, call(): pl.pallas_call(kernel, out_shape=outs, in_specs=[spec for a in args], out...  12 us
    ppermute x8, starting transfers between devices, fetch(): return lax.ppermute(block, tuple(axes), pairs)  11.8 us
    ppermute x8, waiting for transfers between devices, fetch(): return lax.ppermute(block, tuple(axes), pairs)  9.45 us
    ppermute x8, starting transfers between devices, swap(): return lax.ppermute(block, tuple(axes), pairs)  8.14 us
    ppermute x8, waiting for transfers between devices, swap(): return lax.ppermute(block, tuple(axes), pairs)  7.63 us
  transfers between devices with their start and end apart: 16, of which 13 were waited for; matrix products, arithmetic and copies ran while one was open for 2% of the time, Pallas kernels for 2%

profile of v13, /device:TPU:0, one launch (start us, length us, event | category | flops | bytes accessed | tf_op | source)
XLA Modules:
  0.0 50.8 jit_solution(712738154699352194)
XLA Ops:
  0.7 4.6 %shard_map.193 = (bf16[144,256]{1,0:T(8,128)(2,1)S(1)}, bf16[144,192]{1,0:T(8,128)(2,1)S(1)}, bf16[3,144,192]{2,1,0:T(8,128)(2,1)S(1)}, bf16[864,144]{1,0:T(8,12...) custom-call(f32[12,1,3312]{2,1,0:T(1,128)} %bitcast.6, ...), custom_call_target="tpu_custom_call" | custom-call | flops 1000000 | bytes 1000000 | tf_op jit(solution)/shard_map/pallas_call | solution.py:413
  5.3 0.5 collective-permute-start
  5.8 0.9 %collective-permute-done.after = bf16[144,192]{1,0:T(8,128)(2,1)S(1)} collective-permute-done((bf16[144,192]{1,0:T(8,128)(2,1)S(1)}, bf16[144,192]{1,0:T(8,128)(2,1)S(1)}, u32[]{:S(2)}, u32[]{:S(2)}) %collective-permute-start) | collective-permute-done | bytes 55328 | tf_op jit(solution)/shard_map/ppermute | solution.py:440
  6.7 6.9 %collective-permute-start.1 = (bf16[72,192]{1,0:T(8,128)(2,1)S(1)}, bf16[72,192]{1,0:T(8,128)(2,1)S(1)}, u32[]{:S(2)}, u32[]{:S(2)}) collective-permute-start(bf16[72,192]{1,0:T(8,128)(2,1)S(1)} %pad_maximum_fusion), channel_id=1, source_target_pairs={{6,0},{4,2},{10,4},{8,6},{14,8},{12,10},{18,12},{16,14},{22,16},{2... | collective-permute-start | bytes 82952 | tf_op jit(solution)/shard_map/ppermute | solution.py:440
  13.6 0.6 %collective-permute-start.2 = (bf16[72,192]{1,0:T(8,128)(2,1)S(1)}, bf16[72,192]{1,0:T(8,128)(2,1)S(1)}, u32[]{:S(2)}, u32[]{:S(2)}) collective-permute-start(bf16[72,192]{1,0:T(8,128)(2,1)S(1)} %pad_maximum_fusion.1), channel_id=1, source_target_pairs={{4,0},{8,4},{12,8},{16,12},{20,16},{24,20},{28,24},{0,28},{5,1},{9... | collective-permute-start | bytes 82952 | tf_op jit(solution)/shard_map/ppermute | solution.py:440
  14.2 0.6 %collective-permute-start.3 = (bf16[72,192]{1,0:T(8,128)(2,1)S(1)}, bf16[72,192]{1,0:T(8,128)(2,1)S(1)}, u32[]{:S(2)}, u32[]{:S(2)}) collective-permute-start(bf16[72,192]{1,0:T(8,128)(2,1)S(1)} %pad_maximum_fusion.2), channel_id=1, source_target_pairs={{2,0},{0,2},{3,1},{1,3},{6,4},{4,6},{7,5},{5,7},{10,8},{8,10},{11,... | collective-permute-start | bytes 82952 | tf_op jit(solution)/shard_map/ppermute | solution.py:440
  14.9 0.9 %shard_map.194.refs_9_ = f32[864,144]{1,0:T(8,128)S(1)} custom-call(f32[12,1,3312]{2,1,0:T(1,128)S(1)} %bitcast.7, bf16[144,192]{1,0:T(8,128)(2,1)S(1)} %collective-permute-done.after), custom_call_target="tpu_custom_call" | custom-call | flops 1000000 | bytes 1000000 | tf_op jit(solution)/shard_map/pallas_call | solution.py:413
  15.8 1.9 %collective-permute-done.2.refs_1_ = bf16[72,192]{1,0:T(8,128)(2,1)S(1)} collective-permute-done((bf16[72,192]{1,0:T(8,128)(2,1)S(1)}, bf16[72,192]{1,0:T(8,128)(2,1)S(1)}, u32[]{:S(2)}, u32[]{:S(2)}) %collective-permute-start.2) | collective-permute-done | bytes 27680 | tf_op jit(solution)/shard_map/ppermute | solution.py:440
  17.7 0.6 %collective-permute-done.3.refs_2_ = bf16[72,192]{1,0:T(8,128)(2,1)S(1)} collective-permute-done((bf16[72,192]{1,0:T(8,128)(2,1)S(1)}, bf16[72,192]{1,0:T(8,128)(2,1)S(1)}, u32[]{:S(2)}, u32[]{:S(2)}) %collective-permute-start.3) | collective-permute-done | bytes 27680 | tf_op jit(solution)/shard_map/ppermute | solution.py:440
  18.3 3.6 %shard_map.195 = (bf16[72,192]{1,0:T(8,128)(2,1)S(1)}, bf16[18,192]{1,0:T(8,128)(2,1)S(1)}, bf16[18,192]{1,0:T(8,128)(2,1)S(1)}, bf16[18,192]{1,0:T(8,128)(2,1)S(1)}, bf16[18,192]{1,0:T(8,128)(2,1)S(1)}) custom-call(bf16[72,192]{1,0:T(8,128)(2,1)S(1)} %collective-permute-done.1.refs_0_, bf16[72,192]{1,0:T(8,128)(2,1)S(1)} %collective-permute-done.2.refs_1_, ...), custom_call_target="tpu_custom_call" | custom-call | flops 1000000 | bytes 1000000 | tf_op jit(solution)/shard_map/pallas_call | solution.py:413
  21.9 0.1 collective-permute-start.4
  21.9 1.2 %collective-permute-done.4 = bf16[72,192]{1,0:T(8,128)(2,1)S(1)} collective-permute-done((bf16[72,192]{1,0:T(8,128)(2,1)S(1)}, bf16[72,192]{1,0:T(8,128)(2,1)S(1)}, u32[]{:S(2)}, u32[]{:S(2)}) %collective-permute-start.4) | collective-permute-done | bytes 27680 | tf_op jit(solution)/shard_map/ppermute | solution.py:440
  23.2 1.5 %collective-permute-start.5 = (bf16[36,192]{1,0:T(8,128)(2,1)S(1)}, bf16[36,192]{1,0:T(8,128)(2,1)S(1)}, u32[]{:S(2)}, u32[]{:S(2)}) collective-permute-start(bf16[36,192]{1,0:T(8,128)(2,1)S(1)} %pad_maximum_fusion.4), channel_id=1, source_target_pairs={{30,0},{28,2},{2,4},{0,6},{6,8},{4,10},{10,12},{8,14},{14,16},{12,... | collective-permute-start | bytes 41480 | tf_op jit(solution)/shard_map/ppermute | solution.py:440
  24.7 0.1 collective-permute-start.6
  24.9 1.5 %collective-permute-start.7 = (bf16[36,192]{1,0:T(8,128)(2,1)S(1)}, bf16[36,192]{1,0:T(8,128)(2,1)S(1)}, u32[]{:S(2)}, u32[]{:S(2)}) collective-permute-start(bf16[36,192]{1,0:T(8,128)(2,1)S(1)} %pad_maximum_fusion.6), channel_id=1, source_target_pairs={{2,0},{0,2},{3,1},{1,3},{6,4},{4,6},{7,5},{5,7},{10,8},{8,10},{11,... | collective-permute-start | bytes 41480 | tf_op jit(solution)/shard_map/ppermute | solution.py:440
  26.4 4.2 %collective-permute-done.5.refs_0_ = bf16[36,192]{1,0:T(8,128)(2,1)S(1)} collective-permute-done((bf16[36,192]{1,0:T(8,128)(2,1)S(1)}, bf16[36,192]{1,0:T(8,128)(2,1)S(1)}, u32[]{:S(2)}, u32[]{:S(2)}) %collective-permute-start.5) | collective-permute-done | bytes 13856 | tf_op jit(solution)/shard_map/ppermute | solution.py:440
  30.6 0.7 %collective-permute-done.6.refs_1_ = bf16[36,192]{1,0:T(8,128)(2,1)S(1)} collective-permute-done((bf16[36,192]{1,0:T(8,128)(2,1)S(1)}, bf16[36,192]{1,0:T(8,128)(2,1)S(1)}, u32[]{:S(2)}, u32[]{:S(2)}) %collective-permute-start.6) | collective-permute-done | bytes 13856 | tf_op jit(solution)/shard_map/ppermute | solution.py:440
  31.3 2.1 %shard_map.196 = (bf16[2,6,12,192]{3,2,1,0:T(8,128)(2,1)S(1)}, bf16[168,128]{1,0:T(8,128)(2,1)S(1)}, bf16[168,128]{1,0:T(8,128)(2,1)S(1)}) custom-call(bf16[36,192]{1,0:T(8,128)(2,1)S(1)} %collective-permute-done.5.refs_0_, bf16[36,192]{1,0:T(8,128)(2,1)S(1)} %collective-permute-done.6.refs_1_, bf16[36,192]{1,0:T(8,128)(2,1)S(1)} %collective-permute-done.7.refs_2_, ...), custom_call_target="tpu_custom_call" | custom-call | flops 1000000 | bytes 1000000 | tf_op jit(solution)/shard_map/pallas_call | solution.py:413
  33.5 1.2 %collective-permute-done.8 = bf16[168,128]{1,0:T(8,128)(2,1)S(1)} collective-permute-done((bf16[168,128]{1,0:T(8,128)(2,1)S(1)}, bf16[168,128]{1,0:T(8,128)(2,1)S(1)}, u32[]{:S(2)}, u32[]{:S(2)}) %collective-permute-start.8) | collective-permute-done | bytes 43040 | tf_op jit(solution)/shard_map/ppermute | solution.py:465
  34.7 0.1 collective-permute-start.11
  34.8 2.9 %collective-permute-start.10 = (bf16[168,128]{1,0:T(8,128)(2,1)S(1)}, bf16[168,128]{1,0:T(8,128)(2,1)S(1)}, u32[]{:S(2)}, u32[]{:S(2)}) collective-permute-start(bf16[168,128]{1,0:T(8,128)(2,1)S(1)} %add_convert_fusion.2), channel_id=1, source_target_pairs={{4,0},{0,4},{12,8},{8,12},{20,16},{16,20},{28,24},{24,28},{5,1},{1... | collective-permute-start | bytes 129032 | tf_op jit(solution)/shard_map/ppermute | solution.py:465
  37.7 0.5 %collective-permute-start.9 = (bf16[168,128]{1,0:T(8,128)(2,1)S(1)}, bf16[168,128]{1,0:T(8,128)(2,1)S(1)}, u32[]{:S(2)}, u32[]{:S(2)}) collective-permute-start(bf16[168,128]{1,0:T(8,128)(2,1)S(1)} %add_convert_fusion.2), channel_id=1, source_target_pairs={{2,0},{0,2},{3,1},{1,3},{6,4},{4,6},{7,5},{5,7},{10,8},{8,10},{11,... | collective-permute-start | bytes 129032 | tf_op jit(solution)/shard_map/ppermute | solution.py:465
  38.3 1.6 %collective-permute-done.11 = bf16[168,128]{1,0:T(8,128)(2,1)S(1)} collective-permute-done((bf16[168,128]{1,0:T(8,128)(2,1)S(1)}, bf16[168,128]{1,0:T(8,128)(2,1)S(1)}, u32[]{:S(2)}, u32[]{:S(2)}) %collective-permute-start.11) | collective-permute-done | bytes 43040 | tf_op jit(solution)/shard_map/ppermute | solution.py:465
  39.9 0.4 collective-permute-done.10
  40.3 1.5 %collective-permute-done.9 = bf16[168,128]{1,0:T(8,128)(2,1)S(1)} collective-permute-done((bf16[168,128]{1,0:T(8,128)(2,1)S(1)}, bf16[168,128]{1,0:T(8,128)(2,1)S(1)}, u32[]{:S(2)}, u32[]{:S(2)}) %collective-permute-start.9) | collective-permute-done | bytes 43040 | tf_op jit(solution)/shard_map/ppermute | solution.py:465
  41.8 1.2 %collective-permute-start.14 = (bf16[168,128]{1,0:T(8,128)(2,1)S(1)}, bf16[168,128]{1,0:T(8,128)(2,1)S(1)}, u32[]{:S(2)}, u32[]{:S(2)}) collective-permute-start(bf16[168,128]{1,0:T(8,128)(2,1)S(1)} %add_convert_fusion.1), channel_id=1, source_target_pairs={{24,0},{28,4},{16,8},{20,12},{8,16},{12,20},{0,24},{4,28},{25,1},{... | collective-permute-start | bytes 129032 | tf_op jit(solution)/shard_map/ppermute | solution.py:465
  43.0 3.2 %collective-permute-start.12 = (bf16[168,128]{1,0:T(8,128)(2,1)S(1)}, bf16[168,128]{1,0:T(8,128)(2,1)S(1)}, u32[]{:S(2)}, u32[]{:S(2)}) collective-permute-start(bf16[168,128]{1,0:T(8,128)(2,1)S(1)} %add_convert_fusion.1), channel_id=1, source_target_pairs={{8,0},{12,4},{0,8},{4,12},{24,16},{28,20},{16,24},{20,28},{9,1},{1... | collective-permute-start | bytes 129032 | tf_op jit(solution)/shard_map/ppermute | solution.py:465
  46.3 1.4 %collective-permute-done.14 = bf16[168,128]{1,0:T(8,128)(2,1)S(1)} collective-permute-done((bf16[168,128]{1,0:T(8,128)(2,1)S(1)}, bf16[168,128]{1,0:T(8,128)(2,1)S(1)}, u32[]{:S(2)}, u32[]{:S(2)}) %collective-permute-start.14) | collective-permute-done | bytes 43040 | tf_op jit(solution)/shard_map/ppermute | solution.py:465
  47.7 1.0 %collective-permute-done.13 = bf16[168,128]{1,0:T(8,128)(2,1)S(1)} collective-permute-done((bf16[168,128]{1,0:T(8,128)(2,1)S(1)}, bf16[168,128]{1,0:T(8,128)(2,1)S(1)}, u32[]{:S(2)}, u32[]{:S(2)}) %collective-permute-start.13) | collective-permute-done | bytes 43040 | tf_op jit(solution)/shard_map/ppermute | solution.py:465
  48.8 0.7 %copy.21 = bf16[2,6,12,192]{3,0,2,1:T(2,128)(2,1)} copy(bf16[2,6,12,192]{3,2,1,0:T(8,128)(2,1)S(1)} %get-tuple-element.45) | data formatting | bytes 110592
  49.5 0.5 collective-permute-done.15.other
  50.0 0.8 %shard_map.197 = (f32[160,192]{1,0:T(8,128)}, f32[64,192]{1,0:T(8,128)}) custom-call(bf16[168,128]{1,0:T(8,128)(2,1)S(1)} %add_convert_fusion.mine, bf16[168,128]{1,0:T(8,128)(2,1)S(1)} %collective-permute-done.15.other), custom_call_target="tpu_custom_call" | custom-call | flops 1000000 | bytes 1000000 | tf_op jit(solution)/shard_map/pallas_call | solution.py:413
  (39 shorter events, 0.4 us)
Async XLA Ops:
  0.6 17.6 %copy-start.2 = (bf16[2,192,576]{2,1,0:T(8,128)(2,1)S(1)}, bf16[2,192,576]{2,1,0:T(8,128)(2,1)}, u32[]{:S(2)}) copy-start(bf16[2,192,576]{2,1,0:T(8,128)(2,1)} %refs_5_.5) | copy-start | bytes 1327108
  0.6 17.6 %copy-start.5 = (bf16[288,320]{1,0:T(8,128)(2,1)S(1)}, bf16[288,320]{1,0:T(8,128)(2,1)}, u32[]{:S(2)}) copy-start(bf16[288,320]{1,0:T(8,128)(2,1)} %constant.17.clone.refs_10_) | copy-start | bytes 552964
  0.7 17.6 %copy-start.7 = (bf16[168,144]{1,0:T(8,128)(2,1)S(1)}, bf16[168,144]{1,0:T(8,128)(2,1)}, u32[]{:S(2)}) copy-start(bf16[168,144]{1,0:T(8,128)(2,1)} %constant.18.clone.refs_11_) | copy-start | bytes 145156
  5.3 1.4 %collective-permute-start = (bf16[144,192]{1,0:T(8,128)(2,1)S(1)}, bf16[144,192]{1,0:T(8,128)(2,1)S(1)}, u32[]{:S(2)}, u32[]{:S(2)}) collective-permute-start(bf16[144,192]{1,0:T(8,128)(2,1)S(1)} %get-tuple-element.25), channel_id=1, source_target_pairs={{1,0},{0,1},{3,2},{2,3},{5,4},{4,5},{7,6},{6,7},{9,8},{8,9},{11,10... | collective-permute-start | bytes 165896 | tf_op jit(solution)/shard_map/ppermute | solution.py:440
  6.7 8.2 %copy-start.4 = (f32[2,1,1,6,3312]{4,2,3,1,0:T(1,128)S(1)}, f32[2,1,1,6,3312]{4,2,3,1,0:T(1,128)}, u32[]{:S(2)}) copy-start(f32[2,1,1,6,3312]{4,2,3,1,0:T(1,128)} %param.27) | copy-start | bytes 476932
  6.7 11.6 %copy-start.3 = (bf16[2,192,192]{2,1,0:T(8,128)(2,1)S(1)}, bf16[2,192,192]{2,1,0:T(8,128)(2,1)}, u32[]{:S(2)}) copy-start(bf16[2,192,192]{2,1,0:T(8,128)(2,1)} %refs_6_.5) | copy-start | bytes 442372
  6.7 9.1 %collective-permute-start.1 = (bf16[72,192]{1,0:T(8,128)(2,1)S(1)}, bf16[72,192]{1,0:T(8,128)(2,1)S(1)}, u32[]{:S(2)}, u32[]{:S(2)}) collective-permute-start(bf16[72,192]{1,0:T(8,128)(2,1)S(1)} %pad_maximum_fusion), channel_id=1, source_target_pairs={{6,0},{4,2},{10,4},{8,6},{14,8},{12,10},{18,12},{16,14},{22,16},{2... | collective-permute-start | bytes 82952 | tf_op jit(solution)/shard_map/ppermute | solution.py:440
  13.6 4.0 %collective-permute-start.2 = (bf16[72,192]{1,0:T(8,128)(2,1)S(1)}, bf16[72,192]{1,0:T(8,128)(2,1)S(1)}, u32[]{:S(2)}, u32[]{:S(2)}) collective-permute-start(bf16[72,192]{1,0:T(8,128)(2,1)S(1)} %pad_maximum_fusion.1), channel_id=1, source_target_pairs={{4,0},{8,4},{12,8},{16,12},{20,16},{24,20},{28,24},{0,28},{5,1},{9... | collective-permute-start | bytes 82952 | tf_op jit(solution)/shard_map/ppermute | solution.py:440
  14.2 4.0 %collective-permute-start.3 = (bf16[72,192]{1,0:T(8,128)(2,1)S(1)}, bf16[72,192]{1,0:T(8,128)(2,1)S(1)}, u32[]{:S(2)}, u32[]{:S(2)}) collective-permute-start(bf16[72,192]{1,0:T(8,128)(2,1)S(1)} %pad_maximum_fusion.2), channel_id=1, source_target_pairs={{2,0},{0,2},{3,1},{1,3},{6,4},{4,6},{7,5},{5,7},{10,8},{8,10},{11,... | collective-permute-start | bytes 82952 | tf_op jit(solution)/shard_map/ppermute | solution.py:440
  14.8 3.5 %copy-start = (bf16[2,192,768]{2,1,0:T(8,128)(2,1)S(1)}, bf16[2,192,768]{2,1,0:T(8,128)(2,1)}, u32[]{:S(2)}) copy-start(bf16[2,192,768]{2,1,0:T(8,128)(2,1)} %refs_7_.5) | copy-start | bytes 1769476
  14.8 3.5 %copy-start.1 = (bf16[2,768,192]{1,2,0:T(8,128)(2,1)S(1)}, bf16[2,768,192]{1,2,0:T(8,128)(2,1)}, u32[]{:S(2)}) copy-start(bf16[2,768,192]{1,2,0:T(8,128)(2,1)} %param.26) | copy-start | bytes 1769476
  14.9 3.4 %copy-start.9 = (f32[2,2,192]{2,1,0:T(2,128)S(1)}, f32[2,2,192]{2,1,0:T(2,128)}, u32[]{:S(2)}) copy-start(f32[2,2,192]{2,1,0:T(2,128)} %refs_4_.5) | copy-start | bytes 9220
  21.9 1.3 %collective-permute-start.4 = (bf16[72,192]{1,0:T(8,128)(2,1)S(1)}, bf16[72,192]{1,0:T(8,128)(2,1)S(1)}, u32[]{:S(2)}, u32[]{:S(2)}) collective-permute-start(bf16[72,192]{1,0:T(8,128)(2,1)S(1)} %get-tuple-element.30), channel_id=1, source_target_pairs={{1,0},{0,1},{3,2},{2,3},{5,4},{4,5},{7,6},{6,7},{9,8},{8,9},{11,10... | collective-permute-start | bytes 82952 | tf_op jit(solution)/shard_map/ppermute | solution.py:440
  23.2 8.1 %copy-start.6 = (bf16[192,144]{1,0:T(8,128)(2,1)S(1)}, bf16[192,144]{1,0:T(8,128)(2,1)}, u32[]{:S(2)}) copy-start(bf16[192,144]{1,0:T(8,128)(2,1)} %constant.20.clone.refs_16_) | copy-start | bytes 165892
  23.2 7.4 %collective-permute-start.5 = (bf16[36,192]{1,0:T(8,128)(2,1)S(1)}, bf16[36,192]{1,0:T(8,128)(2,1)S(1)}, u32[]{:S(2)}, u32[]{:S(2)}) collective-permute-start(bf16[36,192]{1,0:T(8,128)(2,1)S(1)} %pad_maximum_fusion.4), channel_id=1, source_target_pairs={{30,0},{28,2},{2,4},{0,6},{6,8},{4,10},{10,12},{8,14},{14,16},{12,... | collective-permute-start | bytes 41480 | tf_op jit(solution)/shard_map/ppermute | solution.py:440
  24.7 6.6 %copy-start.8 = (bf16[144,192]{1,0:T(8,128)(2,1)S(1)}, bf16[144,192]{1,0:T(8,128)(2,1)}, u32[]{:S(2)}) copy-start(bf16[144,192]{1,0:T(8,128)(2,1)} %constant.19.clone.refs_15_) | copy-start | bytes 165892
  24.7 6.5 %collective-permute-start.6 = (bf16[36,192]{1,0:T(8,128)(2,1)S(1)}, bf16[36,192]{1,0:T(8,128)(2,1)S(1)}, u32[]{:S(2)}, u32[]{:S(2)}) collective-permute-start(bf16[36,192]{1,0:T(8,128)(2,1)S(1)} %pad_maximum_fusion.5), channel_id=1, source_target_pairs={{28,0},{0,4},{4,8},{8,12},{12,16},{16,20},{20,24},{24,28},{29,1},{... | collective-permute-start | bytes 41480 | tf_op jit(solution)/shard_map/ppermute | solution.py:440
  24.9 6.4 %collective-permute-start.7 = (bf16[36,192]{1,0:T(8,128)(2,1)S(1)}, bf16[36,192]{1,0:T(8,128)(2,1)S(1)}, u32[]{:S(2)}, u32[]{:S(2)}) collective-permute-start(bf16[36,192]{1,0:T(8,128)(2,1)S(1)} %pad_maximum_fusion.6), channel_id=1, source_target_pairs={{2,0},{0,2},{3,1},{1,3},{6,4},{4,6},{7,5},{5,7},{10,8},{8,10},{11,... | collective-permute-start | bytes 41480 | tf_op jit(solution)/shard_map/ppermute | solution.py:440
  33.4 1.3 %collective-permute-start.8 = (bf16[168,128]{1,0:T(8,128)(2,1)S(1)}, bf16[168,128]{1,0:T(8,128)(2,1)S(1)}, u32[]{:S(2)}, u32[]{:S(2)}) collective-permute-start(bf16[168,128]{1,0:T(8,128)(2,1)S(1)} %get-tuple-element.42), channel_id=1, source_target_pairs={{1,0},{0,1},{3,2},{2,3},{5,4},{4,5},{7,6},{6,7},{9,8},{8,9},{11,10... | collective-permute-start | bytes 129032 | tf_op jit(solution)/shard_map/ppermute | solution.py:465
  34.7 5.1 %collective-permute-start.11 = (bf16[168,128]{1,0:T(8,128)(2,1)S(1)}, bf16[168,128]{1,0:T(8,128)(2,1)S(1)}, u32[]{:S(2)}, u32[]{:S(2)}) collective-permute-start(bf16[168,128]{1,0:T(8,128)(2,1)S(1)} %add_convert_fusion.2), channel_id=1, source_target_pairs={{6,0},{4,2},{2,4},{0,6},{14,8},{12,10},{10,12},{8,14},{22,16},{20,... | collective-permute-start | bytes 129032 | tf_op jit(solution)/shard_map/ppermute | solution.py:465
  34.8 5.5 %collective-permute-start.10 = (bf16[168,128]{1,0:T(8,128)(2,1)S(1)}, bf16[168,128]{1,0:T(8,128)(2,1)S(1)}, u32[]{:S(2)}, u32[]{:S(2)}) collective-permute-start(bf16[168,128]{1,0:T(8,128)(2,1)S(1)} %add_convert_fusion.2), channel_id=1, source_target_pairs={{4,0},{0,4},{12,8},{8,12},{20,16},{16,20},{28,24},{24,28},{5,1},{1... | collective-permute-start | bytes 129032 | tf_op jit(solution)/shard_map/ppermute | solution.py:465
  37.7 4.0 %collective-permute-start.9 = (bf16[168,128]{1,0:T(8,128)(2,1)S(1)}, bf16[168,128]{1,0:T(8,128)(2,1)S(1)}, u32[]{:S(2)}, u32[]{:S(2)}) collective-permute-start(bf16[168,128]{1,0:T(8,128)(2,1)S(1)} %add_convert_fusion.2), channel_id=1, source_target_pairs={{2,0},{0,2},{3,1},{1,3},{6,4},{4,6},{7,5},{5,7},{10,8},{8,10},{11,... | collective-permute-start | bytes 129032 | tf_op jit(solution)/shard_map/ppermute | solution.py:465
  41.8 5.9 %collective-permute-start.14 = (bf16[168,128]{1,0:T(8,128)(2,1)S(1)}, bf16[168,128]{1,0:T(8,128)(2,1)S(1)}, u32[]{:S(2)}, u32[]{:S(2)}) collective-permute-start(bf16[168,128]{1,0:T(8,128)(2,1)S(1)} %add_convert_fusion.1), channel_id=1, source_target_pairs={{24,0},{28,4},{16,8},{20,12},{8,16},{12,20},{0,24},{4,28},{25,1},{... | collective-permute-start | bytes 129032 | tf_op jit(solution)/shard_map/ppermute | solution.py:465
  43.0 5.7 %collective-permute-start.13 = (bf16[168,128]{1,0:T(8,128)(2,1)S(1)}, bf16[168,128]{1,0:T(8,128)(2,1)S(1)}, u32[]{:S(2)}, u32[]{:S(2)}) collective-permute-start(bf16[168,128]{1,0:T(8,128)(2,1)S(1)} %add_convert_fusion.1), channel_id=1, source_target_pairs={{16,0},{20,4},{24,8},{28,12},{0,16},{4,20},{8,24},{12,28},{17,1},{... | collective-permute-start | bytes 129032 | tf_op jit(solution)/shard_map/ppermute | solution.py:465
  43.0 5.7 %collective-permute-start.12 = (bf16[168,128]{1,0:T(8,128)(2,1)S(1)}, bf16[168,128]{1,0:T(8,128)(2,1)S(1)}, u32[]{:S(2)}, u32[]{:S(2)}) collective-permute-start(bf16[168,128]{1,0:T(8,128)(2,1)S(1)} %add_convert_fusion.1), channel_id=1, source_target_pairs={{8,0},{12,4},{0,8},{4,12},{24,16},{28,20},{16,24},{20,28},{9,1},{1... | collective-permute-start | bytes 129032 | tf_op jit(solution)/shard_map/ppermute | solution.py:465
  48.7 1.3 %collective-permute-start.15 = (bf16[168,128]{1,0:T(8,128)(2,1)S(1)}, bf16[168,128]{1,0:T(8,128)(2,1)S(1)}, u32[]{:S(2)}, u32[]{:S(2)}) collective-permute-start(bf16[168,128]{1,0:T(8,128)(2,1)S(1)} %add_convert_fusion.mine), channel_id=1, source_target_pairs={{1,0},{0,1},{3,2},{2,3},{5,4},{4,5},{7,6},{6,7},{9,8},{8,9},{11,10... | collective-permute-start | bytes 129032 | tf_op jit(solution)/shard_map/ppermute | solution.py:465
